TPU v7x, 32 devices: a whole 2x2x4 slice. The times are simulated.
32 devices in a mesh: dp: 8 (over z, core), fsdp: 4 (over y, x).
Axes of the slice: x: 2, y: 2, z: 4, core: 2. Of those that a mesh axis runs over, the one named last changes fastest.
Arguments:
- acts: bfloat16 [8192, 4096], P(('dp', 'fsdp')), may hold values from -6 to 6
- cotangent: bfloat16 [8192, 4096], P(('dp', 'fsdp')), may hold values from -0.3125 to 0.3125
- projector: bfloat16 [4096, 512], P('fsdp'), may hold values from -0.09375 to 0.09375
- first_moment: float32 [4096, 512], P('fsdp'), may hold values from -4 to 4
- second_moment: float32 [4096, 512], P('fsdp'), may hold values from 0.0005 to 0.005
Outputs:
- first_new: float32 [4096, 512], P('fsdp')
- second_new: float32 [4096, 512], P('fsdp')
- update: float32 [4096, 4096], P(None, 'fsdp')
All inputs are finite; a program needn't handle non-finite values.
Results may differ from a plain program's by a relative error of at most 0.017.
Values may be sent and summed in bfloat16 or wider, within the bound.
No kernel may reach another device: no remote copies, remote signals or barrier semaphores. Data moves between devices by JAX's collectives and lax.ppermute only.
A program may use at most 128 MiB of HBM per device.

v0:
```python
import jax
import jax.numpy as jnp
from jax import lax
from jax.sharding import PartitionSpec as P

STEP = 2


def on_device(acts, cotangent, projector, first_moment, second_moment):
    full_proj = lax.all_gather(projector, "fsdp", axis=0, tiled=True)
    coords = jnp.dot(acts, full_proj, preferred_element_type=jnp.float32).astype(jnp.bfloat16)
    grad_part = lax.psum_scatter(
        lax.dot_general(
            cotangent, coords, (((0,), (0,)), ((), ())), preferred_element_type=jnp.float32
        ).astype(jnp.bfloat16),
        "fsdp",
        scatter_dimension=0,
        tiled=True,
    ).astype(jnp.float32)
    grad_low = lax.psum(grad_part, "dp")
    first_new = 0.9 * first_moment + 0.1 * grad_low
    second_new = 0.999 * second_moment + 0.001 * grad_low * grad_low
    first_fix = 1.0 - 0.9**STEP
    second_fix = 1.0 - 0.999**STEP
    direction = (first_new / first_fix / (jnp.sqrt(second_new / second_fix) + 1e-08)).astype(
        jnp.bfloat16
    )
    update = lax.dot_general(
        full_proj, direction, (((1,), (1,)), ((), ())), preferred_element_type=jnp.float32
    )
    return (first_new, second_new, update)


def solution(mesh):
    in_specs = (
        P(("dp", "fsdp"), None),
        P(("dp", "fsdp"), None),
        P("fsdp", None),
        P("fsdp", None),
        P("fsdp", None),
    )
    out_specs = (P("fsdp", None), P("fsdp", None), P(None, "fsdp"))
    return jax.shard_map(
        on_device, mesh=mesh, in_specs=in_specs, out_specs=out_specs, check_vma=False
    )
```

profile of v0, /device:TPU:0, one launch (start us, length us, event | category | flops | bytes accessed | tf_op | source)
XLA Modules:
  0.0 240.1 jit_solution(9396510997291641849)
XLA Ops:
  7.2 0.0 copy-start
  7.2 0.0 all-gather.2.cloned.1.call-start
  7.2 0.7 all-gather.2.cloned.1.call-update
  7.9 0.0 reduce-scatter.2.cloned.1.call-start
  8.0 57.3 %all-gather.2.cloned.1.call-done = bf16[4096,512]{1,0:T(8,128)(2,1)} async-done(((bf16[1024,512]{1,0:T(8,128)(2,1)}), bf16[4096,512]{1,0:T(8,128)(2,1)}) %all-gather.2.cloned.1.call-update) | async-done | bytes 4194320 | tf_op jit(solution)/shard_map/all_gather | solution.py:10
  65.3 0.0 copy-done
  65.3 7.4 %fusion = bf16[4096,512]{0,1:T(8,128)(2,1)} fusion(bf16[256,4096]{1,0:T(8,128)(2,1)S(1)} %copy-done, bf16[256,4096]{1,0:T(8,128)(2,1)} %param.5, bf16[4096,512]{1,0:T(8,128)(2,1)} %all-gather.2.cloned.1.call-done), kind=kOutput, calls=%fused_computation.2 | convolution fusion | flops 2149711872 | bytes 12582912 | tf_op jit(solution)/shard_map/dot_general | solution.py:13
  72.7 0.0 reduce-scatter.2.cloned.1.call-update
  72.7 1.9 copy.8
  74.6 2.9 %copy.9 = f32[1024,512]{0,1:T(8,128)} copy(f32[1024,512]{1,0:T(8,128)} %param.9) | data formatting | bytes 4194304 | tf_op args[4]
  77.5 48.0 %reduce-scatter.2.cloned.1.call-done = bf16[1024,512]{0,1:T(8,128)(2,1)} async-done(((bf16[4096,512]{0,1:T(8,128)(2,1)}), bf16[1024,512]{0,1:T(8,128)(2,1)}) %reduce-scatter.2.cloned.1.call-update) | async-done | bytes 1048592 | tf_op jit(solution)/shard_map/reduce_scatter | solution.py:12
  125.5 64.9 %all-reduce.1 = f32[1024,512]{0,1:T(8,128)} all-reduce(bf16[1024,512]{0,1:T(8,128)(2,1)} %reduce-scatter.2.cloned.1.call-done), channel_id=1, replica_groups=mesh['dp'=8,'fsdp'=4] {'dp'}, use_global_device_ids=true, to_apply=%region_1.0 | all-reduce | flops 524288 | bytes 3145728 | tf_op jit(solution)/shard_map/psum | solution.py:20
  190.4 5.5 %fusion.1 = (f32[1024,512]{0,1:T(8,128)}, f32[1024,512]{0,1:T(8,128)}) fusion(f32[1024,512]{0,1:T(8,128)} %all-reduce.1, f32[1024,512]{0,1:T(8,128)} %copy.9, f32[1024,512]{0,1:T(8,128)S(1)} %copy.8), kind=kLoop, calls=%fused_computation.4 | loop fusion | flops 3670016 | bytes 10485760 | tf_op jit(solution)/shard_map/add | solution.py:22
  195.9 2.9 %copy.11 = f32[1024,512]{1,0:T(8,128)} copy(f32[1024,512]{0,1:T(8,128)} %get-tuple-element.6) | data formatting | bytes 4194304
  198.8 0.0 copy-start.2
  198.8 3.0 %copy.10 = f32[1024,512]{1,0:T(8,128)} copy(f32[1024,512]{0,1:T(8,128)} %get-tuple-element.7) | data formatting | bytes 4194304
  201.8 0.0 copy-done.2
  201.8 13.8 %convolution_bitcast_fusion = f32[4096,1024]{0,1:T(8,128)} fusion(bf16[4096,512]{1,0:T(8,128)(2,1)} %all-gather.2.cloned.1.call-done, f32[1024,512]{0,1:T(8,128)S(1)} %copy-done.2, f32[1024,512]{0,1:T(8,128)} %get-tuple-element.7), kind=kOutput, calls=%fused_computation | convolution fusion | flops 4297588736 | bytes 25165824 | tf_op jit(solution)/shard_map/dot_general | solution.py:28
  215.7 0.0 copy-start.1
  215.7 17.6 %copy.12 = f32[4096,1024]{1,0:T(8,128)} copy(f32[4096,1024]{0,1:T(8,128)} %convolution_bitcast_fusion) | data formatting | bytes 33554432
  233.2 0.0 copy-done.1
Async XLA Ops:
  7.2 58.1 %copy-start = (bf16[256,4096]{1,0:T(8,128)(2,1)S(1)}, bf16[256,4096]{1,0:T(8,128)(2,1)}, u32[]{:S(2)}) copy-start(bf16[256,4096]{1,0:T(8,128)(2,1)} %param.6) | copy-start | bytes 6291460
  7.2 58.1 %all-gather.2.cloned.1.call-start = ((), (), s32[]{:S(2)}) async-start(), calls=%async_computation.1 | async-start | bytes 5242880 | tf_op jit(solution)/shard_map/all_gather | solution.py:10
  7.9 117.6 %reduce-scatter.2.cloned.1.call-start = ((), (), s32[]{:S(2)}) async-start(), calls=%async_computation.2 | async-start | bytes 5242880 | tf_op jit(solution)/shard_map/reduce_scatter | solution.py:12
  198.8 3.0 %copy-start.2 = (f32[1024,512]{0,1:T(8,128)S(1)}, f32[1024,512]{0,1:T(8,128)}, u32[]{:S(2)}) copy-start(f32[1024,512]{0,1:T(8,128)} %get-tuple-element.6) | copy-start | bytes 6291460
  215.7 17.6 %copy-start.1 = (bf16[256,4096]{1,0:T(8,128)(2,1)S(1)}, bf16[256,4096]{1,0:T(8,128)(2,1)}, u32[]{:S(2)}) copy-start(bf16[256,4096]{1,0:T(8,128)(2,1)} %param.6) | copy-start | bytes 6291460
Sparse Core Ops, SparseCore 0:
  9.9 55.3 all-gather.1
  72.8 52.6 reduce-scatter.1
where the time goes:
time: 241 us; the launch traced here: 240 us
  waiting for transfers between devices  106 us (44%)
  blocking collectives  64.9 us (27%)
  local copies, waits for them, and re-layouts  28.3 us (12%)
  matrix products  21.2 us (9%)
  between operations  14.1 us (6%)
  other arithmetic  5.49 us (2%)
    psum x1, blocking collectives, on_device(): grad_low = lax.psum(grad_part, 'dp')  64.9 us
    all_gather x1, waiting for transfers between devices, on_device(): full_proj = lax.all_gather(projector, 'fsdp', axis=0, tiled=True)  57.3 us
    reduce_scatter x1, waiting for transfers between devices, on_device(): lax.psum_scatter(lax.dot_general(cotangent, coords, (((0,), (0,)), ((), (...  48 us
    unnamed x11, local copies, waits for them, and re-layouts  28.3 us
    dot_general x1, matrix products, on_device(): lax.dot_general(full_proj, direction, (((1,), (1,)), ((), ())), preferred...  13.8 us
    dot_general x1, matrix products, on_device(): lax.dot_general(cotangent, coords, (((0,), (0,)), ((), ())), preferred_el...  7.35 us
    add x1, other arithmetic, on_device(): second_new = 0.999 * second_moment + 0.001 * grad_low * grad_low  5.49 us
  transfers between devices with their start and end apart: 2, of which 2 were waited for; matrix products, arithmetic and copies ran while one was open for 2% of the time, Pallas kernels for 0%

commit v1 on v0

v1 whole, which is shorter than its diff:
```python
import functools

import jax
import jax.numpy as jnp
from jax import lax
from jax.experimental import pallas as pl
from jax.experimental.pallas import tpu as pltpu
from jax.sharding import PartitionSpec as P

STEP = 2
CORES = 2
CHUNKS = 2
MIB = 1024 * 1024
BF16 = jnp.bfloat16
F32 = jnp.float32


def cost(flops, bytes_accessed):
    return pl.CostEstimate(flops=flops, bytes_accessed=bytes_accessed, transcendentals=0)


def whole(array):
    zeros = (0,) * array.ndim
    return pl.BlockSpec(array.shape, lambda i, w: zeros)


def call(body, where, inputs, in_specs, out_shape, limit, scratch=(), name=None, estimate=None):
    return pl.pallas_call(
        body,
        out_shape=out_shape,
        grid_spec=pltpu.PrefetchScalarGridSpec(
            num_scalar_prefetch=1,
            grid=(1,),
            in_specs=in_specs,
            out_specs=[whole(x) for x in out_shape],
            scratch_shapes=scratch,
        ),
        compiler_params=pltpu.CompilerParams(vmem_limit_bytes=limit),
        cost_estimate=estimate,
        name=name,
    )(where, *inputs)


def own_columns(where, projector):
    rows, rank = projector.shape
    half = rank // CORES

    def body(w, x_ref, y_ref, sem):
        columns = pl.ds(pl.multiple_of(w[1] * half, half), half)
        copy = pltpu.make_async_copy(x_ref.at[:, columns], y_ref, sem)
        copy.start()
        copy.wait()

    return pl.pallas_call(
        body,
        out_shape=jax.ShapeDtypeStruct((rows, half), BF16),
        in_specs=[
            pl.BlockSpec(memory_space=pltpu.SMEM),
            pl.BlockSpec(memory_space=pltpu.HBM),
        ],
        out_specs=pl.BlockSpec(memory_space=pltpu.VMEM),
        scratch_shapes=[pltpu.SemaphoreType.DMA],
        compiler_params=pltpu.CompilerParams(vmem_limit_bytes=4 * MIB),
        cost_estimate=cost(0, 4 * rows * half),
        name="own_columns",
    )(where, projector)


def stage(where, acts, cots, proj, total, coords, terms, rows, last, name):
    tokens = cots[0].shape[0]
    half = proj[0][2].shape[1] if proj else coords.shape[0]
    inputs, specs, out_shape = [], [], []

    def add(array, spec):
        inputs.append(array)
        specs.append(spec)

    for s, low, block in proj:
        size = block.shape[0]
        at = functools.partial(
            lambda s, low, size, i, w: (0, ((w[0] ^ s) * rows + low) // size), s, low, size
        )
        for x in acts:
            add(x, pl.BlockSpec((tokens, size), at))
        add(block, whole(block))
    if total is not None:
        add(total, whole(total))
    if coords is not None:
        add(coords, whole(coords))
    for s, j, chunk, added, pieces, cuts in terms:
        at = functools.partial(
            lambda s, j, chunk, i, w: (0, (w[0] ^ s) * (rows // chunk) + j), s, j, chunk
        )
        for x in cots:
            add(x, pl.BlockSpec((tokens, chunk), at))
        for _, x in added:
            at = functools.partial(lambda j, i, w: (0, j), j if x.shape[1] > chunk else 0)
            add(x, pl.BlockSpec((x.shape[0], chunk), at))
    if last:
        out_shape.append(jax.ShapeDtypeStruct((half, 2 * tokens), BF16))
    elif proj:
        out_shape.append(jax.ShapeDtypeStruct((2 * tokens, half), F32))
    widest = 128
    for _, _, chunk, _, pieces, cuts in terms:
        widest = max(widest, chunk)
        for a, b in cuts:
            out_shape += [jax.ShapeDtypeStruct((b - a, chunk // pieces), BF16)] * pieces

    def body(w, *refs):
        ins = iter(refs[: len(inputs)])
        outs = iter(refs[len(inputs) : len(inputs) + len(out_shape)])
        value = refs[-1]
        if proj:
            sums = [None, None]
            for _ in proj:
                a, b, block = next(ins), next(ins), next(ins)
                for t, x in enumerate((a, b)):
                    part = jnp.dot(x[...], block[...], preferred_element_type=F32)
                    sums[t] = part if sums[t] is None else sums[t] + part
            if total is not None:
                before = next(ins)
                sums = [x + before[t * tokens : (t + 1) * tokens, :] for t, x in enumerate(sums)]
            out = next(outs)
            for t, x in enumerate(sums):
                span = slice(t * tokens, (t + 1) * tokens)
                if last:
                    out[:, span] = x.T.astype(BF16)
                else:
                    out[span, :] = x
            coords_ref = out
        if coords is not None:
            coords_ref = next(ins)
        for _, _, chunk, added, pieces, cuts in terms:
            a, b = next(ins), next(ins)
            term = jnp.dot(coords_ref[:, :tokens], a[...], preferred_element_type=F32)
            term += jnp.dot(coords_ref[:, tokens:], b[...], preferred_element_type=F32)
            value[:, :chunk] = term
            for low, x in added:
                ref = next(ins)
                value[low : low + x.shape[0], :chunk] += ref[...].astype(F32)
            size = chunk // pieces
            for a, b in cuts:
                for k in range(pieces):
                    at = 0
                    if pieces > 1:
                        at = pl.multiple_of(lax.rem(w[2] + k, pieces) * size, size)
                    next(outs)[...] = value[a:b, pl.ds(at, size)].astype(BF16)

    flops = sum(4 * tokens * half * x[2].shape[0] for x in proj)
    flops += sum(4 * tokens * half * x[2] for x in terms)
    return call(
        body,
        where,
        inputs,
        specs,
        out_shape,
        20 * MIB,
        scratch=[pltpu.VMEM((half, widest), F32)],
        name=name,
        estimate=cost(flops, flops // (2 * half)),
    )


def assemble(where, projector, own, other, rows):
    half = own[0][2].shape[1]
    parts = sum(x[2].shape[0] for x in own) // rows
    inputs = [projector] + [x for _, _, x in own + other]

    def body(w, *refs):
        ins, out = refs[:-1], refs[-1]
        out[pl.ds(pl.multiple_of(w[0] * rows, rows), rows), :] = ins[0][...]
        blocks = ins[1:]
        for n, (s, low, x) in enumerate(own):
            if s == 0:
                continue
            size = x.shape[0]
            at = pl.ds(pl.multiple_of((w[0] ^ s) * rows + low, size), size)
            mine, others = blocks[n], blocks[len(own) + n]

            @pl.when(w[1] == 0)
            def _():
                out[at, :half] = mine[...]
                out[at, half:] = others[...]

            @pl.when(w[1] != 0)
            def _():
                out[at, :half] = others[...]
                out[at, half:] = mine[...]

    shape = (parts * rows, 2 * half)
    return call(
        body,
        where,
        inputs,
        [whole(x) for x in inputs],
        [jax.ShapeDtypeStruct(shape, BF16)],
        28 * MIB,
        name="assemble",
        estimate=cost(0, 8 * parts * rows * half),
    )[0]


def update_step(where, j, k, pieces, own_grad, other_grad, proj, first, second, before):
    half, chunk = own_grad.shape
    rank = CORES * half
    features = first.shape[0]
    width = proj.shape[0]
    rows = min(512, width)

    def column(w):
        return j * pieces + lax.rem(w[2] + pieces - k, pieces)

    moment_block = pl.BlockSpec((chunk, rank), lambda i, w: (column(w), 0))

    def body(w, own_ref, other_ref, proj_ref, first_ref, second_ref, *refs):
        first_out, second_out, update, grad, direction = refs[-5:]

        @pl.when(pl.program_id(0) == 0)
        def _():
            at = pl.multiple_of(w[1] * half, half)
            grad[pl.ds(at, half), :] = own_ref[...].astype(F32)
            at = pl.multiple_of((1 - w[1]) * half, half)
            grad[pl.ds(at, half), :] = other_ref[...].astype(F32)
            grad_low = grad[...].T
            first_new = 0.9 * first_ref[...] + 0.1 * grad_low
            second_new = 0.999 * second_ref[...] + 0.001 * grad_low * grad_low
            first_out[...] = first_new
            second_out[...] = second_new
            first_fix = 1.0 - 0.9**STEP
            second_fix = 1.0 - 0.999**STEP
            ratio = first_new / first_fix / (jnp.sqrt(second_new / second_fix) + 1e-08)
            direction[...] = ratio.T.astype(BF16)

        update[...] = jnp.dot(proj_ref[...], direction[...], preferred_element_type=F32)

    inputs = [own_grad, other_grad, proj, first, second]
    in_specs = [whole(own_grad), whole(other_grad)]
    in_specs += [pl.BlockSpec((rows, rank), lambda i, w: (i, 0)), moment_block, moment_block]
    aliases = {}
    if before is not None:
        aliases = {1 + len(inputs) + n: n for n in range(3)}
        inputs += before
        in_specs += [pl.BlockSpec(memory_space=pl.ANY)] * 3
    return pl.pallas_call(
        body,
        out_shape=[
            jax.ShapeDtypeStruct(first.shape, F32),
            jax.ShapeDtypeStruct(second.shape, F32),
            jax.ShapeDtypeStruct((width, features), F32),
        ],
        grid_spec=pltpu.PrefetchScalarGridSpec(
            num_scalar_prefetch=1,
            grid=(width // rows,),
            in_specs=in_specs,
            out_specs=[moment_block, moment_block]
            + [pl.BlockSpec((rows, chunk), lambda i, w: (i, column(w)))],
            scratch_shapes=[pltpu.VMEM((rank, chunk), F32), pltpu.VMEM((rank, chunk), BF16)],
        ),
        input_output_aliases=aliases,
        compiler_params=pltpu.CompilerParams(vmem_limit_bytes=20 * MIB),
        cost_estimate=cost(2 * width * rank * chunk, 4 * width * chunk + 18 * chunk * rank),
        name="update_step",
    )(where, *inputs)


def add_up(arrays):
    return functools.reduce(jnp.add, [x.astype(F32) for x in arrays]).astype(BF16)


def on_device(dp, fsdp, acts, cotangent, projector, first_moment, second_moment):
    rows, rank = projector.shape
    half = rank // CORES
    groups = dp // CORES
    chunks = CHUNKS if rows % (256 * CHUNKS) == 0 else 1
    chunk = rows // chunks
    pieces = 2 if groups % 2 == 0 and chunk % 256 == 0 else 1
    fsdp_at = lax.axis_index("fsdp")
    dp_at = lax.axis_index("dp")
    where = jnp.stack([fsdp_at, dp_at % CORES, (dp_at // CORES) % pieces]).astype(jnp.int32)

    def to_core(x):
        return lax.ppermute(x, "dp", [(i, i ^ 1) for i in range(dp)])

    def to_fsdp(x, s):
        return lax.ppermute(x, "fsdp", [(i, i ^ s) for i in range(fsdp)])

    def to_piece(x, k):
        pairs = []
        for i in range(dp):
            group, core = divmod(i, CORES)
            base = group - group % pieces
            pairs.append((i, (base + (group + k) % pieces) * CORES + core))
        return lax.ppermute(x, "dp", pairs)

    def to_base(x, k):
        return lax.ppermute(x, "dp", [(i, (i + k * pieces * CORES) % dp) for i in range(dp)])

    def links(s):
        return (s & -s, 1 << (s.bit_length() - 1))

    levels = [
        [s for s in range(fsdp) if s.bit_count() == n] for n in range(fsdp.bit_length())
    ]

    own_half = own_columns(where, projector)
    held = {0: [(0, 0, own_half)]}
    for level in levels[1:]:
        for s in level:
            if s.bit_count() == 1:
                held[s] = [(s, 0, to_fsdp(own_half, s))]
                continue
            held[s] = []
            for n, link in enumerate(links(s)):
                source = held[s ^ link]
                low = n * rows // 2
                if len(source) == 1:
                    part = source[0][2][low : low + rows // 2]
                else:
                    part = source[n][2]
                held[s].append((s, low, to_fsdp(part, link)))
    acts_pair = [acts, to_core(acts)]
    cots_pair = [cotangent, to_core(cotangent)]

    run = functools.partial(stage, where, acts_pair, cots_pair, rows=rows)
    far = levels[-1][0]
    middle = half // 2
    halves = [(0, middle), (middle, half)]
    total = None
    for n, level in enumerate(levels[:-1]):
        entries = [x for s in level for x in held[s]]
        (total,) = run(entries, total, None, [], last=False, name=f"coords_{n}")
    coords, *far_terms = run(
        held[far], total, None, [(far, 0, rows, [], 1, halves)], last=True, name="coords_last"
    )

    landed = {s: [] for s in range(fsdp)}
    for level in reversed(levels[2:]):
        outs = far_terms
        if level != levels[-1]:
            entries = [(s, 0, rows, landed[s], 1, halves) for s in level]
            outs = run([], None, coords, entries, last=False, name="terms_far")
        outs = iter(outs)
        for s in level:
            for n, link in enumerate(links(s)):
                landed[s ^ link].append((n * middle, to_fsdp(next(outs), link)))

    grads = []
    for j in range(chunks):
        entries = [(s, j, chunk, landed[s], 1, [(0, half)]) for s in levels[1]]
        outs = run([], None, coords, entries, last=False, name=f"terms_near_{j}")
        added = [(0, to_fsdp(x, s)) for s, x in zip(levels[1], outs)]
        entries = [(0, j, chunk, added, pieces, [(0, half)])]
        outs = run([], None, coords, entries, last=False, name=f"terms_own_{j}")
        mine = outs[0]
        for k in range(1, pieces):
            mine = add_up([mine, to_piece(outs[k], k)])
        mine = add_up([mine] + [to_base(mine, k) for k in range(1, groups // pieces)])
        own_grad = [mine] + [to_piece(mine, k) for k in range(1, pieces)]
        grads.append((own_grad, [to_core(x) for x in own_grad]))

    own = [x for s in range(fsdp) for x in held[s]]
    other = [(s, low, x if s == 0 else to_core(x)) for s, low, x in own]
    proj = assemble(where, projector, own, other, rows)
    outputs = None
    for j, pair in enumerate(grads):
        for k, (mine, others) in enumerate(zip(*pair)):
            outputs = update_step(
                where, j, k, pieces, mine, others, proj, first_moment, second_moment, outputs
            )
    return tuple(outputs)


def solution(mesh):
    in_specs = (
        P(("dp", "fsdp"), None),
        P(("dp", "fsdp"), None),
        P("fsdp", None),
        P("fsdp", None),
        P("fsdp", None),
    )
    out_specs = (P("fsdp", None), P("fsdp", None), P(None, "fsdp"))
    body = functools.partial(on_device, mesh.shape["dp"], mesh.shape["fsdp"])
    return jax.shard_map(body, mesh=mesh, in_specs=in_specs, out_specs=out_specs, check_vma=False)
```

time: 241 us -> 106 us (0.44)
  waiting for transfers between devices: 106 us -> 37.2 us
  blocking collectives: 64.9 us -> 0 us
  Pallas kernels: 0 us -> 36.9 us
  starting transfers between devices: 0.08 us -> 29.5 us
  local copies, waits for them, and re-layouts: 28.3 us -> 1.42 us
  matrix products: 21.2 us -> 0 us
  between operations: 14.1 us -> 0.82 us
  other arithmetic: 5.49 us -> 0.21 us
    psum x1 -> x0, blocking collectives: 64.9 us -> none  [on_device(): grad_low = lax.psum(grad_part, 'dp')]
    all_gather x1 -> x0, waiting for transfers between devices: 57.3 us -> none  [on_device(): full_proj = lax.all_gather(projector, 'fsdp', axis=0, tiled=True)]
    reduce_scatter x1 -> x0, waiting for transfers between devices: 48 us -> none  [on_device(): lax.psum_scatter(lax.dot_general(cotangent, coords, (((0,), (0,)), ((), (...]
    ppermute x0 -> x26, waiting for transfers between devices: none -> 37.2 us  [the longest x10 20.6 us: to_fsdp(): return lax.ppermute(x, 'fsdp', [(i, i ^ s) for i in range(fsdp)])]
    pallas_call x0 -> x13, Pallas kernels: none -> 36.9 us  [the longest x4 24.4 us: update_step(): pl.pallas_call(body, out_shape=[jax.ShapeDtypeStruct(first.shape, F32), j...]
    ppermute x0 -> x26, starting transfers between devices: none -> 29.5 us  [the longest x10 14.1 us: to_fsdp(): return lax.ppermute(x, 'fsdp', [(i, i ^ s) for i in range(fsdp)])]
    unnamed x11 -> x10, local copies, waits for them, and re-layouts: 28.3 us -> 1.38 us
    dot_general x2 -> x0, matrix products: 21.2 us -> none  [the longest x1 13.8 us: on_device(): lax.dot_general(full_proj, direction, (((1,), (1,)), ((), ())), preferred...]
  transfers between devices with their start and end apart: 2 -> 26, of which waited for: 2 -> 12; matrix products, arithmetic and copies ran while one was open for 2% -> 0% of each run, Pallas kernels for 0% -> 26%
where the time goes in v1:
time: 106 us
  waiting for transfers between devices  37.2 us (35%)
  Pallas kernels  36.9 us (35%)
  starting transfers between devices  29.5 us (28%)
  local copies, waits for them, and re-layouts  1.42 us (1%)
    pallas_call x4, Pallas kernels, update_step(): pl.pallas_call(body, out_shape=[jax.ShapeDtypeStruct(first.shape, F32), j...  24.4 us
    ppermute x10, waiting for transfers between devices, to_fsdp(): return lax.ppermute(x, 'fsdp', [(i, i ^ s) for i in range(fsdp)])  20.6 us
    ppermute x10, starting transfers between devices, to_fsdp(): return lax.ppermute(x, 'fsdp', [(i, i ^ s) for i in range(fsdp)])  14.1 us
    pallas_call x8, Pallas kernels, call(): pl.pallas_call(body, out_shape=out_shape, grid_spec=pltpu.PrefetchScalarG...  11.9 us
    ppermute x2, waiting for transfers between devices, to_base(): lax.ppermute(x, 'dp', [(i, (i + k * pieces * CORES) % dp) for i in range(...  8.41 us
    ppermute x4, starting transfers between devices, to_piece(): return lax.ppermute(x, 'dp', pairs)  8.35 us
    ppermute x4, waiting for transfers between devices, to_piece(): return lax.ppermute(x, 'dp', pairs)  8.14 us
    ppermute x2, starting transfers between devices, to_base(): lax.ppermute(x, 'dp', [(i, (i + k * pieces * CORES) % dp) for i in range(...  4.72 us
  transfers between devices with their start and end apart: 26, of which 12 were waited for; matrix products, arithmetic and copies ran while one was open for 0% of the time, Pallas kernels for 26%

profile of v1, /device:TPU:0, one launch (start us, length us, event | category | flops | bytes accessed | tf_op | source)
XLA Modules:
  0.0 106.0 jit_solution(5422688569793110877)
XLA Ops:
  3.3 3.0 %collective-permute-start.3 = (bf16[1024,256]{1,0:T(8,128)(2,1)S(1)}, bf16[1024,256]{1,0:T(8,128)(2,1)S(1)}, u32[]{:S(2)}, u32[]{:S(2)}) collective-permute-start(bf16[1024,256]{1,0:T(8,128)(2,1)S(1)} %own_columns.1.refs_2_.refs_1_.refs_6_), channel_id=1, source_target_pairs={{0,1},{1,0},{2,3},{3,2},{4,5},{5,4},{6,7},{7,6},{8,9},{9,8},{10,11... | collective-permute-start | bytes 1572872 | tf_op jit(solution)/shard_map/ppermute | solution.py:285
  6.2 1.5 %collective-permute-start.1 = (bf16[1024,256]{1,0:T(8,128)(2,1)S(1)}, bf16[1024,256]{1,0:T(8,128)(2,1)S(1)}, u32[]{:S(2)}, u32[]{:S(2)}) collective-permute-start(bf16[1024,256]{1,0:T(8,128)(2,1)S(1)} %own_columns.1.refs_2_.refs_1_.refs_6_), channel_id=1, source_target_pairs={{0,2},{1,3},{2,0},{3,1},{4,6},{5,7},{6,4},{7,5},{8,10},{9,11},{10,... | collective-permute-start | bytes 1572872 | tf_op jit(solution)/shard_map/ppermute | solution.py:285
  7.8 10.6 %collective-permute-done.3.refs_2_ = bf16[1024,256]{1,0:T(8,128)(2,1)S(1)} collective-permute-done((bf16[1024,256]{1,0:T(8,128)(2,1)S(1)}, bf16[1024,256]{1,0:T(8,128)(2,1)S(1)}, u32[]{:S(2)}, u32[]{:S(2)}) %collective-permute-start.3) | collective-permute-done | bytes 524320 | tf_op jit(solution)/shard_map/ppermute | solution.py:285
  18.4 1.8 %collective-permute-start.4 = (bf16[512,256]{1,0:T(8,128)(2,1)S(1)}, bf16[512,256]{1,0:T(8,128)(2,1)S(1)}, u32[]{:S(2)}, u32[]{:S(2)}) collective-permute-start(bf16[512,256]{1,0:T(8,128)(2,1)S(1)} %slice.9), channel_id=1, source_target_pairs={{0,2},{1,3},{2,0},{3,1},{4,6},{5,7},{6,4},{7,5},{8,10},{9,11},{10,... | collective-permute-start | bytes 786440 | tf_op jit(solution)/shard_map/ppermute | solution.py:285
  20.3 1.6 %collective-permute-start.2 = (bf16[512,256]{1,0:T(8,128)(2,1)S(1)}, bf16[512,256]{1,0:T(8,128)(2,1)S(1)}, u32[]{:S(2)}, u32[]{:S(2)}) collective-permute-start(bf16[512,256]{1,0:T(8,128)(2,1)S(1)} %slice.8), channel_id=1, source_target_pairs={{0,1},{1,0},{2,3},{3,2},{4,5},{5,4},{6,7},{7,6},{8,9},{9,8},{10,11... | collective-permute-start | bytes 786440 | tf_op jit(solution)/shard_map/ppermute | solution.py:285
  21.9 2.1 %coords_0.1.refs_6_ = f32[512,256]{1,0:T(8,128)S(1)} custom-call(s32[3]{0:T(128)S(1)} %pad_add_fusion.w, bf16[256,4096]{1,0:T(8,128)(2,1)S(1)} %copy-done.1, bf16[256,4096]{1,0:T(8,128)(2,1)} %collective-permute-done.refs_1_.refs_4_, bf16[1024,256]{1,0:T(8,128)(2,1)S(1)} %own_columns.1.refs_2_.refs_1_.refs_6_), custom_call_target="tpu_custom_call" | custom-call | flops 268435456 | bytes 524288 | tf_op jit(solution)/shard_map/coords_0/pallas_call | solution.py:28
  23.9 2.5 %coords_1.1.refs_6_ = f32[512,256]{1,0:T(8,128)S(1)} custom-call(s32[3]{0:T(128)S(1)} %pad_add_fusion.w, bf16[256,4096]{1,0:T(8,128)(2,1)S(1)} %copy-done.1, bf16[256,4096]{1,0:T(8,128)(2,1)} %collective-permute-done.refs_1_.refs_4_, bf16[1024,256]{1,0:T(8,128)(2,1)S(1)} %collective-permute-done.3.refs_2_, bf16[256,4096]{1,0:T(8,128)(2,1)S(1)} %copy-done.1, ...), custom_call_target="tpu_custom_call" | custom-call | flops 536870912 | bytes 1048576 | tf_op jit(solution)/shard_map/coords_1/pallas_call | solution.py:28
  27.5 2.5 %coords_last.1 = (bf16[256,512]{1,0:T(8,128)(2,1)S(1)}, bf16[128,1024]{1,0:T(8,128)(2,1)S(1)}, bf16[128,1024]{1,0:T(8,128)(2,1)S(1)}) custom-call(s32[3]{0:T(128)S(1)} %pad_add_fusion.w, bf16[256,4096]{1,0:T(8,128)(2,1)S(1)} %copy-done.1, bf16[256,4096]{1,0:T(8,128)(2,1)} %collective-permute-done.refs_1_.refs_4_, ...), custom_call_target="tpu_custom_call" | custom-call | flops 536870912 | bytes 1048576 | tf_op jit(solution)/shard_map/coords_last/pallas_call | solution.py:28
  32.1 4.4 %collective-permute-done.6.refs_3_ = bf16[128,1024]{1,0:T(8,128)(2,1)S(1)} collective-permute-done((bf16[128,1024]{1,0:T(8,128)(2,1)S(1)}, bf16[128,1024]{1,0:T(8,128)(2,1)S(1)}, u32[]{:S(2)}, u32[]{:S(2)}) %collective-permute-start.6) | collective-permute-done | bytes 262176 | tf_op jit(solution)/shard_map/ppermute | solution.py:285
  39.5 1.5 %collective-permute-start.20 = (bf16[256,512]{1,0:T(8,128)(2,1)S(1)}, bf16[256,512]{1,0:T(8,128)(2,1)S(1)}, u32[]{:S(2)}, u32[]{:S(2)}) collective-permute-start(bf16[256,512]{1,0:T(8,128)(2,1)S(1)} %get-tuple-element.31), channel_id=1, source_target_pairs={{0,2},{1,3},{2,0},{3,1},{4,6},{5,7},{6,4},{7,5},{8,10},{9,11},{10,... | collective-permute-start | bytes 786440 | tf_op jit(solution)/shard_map/ppermute | solution.py:285
  43.7 2.9 %collective-permute-done.19.refs_3_ = bf16[256,512]{1,0:T(8,128)(2,1)S(1)} collective-permute-done((bf16[256,512]{1,0:T(8,128)(2,1)S(1)}, bf16[256,512]{1,0:T(8,128)(2,1)S(1)}, u32[]{:S(2)}, u32[]{:S(2)}) %collective-permute-start.19) | collective-permute-done | bytes 262176 | tf_op jit(solution)/shard_map/ppermute | solution.py:285
  48.1 1.6 %collective-permute-start.21 = (bf16[256,256]{1,0:T(8,128)(2,1)S(1)}, bf16[256,256]{1,0:T(8,128)(2,1)S(1)}, u32[]{:S(2)}, u32[]{:S(2)}) collective-permute-start(bf16[256,256]{1,0:T(8,128)(2,1)S(1)} %get-tuple-element.33), channel_id=1, source_target_pairs={{0,8},{4,12},{8,0},{12,4},{16,24},{20,28},{24,16},{28,20},{1,9},{5... | collective-permute-start | bytes 393224 | tf_op jit(solution)/shard_map/ppermute | solution.py:293
  53.2 1.6 %collective-permute-start.10 = (bf16[256,256]{1,0:T(8,128)(2,1)S(1)}, bf16[256,256]{1,0:T(8,128)(2,1)S(1)}, u32[]{:S(2)}, u32[]{:S(2)}) collective-permute-start(bf16[256,256]{1,0:T(8,128)(2,1)S(1)} %get-tuple-element.29), channel_id=1, source_target_pairs={{0,8},{4,12},{8,0},{12,4},{16,24},{20,28},{24,16},{28,20},{1,9},{5... | collective-permute-start | bytes 393224 | tf_op jit(solution)/shard_map/ppermute | solution.py:293
  54.8 3.4 %collective-permute-done.10 = bf16[256,256]{1,0:T(8,128)(2,1)S(1)} collective-permute-done((bf16[256,256]{1,0:T(8,128)(2,1)S(1)}, bf16[256,256]{1,0:T(8,128)(2,1)S(1)}, u32[]{:S(2)}, u32[]{:S(2)}) %collective-permute-start.10) | collective-permute-done | bytes 131104 | tf_op jit(solution)/shard_map/ppermute | solution.py:293
  58.1 2.9 %collective-permute-start.22 = (bf16[256,256]{1,0:T(8,128)(2,1)S(1)}, bf16[256,256]{1,0:T(8,128)(2,1)S(1)}, u32[]{:S(2)}, u32[]{:S(2)}) collective-permute-start(bf16[256,256]{1,0:T(8,128)(2,1)S(1)} %add_convert_fusion.1), channel_id=1, source_target_pairs={{0,16},{4,20},{8,24},{12,28},{16,0},{20,4},{24,8},{28,12},{1,17},{... | collective-permute-start | bytes 393224 | tf_op jit(solution)/shard_map/ppermute | solution.py:296
  61.1 4.4 %collective-permute-done.22 = bf16[256,256]{1,0:T(8,128)(2,1)S(1)} collective-permute-done((bf16[256,256]{1,0:T(8,128)(2,1)S(1)}, bf16[256,256]{1,0:T(8,128)(2,1)S(1)}, u32[]{:S(2)}, u32[]{:S(2)}) %collective-permute-start.22) | collective-permute-done | bytes 131104 | tf_op jit(solution)/shard_map/ppermute | solution.py:296
  65.4 1.8 %collective-permute-start.11 = (bf16[256,256]{1,0:T(8,128)(2,1)S(1)}, bf16[256,256]{1,0:T(8,128)(2,1)S(1)}, u32[]{:S(2)}, u32[]{:S(2)}) collective-permute-start(bf16[256,256]{1,0:T(8,128)(2,1)S(1)} %add_convert_fusion.3), channel_id=1, source_target_pairs={{0,16},{4,20},{8,24},{12,28},{16,0},{20,4},{24,8},{28,12},{1,17},{... | collective-permute-start | bytes 393224 | tf_op jit(solution)/shard_map/ppermute | solution.py:296
  67.3 4.1 %collective-permute-done.11 = bf16[256,256]{1,0:T(8,128)(2,1)S(1)} collective-permute-done((bf16[256,256]{1,0:T(8,128)(2,1)S(1)}, bf16[256,256]{1,0:T(8,128)(2,1)S(1)}, u32[]{:S(2)}, u32[]{:S(2)}) %collective-permute-start.11) | collective-permute-done | bytes 131104 | tf_op jit(solution)/shard_map/ppermute | solution.py:296
  71.3 5.1 %collective-permute-start.23 = (bf16[256,256]{1,0:T(8,128)(2,1)S(1)}, bf16[256,256]{1,0:T(8,128)(2,1)S(1)}, u32[]{:S(2)}, u32[]{:S(2)}) collective-permute-start(bf16[256,256]{1,0:T(8,128)(2,1)S(1)} %add_convert_fusion.own_ref), channel_id=1, source_target_pairs={{0,8},{4,12},{8,0},{12,4},{16,24},{20,28},{24,16},{28,20},{1,9},{5... | collective-permute-start | bytes 393224 | tf_op jit(solution)/shard_map/ppermute | solution.py:293
  76.6 2.7 %collective-permute-done.23.own_ref = bf16[256,256]{1,0:T(8,128)(2,1)S(1)} collective-permute-done((bf16[256,256]{1,0:T(8,128)(2,1)S(1)}, bf16[256,256]{1,0:T(8,128)(2,1)S(1)}, u32[]{:S(2)}, u32[]{:S(2)}) %collective-permute-start.23) | collective-permute-done | bytes 131104 | tf_op jit(solution)/shard_map/ppermute | solution.py:293
  81.5 6.1 %update_step.4 = (f32[1024,512]{1,0:T(8,128)}, f32[1024,512]{1,0:T(8,128)}, f32[4096,1024]{1,0:T(8,128)}) custom-call(s32[3]{0:T(128)S(1)} %pad_add_fusion.w, bf16[256,256]{1,0:T(8,128)(2,1)S(1)} %add_convert_fusion.own_ref, bf16[256,256]{1,0:T(8,128)(2,1)S(1)} %collective-permute-done.25.other_ref, bf16[4096,512]{1,0:T(8,128)(2,1)S(1)} %assemble.1.proj_ref, ...), custom_call_target="tpu_custom_call" | custom-call | flops 1073741824 | bytes 6553600 | tf_op jit(solution)/shard_map/update_step/pallas_call | solution.py:244
  87.6 6.1 %update_step.5 = (f32[1024,512]{1,0:T(8,128)}, f32[1024,512]{1,0:T(8,128)}, f32[4096,1024]{1,0:T(8,128)}) custom-call(s32[3]{0:T(128)S(1)} %pad_add_fusion.w, bf16[256,256]{1,0:T(8,128)(2,1)S(1)} %collective-permute-done.23.own_ref, ...), custom_call_target="tpu_custom_call", output_to_operand_aliasing={{0}: (6, {}), {1}: (7, {}), {2}: (8, {})} | custom-call | flops 1073741824 | bytes 6553600 | tf_op jit(solution)/shard_map/update_step/pallas_call | solution.py:244
  93.8 6.1 %update_step.6 = (f32[1024,512]{1,0:T(8,128)}, f32[1024,512]{1,0:T(8,128)}, f32[4096,1024]{1,0:T(8,128)}) custom-call(s32[3]{0:T(128)S(1)} %pad_add_fusion.w, bf16[256,256]{1,0:T(8,128)(2,1)S(1)} %add_convert_fusion.2.own_ref, bf16[256,256]{1,0:T(8,128)(2,1)S(1)} %collective-permute-done.18.other_ref, ...), custom_call_target="tpu_custom_call", output_to_operand_aliasing={{0}: (6, {}), {1}: (7, {}), {2}: (8, {})} | custom-call | flops 1073741824 | bytes 6553600 | tf_op jit(solution)/shard_map/update_step/pallas_call | solution.py:244
  99.9 6.1 %update_step.7 = (f32[1024,512]{1,0:T(8,128)}, f32[1024,512]{1,0:T(8,128)}, f32[4096,1024]{1,0:T(8,128)}) custom-call(s32[3]{0:T(128)S(1)} %pad_add_fusion.w, bf16[256,256]{1,0:T(8,128)(2,1)S(1)} %collective-permute-done.12.own_ref, ...), custom_call_target="tpu_custom_call", output_to_operand_aliasing={{0}: (6, {}), {1}: (7, {}), {2}: (8, {})} | custom-call | flops 1073741824 | bytes 6553600 | tf_op jit(solution)/shard_map/update_step/pallas_call | solution.py:244
  (58 shorter events, 18.8 us)
Async XLA Ops:
  0.6 21.2 %collective-permute-start = (bf16[256,4096]{1,0:T(8,128)(2,1)}, bf16[256,4096]{1,0:T(8,128)(2,1)}, u32[]{:S(2)}, u32[]{:S(2)}) collective-permute-start(bf16[256,4096]{1,0:T(8,128)(2,1)} %refs_3_.3), channel_id=1, source_target_pairs={{0,4},{4,0},{8,12},{12,8},{16,20},{20,16},{24,28},{28,24},{1,5},{5... | collective-permute-start | bytes 6291464 | tf_op jit(solution)/shard_map/ppermute | solution.py:282
  1.1 26.4 %collective-permute-start.5 = (bf16[256,4096]{1,0:T(8,128)(2,1)}, bf16[256,4096]{1,0:T(8,128)(2,1)S(1)}, u32[]{:S(2)}, u32[]{:S(2)}) collective-permute-start(bf16[256,4096]{1,0:T(8,128)(2,1)} %refs_1_.7), channel_id=1, source_target_pairs={{0,4},{4,0},{8,12},{12,8},{16,20},{20,16},{24,28},{28,24},{1,5},{5... | collective-permute-start | bytes 6291464 | tf_op jit(solution)/shard_map/ppermute | solution.py:282
  3.3 15.2 %collective-permute-start.3 = (bf16[1024,256]{1,0:T(8,128)(2,1)S(1)}, bf16[1024,256]{1,0:T(8,128)(2,1)S(1)}, u32[]{:S(2)}, u32[]{:S(2)}) collective-permute-start(bf16[1024,256]{1,0:T(8,128)(2,1)S(1)} %own_columns.1.refs_2_.refs_1_.refs_6_), channel_id=1, source_target_pairs={{0,1},{1,0},{2,3},{3,2},{4,5},{5,4},{6,7},{7,6},{8,9},{9,8},{10,11... | collective-permute-start | bytes 1572872 | tf_op jit(solution)/shard_map/ppermute | solution.py:285
  6.2 14.0 %collective-permute-start.1 = (bf16[1024,256]{1,0:T(8,128)(2,1)S(1)}, bf16[1024,256]{1,0:T(8,128)(2,1)S(1)}, u32[]{:S(2)}, u32[]{:S(2)}) collective-permute-start(bf16[1024,256]{1,0:T(8,128)(2,1)S(1)} %own_columns.1.refs_2_.refs_1_.refs_6_), channel_id=1, source_target_pairs={{0,2},{1,3},{2,0},{3,1},{4,6},{5,7},{6,4},{7,5},{8,10},{9,11},{10,... | collective-permute-start | bytes 1572872 | tf_op jit(solution)/shard_map/ppermute | solution.py:285
  18.4 8.1 %collective-permute-start.4 = (bf16[512,256]{1,0:T(8,128)(2,1)S(1)}, bf16[512,256]{1,0:T(8,128)(2,1)S(1)}, u32[]{:S(2)}, u32[]{:S(2)}) collective-permute-start(bf16[512,256]{1,0:T(8,128)(2,1)S(1)} %slice.9), channel_id=1, source_target_pairs={{0,2},{1,3},{2,0},{3,1},{4,6},{5,7},{6,4},{7,5},{8,10},{9,11},{10,... | collective-permute-start | bytes 786440 | tf_op jit(solution)/shard_map/ppermute | solution.py:285
  20.3 7.2 %collective-permute-start.2 = (bf16[512,256]{1,0:T(8,128)(2,1)S(1)}, bf16[512,256]{1,0:T(8,128)(2,1)S(1)}, u32[]{:S(2)}, u32[]{:S(2)}) collective-permute-start(bf16[512,256]{1,0:T(8,128)(2,1)S(1)} %slice.8), channel_id=1, source_target_pairs={{0,1},{1,0},{2,3},{3,2},{4,5},{5,4},{6,7},{7,6},{8,9},{9,8},{10,11... | collective-permute-start | bytes 786440 | tf_op jit(solution)/shard_map/ppermute | solution.py:285
  30.0 6.4 %collective-permute-start.6 = (bf16[128,1024]{1,0:T(8,128)(2,1)S(1)}, bf16[128,1024]{1,0:T(8,128)(2,1)S(1)}, u32[]{:S(2)}, u32[]{:S(2)}) collective-permute-start(bf16[128,1024]{1,0:T(8,128)(2,1)S(1)} %get-tuple-element.24), channel_id=1, source_target_pairs={{0,2},{1,3},{2,0},{3,1},{4,6},{5,7},{6,4},{7,5},{8,10},{9,11},{10,... | collective-permute-start | bytes 786440 | tf_op jit(solution)/shard_map/ppermute | solution.py:285
  31.2 6.4 %collective-permute-start.7 = (bf16[128,1024]{1,0:T(8,128)(2,1)S(1)}, bf16[128,1024]{1,0:T(8,128)(2,1)S(1)}, u32[]{:S(2)}, u32[]{:S(2)}) collective-permute-start(bf16[128,1024]{1,0:T(8,128)(2,1)S(1)} %get-tuple-element.25), channel_id=1, source_target_pairs={{0,1},{1,0},{2,3},{3,2},{4,5},{5,4},{6,7},{7,6},{8,9},{9,8},{10,11... | collective-permute-start | bytes 786440 | tf_op jit(solution)/shard_map/ppermute | solution.py:285
  38.5 8.1 %collective-permute-start.19 = (bf16[256,512]{1,0:T(8,128)(2,1)S(1)}, bf16[256,512]{1,0:T(8,128)(2,1)S(1)}, u32[]{:S(2)}, u32[]{:S(2)}) collective-permute-start(bf16[256,512]{1,0:T(8,128)(2,1)S(1)} %get-tuple-element.30), channel_id=1, source_target_pairs={{0,1},{1,0},{2,3},{3,2},{4,5},{5,4},{6,7},{7,6},{8,9},{9,8},{10,11... | collective-permute-start | bytes 786440 | tf_op jit(solution)/shard_map/ppermute | solution.py:285
  39.5 7.6 %collective-permute-start.20 = (bf16[256,512]{1,0:T(8,128)(2,1)S(1)}, bf16[256,512]{1,0:T(8,128)(2,1)S(1)}, u32[]{:S(2)}, u32[]{:S(2)}) collective-permute-start(bf16[256,512]{1,0:T(8,128)(2,1)S(1)} %get-tuple-element.31), channel_id=1, source_target_pairs={{0,2},{1,3},{2,0},{3,1},{4,6},{5,7},{6,4},{7,5},{8,10},{9,11},{10,... | collective-permute-start | bytes 786440 | tf_op jit(solution)/shard_map/ppermute | solution.py:285
  42.0 8.3 %collective-permute-start.8 = (bf16[256,512]{1,0:T(8,128)(2,1)S(1)}, bf16[256,512]{1,0:T(8,128)(2,1)S(1)}, u32[]{:S(2)}, u32[]{:S(2)}) collective-permute-start(bf16[256,512]{1,0:T(8,128)(2,1)S(1)} %get-tuple-element.26), channel_id=1, source_target_pairs={{0,1},{1,0},{2,3},{3,2},{4,5},{5,4},{6,7},{7,6},{8,9},{9,8},{10,11... | collective-permute-start | bytes 786440 | tf_op jit(solution)/shard_map/ppermute | solution.py:285
  42.6 7.7 %collective-permute-start.9 = (bf16[256,512]{1,0:T(8,128)(2,1)S(1)}, bf16[256,512]{1,0:T(8,128)(2,1)S(1)}, u32[]{:S(2)}, u32[]{:S(2)}) collective-permute-start(bf16[256,512]{1,0:T(8,128)(2,1)S(1)} %get-tuple-element.27), channel_id=1, source_target_pairs={{0,2},{1,3},{2,0},{3,1},{4,6},{5,7},{6,4},{7,5},{8,10},{9,11},{10,... | collective-permute-start | bytes 786440 | tf_op jit(solution)/shard_map/ppermute | solution.py:285
  48.1 5.0 %collective-permute-start.21 = (bf16[256,256]{1,0:T(8,128)(2,1)S(1)}, bf16[256,256]{1,0:T(8,128)(2,1)S(1)}, u32[]{:S(2)}, u32[]{:S(2)}) collective-permute-start(bf16[256,256]{1,0:T(8,128)(2,1)S(1)} %get-tuple-element.33), channel_id=1, source_target_pairs={{0,8},{4,12},{8,0},{12,4},{16,24},{20,28},{24,16},{28,20},{1,9},{5... | collective-permute-start | bytes 393224 | tf_op jit(solution)/shard_map/ppermute | solution.py:293
  49.8 26.8 %collective-permute-start.14 = (bf16[1024,256]{1,0:T(8,128)(2,1)S(1)}, bf16[1024,256]{1,0:T(8,128)(2,1)S(1)}, u32[]{:S(2)}, u32[]{:S(2)}) collective-permute-start(bf16[1024,256]{1,0:T(8,128)(2,1)S(1)} %collective-permute-done.3.refs_2_), channel_id=1, source_target_pairs={{0,4},{4,0},{8,12},{12,8},{16,20},{20,16},{24,28},{28,24},{1,5},{5... | collective-permute-start | bytes 1572872 | tf_op jit(solution)/shard_map/ppermute | solution.py:282
  49.8 29.6 %collective-permute-start.15 = (bf16[1024,256]{1,0:T(8,128)(2,1)S(1)}, bf16[1024,256]{1,0:T(8,128)(2,1)S(1)}, u32[]{:S(2)}, u32[]{:S(2)}) collective-permute-start(bf16[1024,256]{1,0:T(8,128)(2,1)S(1)} %collective-permute-done.1.refs_5_.refs_3_), channel_id=1, source_target_pairs={{0,4},{4,0},{8,12},{12,8},{16,20},{20,16},{24,28},{28,24},{1,5},{5... | collective-permute-start | bytes 1572872 | tf_op jit(solution)/shard_map/ppermute | solution.py:282
  50.3 26.2 %collective-permute-start.17 = (bf16[512,256]{1,0:T(8,128)(2,1)S(1)}, bf16[512,256]{1,0:T(8,128)(2,1)S(1)}, u32[]{:S(2)}, u32[]{:S(2)}) collective-permute-start(bf16[512,256]{1,0:T(8,128)(2,1)S(1)} %collective-permute-done.4.refs_5_), channel_id=1, source_target_pairs={{0,4},{4,0},{8,12},{12,8},{16,20},{20,16},{24,28},{28,24},{1,5},{5... | collective-permute-start | bytes 786440 | tf_op jit(solution)/shard_map/ppermute | solution.py:282
  50.3 29.0 %collective-permute-start.16 = (bf16[512,256]{1,0:T(8,128)(2,1)S(1)}, bf16[512,256]{1,0:T(8,128)(2,1)S(1)}, u32[]{:S(2)}, u32[]{:S(2)}) collective-permute-start(bf16[512,256]{1,0:T(8,128)(2,1)S(1)} %collective-permute-done.2.refs_2_.refs_4_), channel_id=1, source_target_pairs={{0,4},{4,0},{8,12},{12,8},{16,20},{20,16},{24,28},{28,24},{1,5},{5... | collective-permute-start | bytes 786440 | tf_op jit(solution)/shard_map/ppermute | solution.py:282
  58.1 7.3 %collective-permute-start.22 = (bf16[256,256]{1,0:T(8,128)(2,1)S(1)}, bf16[256,256]{1,0:T(8,128)(2,1)S(1)}, u32[]{:S(2)}, u32[]{:S(2)}) collective-permute-start(bf16[256,256]{1,0:T(8,128)(2,1)S(1)} %add_convert_fusion.1), channel_id=1, source_target_pairs={{0,16},{4,20},{8,24},{12,28},{16,0},{20,4},{24,8},{28,12},{1,17},{... | collective-permute-start | bytes 393224 | tf_op jit(solution)/shard_map/ppermute | solution.py:296
  65.4 5.9 %collective-permute-start.11 = (bf16[256,256]{1,0:T(8,128)(2,1)S(1)}, bf16[256,256]{1,0:T(8,128)(2,1)S(1)}, u32[]{:S(2)}, u32[]{:S(2)}) collective-permute-start(bf16[256,256]{1,0:T(8,128)(2,1)S(1)} %add_convert_fusion.3), channel_id=1, source_target_pairs={{0,16},{4,20},{8,24},{12,28},{16,0},{20,4},{24,8},{28,12},{1,17},{... | collective-permute-start | bytes 393224 | tf_op jit(solution)/shard_map/ppermute | solution.py:296
  71.3 8.0 %collective-permute-start.23 = (bf16[256,256]{1,0:T(8,128)(2,1)S(1)}, bf16[256,256]{1,0:T(8,128)(2,1)S(1)}, u32[]{:S(2)}, u32[]{:S(2)}) collective-permute-start(bf16[256,256]{1,0:T(8,128)(2,1)S(1)} %add_convert_fusion.own_ref), channel_id=1, source_target_pairs={{0,8},{4,12},{8,0},{12,4},{16,24},{20,28},{24,16},{28,20},{1,9},{5... | collective-permute-start | bytes 393224 | tf_op jit(solution)/shard_map/ppermute | solution.py:293
  76.5 5.0 %collective-permute-start.12 = (bf16[256,256]{1,0:T(8,128)(2,1)S(1)}, bf16[256,256]{1,0:T(8,128)(2,1)S(1)}, u32[]{:S(2)}, u32[]{:S(2)}) collective-permute-start(bf16[256,256]{1,0:T(8,128)(2,1)S(1)} %add_convert_fusion.2.own_ref), channel_id=1, source_target_pairs={{0,8},{4,12},{8,0},{12,4},{16,24},{20,28},{24,16},{28,20},{1,9},{5... | collective-permute-start | bytes 393224 | tf_op jit(solution)/shard_map/ppermute | solution.py:293
  79.3 8.3 %collective-permute-start.24 = (bf16[256,256]{1,0:T(8,128)(2,1)S(1)}, bf16[256,256]{1,0:T(8,128)(2,1)S(1)}, u32[]{:S(2)}, u32[]{:S(2)}) collective-permute-start(bf16[256,256]{1,0:T(8,128)(2,1)S(1)} %collective-permute-done.23.own_ref), channel_id=1, source_target_pairs={{0,4},{4,0},{8,12},{12,8},{16,20},{20,16},{24,28},{28,24},{1,5},{5... | collective-permute-start | bytes 393224 | tf_op jit(solution)/shard_map/ppermute | solution.py:282
  80.3 13.5 %collective-permute-start.18 = (bf16[256,256]{1,0:T(8,128)(2,1)S(1)}, bf16[256,256]{1,0:T(8,128)(2,1)S(1)}, u32[]{:S(2)}, u32[]{:S(2)}) collective-permute-start(bf16[256,256]{1,0:T(8,128)(2,1)S(1)} %add_convert_fusion.2.own_ref), channel_id=1, source_target_pairs={{0,4},{4,0},{8,12},{12,8},{16,20},{20,16},{24,28},{28,24},{1,5},{5... | collective-permute-start | bytes 393224 | tf_op jit(solution)/shard_map/ppermute | solution.py:282
  81.5 18.4 %collective-permute-start.13 = (bf16[256,256]{1,0:T(8,128)(2,1)S(1)}, bf16[256,256]{1,0:T(8,128)(2,1)S(1)}, u32[]{:S(2)}, u32[]{:S(2)}) collective-permute-start(bf16[256,256]{1,0:T(8,128)(2,1)S(1)} %collective-permute-done.12.own_ref), channel_id=1, source_target_pairs={{0,4},{4,0},{8,12},{12,8},{16,20},{20,16},{24,28},{28,24},{1,5},{5... | collective-permute-start | bytes 393224 | tf_op jit(solution)/shard_map/ppermute | solution.py:282
  (7 other events, 45.7 us)

commit v2 on v0

v2 whole, which is shorter than its diff:
```python
import functools

import jax
import jax.numpy as jnp
from jax import lax
from jax.experimental import pallas as pl
from jax.experimental.pallas import tpu as pltpu
from jax.sharding import PartitionSpec as P

STEP = 2
CORES = 2
MIB = 1024 * 1024
BF16 = jnp.bfloat16
F32 = jnp.float32


def cost(flops, bytes_accessed):
    return pl.CostEstimate(flops=flops, bytes_accessed=bytes_accessed, transcendentals=0)


def busy(us):
    return cost(int(us * 1.15e9), 0)


def whole(array):
    zeros = (0,) * array.ndim
    return pl.BlockSpec(array.shape, lambda i, w: zeros)


def call(body, where, inputs, in_specs, out_shape, limit, scratch=(), name=None, estimate=None):
    return pl.pallas_call(
        body,
        out_shape=out_shape,
        grid_spec=pltpu.PrefetchScalarGridSpec(
            num_scalar_prefetch=1,
            grid=(1,),
            in_specs=in_specs,
            out_specs=[whole(x) for x in out_shape],
            scratch_shapes=scratch,
        ),
        compiler_params=pltpu.CompilerParams(vmem_limit_bytes=limit),
        cost_estimate=estimate,
        name=name,
    )(where, *inputs)


def cut_out(core, piece, projector, cotangent, fsdp, pieces):
    rows, rank = projector.shape
    half = rank // CORES
    tokens, width = cotangent.shape
    span = width // (fsdp * pieces)
    steps = 4

    def body(core_ref, piece_ref, proj_ref, cot_ref, proj_out, cot_out, sems):
        copies = []
        for s in range(fsdp):
            at = pl.multiple_of((s * pieces + pieces - 1 - piece_ref[0]) * span, span)
            copies.append((cot_ref.at[:, pl.ds(at, span)], cot_out.at[:, pl.ds(s * span, span)]))
        columns = pl.ds(pl.multiple_of(core_ref[0] * half, half), half)
        for n in range(steps):
            at = pl.ds(n * (rows // steps), rows // steps)
            copies.append((proj_ref.at[at, columns], proj_out.at[at, :]))
        copies = [pltpu.make_async_copy(x, y, sems.at[n]) for n, (x, y) in enumerate(copies)]
        for copy in copies:
            copy.start()
        for copy in copies:
            copy.wait()

    hbm = [pltpu.with_memory_space_constraint(x, pltpu.HBM) for x in (projector, cotangent)]
    return pl.pallas_call(
        body,
        out_shape=[
            jax.ShapeDtypeStruct((rows, half), BF16),
            jax.ShapeDtypeStruct((tokens, width // pieces), BF16),
        ],
        in_specs=[pl.BlockSpec(memory_space=pltpu.SMEM)] * 2
        + [pl.BlockSpec(memory_space=pl.ANY)] * 2,
        out_specs=[pl.BlockSpec(memory_space=pltpu.VMEM)] * 2,
        scratch_shapes=[pltpu.SemaphoreType.DMA((fsdp + steps,))],
        compiler_params=pltpu.CompilerParams(vmem_limit_bytes=8 * MIB),
        cost_estimate=busy(1),
        name="cut_out",
    )(core, piece, *hbm)


def coords_step(where, acts, proj, total, rows, last, name):
    tokens = acts[0].shape[0]
    half = proj[0][2].shape[1]
    inputs, specs = [], []
    for s, low, block in proj:
        size = block.shape[0]
        at = functools.partial(
            lambda s, low, size, i, w: (0, ((w[0] ^ s) * rows + low) // size), s, low, size
        )
        inputs += [*acts, block]
        specs += [pl.BlockSpec((tokens, size), at)] * 2 + [whole(block)]
    if total is not None:
        inputs.append(total)
        specs.append(whole(total))
    if last:
        shape = jax.ShapeDtypeStruct((half, 2 * tokens), BF16)
    else:
        shape = jax.ShapeDtypeStruct((2 * tokens, half), F32)

    def body(w, *refs):
        out = refs[len(inputs)]
        for t in range(2):
            span = slice(t * tokens, (t + 1) * tokens)
            value = None if total is None else refs[3 * len(proj)][span, :]
            for n in range(len(proj)):
                part = jnp.dot(
                    refs[3 * n + t][...], refs[3 * n + 2][...], preferred_element_type=F32
                )
                value = part if value is None else value + part
            if last:
                out[:, span] = value.T.astype(BF16)
            else:
                out[span, :] = value

    return call(
        body,
        where,
        inputs,
        specs,
        [shape],
        16 * MIB,
        name=name,
        estimate=busy(8),
    )[0]


def terms_step(where, cots, coords, span, pieces, entries, name, kind=BF16):
    tokens = cots[0][0].shape[0]
    half = coords[0].shape[0]
    inputs = list(coords)
    specs = [whole(x) for x in coords]
    out_shape = []
    for s, added, cuts in entries:
        for x, packed in cots:
            step = 1 if packed else pieces
            at = functools.partial(
                lambda s, step, i, w: (0, (w[0] ^ s) * step + (w[2] if step > 1 else 0)),
                s,
                step,
            )
            inputs.append(x)
            specs.append(pl.BlockSpec((tokens, span), at))
        for _, x in added:
            inputs.append(x)
            specs.append(whole(x))
        out_shape += [jax.ShapeDtypeStruct((b - a, span), kind) for a, b in cuts]

    def body(w, *refs):
        ins = iter(refs[len(coords) : len(inputs)])
        outs = iter(refs[len(inputs) : len(inputs) + len(out_shape)])
        value = refs[-1]
        for s, added, cuts in entries:
            term = None
            for n in range(len(cots)):
                at = slice(n % 2 * tokens, (n % 2 + 1) * tokens)
                part = jnp.dot(
                    refs[n // 2][:, at], next(ins)[...], preferred_element_type=F32
                )
                term = part if term is None else term + part
            value[...] = term
            for low, x in added:
                value[low : low + x.shape[0], :] += next(ins)[...].astype(F32)
            for a, b in cuts:
                next(outs)[...] = value[a:b, :].astype(kind)

    return call(
        body,
        where,
        inputs,
        specs,
        out_shape,
        16 * MIB,
        scratch=[pltpu.VMEM((half, span), F32)],
        name=name,
        estimate=busy(8 if kind == F32 else 1),
    )


def assemble(where, blocks, rows, parts):
    half = blocks[0][2].shape[1]
    inputs = [x for _, _, x in blocks]

    def body(w, *refs):
        out, sems = refs[-2:]
        copies = []
        for n, (s, low, x) in enumerate(blocks):
            size = x.shape[0]
            at = pl.ds(pl.multiple_of((w[0] ^ s) * rows + low, size), size)
            copies.append(pltpu.make_async_copy(refs[n], out.at[at, :], sems.at[n]))
        for copy in copies:
            copy.start()
        for copy in copies:
            copy.wait()

    return pl.pallas_call(
        body,
        out_shape=jax.ShapeDtypeStruct((parts * rows, half), BF16),
        in_specs=[pl.BlockSpec(memory_space=pltpu.SMEM)]
        + [pl.BlockSpec(memory_space=pl.ANY)] * len(inputs),
        out_specs=pl.BlockSpec(memory_space=pl.ANY),
        scratch_shapes=[pltpu.SemaphoreType.DMA((len(inputs),))],
        compiler_params=pltpu.CompilerParams(vmem_limit_bytes=4 * MIB),
        cost_estimate=busy(2),
        name="assemble",
    )(where, *inputs)


def update_step(where, k, pieces, own_grad, other_grad, own_proj, other_proj, moments, before):
    half, span = own_grad.shape
    rank = CORES * half
    features = moments[0].shape[0]
    width = own_proj.shape[0]
    rows = min(1024, width)
    steps = width // rows
    part = min(256, rows)

    def body(w, *refs):
        grads, projs, ins = refs[:2], refs[2:4], refs[4:6]
        first_out, second_out, update = refs[-11:-8]
        moment, proj, direction, out = refs[-8:-4]
        moment_in, moment_out, proj_in, update_out = refs[-4:]
        base = lax.rem(w[2] + pieces - k, pieces) * span
        features_at = pl.ds(pl.multiple_of(base, span), span)

        def columns(h):
            core = w[1] if h == 0 else 1 - w[1]
            return pl.ds(pl.multiple_of(core * half, half), half)

        def here(h):
            return pl.ds(h * half, half)

        loads = [
            [
                pltpu.make_async_copy(
                    ins[n].at[features_at, columns(h)],
                    moment.at[n, :, here(h)],
                    moment_in.at[h, n],
                )
                for n in range(2)
            ]
            for h in range(2)
        ]
        stores = [
            [
                pltpu.make_async_copy(
                    moment.at[n, :, here(h)],
                    (first_out, second_out)[n].at[features_at, columns(h)],
                    moment_out.at[h, n],
                )
                for n in range(2)
            ]
            for h in range(2)
        ]
        proj_loads = [
            [
                pltpu.make_async_copy(
                    projs[h].at[pl.ds(r * rows, rows), :],
                    proj.at[pl.ds(r * rows, rows), here(h)],
                    proj_in.at[h, r],
                )
                for h in range(2)
            ]
            for r in range(steps)
        ]
        update_stores = [
            [
                pltpu.make_async_copy(
                    out.at[pl.ds(r * rows + m * part, part), :],
                    update.at[pl.ds(r * rows + m * part, part), features_at],
                    update_out.at[r, m],
                )
                for m in range(rows // part)
            ]
            for r in range(steps)
        ]
        for copy in sum(loads, []) + sum(proj_loads, []):
            copy.start()
        first_scale = 1.0 / (1.0 - 0.9**STEP)
        second_scale = 1.0 / (1.0 - 0.999**STEP)
        for h in range(2):
            grad_low = grads[h][...].T.astype(F32)
            for copy in loads[h]:
                copy.wait()
            first_new = 0.9 * moment[0, :, here(h)] + 0.1 * grad_low
            second_new = 0.999 * moment[1, :, here(h)] + 0.001 * grad_low * grad_low
            moment[0, :, here(h)] = first_new
            moment[1, :, here(h)] = second_new
            for copy in stores[h]:
                copy.start()
            ratio = (first_new * first_scale) / (jnp.sqrt(second_new * second_scale) + 1e-08)
            direction[here(h), :] = ratio.astype(BF16).T
        for r in range(steps):
            for copy in proj_loads[r]:
                copy.wait()
            at = pl.ds(r * rows, rows)
            out[at, :] = jnp.dot(proj[at, :], direction[...], preferred_element_type=F32)
            for copy in update_stores[r]:
                copy.start()
        for copy in sum(stores, []) + sum(update_stores, []):
            copy.wait()

    inputs = [own_grad, other_grad, own_proj, other_proj, *moments]
    any_space = pl.BlockSpec(memory_space=pl.ANY)
    in_specs = [whole(own_grad), whole(other_grad)] + [any_space] * 4
    aliases = {}
    if before is not None:
        aliases = {1 + len(inputs) + n: n for n in range(3)}
        inputs += before
        in_specs += [any_space] * 3
    return pl.pallas_call(
        body,
        out_shape=[jax.ShapeDtypeStruct(x.shape, F32) for x in moments]
        + [jax.ShapeDtypeStruct((width, features), F32)],
        grid_spec=pltpu.PrefetchScalarGridSpec(
            num_scalar_prefetch=1,
            grid=(1,),
            in_specs=in_specs,
            out_specs=[any_space] * 3,
            scratch_shapes=[
                pltpu.VMEM((2, span, rank), F32),
                pltpu.VMEM((width, rank), BF16),
                pltpu.VMEM((rank, span), BF16),
                pltpu.VMEM((width, span), F32),
                pltpu.SemaphoreType.DMA((2, 2)),
                pltpu.SemaphoreType.DMA((2, 2)),
                pltpu.SemaphoreType.DMA((2, steps)),
                pltpu.SemaphoreType.DMA((steps, rows // part)),
            ],
        ),
        input_output_aliases=aliases,
        compiler_params=pltpu.CompilerParams(vmem_limit_bytes=28 * MIB),
        cost_estimate=cost(2 * width * rank * span, 4 * width * span + 18 * span * rank),
        name="update_step",
    )(where, *inputs)


def after(x, *others):
    return lax.optimization_barrier((x, *others))[0]


def add_up(arrays):
    return functools.reduce(jnp.add, [x.astype(F32) for x in arrays]).astype(BF16)


def on_device(dp, fsdp, acts, cotangent, projector, first_moment, second_moment):
    rows, rank = projector.shape
    half = rank // CORES
    groups = dp // CORES
    pieces = 2 if groups % 2 == 0 else 1
    span = rows // pieces
    fsdp_at = lax.axis_index("fsdp")
    dp_at = lax.axis_index("dp")
    where = jnp.stack([fsdp_at, dp_at % CORES, (dp_at // CORES) % pieces]).astype(jnp.int32)

    def to_core(x):
        return lax.ppermute(x, "dp", [(i, i ^ 1) for i in range(dp)])

    def to_fsdp(x, s):
        return lax.ppermute(x, "fsdp", [(i, i ^ s) for i in range(fsdp)])

    def to_piece(x, k):
        pairs = []
        for i in range(dp):
            group, core = divmod(i, CORES)
            base = group - group % pieces
            pairs.append((i, (base + (group + k) % pieces) * CORES + core))
        return lax.ppermute(x, "dp", pairs)

    def to_base(x, k):
        return lax.ppermute(x, "dp", [(i, (i + k * pieces * CORES) % dp) for i in range(dp)])

    def links(s):
        return (s & -s, 1 << (s.bit_length() - 1))

    levels = [
        [s for s in range(fsdp) if s.bit_count() == n] for n in range(fsdp.bit_length())
    ]

    part = rows // 2
    piece_at = ((dp_at // CORES) % pieces).astype(jnp.int32)
    core_at = (dp_at % CORES).astype(jnp.int32)
    own_half, cot_out = cut_out(
        core_at[None], piece_at[None], projector, cotangent, fsdp, pieces
    )
    held = {0: [(0, 0, own_half)]}
    for level in levels[1:]:
        for s in level:
            if s.bit_count() == 1:
                held[s] = [(s, 0, to_fsdp(own_half, s))]
                continue
            held[s] = []
            for n, link in enumerate(links(s)):
                source = held[s ^ link]
                x = source[n][2] if len(source) > 1 else source[0][2][n * part : (n + 1) * part]
                held[s].append((s, n * part, to_fsdp(x, link)))
    acts_pair = [acts, to_core(acts)]
    cots = [(cotangent, False), (to_core(after(cotangent, own_half)), False)]

    total = None
    for n, level in enumerate(levels):
        entries = [x for s in level for x in held[s]]
        last = n == len(levels) - 1
        total = coords_step(where, acts_pair, entries, total, rows, last, f"coords_{n}")
    coords = [total]
    landed = {s: [] for s in range(fsdp)}
    if pieces > 1:
        coords = [to_piece(total, 1)]
        entries = [(s, [], [(0, half)]) for s in range(fsdp)]
        sums = terms_step(where, cots, [total], span, pieces, entries, "terms_chip", F32)
        for s in range(fsdp):
            landed[s].append((0, sums[s]))
        arrived = after(to_piece(cot_out, 1), *sums)
        cots = [(arrived, True), (to_core(arrived), True)]

    middle = half // 2
    halves = [(0, middle), (middle, half)]
    for n in range(len(levels) - 1, -1, -1):
        level = levels[n]
        cuts = halves if n > 1 else [(0, half)]
        entries = [(s, landed[s], cuts) for s in level]
        outs = terms_step(where, cots, coords, span, pieces, entries, f"terms_{n}")
        outs = iter(outs)
        for s in level:
            if n > 1:
                for m, link in enumerate(links(s)):
                    landed[s ^ link].append((m * middle, to_fsdp(next(outs), link)))
            elif n == 1:
                landed[0].append((0, to_fsdp(next(outs), s)))
            else:
                mine = next(outs)
    mine = add_up([mine] + [to_base(mine, k) for k in range(1, groups // pieces)])
    grads = [mine] + [to_piece(mine, k) for k in range(1, pieces)]

    blocks = [(s, low, after(x, *coords)) for s in range(fsdp) for s, low, x in held[s]]
    own_proj = assemble(where, blocks, rows, fsdp)
    other_proj = to_core(own_proj)
    outputs = None
    for k, grad in enumerate(grads):
        if outputs is not None:
            grad = after(grad, *outputs)
        outputs = update_step(
            where,
            k,
            pieces,
            grad,
            to_core(grad),
            own_proj,
            other_proj,
            (first_moment, second_moment),
            outputs,
        )
    return tuple(outputs)


def solution(mesh):
    in_specs = (
        P(("dp", "fsdp"), None),
        P(("dp", "fsdp"), None),
        P("fsdp", None),
        P("fsdp", None),
        P("fsdp", None),
    )
    out_specs = (P("fsdp", None), P("fsdp", None), P(None, "fsdp"))
    body = functools.partial(on_device, mesh.shape["dp"], mesh.shape["fsdp"])
    return jax.shard_map(body, mesh=mesh, in_specs=in_specs, out_specs=out_specs, check_vma=False)
```

time: 241 us -> 87.5 us (0.36)
  waiting for transfers between devices: 106 us -> 36.5 us
  blocking collectives: 64.9 us -> 0 us
  Pallas kernels: 0 us -> 29.4 us
  local copies, waits for them, and re-layouts: 28.3 us -> 1.64 us
  matrix products: 21.2 us -> 0 us
  starting transfers between devices: 0.08 us -> 18.7 us
  between operations: 14.1 us -> 0.8 us
  other arithmetic: 5.49 us -> 0.14 us
    psum x1 -> x0, blocking collectives: 64.9 us -> none  [on_device(): grad_low = lax.psum(grad_part, 'dp')]
    all_gather x1 -> x0, waiting for transfers between devices: 57.3 us -> none  [on_device(): full_proj = lax.all_gather(projector, 'fsdp', axis=0, tiled=True)]
    reduce_scatter x1 -> x0, waiting for transfers between devices: 48 us -> none  [on_device(): lax.psum_scatter(lax.dot_general(cotangent, coords, (((0,), (0,)), ((), (...]
    ppermute x0 -> x18, waiting for transfers between devices: none -> 36.5 us  [the longest x8 20.4 us: to_fsdp(): return lax.ppermute(x, 'fsdp', [(i, i ^ s) for i in range(fsdp)])]
    pallas_call x0 -> x11, Pallas kernels: none -> 29.4 us  [the longest x2 13.1 us: update_step(): pl.pallas_call(body, out_shape=[jax.ShapeDtypeStruct(x.shape, F32) for x...]
    unnamed x11 -> x8, local copies, waits for them, and re-layouts: 28.3 us -> 1.6 us
    dot_general x2 -> x0, matrix products: 21.2 us -> none  [the longest x1 13.8 us: on_device(): lax.dot_general(full_proj, direction, (((1,), (1,)), ((), ())), preferred...]
    ppermute x0 -> x18, starting transfers between devices: none -> 18.7 us  [the longest x8 11.3 us: to_fsdp(): return lax.ppermute(x, 'fsdp', [(i, i ^ s) for i in range(fsdp)])]
  transfers between devices with their start and end apart: 2 -> 18, of which waited for: 2 -> 10; matrix products, arithmetic and copies ran while one was open for 2% -> 0% of each run, Pallas kernels for 0% -> 26%
where the time goes in v2:
time: 87.5 us; the launch traced here: 87.2 us
  waiting for transfers between devices  36.5 us (42%)
  Pallas kernels  29.4 us (34%)
  starting transfers between devices  18.7 us (21%)
  local copies, waits for them, and re-layouts  1.64 us (2%)
    ppermute x8, waiting for transfers between devices, to_fsdp(): return lax.ppermute(x, 'fsdp', [(i, i ^ s) for i in range(fsdp)])  20.4 us
    pallas_call x2, Pallas kernels, update_step(): pl.pallas_call(body, out_shape=[jax.ShapeDtypeStruct(x.shape, F32) for x...  13.1 us
    pallas_call x7, Pallas kernels, call(): pl.pallas_call(body, out_shape=out_shape, grid_spec=pltpu.PrefetchScalarG...  12.4 us
    ppermute x8, starting transfers between devices, to_fsdp(): return lax.ppermute(x, 'fsdp', [(i, i ^ s) for i in range(fsdp)])  11.3 us
    ppermute x1, waiting for transfers between devices, to_base(): lax.ppermute(x, 'dp', [(i, (i + k * pieces * CORES) % dp) for i in range(...  10.3 us
    ppermute x3, starting transfers between devices, to_piece(): return lax.ppermute(x, 'dp', pairs)  3.97 us
    ppermute x3, waiting for transfers between devices, to_piece(): return lax.ppermute(x, 'dp', pairs)  3.47 us
    ppermute x1, starting transfers between devices, to_base(): lax.ppermute(x, 'dp', [(i, (i + k * pieces * CORES) % dp) for i in range(...  2.66 us
  transfers between devices with their start and end apart: 18, of which 10 were waited for; matrix products, arithmetic and copies ran while one was open for 0% of the time, Pallas kernels for 26%

profile of v2, /device:TPU:0, one launch (start us, length us, event | category | flops | bytes accessed | tf_op | source)
XLA Modules:
  0.0 87.2 jit_solution(15792066746571994340)
XLA Ops:
  1.1 2.2 %cut_out.1 = (bf16[1024,256]{1,0:T(8,128)(2,1)}, bf16[256,2048]{1,0:T(8,128)(2,1)S(1)}) custom-call(s32[1]{0:T(128)} %bitcast.1.core_ref, s32[1]{0:T(128)} %bitcast.2.piece_ref, bf16[1024,512]{1,0:T(8,128)(2,1)} %proj_ref.1, bf16[256,4096]{1,0:T(8,128)(2,1)} %refs_7_.1), custom_call_target="tpu_custom_call" | custom-call | flops 1150000000 | tf_op jit(solution)/shard_map/cut_out/pallas_call | solution.py:70
  3.4 2.6 %collective-permute-start.3 = (bf16[1024,256]{1,0:T(8,128)(2,1)}, bf16[1024,256]{1,0:T(8,128)(2,1)S(1)}, u32[]{:S(2)}, u32[]{:S(2)}) collective-permute-start(bf16[1024,256]{1,0:T(8,128)(2,1)} %get-tuple-element.36.refs_2_.refs_0_), channel_id=1, source_target_pairs={{0,1},{1,0},{2,3},{3,2},{4,5},{5,4},{6,7},{7,6},{8,9},{9,8},{10,11... | collective-permute-start | bytes 1572872 | tf_op jit(solution)/shard_map/ppermute | solution.py:364
  6.0 1.5 %collective-permute-start.1 = (bf16[1024,256]{1,0:T(8,128)(2,1)}, bf16[1024,256]{1,0:T(8,128)(2,1)S(1)}, u32[]{:S(2)}, u32[]{:S(2)}) collective-permute-start(bf16[1024,256]{1,0:T(8,128)(2,1)} %get-tuple-element.36.refs_2_.refs_0_), channel_id=1, source_target_pairs={{0,2},{1,3},{2,0},{3,1},{4,6},{5,7},{6,4},{7,5},{8,10},{9,11},{10,... | collective-permute-start | bytes 1572872 | tf_op jit(solution)/shard_map/ppermute | solution.py:364
  7.5 1.6 %collective-permute-start.6 = (bf16[256,2048]{1,0:T(8,128)(2,1)S(1)}, bf16[256,2048]{1,0:T(8,128)(2,1)S(1)}, u32[]{:S(2)}, u32[]{:S(2)}) collective-permute-start(bf16[256,2048]{1,0:T(8,128)(2,1)S(1)} %get-tuple-element.25), channel_id=1, source_target_pairs={{0,8},{4,12},{8,0},{12,4},{16,24},{20,28},{24,16},{28,20},{1,9},{5... | collective-permute-start | bytes 3145736 | tf_op jit(solution)/shard_map/ppermute | solution.py:372
  9.2 9.6 %collective-permute-done.3.refs_2_.refs_1_ = bf16[1024,256]{1,0:T(8,128)(2,1)S(1)} collective-permute-done((bf16[1024,256]{1,0:T(8,128)(2,1)}, bf16[1024,256]{1,0:T(8,128)(2,1)S(1)}, u32[]{:S(2)}, u32[]{:S(2)}) %collective-permute-start.3) | collective-permute-done | bytes 524320 | tf_op jit(solution)/shard_map/ppermute | solution.py:364
  18.7 1.8 %collective-permute-start.4 = (bf16[512,256]{1,0:T(8,128)(2,1)S(1)}, bf16[512,256]{1,0:T(8,128)(2,1)S(1)}, u32[]{:S(2)}, u32[]{:S(2)}) collective-permute-start(bf16[512,256]{1,0:T(8,128)(2,1)S(1)} %slice.9), channel_id=1, source_target_pairs={{0,2},{1,3},{2,0},{3,1},{4,6},{5,7},{6,4},{7,5},{8,10},{9,11},{10,... | collective-permute-start | bytes 786440 | tf_op jit(solution)/shard_map/ppermute | solution.py:364
  20.6 1.6 %collective-permute-start.2 = (bf16[512,256]{1,0:T(8,128)(2,1)S(1)}, bf16[512,256]{1,0:T(8,128)(2,1)S(1)}, u32[]{:S(2)}, u32[]{:S(2)}) collective-permute-start(bf16[512,256]{1,0:T(8,128)(2,1)S(1)} %slice.8), channel_id=1, source_target_pairs={{0,1},{1,0},{2,3},{3,2},{4,5},{5,4},{6,7},{7,6},{8,9},{9,8},{10,11... | collective-permute-start | bytes 786440 | tf_op jit(solution)/shard_map/ppermute | solution.py:364
  22.2 1.6 %copy-done.2 = bf16[256,4096]{1,0:T(8,128)(2,1)S(1)} copy-done((bf16[256,4096]{1,0:T(8,128)(2,1)S(1)}, bf16[256,4096]{1,0:T(8,128)(2,1)}, u32[]{:S(2)}) %copy-start.2) | copy-done | bytes 2097176
  23.8 2.3 %coords_0.1.refs_6_ = f32[512,256]{1,0:T(8,128)S(1)} custom-call(s32[3]{0:T(128)S(1)} %pad_add_fusion.w, bf16[256,4096]{1,0:T(8,128)(2,1)S(1)} %copy-done.2, bf16[256,4096]{1,0:T(8,128)(2,1)} %collective-permute-done.refs_1_.refs_4_, bf16[1024,256]{1,0:T(8,128)(2,1)} %get-tuple-element.36.refs_2_.refs_0_), custom_call_target="tpu_custom_call" | custom-call | flops 9200000000 | tf_op jit(solution)/shard_map/coords_0/pallas_call | solution.py:31
  26.0 2.5 %coords_1.1.refs_6_ = f32[512,256]{1,0:T(8,128)S(1)} custom-call(s32[3]{0:T(128)S(1)} %pad_add_fusion.w, bf16[256,4096]{1,0:T(8,128)(2,1)S(1)} %copy-done.3, bf16[256,4096]{1,0:T(8,128)(2,1)} %collective-permute-done.refs_1_.refs_4_, bf16[1024,256]{1,0:T(8,128)(2,1)S(1)} %collective-permute-done.3.refs_2_.refs_1_, bf16[256,4096]{1,0:T(8,128)(2,1)S(1)} %copy-done.3, ...), custom_call_target="tpu_custom_call" | custom-call | flops 9200000000 | tf_op jit(solution)/shard_map/coords_1/pallas_call | solution.py:31
  28.6 2.1 %coords_2.1.refs_0_ = bf16[256,512]{1,0:T(8,128)(2,1)S(1)} custom-call(s32[3]{0:T(128)S(1)} %pad_add_fusion.w, bf16[256,4096]{1,0:T(8,128)(2,1)S(1)} %copy-done.3, bf16[256,4096]{1,0:T(8,128)(2,1)} %collective-permute-done.refs_1_.refs_4_, bf16[512,256]{1,0:T(8,128)(2,1)S(1)} %collective-permute-done.2.refs_2_.refs_3_, bf16[256,4096]{1,0:T(8,128)(2,1)S(1)} %copy-done.3, ...), custom_call_target="tpu_custom_call" | custom-call | flops 9200000000 | tf_op jit(solution)/shard_map/coords_2/pallas_call | solution.py:31
  30.7 1.6 %collective-permute-start.5 = (bf16[256,512]{1,0:T(8,128)(2,1)S(1)}, bf16[256,512]{1,0:T(8,128)(2,1)S(1)}, u32[]{:S(2)}, u32[]{:S(2)}) collective-permute-start(bf16[256,512]{1,0:T(8,128)(2,1)S(1)} %coords_2.1.refs_0_), channel_id=1, source_target_pairs={{0,8},{4,12},{8,0},{12,4},{16,24},{20,28},{24,16},{28,20},{1,9},{5... | collective-permute-start | bytes 786440 | tf_op jit(solution)/shard_map/ppermute | solution.py:372
  32.4 2.8 %terms_chip.1 = (f32[256,512]{1,0:T(8,128)S(1)}, f32[256,512]{1,0:T(8,128)S(1)}, f32[256,512]{1,0:T(8,128)S(1)}, f32[256,512]{1,0:T(8,128)S(1)}) custom-call(s32[3]{0:T(128)S(1)} %pad_add_fusion.w, bf16[256,512]{1,0:T(8,128)(2,1)S(1)} %coords_2.1.refs_0_, bf16[256,4096]{1,0:T(8,128)(2,1)} %refs_7_.1, ...), custom_call_target="tpu_custom_call" | custom-call | flops 9200000000 | tf_op jit(solution)/shard_map/terms_chip/pallas_call | solution.py:31
  35.2 2.9 %collective-permute-done.5.refs_0_ = bf16[256,512]{1,0:T(8,128)(2,1)S(1)} collective-permute-done((bf16[256,512]{1,0:T(8,128)(2,1)S(1)}, bf16[256,512]{1,0:T(8,128)(2,1)S(1)}, u32[]{:S(2)}, u32[]{:S(2)}) %collective-permute-start.5) | collective-permute-done | bytes 262176 | tf_op jit(solution)/shard_map/ppermute | solution.py:372
  38.1 1.6 %assemble.1.refs_2_ = bf16[4096,256]{1,0:T(8,128)(2,1)S(1)} custom-call(s32[3]{0:T(128)S(1)} %pad_add_fusion.w, bf16[1024,256]{1,0:T(8,128)(2,1)} %get-tuple-element.36.refs_2_.refs_0_, bf16[1024,256]{1,0:T(8,128)(2,1)S(1)} %collective-permute-done.3.refs_2_.refs_1_, bf16[1024,256]{1,0:T(8,128)(2,1)S(1)} %collective-permute-done.1.refs_5_.refs_2_, ...), custom_call_target="tpu_custom_call" | custom-call | flops 2300000000 | tf_op jit(solution)/shard_map/assemble/pallas_call | solution.py:200
  41.2 1.1 %collective-permute-start.10 = (bf16[128,512]{1,0:T(8,128)(2,1)S(1)}, bf16[128,512]{1,0:T(8,128)(2,1)S(1)}, u32[]{:S(2)}, u32[]{:S(2)}) collective-permute-start(bf16[128,512]{1,0:T(8,128)(2,1)S(1)} %get-tuple-element.33), channel_id=1, source_target_pairs={{0,1},{1,0},{2,3},{3,2},{4,5},{5,4},{6,7},{7,6},{8,9},{9,8},{10,11... | collective-permute-start | bytes 393224 | tf_op jit(solution)/shard_map/ppermute | solution.py:364
  42.3 4.3 %collective-permute-done.9.refs_4_ = bf16[128,512]{1,0:T(8,128)(2,1)S(1)} collective-permute-done((bf16[128,512]{1,0:T(8,128)(2,1)S(1)}, bf16[128,512]{1,0:T(8,128)(2,1)S(1)}, u32[]{:S(2)}, u32[]{:S(2)}) %collective-permute-start.9) | collective-permute-done | bytes 131104 | tf_op jit(solution)/shard_map/ppermute | solution.py:364
  47.8 1.2 %collective-permute-start.11 = (bf16[256,512]{1,0:T(8,128)(2,1)S(1)}, bf16[256,512]{1,0:T(8,128)(2,1)S(1)}, u32[]{:S(2)}, u32[]{:S(2)}) collective-permute-start(bf16[256,512]{1,0:T(8,128)(2,1)S(1)} %get-tuple-element.34), channel_id=1, source_target_pairs={{0,1},{1,0},{2,3},{3,2},{4,5},{5,4},{6,7},{7,6},{8,9},{9,8},{10,11... | collective-permute-start | bytes 786440 | tf_op jit(solution)/shard_map/ppermute | solution.py:364
  50.0 5.6 %collective-permute-done.11.refs_4_ = bf16[256,512]{1,0:T(8,128)(2,1)S(1)} collective-permute-done((bf16[256,512]{1,0:T(8,128)(2,1)S(1)}, bf16[256,512]{1,0:T(8,128)(2,1)S(1)}, u32[]{:S(2)}, u32[]{:S(2)}) %collective-permute-start.11) | collective-permute-done | bytes 262176 | tf_op jit(solution)/shard_map/ppermute | solution.py:364
  57.2 2.7 %collective-permute-start.13 = (bf16[256,512]{1,0:T(8,128)(2,1)S(1)}, bf16[256,512]{1,0:T(8,128)(2,1)S(1)}, u32[]{:S(2)}, u32[]{:S(2)}) collective-permute-start(bf16[256,512]{1,0:T(8,128)(2,1)S(1)} %terms_0.1), channel_id=1, source_target_pairs={{0,16},{4,20},{8,24},{12,28},{16,0},{20,4},{24,8},{28,12},{1,17},{... | collective-permute-start | bytes 786440 | tf_op jit(solution)/shard_map/ppermute | solution.py:375
  59.9 10.3 %collective-permute-done.13 = bf16[256,512]{1,0:T(8,128)(2,1)S(1)} collective-permute-done((bf16[256,512]{1,0:T(8,128)(2,1)S(1)}, bf16[256,512]{1,0:T(8,128)(2,1)S(1)}, u32[]{:S(2)}, u32[]{:S(2)}) %collective-permute-start.13) | collective-permute-done | bytes 262176 | tf_op jit(solution)/shard_map/ppermute | solution.py:375
  71.9 6.6 %update_step.2 = (f32[1024,512]{1,0:T(8,128)}, f32[1024,512]{1,0:T(8,128)}, f32[4096,1024]{1,0:T(8,128)}) custom-call(s32[3]{0:T(128)S(1)} %pad_add_fusion.w, bf16[256,512]{1,0:T(8,128)(2,1)S(1)} %add_convert_fusion.refs_0_, bf16[256,512]{1,0:T(8,128)(2,1)S(1)} %collective-permute-done.15.refs_1_, bf16[4096,256]{1,0:T(8,128)(2,1)S(1)} %assemble.1.refs_2_, ...), custom_call_target="tpu_custom_call" | custom-call | flops 2147483648 | bytes 13107200 | tf_op jit(solution)/shard_map/update_step/pallas_call | solution.py:315
  79.1 1.5 %collective-permute-done.17.refs_1_ = bf16[256,512]{1,0:T(8,128)(2,1)S(1)} collective-permute-done((bf16[256,512]{1,0:T(8,128)(2,1)S(1)}, bf16[256,512]{1,0:T(8,128)(2,1)S(1)}, u32[]{:S(2)}, u32[]{:S(2)}) %collective-permute-start.17) | collective-permute-done | bytes 262176 | tf_op jit(solution)/shard_map/ppermute | solution.py:361
  80.6 6.6 %update_step.3 = (f32[1024,512]{1,0:T(8,128)}, f32[1024,512]{1,0:T(8,128)}, f32[4096,1024]{1,0:T(8,128)}) custom-call(s32[3]{0:T(128)S(1)} %pad_add_fusion.w, bf16[256,512]{1,0:T(8,128)(2,1)S(1)} %collective-permute-done.14.refs_0_, bf16[256,512]{1,0:T(8,128)(2,1)S(1)} %collective-permute-done.17.refs_1_, ...), custom_call_target="tpu_custom_call", output_to_operand_aliasing={{0}: (7, {}), {1}: (8, {}), {2}: (9, {})} | custom-call | flops 2147483648 | bytes 13107200 | tf_op jit(solution)/shard_map/update_step/pallas_call | solution.py:315
  (35 shorter events, 8.3 us)
Async XLA Ops:
  0.6 21.5 %collective-permute-start = (bf16[256,4096]{1,0:T(8,128)(2,1)}, bf16[256,4096]{1,0:T(8,128)(2,1)}, u32[]{:S(2)}, u32[]{:S(2)}) collective-permute-start(bf16[256,4096]{1,0:T(8,128)(2,1)} %refs_3_.4), channel_id=1, source_target_pairs={{0,4},{4,0},{8,12},{12,8},{16,20},{20,16},{24,28},{28,24},{1,5},{5... | collective-permute-start | bytes 6291464 | tf_op jit(solution)/shard_map/ppermute | solution.py:361
  3.4 15.3 %collective-permute-start.3 = (bf16[1024,256]{1,0:T(8,128)(2,1)}, bf16[1024,256]{1,0:T(8,128)(2,1)S(1)}, u32[]{:S(2)}, u32[]{:S(2)}) collective-permute-start(bf16[1024,256]{1,0:T(8,128)(2,1)} %get-tuple-element.36.refs_2_.refs_0_), channel_id=1, source_target_pairs={{0,1},{1,0},{2,3},{3,2},{4,5},{5,4},{6,7},{7,6},{8,9},{9,8},{10,11... | collective-permute-start | bytes 1572872 | tf_op jit(solution)/shard_map/ppermute | solution.py:364
  6.0 14.6 %collective-permute-start.1 = (bf16[1024,256]{1,0:T(8,128)(2,1)}, bf16[1024,256]{1,0:T(8,128)(2,1)S(1)}, u32[]{:S(2)}, u32[]{:S(2)}) collective-permute-start(bf16[1024,256]{1,0:T(8,128)(2,1)} %get-tuple-element.36.refs_2_.refs_0_), channel_id=1, source_target_pairs={{0,2},{1,3},{2,0},{3,1},{4,6},{5,7},{6,4},{7,5},{8,10},{9,11},{10,... | collective-permute-start | bytes 1572872 | tf_op jit(solution)/shard_map/ppermute | solution.py:364
  7.5 27.6 %collective-permute-start.6 = (bf16[256,2048]{1,0:T(8,128)(2,1)S(1)}, bf16[256,2048]{1,0:T(8,128)(2,1)S(1)}, u32[]{:S(2)}, u32[]{:S(2)}) collective-permute-start(bf16[256,2048]{1,0:T(8,128)(2,1)S(1)} %get-tuple-element.25), channel_id=1, source_target_pairs={{0,8},{4,12},{8,0},{12,4},{16,24},{20,28},{24,16},{28,20},{1,9},{5... | collective-permute-start | bytes 3145736 | tf_op jit(solution)/shard_map/ppermute | solution.py:372
  9.1 23.3 %collective-permute-start.7 = (bf16[256,4096]{1,0:T(8,128)(2,1)}, bf16[256,4096]{1,0:T(8,128)(2,1)}, u32[]{:S(2)}, u32[]{:S(2)}) collective-permute-start(bf16[256,4096]{1,0:T(8,128)(2,1)} %refs_7_.1), channel_id=1, source_target_pairs={{0,4},{4,0},{8,12},{12,8},{16,20},{20,16},{24,28},{28,24},{1,5},{5... | collective-permute-start | bytes 6291464 | tf_op jit(solution)/shard_map/ppermute | solution.py:361
  18.7 9.8 %collective-permute-start.4 = (bf16[512,256]{1,0:T(8,128)(2,1)S(1)}, bf16[512,256]{1,0:T(8,128)(2,1)S(1)}, u32[]{:S(2)}, u32[]{:S(2)}) collective-permute-start(bf16[512,256]{1,0:T(8,128)(2,1)S(1)} %slice.9), channel_id=1, source_target_pairs={{0,2},{1,3},{2,0},{3,1},{4,6},{5,7},{6,4},{7,5},{8,10},{9,11},{10,... | collective-permute-start | bytes 786440 | tf_op jit(solution)/shard_map/ppermute | solution.py:364
  20.6 7.9 %collective-permute-start.2 = (bf16[512,256]{1,0:T(8,128)(2,1)S(1)}, bf16[512,256]{1,0:T(8,128)(2,1)S(1)}, u32[]{:S(2)}, u32[]{:S(2)}) collective-permute-start(bf16[512,256]{1,0:T(8,128)(2,1)S(1)} %slice.8), channel_id=1, source_target_pairs={{0,1},{1,0},{2,3},{3,2},{4,5},{5,4},{6,7},{7,6},{8,9},{9,8},{10,11... | collective-permute-start | bytes 786440 | tf_op jit(solution)/shard_map/ppermute | solution.py:364
  22.2 1.6 %copy-start.2 = (bf16[256,4096]{1,0:T(8,128)(2,1)S(1)}, bf16[256,4096]{1,0:T(8,128)(2,1)}, u32[]{:S(2)}) copy-start(bf16[256,4096]{1,0:T(8,128)(2,1)} %refs_3_.4) | copy-start | bytes 6291460
  23.8 2.3 %copy-start.3 = (bf16[256,4096]{1,0:T(8,128)(2,1)S(1)}, bf16[256,4096]{1,0:T(8,128)(2,1)}, u32[]{:S(2)}) copy-start(bf16[256,4096]{1,0:T(8,128)(2,1)} %refs_3_.4) | copy-start | bytes 6291460
  30.7 7.4 %collective-permute-start.5 = (bf16[256,512]{1,0:T(8,128)(2,1)S(1)}, bf16[256,512]{1,0:T(8,128)(2,1)S(1)}, u32[]{:S(2)}, u32[]{:S(2)}) collective-permute-start(bf16[256,512]{1,0:T(8,128)(2,1)S(1)} %coords_2.1.refs_0_), channel_id=1, source_target_pairs={{0,8},{4,12},{8,0},{12,4},{16,24},{20,28},{24,16},{28,20},{1,9},{5... | collective-permute-start | bytes 786440 | tf_op jit(solution)/shard_map/ppermute | solution.py:372
  35.1 4.7 %collective-permute-start.8 = (bf16[256,2048]{1,0:T(8,128)(2,1)S(1)}, bf16[256,2048]{1,0:T(8,128)(2,1)S(1)}, u32[]{:S(2)}, u32[]{:S(2)}) collective-permute-start(bf16[256,2048]{1,0:T(8,128)(2,1)S(1)} %collective-permute-done.6.refs_1_.refs_5_), channel_id=1, source_target_pairs={{0,4},{4,0},{8,12},{12,8},{16,20},{20,16},{24,28},{28,24},{1,5},{5... | collective-permute-start | bytes 3145736 | tf_op jit(solution)/shard_map/ppermute | solution.py:361
  39.7 32.2 %collective-permute-start.16 = (bf16[4096,256]{1,0:T(8,128)(2,1)S(1)}, bf16[4096,256]{1,0:T(8,128)(2,1)S(1)}, u32[]{:S(2)}, u32[]{:S(2)}) collective-permute-start(bf16[4096,256]{1,0:T(8,128)(2,1)S(1)} %assemble.1.refs_2_), channel_id=1, source_target_pairs={{0,4},{4,0},{8,12},{12,8},{16,20},{20,16},{24,28},{28,24},{1,5},{5... | collective-permute-start | bytes 6291464 | tf_op jit(solution)/shard_map/ppermute | solution.py:361
  40.7 6.0 %collective-permute-start.9 = (bf16[128,512]{1,0:T(8,128)(2,1)S(1)}, bf16[128,512]{1,0:T(8,128)(2,1)S(1)}, u32[]{:S(2)}, u32[]{:S(2)}) collective-permute-start(bf16[128,512]{1,0:T(8,128)(2,1)S(1)} %get-tuple-element.32), channel_id=1, source_target_pairs={{0,2},{1,3},{2,0},{3,1},{4,6},{5,7},{6,4},{7,5},{8,10},{9,11},{10,... | collective-permute-start | bytes 393224 | tf_op jit(solution)/shard_map/ppermute | solution.py:364
  41.2 5.6 %collective-permute-start.10 = (bf16[128,512]{1,0:T(8,128)(2,1)S(1)}, bf16[128,512]{1,0:T(8,128)(2,1)S(1)}, u32[]{:S(2)}, u32[]{:S(2)}) collective-permute-start(bf16[128,512]{1,0:T(8,128)(2,1)S(1)} %get-tuple-element.33), channel_id=1, source_target_pairs={{0,1},{1,0},{2,3},{3,2},{4,5},{5,4},{6,7},{7,6},{8,9},{9,8},{10,11... | collective-permute-start | bytes 393224 | tf_op jit(solution)/shard_map/ppermute | solution.py:364
  47.8 7.8 %collective-permute-start.11 = (bf16[256,512]{1,0:T(8,128)(2,1)S(1)}, bf16[256,512]{1,0:T(8,128)(2,1)S(1)}, u32[]{:S(2)}, u32[]{:S(2)}) collective-permute-start(bf16[256,512]{1,0:T(8,128)(2,1)S(1)} %get-tuple-element.34), channel_id=1, source_target_pairs={{0,1},{1,0},{2,3},{3,2},{4,5},{5,4},{6,7},{7,6},{8,9},{9,8},{10,11... | collective-permute-start | bytes 786440 | tf_op jit(solution)/shard_map/ppermute | solution.py:364
  49.0 22.9 %copy-start = (f32[1024,512]{1,0:T(8,128)S(1)}, f32[1024,512]{1,0:T(8,128)}, u32[]{:S(2)}) copy-start(f32[1024,512]{1,0:T(8,128)} %refs_4_.3) | copy-start | bytes 6291460
  49.0 22.9 %copy-start.1 = (f32[1024,512]{1,0:T(8,128)S(1)}, f32[1024,512]{1,0:T(8,128)}, u32[]{:S(2)}) copy-start(f32[1024,512]{1,0:T(8,128)} %refs_5_.5) | copy-start | bytes 6291460
  49.0 7.3 %collective-permute-start.12 = (bf16[256,512]{1,0:T(8,128)(2,1)S(1)}, bf16[256,512]{1,0:T(8,128)(2,1)S(1)}, u32[]{:S(2)}, u32[]{:S(2)}) collective-permute-start(bf16[256,512]{1,0:T(8,128)(2,1)S(1)} %get-tuple-element.35), channel_id=1, source_target_pairs={{0,2},{1,3},{2,0},{3,1},{4,6},{5,7},{6,4},{7,5},{8,10},{9,11},{10,... | collective-permute-start | bytes 786440 | tf_op jit(solution)/shard_map/ppermute | solution.py:364
  57.2 13.0 %collective-permute-start.13 = (bf16[256,512]{1,0:T(8,128)(2,1)S(1)}, bf16[256,512]{1,0:T(8,128)(2,1)S(1)}, u32[]{:S(2)}, u32[]{:S(2)}) collective-permute-start(bf16[256,512]{1,0:T(8,128)(2,1)S(1)} %terms_0.1), channel_id=1, source_target_pairs={{0,16},{4,20},{8,24},{12,28},{16,0},{20,4},{24,8},{28,12},{1,17},{... | collective-permute-start | bytes 786440 | tf_op jit(solution)/shard_map/ppermute | solution.py:375
  70.3 1.6 %collective-permute-start.15 = (bf16[256,512]{1,0:T(8,128)(2,1)S(1)}, bf16[256,512]{1,0:T(8,128)(2,1)S(1)}, u32[]{:S(2)}, u32[]{:S(2)}) collective-permute-start(bf16[256,512]{1,0:T(8,128)(2,1)S(1)} %add_convert_fusion.refs_0_), channel_id=1, source_target_pairs={{0,4},{4,0},{8,12},{12,8},{16,20},{20,16},{24,28},{28,24},{1,5},{5... | collective-permute-start | bytes 786440 | tf_op jit(solution)/shard_map/ppermute | solution.py:361
  70.3 8.7 %collective-permute-start.14 = (bf16[256,512]{1,0:T(8,128)(2,1)S(1)}, bf16[256,512]{1,0:T(8,128)(2,1)S(1)}, u32[]{:S(2)}, u32[]{:S(2)}) collective-permute-start(bf16[256,512]{1,0:T(8,128)(2,1)S(1)} %add_convert_fusion.refs_0_), channel_id=1, source_target_pairs={{0,8},{4,12},{8,0},{12,4},{16,24},{20,28},{24,16},{28,20},{1,9},{5... | collective-permute-start | bytes 786440 | tf_op jit(solution)/shard_map/ppermute | solution.py:372
  79.1 1.5 %collective-permute-start.17 = (bf16[256,512]{1,0:T(8,128)(2,1)S(1)}, bf16[256,512]{1,0:T(8,128)(2,1)S(1)}, u32[]{:S(2)}, u32[]{:S(2)}) collective-permute-start(bf16[256,512]{1,0:T(8,128)(2,1)S(1)} %collective-permute-done.14.refs_0_), channel_id=1, source_target_pairs={{0,4},{4,0},{8,12},{12,8},{16,20},{20,16},{24,28},{28,24},{1,5},{5... | collective-permute-start | bytes 786440 | tf_op jit(solution)/shard_map/ppermute | solution.py:361

commit v3 on v2

--- a/solution.py
+++ b/solution.py
@@ -44,18 +44,19 @@
     )(where, *inputs)
 
 
-def cut_out(core, piece, projector, cotangent, fsdp, pieces):
+def cut_out(fsdp_at, core, piece, projector, cotangent, fsdp, pieces):
     rows, rank = projector.shape
     half = rank // CORES
     tokens, width = cotangent.shape
     span = width // (fsdp * pieces)
     steps = 4
 
-    def body(core_ref, piece_ref, proj_ref, cot_ref, proj_out, cot_out, sems):
+    def body(fsdp_ref, core_ref, piece_ref, proj_ref, cot_ref, proj_out, cot_out, sems):
         copies = []
-        for s in range(fsdp):
-            at = pl.multiple_of((s * pieces + pieces - 1 - piece_ref[0]) * span, span)
-            copies.append((cot_ref.at[:, pl.ds(at, span)], cot_out.at[:, pl.ds(s * span, span)]))
+        for s in range(1, fsdp):
+            block = (fsdp_ref[0] ^ s) * pieces + pieces - 1 - piece_ref[0]
+            source = cot_ref.at[:, pl.ds(pl.multiple_of(block * span, span), span)]
+            copies.append((source, cot_out.at[:, pl.ds((s - 1) * span, span)]))
         columns = pl.ds(pl.multiple_of(core_ref[0] * half, half), half)
         for n in range(steps):
             at = pl.ds(n * (rows // steps), rows // steps)
@@ -71,16 +72,16 @@
         body,
         out_shape=[
             jax.ShapeDtypeStruct((rows, half), BF16),
-            jax.ShapeDtypeStruct((tokens, width // pieces), BF16),
+            jax.ShapeDtypeStruct((tokens, (fsdp - 1) * span), BF16),
         ],
-        in_specs=[pl.BlockSpec(memory_space=pltpu.SMEM)] * 2
+        in_specs=[pl.BlockSpec(memory_space=pltpu.SMEM)] * 3
         + [pl.BlockSpec(memory_space=pl.ANY)] * 2,
         out_specs=[pl.BlockSpec(memory_space=pltpu.VMEM)] * 2,
         scratch_shapes=[pltpu.SemaphoreType.DMA((fsdp + steps,))],
         compiler_params=pltpu.CompilerParams(vmem_limit_bytes=8 * MIB),
         cost_estimate=busy(1),
         name="cut_out",
-    )(core, piece, *hbm)
+    )(fsdp_at, core, piece, *hbm)
 
 
 def coords_step(where, acts, proj, total, rows, last, name):
@@ -129,42 +130,58 @@
     )[0]
 
 
-def terms_step(where, cots, coords, span, pieces, entries, name, kind=BF16):
-    tokens = cots[0][0].shape[0]
-    half = coords[0].shape[0]
-    inputs = list(coords)
-    specs = [whole(x) for x in coords]
+def terms_step(where, cots, coords, entries, pieces, span, chunk, name, kind=BF16, estimate=1):
+    per_piece = span // chunk
+    half = entries[0][4][-1][1]
+    inputs = [] if coords is None else [coords]
+    specs = [whole(x) for x in inputs]
     out_shape = []
-    for s, added, cuts in entries:
+    for s, other, j, added, cuts in entries:
         for x, packed in cots:
-            step = 1 if packed else pieces
-            at = functools.partial(
-                lambda s, step, i, w: (0, (w[0] ^ s) * step + (w[2] if step > 1 else 0)),
-                s,
-                step,
-            )
+            if packed and s == 0:
+                continue
+
+            def at(i, w, s=s, other=other, j=j, packed=packed):
+                if packed:
+                    return (0, (s - 1) * per_piece + j)
+                piece = lax.rem(w[2] + other, pieces)
+                return (0, ((w[0] ^ s) * pieces + piece) * per_piece + j)
+
             inputs.append(x)
-            specs.append(pl.BlockSpec((tokens, span), at))
+            specs.append(pl.BlockSpec((x.shape[0], chunk), at))
         for _, x in added:
+            column = j if x.shape[1] > chunk else 0
+            at = functools.partial(lambda c, i, w: (0, c), column)
             inputs.append(x)
-            specs.append(whole(x))
-        out_shape += [jax.ShapeDtypeStruct((b - a, span), kind) for a, b in cuts]
+            specs.append(pl.BlockSpec((x.shape[0], chunk), at))
+        out_shape += [jax.ShapeDtypeStruct((b - a, chunk), kind) for a, b in cuts]
 
     def body(w, *refs):
-        ins = iter(refs[len(coords) : len(inputs)])
+        ins = iter(refs[: len(inputs)])
         outs = iter(refs[len(inputs) : len(inputs) + len(out_shape)])
         value = refs[-1]
-        for s, added, cuts in entries:
+        coords_ref = None if coords is None else next(ins)
+        for s, _, _, added, cuts in entries:
             term = None
-            for n in range(len(cots)):
-                at = slice(n % 2 * tokens, (n % 2 + 1) * tokens)
+            for n, (x, packed) in enumerate(cots):
+                if packed and s == 0:
+                    continue
+                tokens = x.shape[0]
                 part = jnp.dot(
-                    refs[n // 2][:, at], next(ins)[...], preferred_element_type=F32
+                    coords_ref[:, n * tokens : (n + 1) * tokens],
+                    next(ins)[...],
+                    preferred_element_type=F32,
                 )
                 term = part if term is None else term + part
+            extra = [(low, x.shape[0], next(ins)) for low, x in added]
+            for low, size, ref in extra:
+                if size == half:
+                    part = ref[...].astype(F32)
+                    term = part if term is None else term + part
             value[...] = term
-            for low, x in added:
-                value[low : low + x.shape[0], :] += next(ins)[...].astype(F32)
+            for low, size, ref in extra:
+                if size < half:
+                    value[low : low + size, :] += ref[...].astype(F32)
             for a, b in cuts:
                 next(outs)[...] = value[a:b, :].astype(kind)
 
@@ -174,10 +191,10 @@
         inputs,
         specs,
         out_shape,
-        16 * MIB,
-        scratch=[pltpu.VMEM((half, span), F32)],
+        20 * MIB,
+        scratch=[pltpu.VMEM((half, chunk), F32)],
         name=name,
-        estimate=busy(8 if kind == F32 else 1),
+        estimate=busy(estimate),
     )
 
 
@@ -210,22 +227,25 @@
     )(where, *inputs)
 
 
-def update_step(where, k, pieces, own_grad, other_grad, own_proj, other_proj, moments, before):
-    half, span = own_grad.shape
+def update_step(where, k, pieces, low, grads, own_proj, other_proj, moments, before):
+    half, chunk = grads[0][0].shape
+    span = chunk * len(grads)
     rank = CORES * half
     features = moments[0].shape[0]
     width = own_proj.shape[0]
     rows = min(1024, width)
     steps = width // rows
     part = min(256, rows)
+    flat = [x for pair in grads for x in pair]
 
     def body(w, *refs):
-        grads, projs, ins = refs[:2], refs[2:4], refs[4:6]
+        grad_refs, refs = refs[: len(flat)], refs[len(flat) :]
+        projs, ins = refs[:2], refs[2:4]
         first_out, second_out, update = refs[-11:-8]
         moment, proj, direction, out = refs[-8:-4]
         moment_in, moment_out, proj_in, update_out = refs[-4:]
-        base = lax.rem(w[2] + pieces - k, pieces) * span
-        features_at = pl.ds(pl.multiple_of(base, span), span)
+        base = lax.rem(w[2] + pieces - k, pieces) * (features // pieces) + low
+        features_at = pl.ds(pl.multiple_of(base, chunk), span)
 
         def columns(h):
             core = w[1] if h == 0 else 1 - w[1]
@@ -234,28 +254,21 @@
         def here(h):
             return pl.ds(h * half, half)
 
-        loads = [
-            [
-                pltpu.make_async_copy(
-                    ins[n].at[features_at, columns(h)],
-                    moment.at[n, :, here(h)],
-                    moment_in.at[h, n],
-                )
-                for n in range(2)
-            ]
-            for h in range(2)
-        ]
-        stores = [
-            [
-                pltpu.make_async_copy(
-                    moment.at[n, :, here(h)],
-                    (first_out, second_out)[n].at[features_at, columns(h)],
-                    moment_out.at[h, n],
-                )
-                for n in range(2)
-            ]
-            for h in range(2)
-        ]
+        def each(make):
+            return [[make(h, n) for n in range(2)] for h in range(2)]
+
+        loads = each(
+            lambda h, n: pltpu.make_async_copy(
+                ins[n].at[features_at, columns(h)], moment.at[n, :, here(h)], moment_in.at[h, n]
+            )
+        )
+        stores = each(
+            lambda h, n: pltpu.make_async_copy(
+                moment.at[n, :, here(h)],
+                (first_out, second_out)[n].at[features_at, columns(h)],
+                moment_out.at[h, n],
+            )
+        )
         proj_loads = [
             [
                 pltpu.make_async_copy(
@@ -283,17 +296,21 @@
         first_scale = 1.0 / (1.0 - 0.9**STEP)
         second_scale = 1.0 / (1.0 - 0.999**STEP)
         for h in range(2):
-            grad_low = grads[h][...].T.astype(F32)
             for copy in loads[h]:
                 copy.wait()
-            first_new = 0.9 * moment[0, :, here(h)] + 0.1 * grad_low
-            second_new = 0.999 * moment[1, :, here(h)] + 0.001 * grad_low * grad_low
-            moment[0, :, here(h)] = first_new
-            moment[1, :, here(h)] = second_new
+            for m in range(len(grads)):
+                at = pl.ds(m * chunk, chunk)
+                grad_low = grad_refs[2 * m + h][...].T.astype(F32)
+                first_new = 0.9 * moment[0, at, here(h)] + 0.1 * grad_low
+                second_new = 0.999 * moment[1, at, here(h)] + 0.001 * grad_low * grad_low
+                moment[0, at, here(h)] = first_new
+                moment[1, at, here(h)] = second_new
+                ratio = (first_new * first_scale) / (
+                    jnp.sqrt(second_new * second_scale) + 1e-08
+                )
+                direction[here(h), at] = ratio.astype(BF16).T
             for copy in stores[h]:
                 copy.start()
-            ratio = (first_new * first_scale) / (jnp.sqrt(second_new * second_scale) + 1e-08)
-            direction[here(h), :] = ratio.astype(BF16).T
         for r in range(steps):
             for copy in proj_loads[r]:
                 copy.wait()
@@ -304,9 +321,9 @@
         for copy in sum(stores, []) + sum(update_stores, []):
             copy.wait()
 
-    inputs = [own_grad, other_grad, own_proj, other_proj, *moments]
+    inputs = [*flat, own_proj, other_proj, *moments]
     any_space = pl.BlockSpec(memory_space=pl.ANY)
-    in_specs = [whole(own_grad), whole(other_grad)] + [any_space] * 4
+    in_specs = [whole(x) for x in flat] + [any_space] * 4
     aliases = {}
     if before is not None:
         aliases = {1 + len(inputs) + n: n for n in range(3)}
@@ -334,9 +351,13 @@
         ),
         input_output_aliases=aliases,
         compiler_params=pltpu.CompilerParams(vmem_limit_bytes=28 * MIB),
-        cost_estimate=cost(2 * width * rank * span, 4 * width * span + 18 * span * rank),
+        cost_estimate=busy(6),
         name="update_step",
     )(where, *inputs)
+
+
+def in_vmem(x):
+    return pltpu.with_memory_space_constraint(x, pltpu.VMEM)
 
 
 def after(x, *others):
@@ -353,9 +374,13 @@
     groups = dp // CORES
     pieces = 2 if groups % 2 == 0 else 1
     span = rows // pieces
-    fsdp_at = lax.axis_index("fsdp")
+    chunk = span // 2 if span % 256 == 0 else span
+    chunks = range(span // chunk)
+    fsdp_at = lax.axis_index("fsdp").astype(jnp.int32)
     dp_at = lax.axis_index("dp")
-    where = jnp.stack([fsdp_at, dp_at % CORES, (dp_at // CORES) % pieces]).astype(jnp.int32)
+    core_at = (dp_at % CORES).astype(jnp.int32)
+    piece_at = ((dp_at // CORES) % pieces).astype(jnp.int32)
+    where = jnp.stack([fsdp_at, core_at, piece_at])
 
     def to_core(x):
         return lax.ppermute(x, "dp", [(i, i ^ 1) for i in range(dp)])
@@ -382,10 +407,8 @@
     ]
 
     part = rows // 2
-    piece_at = ((dp_at // CORES) % pieces).astype(jnp.int32)
-    core_at = (dp_at % CORES).astype(jnp.int32)
     own_half, cot_out = cut_out(
-        core_at[None], piece_at[None], projector, cotangent, fsdp, pieces
+        fsdp_at[None], core_at[None], piece_at[None], projector, cotangent, fsdp, pieces
     )
     held = {0: [(0, 0, own_half)]}
     for level in levels[1:]:
@@ -398,62 +421,76 @@
                 source = held[s ^ link]
                 x = source[n][2] if len(source) > 1 else source[0][2][n * part : (n + 1) * part]
                 held[s].append((s, n * part, to_fsdp(x, link)))
-    acts_pair = [acts, to_core(acts)]
-    cots = [(cotangent, False), (to_core(after(cotangent, own_half)), False)]
+    acts_pair = [acts, in_vmem(to_core(acts))]
+    cots = [(cotangent, False), (in_vmem(to_core(after(cotangent, own_half))), False)]
 
     total = None
     for n, level in enumerate(levels):
         entries = [x for s in level for x in held[s]]
         last = n == len(levels) - 1
         total = coords_step(where, acts_pair, entries, total, rows, last, f"coords_{n}")
-    coords = [total]
-    landed = {s: [] for s in range(fsdp)}
+    full = [(0, half)]
+    entries = [(s, 0, 0, [], full) for s in range(fsdp)]
+    far_coords = None
     if pieces > 1:
-        coords = [to_piece(total, 1)]
-        entries = [(s, [], [(0, half)]) for s in range(fsdp)]
-        sums = terms_step(where, cots, [total], span, pieces, entries, "terms_chip", F32)
-        for s in range(fsdp):
-            landed[s].append((0, sums[s]))
-        arrived = after(to_piece(cot_out, 1), *sums)
-        cots = [(arrived, True), (to_core(arrived), True)]
+        far_coords = to_piece(total, 1)
+    sums = terms_step(
+        where, cots, total, entries, pieces, span, span, "terms_chip", F32, 12
+    )
+    landed = {s: [(0, x)] for s, x in enumerate(sums)}
+    cots_far = []
+    if pieces > 1:
+        arrived = after(to_piece(cot_out, 1), total)
+        cots_far = [(arrived, True), (in_vmem(to_core(arrived)), True)]
+        entries = [(0, 1, 0, [], full)]
+        (pair_sum,) = terms_step(
+            where, cots, total, entries, pieces, span, span, "terms_pair"
+        )
+        landed[0].append((0, to_piece(pair_sum, 1)))
 
     middle = half // 2
     halves = [(0, middle), (middle, half)]
-    for n in range(len(levels) - 1, -1, -1):
-        level = levels[n]
-        cuts = halves if n > 1 else [(0, half)]
-        entries = [(s, landed[s], cuts) for s in level]
-        outs = terms_step(where, cots, coords, span, pieces, entries, f"terms_{n}")
-        outs = iter(outs)
-        for s in level:
-            if n > 1:
-                for m, link in enumerate(links(s)):
-                    landed[s ^ link].append((m * middle, to_fsdp(next(outs), link)))
-            elif n == 1:
-                landed[0].append((0, to_fsdp(next(outs), s)))
-            else:
-                mine = next(outs)
-    mine = add_up([mine] + [to_base(mine, k) for k in range(1, groups // pieces)])
-    grads = [mine] + [to_piece(mine, k) for k in range(1, pieces)]
-
-    blocks = [(s, low, after(x, *coords)) for s in range(fsdp) for s, low, x in held[s]]
+    for n in range(len(levels) - 1, 1, -1):
+        entries = [(s, 0, 0, landed[s], halves) for s in levels[n]]
+        outs = iter(
+            terms_step(
+                where, cots_far, far_coords, entries, pieces, span, span, f"terms_{n}"
+            )
+        )
+        for s in levels[n]:
+            for m, link in enumerate(links(s)):
+                landed[s ^ link].append((m * middle, to_fsdp(next(outs), link)))
+    near = {j: [] for j in chunks}
+    if fsdp > 1:
+        entries = [(s, 0, j, landed[s], full) for j in chunks for s in levels[1]]
+        outs = terms_step(
+            where, cots_far, far_coords, entries, pieces, span, chunk, "terms_1"
+        )
+        for (s, _, j, _, _), x in zip(entries, outs):
+            near[j].append((0, to_fsdp(x, s)))
+    parts = []
+    for j in chunks:
+        entries = [(0, 0, j, landed[0] + near[j], full)]
+        (x,) = terms_step(where, [], None, entries, pieces, span, chunk, "terms_0", BF16, 1)
+        parts.append([x] + [to_base(x, k) for k in range(1, groups // pieces)])
+    parts[0] = [after(x, parts[-1][0]) for x in parts[0]]
+
+    blocks = [(s, low, after(x, total)) for s in range(fsdp) for s, low, x in held[s]]
     own_proj = assemble(where, blocks, rows, fsdp)
     other_proj = to_core(own_proj)
-    outputs = None
-    for k, grad in enumerate(grads):
+    common = (own_proj, other_proj, (first_moment, second_moment))
+    outputs, others = None, []
+    for j in chunks:
         if outputs is not None:
-            grad = after(grad, *outputs)
-        outputs = update_step(
-            where,
-            k,
-            pieces,
-            grad,
-            to_core(grad),
-            own_proj,
-            other_proj,
-            (first_moment, second_moment),
-            outputs,
-        )
+            parts[j] = [after(x, *outputs, *others) for x in parts[j]]
+        mine = add_up(parts[j])
+        if pieces > 1:
+            others.append(to_piece(mine, 1))
+        pair = (mine, to_core(mine))
+        outputs = update_step(where, 0, pieces, j * chunk, [pair], *common, outputs)
+    if pieces > 1:
+        pairs = [(x, to_core(after(x, *outputs))) for x in others]
+        outputs = update_step(where, 1, pieces, 0, pairs, *common, outputs)
     return tuple(outputs)
 
 

time: 87.5 us -> 82.7 us (0.945)
  waiting for transfers between devices: 36.5 us -> 25.5 us
  starting transfers between devices: 18.7 us -> 27.4 us
  local copies, waits for them, and re-layouts: 1.64 us -> 0.06 us
    ppermute x1 -> x2, waiting for transfers between devices: 10.3 us -> 4.09 us  [to_base(): lax.ppermute(x, 'dp', [(i, (i + k * pieces * CORES) % dp) for i in range(...]
    pallas_call x2 -> x3, Pallas kernels: 13.1 us -> 18 us  [update_step(): pl.pallas_call(body, out_shape=[jax.ShapeDtypeStruct(x.shape, F32) for x...]
    pallas_call x7 -> x9, Pallas kernels: 12.4 us -> 8.41 us  [call(): pl.pallas_call(body, out_shape=out_shape, grid_spec=pltpu.PrefetchScalarG...]
    ppermute x3 -> x5, starting transfers between devices: 3.97 us -> 7.86 us  [to_piece(): return lax.ppermute(x, 'dp', pairs)]
    ppermute x8 -> x10, waiting for transfers between devices: 20.4 us -> 16.8 us  [to_fsdp(): return lax.ppermute(x, 'fsdp', [(i, i ^ s) for i in range(fsdp)])]
    ppermute x8 -> x10, starting transfers between devices: 11.3 us -> 13.7 us  [to_fsdp(): return lax.ppermute(x, 'fsdp', [(i, i ^ s) for i in range(fsdp)])]
    unnamed x8, local copies, waits for them, and re-layouts: 1.6 us -> 0.02 us
    ppermute x1 -> x2, starting transfers between devices: 2.66 us -> 3.97 us  [to_base(): lax.ppermute(x, 'dp', [(i, (i + k * pieces * CORES) % dp) for i in range(...]
  transfers between devices with their start and end apart: 18 -> 25, of which waited for: 10 -> 12; matrix products, arithmetic and copies ran while one was open for 0% -> 0% of each run, Pallas kernels for 26% -> 27%
where the time goes in v3:
time: 82.7 us; the launch traced here: 82.5 us
  Pallas kernels  28.6 us (35%)
  starting transfers between devices  27.4 us (33%)
  waiting for transfers between devices  25.5 us (31%)
  between operations  0.83 us (1%)
    pallas_call x3, Pallas kernels, update_step(): pl.pallas_call(body, out_shape=[jax.ShapeDtypeStruct(x.shape, F32) for x...  18 us
    ppermute x10, waiting for transfers between devices, to_fsdp(): return lax.ppermute(x, 'fsdp', [(i, i ^ s) for i in range(fsdp)])  16.8 us
    ppermute x10, starting transfers between devices, to_fsdp(): return lax.ppermute(x, 'fsdp', [(i, i ^ s) for i in range(fsdp)])  13.7 us
    pallas_call x9, Pallas kernels, call(): pl.pallas_call(body, out_shape=out_shape, grid_spec=pltpu.PrefetchScalarG...  8.41 us
    ppermute x5, starting transfers between devices, to_piece(): return lax.ppermute(x, 'dp', pairs)  7.86 us
    ppermute x2, waiting for transfers between devices, to_base(): lax.ppermute(x, 'dp', [(i, (i + k * pieces * CORES) % dp) for i in range(...  4.09 us
    ppermute x2, starting transfers between devices, to_base(): lax.ppermute(x, 'dp', [(i, (i + k * pieces * CORES) % dp) for i in range(...  3.97 us
    ppermute x5, waiting for transfers between devices, to_piece(): return lax.ppermute(x, 'dp', pairs)  2.51 us
  transfers between devices with their start and end apart: 25, of which 12 were waited for; matrix products, arithmetic and copies ran while one was open for 0% of the time, Pallas kernels for 27%

profile of v3, /device:TPU:0, one launch (start us, length us, event | category | flops | bytes accessed | tf_op | source)
XLA Modules:
  0.0 82.5 jit_solution(3184440072987520776)
XLA Ops:
  1.2 1.5 %cut_out.1 = (bf16[1024,256]{1,0:T(8,128)(2,1)S(1)}, bf16[256,1536]{1,0:T(8,128)(2,1)S(1)}) custom-call(s32[1]{0:T(128)} %bitcast.fsdp_ref, s32[1]{0:T(128)} %bitcast.1.core_ref, s32[1]{0:T(128)} %bitcast.2.piece_ref, bf16[1024,512]{1,0:T(8,128)(2,1)} %proj_ref.1, bf16[256,4096]{1,0:T(8,128)(2,1)} %refs_1_.3), custom_call_target="tpu_custom_call" | custom-call | flops 1150000000 | tf_op jit(solution)/shard_map/cut_out/pallas_call | solution.py:71
  2.6 2.6 %collective-permute-start.3 = (bf16[1024,256]{1,0:T(8,128)(2,1)S(1)}, bf16[1024,256]{1,0:T(8,128)(2,1)S(1)}, u32[]{:S(2)}, u32[]{:S(2)}) collective-permute-start(bf16[1024,256]{1,0:T(8,128)(2,1)S(1)} %get-tuple-element.50.refs_2_.refs_0_), channel_id=1, source_target_pairs={{0,1},{1,0},{2,3},{3,2},{4,5},{5,4},{6,7},{7,6},{8,9},{9,8},{10,11... | collective-permute-start | bytes 1572872 | tf_op jit(solution)/shard_map/ppermute | solution.py:389
  5.3 1.5 %collective-permute-start.1 = (bf16[1024,256]{1,0:T(8,128)(2,1)S(1)}, bf16[1024,256]{1,0:T(8,128)(2,1)S(1)}, u32[]{:S(2)}, u32[]{:S(2)}) collective-permute-start(bf16[1024,256]{1,0:T(8,128)(2,1)S(1)} %get-tuple-element.50.refs_2_.refs_0_), channel_id=1, source_target_pairs={{0,2},{1,3},{2,0},{3,1},{4,6},{5,7},{6,4},{7,5},{8,10},{9,11},{10,... | collective-permute-start | bytes 1572872 | tf_op jit(solution)/shard_map/ppermute | solution.py:389
  6.8 1.6 %collective-permute-start.8 = (bf16[256,1536]{1,0:T(8,128)(2,1)S(1)}, bf16[256,1536]{1,0:T(8,128)(2,1)S(1)}, u32[]{:S(2)}, u32[]{:S(2)}) collective-permute-start(bf16[256,1536]{1,0:T(8,128)(2,1)S(1)} %get-tuple-element.37), channel_id=1, source_target_pairs={{0,8},{4,12},{8,0},{12,4},{16,24},{20,28},{24,16},{28,20},{1,9},{5... | collective-permute-start | bytes 2359304 | tf_op jit(solution)/shard_map/ppermute | solution.py:397
  8.4 9.3 %collective-permute-done.3.refs_2_.refs_1_ = bf16[1024,256]{1,0:T(8,128)(2,1)S(1)} collective-permute-done((bf16[1024,256]{1,0:T(8,128)(2,1)S(1)}, bf16[1024,256]{1,0:T(8,128)(2,1)S(1)}, u32[]{:S(2)}, u32[]{:S(2)}) %collective-permute-start.3) | collective-permute-done | bytes 524320 | tf_op jit(solution)/shard_map/ppermute | solution.py:389
  17.8 1.8 %collective-permute-start.4 = (bf16[512,256]{1,0:T(8,128)(2,1)S(1)}, bf16[512,256]{1,0:T(8,128)(2,1)S(1)}, u32[]{:S(2)}, u32[]{:S(2)}) collective-permute-start(bf16[512,256]{1,0:T(8,128)(2,1)S(1)} %slice.9), channel_id=1, source_target_pairs={{0,2},{1,3},{2,0},{3,1},{4,6},{5,7},{6,4},{7,5},{8,10},{9,11},{10,... | collective-permute-start | bytes 786440 | tf_op jit(solution)/shard_map/ppermute | solution.py:389
  19.7 1.6 %collective-permute-start.2 = (bf16[512,256]{1,0:T(8,128)(2,1)S(1)}, bf16[512,256]{1,0:T(8,128)(2,1)S(1)}, u32[]{:S(2)}, u32[]{:S(2)}) collective-permute-start(bf16[512,256]{1,0:T(8,128)(2,1)S(1)} %slice.8), channel_id=1, source_target_pairs={{0,1},{1,0},{2,3},{3,2},{4,5},{5,4},{6,7},{7,6},{8,9},{9,8},{10,11... | collective-permute-start | bytes 786440 | tf_op jit(solution)/shard_map/ppermute | solution.py:389
  22.2 1.3 %coords_1.1.refs_6_ = f32[512,256]{1,0:T(8,128)S(1)} custom-call(s32[3]{0:T(128)S(1)} %pad_add_fusion.w, bf16[256,4096]{1,0:T(8,128)(2,1)S(1)} %copy-done.3, bf16[256,4096]{1,0:T(8,128)(2,1)S(1)} %collective-permute-done.refs_1_.refs_4_, bf16[1024,256]{1,0:T(8,128)(2,1)S(1)} %collective-permute-done.3.refs_2_.refs_1_, bf16[256,4096]{1,0:T(8,128)(2,1)S(1)} %copy-done.3, ...), custom_call_target="tpu_custom_call" | custom-call | flops 9200000000 | tf_op jit(solution)/shard_map/coords_1/pallas_call | solution.py:31
  23.5 2.5 %collective-permute-done.4.refs_5_.refs_4_ = bf16[512,256]{1,0:T(8,128)(2,1)S(1)} collective-permute-done((bf16[512,256]{1,0:T(8,128)(2,1)S(1)}, bf16[512,256]{1,0:T(8,128)(2,1)S(1)}, u32[]{:S(2)}, u32[]{:S(2)}) %collective-permute-start.4) | collective-permute-done | bytes 262176 | tf_op jit(solution)/shard_map/ppermute | solution.py:389
  25.9 1.4 %collective-permute-done.2.refs_2_.refs_3_ = bf16[512,256]{1,0:T(8,128)(2,1)S(1)} collective-permute-done((bf16[512,256]{1,0:T(8,128)(2,1)S(1)}, bf16[512,256]{1,0:T(8,128)(2,1)S(1)}, u32[]{:S(2)}, u32[]{:S(2)}) %collective-permute-start.2) | collective-permute-done | bytes 262176 | tf_op jit(solution)/shard_map/ppermute | solution.py:389
  28.4 1.6 %collective-permute-start.7 = (bf16[256,512]{1,0:T(8,128)(2,1)S(1)}, bf16[256,512]{1,0:T(8,128)(2,1)S(1)}, u32[]{:S(2)}, u32[]{:S(2)}) collective-permute-start(bf16[256,512]{1,0:T(8,128)(2,1)S(1)} %coords_2.1.refs_0_), channel_id=1, source_target_pairs={{0,8},{4,12},{8,0},{12,4},{16,24},{20,28},{24,16},{28,20},{1,9},{5... | collective-permute-start | bytes 786440 | tf_op jit(solution)/shard_map/ppermute | solution.py:397
  31.4 1.2 %terms_chip.1 = (f32[256,512]{1,0:T(8,128)S(1)}, f32[256,512]{1,0:T(8,128)S(1)}, f32[256,512]{1,0:T(8,128)S(1)}, f32[256,512]{1,0:T(8,128)S(1)}) custom-call(s32[3]{0:T(128)S(1)} %pad_add_fusion.w, bf16[256,512]{1,0:T(8,128)(2,1)S(1)} %coords_2.1.refs_0_, bf16[256,4096]{1,0:T(8,128)(2,1)S(1)} %copy-done.2, ...), custom_call_target="tpu_custom_call" | custom-call | flops 13799999488 | tf_op jit(solution)/shard_map/terms_chip/pallas_call | solution.py:31
  32.6 2.5 %collective-permute-done.7.refs_0_ = bf16[256,512]{1,0:T(8,128)(2,1)S(1)} collective-permute-done((bf16[256,512]{1,0:T(8,128)(2,1)S(1)}, bf16[256,512]{1,0:T(8,128)(2,1)S(1)}, u32[]{:S(2)}, u32[]{:S(2)}) %collective-permute-start.7) | collective-permute-done | bytes 262176 | tf_op jit(solution)/shard_map/ppermute | solution.py:397
  36.0 1.1 %collective-permute-start.10 = (bf16[128,512]{1,0:T(8,128)(2,1)S(1)}, bf16[128,512]{1,0:T(8,128)(2,1)S(1)}, u32[]{:S(2)}, u32[]{:S(2)}) collective-permute-start(bf16[128,512]{1,0:T(8,128)(2,1)S(1)} %get-tuple-element.41), channel_id=1, source_target_pairs={{0,2},{1,3},{2,0},{3,1},{4,6},{5,7},{6,4},{7,5},{8,10},{9,11},{10,... | collective-permute-start | bytes 393224 | tf_op jit(solution)/shard_map/ppermute | solution.py:389
  38.9 1.6 %collective-permute-start.6 = (bf16[256,512]{1,0:T(8,128)(2,1)S(1)}, bf16[256,512]{1,0:T(8,128)(2,1)S(1)}, u32[]{:S(2)}, u32[]{:S(2)}) collective-permute-start(bf16[256,512]{1,0:T(8,128)(2,1)S(1)} %terms_pair.1), channel_id=1, source_target_pairs={{0,8},{4,12},{8,0},{12,4},{16,24},{20,28},{24,16},{28,20},{1,9},{5... | collective-permute-start | bytes 786440 | tf_op jit(solution)/shard_map/ppermute | solution.py:397
  41.0 1.2 %collective-permute-done.11.refs_8_.refs_16_ = bf16[128,512]{1,0:T(8,128)(2,1)S(1)} collective-permute-done((bf16[128,512]{1,0:T(8,128)(2,1)S(1)}, bf16[128,512]{1,0:T(8,128)(2,1)S(1)}, u32[]{:S(2)}, u32[]{:S(2)}) %collective-permute-start.11) | collective-permute-done | bytes 131104 | tf_op jit(solution)/shard_map/ppermute | solution.py:389
  44.3 1.5 %collective-permute-start.13 = (bf16[256,256]{1,0:T(8,128)(2,1)S(1)}, bf16[256,256]{1,0:T(8,128)(2,1)S(1)}, u32[]{:S(2)}, u32[]{:S(2)}) collective-permute-start(bf16[256,256]{1,0:T(8,128)(2,1)S(1)} %get-tuple-element.45), channel_id=1, source_target_pairs={{0,2},{1,3},{2,0},{3,1},{4,6},{5,7},{6,4},{7,5},{8,10},{9,11},{10,... | collective-permute-start | bytes 393224 | tf_op jit(solution)/shard_map/ppermute | solution.py:389
  49.9 2.6 %collective-permute-start.16 = (bf16[256,256]{1,0:T(8,128)(2,1)S(1)}, bf16[256,256]{1,0:T(8,128)(2,1)S(1)}, u32[]{:S(2)}, u32[]{:S(2)}) collective-permute-start(bf16[256,256]{1,0:T(8,128)(2,1)S(1)} %terms_0.2), channel_id=1, source_target_pairs={{0,16},{4,20},{8,24},{12,28},{16,0},{20,4},{24,8},{28,12},{1,17},{... | collective-permute-start | bytes 393224 | tf_op jit(solution)/shard_map/ppermute | solution.py:400
  53.1 4.1 %collective-permute-done.16 = bf16[256,256]{1,0:T(8,128)(2,1)S(1)} collective-permute-done((bf16[256,256]{1,0:T(8,128)(2,1)S(1)}, bf16[256,256]{1,0:T(8,128)(2,1)S(1)}, u32[]{:S(2)}, u32[]{:S(2)}) %collective-permute-start.16) | collective-permute-done | bytes 131104 | tf_op jit(solution)/shard_map/ppermute | solution.py:400
  57.3 1.3 %collective-permute-start.20 = (bf16[256,256]{1,0:T(8,128)(2,1)S(1)}, bf16[256,256]{1,0:T(8,128)(2,1)S(1)}, u32[]{:S(2)}, u32[]{:S(2)}) collective-permute-start(bf16[256,256]{1,0:T(8,128)(2,1)S(1)} %terms_0.3), channel_id=1, source_target_pairs={{0,16},{4,20},{8,24},{12,28},{16,0},{20,4},{24,8},{28,12},{1,17},{... | collective-permute-start | bytes 393224 | tf_op jit(solution)/shard_map/ppermute | solution.py:400
  58.6 2.8 %collective-permute-start.17 = (bf16[256,256]{1,0:T(8,128)(2,1)S(1)}, bf16[256,256]{1,0:T(8,128)(2,1)S(1)}, u32[]{:S(2)}, u32[]{:S(2)}) collective-permute-start(bf16[256,256]{1,0:T(8,128)(2,1)S(1)} %add_convert_fusion.1.refs_0_), channel_id=1, source_target_pairs={{0,8},{4,12},{8,0},{12,4},{16,24},{20,28},{24,16},{28,20},{1,9},{5... | collective-permute-start | bytes 393224 | tf_op jit(solution)/shard_map/ppermute | solution.py:397
  61.4 5.7 %update_step.3 = (f32[1024,512]{1,0:T(8,128)}, f32[1024,512]{1,0:T(8,128)}, f32[4096,1024]{1,0:T(8,128)}) custom-call(s32[3]{0:T(128)S(1)} %pad_add_fusion.w, bf16[256,256]{1,0:T(8,128)(2,1)S(1)} %add_convert_fusion.1.refs_0_, bf16[256,256]{1,0:T(8,128)(2,1)S(1)} %collective-permute-done.18.refs_1_, bf16[4096,256]{1,0:T(8,128)(2,1)S(1)} %assemble.1.refs_2_.refs_4_, ...), custom_call_target="tpu_custom_call" | custom-call | flops 6899999744 | tf_op jit(solution)/shard_map/update_step/pallas_call | solution.py:332
  68.6 5.7 %update_step.4 = (f32[1024,512]{1,0:T(8,128)}, f32[1024,512]{1,0:T(8,128)}, f32[4096,1024]{1,0:T(8,128)}) custom-call(s32[3]{0:T(128)S(1)} %pad_add_fusion.w, bf16[256,256]{1,0:T(8,128)(2,1)S(1)} %add_convert_fusion.refs_0_, bf16[256,256]{1,0:T(8,128)(2,1)S(1)} %collective-permute-done.21.refs_1_, ...), custom_call_target="tpu_custom_call", output_to_operand_aliasing={{0}: (7, {}), {1}: (8, {}), {2}: (9, {})} | custom-call | flops 6899999744 | tf_op jit(solution)/shard_map/update_step/pallas_call | solution.py:332
  75.8 6.7 %update_step.5 = (f32[1024,512]{1,0:T(8,128)}, f32[1024,512]{1,0:T(8,128)}, f32[4096,1024]{1,0:T(8,128)}) custom-call(s32[3]{0:T(128)S(1)} %pad_add_fusion.w, bf16[256,256]{1,0:T(8,128)(2,1)S(1)} %collective-permute-done.17.refs_0_, ...), custom_call_target="tpu_custom_call", output_to_operand_aliasing={{0}: (9, {}), {1}: (10, {}), {2}: (11, {})} | custom-call | flops 6899999744 | tf_op jit(solution)/shard_map/update_step/pallas_call | solution.py:332
  (53 shorter events, 17.0 us)
Async XLA Ops:
  0.6 20.6 %collective-permute-start = (bf16[256,4096]{1,0:T(8,128)(2,1)}, bf16[256,4096]{1,0:T(8,128)(2,1)S(1)}, u32[]{:S(2)}, u32[]{:S(2)}) collective-permute-start(bf16[256,4096]{1,0:T(8,128)(2,1)} %refs_3_.4), channel_id=1, source_target_pairs={{0,4},{4,0},{8,12},{12,8},{16,20},{20,16},{24,28},{28,24},{1,5},{5... | collective-permute-start | bytes 6291464 | tf_op jit(solution)/shard_map/ppermute | solution.py:386
  2.6 15.2 %collective-permute-start.3 = (bf16[1024,256]{1,0:T(8,128)(2,1)S(1)}, bf16[1024,256]{1,0:T(8,128)(2,1)S(1)}, u32[]{:S(2)}, u32[]{:S(2)}) collective-permute-start(bf16[1024,256]{1,0:T(8,128)(2,1)S(1)} %get-tuple-element.50.refs_2_.refs_0_), channel_id=1, source_target_pairs={{0,1},{1,0},{2,3},{3,2},{4,5},{5,4},{6,7},{7,6},{8,9},{9,8},{10,11... | collective-permute-start | bytes 1572872 | tf_op jit(solution)/shard_map/ppermute | solution.py:389
  5.3 14.4 %collective-permute-start.1 = (bf16[1024,256]{1,0:T(8,128)(2,1)S(1)}, bf16[1024,256]{1,0:T(8,128)(2,1)S(1)}, u32[]{:S(2)}, u32[]{:S(2)}) collective-permute-start(bf16[1024,256]{1,0:T(8,128)(2,1)S(1)} %get-tuple-element.50.refs_2_.refs_0_), channel_id=1, source_target_pairs={{0,2},{1,3},{2,0},{3,1},{4,6},{5,7},{6,4},{7,5},{8,10},{9,11},{10,... | collective-permute-start | bytes 1572872 | tf_op jit(solution)/shard_map/ppermute | solution.py:389
  6.8 23.3 %collective-permute-start.8 = (bf16[256,1536]{1,0:T(8,128)(2,1)S(1)}, bf16[256,1536]{1,0:T(8,128)(2,1)S(1)}, u32[]{:S(2)}, u32[]{:S(2)}) collective-permute-start(bf16[256,1536]{1,0:T(8,128)(2,1)S(1)} %get-tuple-element.37), channel_id=1, source_target_pairs={{0,8},{4,12},{8,0},{12,4},{16,24},{20,28},{24,16},{28,20},{1,9},{5... | collective-permute-start | bytes 2359304 | tf_op jit(solution)/shard_map/ppermute | solution.py:397
  8.4 23.0 %collective-permute-start.5 = (bf16[256,4096]{1,0:T(8,128)(2,1)S(1)}, bf16[256,4096]{1,0:T(8,128)(2,1)S(1)}, u32[]{:S(2)}, u32[]{:S(2)}) collective-permute-start(bf16[256,4096]{1,0:T(8,128)(2,1)S(1)} %copy-done.2), channel_id=1, source_target_pairs={{0,4},{4,0},{8,12},{12,8},{16,20},{20,16},{24,28},{28,24},{1,5},{5... | collective-permute-start | bytes 6291464 | tf_op jit(solution)/shard_map/ppermute | solution.py:386
  17.8 8.1 %collective-permute-start.4 = (bf16[512,256]{1,0:T(8,128)(2,1)S(1)}, bf16[512,256]{1,0:T(8,128)(2,1)S(1)}, u32[]{:S(2)}, u32[]{:S(2)}) collective-permute-start(bf16[512,256]{1,0:T(8,128)(2,1)S(1)} %slice.9), channel_id=1, source_target_pairs={{0,2},{1,3},{2,0},{3,1},{4,6},{5,7},{6,4},{7,5},{8,10},{9,11},{10,... | collective-permute-start | bytes 786440 | tf_op jit(solution)/shard_map/ppermute | solution.py:389
  19.7 7.6 %collective-permute-start.2 = (bf16[512,256]{1,0:T(8,128)(2,1)S(1)}, bf16[512,256]{1,0:T(8,128)(2,1)S(1)}, u32[]{:S(2)}, u32[]{:S(2)}) collective-permute-start(bf16[512,256]{1,0:T(8,128)(2,1)S(1)} %slice.8), channel_id=1, source_target_pairs={{0,1},{1,0},{2,3},{3,2},{4,5},{5,4},{6,7},{7,6},{8,9},{9,8},{10,11... | collective-permute-start | bytes 786440 | tf_op jit(solution)/shard_map/ppermute | solution.py:389
  28.4 6.7 %collective-permute-start.7 = (bf16[256,512]{1,0:T(8,128)(2,1)S(1)}, bf16[256,512]{1,0:T(8,128)(2,1)S(1)}, u32[]{:S(2)}, u32[]{:S(2)}) collective-permute-start(bf16[256,512]{1,0:T(8,128)(2,1)S(1)} %coords_2.1.refs_0_), channel_id=1, source_target_pairs={{0,8},{4,12},{8,0},{12,4},{16,24},{20,28},{24,16},{28,20},{1,9},{5... | collective-permute-start | bytes 786440 | tf_op jit(solution)/shard_map/ppermute | solution.py:397
  30.0 5.1 %collective-permute-start.9 = (bf16[256,1536]{1,0:T(8,128)(2,1)S(1)}, bf16[256,1536]{1,0:T(8,128)(2,1)S(1)}, u32[]{:S(2)}, u32[]{:S(2)}) collective-permute-start(bf16[256,1536]{1,0:T(8,128)(2,1)S(1)} %collective-permute-done.8.refs_1_.refs_5_.refs_9_.refs_13_), channel_id=1, source_target_pairs={{0,4},{4,0},{8,12},{12,8},{16,20},{20,16},{24,28},{28,24},{1,5},{5... | collective-permute-start | bytes 2359304 | tf_op jit(solution)/shard_map/ppermute | solution.py:386
  30.8 30.6 %collective-permute-start.19 = (bf16[4096,256]{1,0:T(8,128)(2,1)S(1)}, bf16[4096,256]{1,0:T(8,128)(2,1)S(1)}, u32[]{:S(2)}, u32[]{:S(2)}) collective-permute-start(bf16[4096,256]{1,0:T(8,128)(2,1)S(1)} %assemble.1.refs_2_.refs_4_), channel_id=1, source_target_pairs={{0,4},{4,0},{8,12},{12,8},{16,20},{20,16},{24,28},{28,24},{1,5},{5... | collective-permute-start | bytes 6291464 | tf_op jit(solution)/shard_map/ppermute | solution.py:386
  36.0 5.0 %collective-permute-start.10 = (bf16[128,512]{1,0:T(8,128)(2,1)S(1)}, bf16[128,512]{1,0:T(8,128)(2,1)S(1)}, u32[]{:S(2)}, u32[]{:S(2)}) collective-permute-start(bf16[128,512]{1,0:T(8,128)(2,1)S(1)} %get-tuple-element.41), channel_id=1, source_target_pairs={{0,2},{1,3},{2,0},{3,1},{4,6},{5,7},{6,4},{7,5},{8,10},{9,11},{10,... | collective-permute-start | bytes 393224 | tf_op jit(solution)/shard_map/ppermute | solution.py:389
  37.1 5.1 %collective-permute-start.11 = (bf16[128,512]{1,0:T(8,128)(2,1)S(1)}, bf16[128,512]{1,0:T(8,128)(2,1)S(1)}, u32[]{:S(2)}, u32[]{:S(2)}) collective-permute-start(bf16[128,512]{1,0:T(8,128)(2,1)S(1)} %get-tuple-element.43), channel_id=1, source_target_pairs={{0,1},{1,0},{2,3},{3,2},{4,5},{5,4},{6,7},{7,6},{8,9},{9,8},{10,11... | collective-permute-start | bytes 393224 | tf_op jit(solution)/shard_map/ppermute | solution.py:389
  38.9 7.4 %collective-permute-start.6 = (bf16[256,512]{1,0:T(8,128)(2,1)S(1)}, bf16[256,512]{1,0:T(8,128)(2,1)S(1)}, u32[]{:S(2)}, u32[]{:S(2)}) collective-permute-start(bf16[256,512]{1,0:T(8,128)(2,1)S(1)} %terms_pair.1), channel_id=1, source_target_pairs={{0,8},{4,12},{8,0},{12,4},{16,24},{20,28},{24,16},{28,20},{1,9},{5... | collective-permute-start | bytes 786440 | tf_op jit(solution)/shard_map/ppermute | solution.py:397
  43.2 5.0 %collective-permute-start.12 = (bf16[256,256]{1,0:T(8,128)(2,1)S(1)}, bf16[256,256]{1,0:T(8,128)(2,1)S(1)}, u32[]{:S(2)}, u32[]{:S(2)}) collective-permute-start(bf16[256,256]{1,0:T(8,128)(2,1)S(1)} %get-tuple-element.44), channel_id=1, source_target_pairs={{0,1},{1,0},{2,3},{3,2},{4,5},{5,4},{6,7},{7,6},{8,9},{9,8},{10,11... | collective-permute-start | bytes 393224 | tf_op jit(solution)/shard_map/ppermute | solution.py:389
  44.3 5.0 %collective-permute-start.13 = (bf16[256,256]{1,0:T(8,128)(2,1)S(1)}, bf16[256,256]{1,0:T(8,128)(2,1)S(1)}, u32[]{:S(2)}, u32[]{:S(2)}) collective-permute-start(bf16[256,256]{1,0:T(8,128)(2,1)S(1)} %get-tuple-element.45), channel_id=1, source_target_pairs={{0,2},{1,3},{2,0},{3,1},{4,6},{5,7},{6,4},{7,5},{8,10},{9,11},{10,... | collective-permute-start | bytes 393224 | tf_op jit(solution)/shard_map/ppermute | solution.py:389
  45.8 6.7 %collective-permute-start.14 = (bf16[256,256]{1,0:T(8,128)(2,1)S(1)}, bf16[256,256]{1,0:T(8,128)(2,1)S(1)}, u32[]{:S(2)}, u32[]{:S(2)}) collective-permute-start(bf16[256,256]{1,0:T(8,128)(2,1)S(1)} %get-tuple-element.46), channel_id=1, source_target_pairs={{0,1},{1,0},{2,3},{3,2},{4,5},{5,4},{6,7},{7,6},{8,9},{9,8},{10,11... | collective-permute-start | bytes 393224 | tf_op jit(solution)/shard_map/ppermute | solution.py:389
  46.3 6.2 %collective-permute-start.15 = (bf16[256,256]{1,0:T(8,128)(2,1)S(1)}, bf16[256,256]{1,0:T(8,128)(2,1)S(1)}, u32[]{:S(2)}, u32[]{:S(2)}) collective-permute-start(bf16[256,256]{1,0:T(8,128)(2,1)S(1)} %get-tuple-element.47), channel_id=1, source_target_pairs={{0,2},{1,3},{2,0},{3,1},{4,6},{5,7},{6,4},{7,5},{8,10},{9,11},{10,... | collective-permute-start | bytes 393224 | tf_op jit(solution)/shard_map/ppermute | solution.py:389
  49.9 7.3 %collective-permute-start.16 = (bf16[256,256]{1,0:T(8,128)(2,1)S(1)}, bf16[256,256]{1,0:T(8,128)(2,1)S(1)}, u32[]{:S(2)}, u32[]{:S(2)}) collective-permute-start(bf16[256,256]{1,0:T(8,128)(2,1)S(1)} %terms_0.2), channel_id=1, source_target_pairs={{0,16},{4,20},{8,24},{12,28},{16,0},{20,4},{24,8},{28,12},{1,17},{... | collective-permute-start | bytes 393224 | tf_op jit(solution)/shard_map/ppermute | solution.py:400
  57.2 4.2 %collective-permute-start.18 = (bf16[256,256]{1,0:T(8,128)(2,1)S(1)}, bf16[256,256]{1,0:T(8,128)(2,1)S(1)}, u32[]{:S(2)}, u32[]{:S(2)}) collective-permute-start(bf16[256,256]{1,0:T(8,128)(2,1)S(1)} %add_convert_fusion.1.refs_0_), channel_id=1, source_target_pairs={{0,4},{4,0},{8,12},{12,8},{16,20},{20,16},{24,28},{28,24},{1,5},{5... | collective-permute-start | bytes 393224 | tf_op jit(solution)/shard_map/ppermute | solution.py:386
  57.3 9.8 %collective-permute-start.20 = (bf16[256,256]{1,0:T(8,128)(2,1)S(1)}, bf16[256,256]{1,0:T(8,128)(2,1)S(1)}, u32[]{:S(2)}, u32[]{:S(2)}) collective-permute-start(bf16[256,256]{1,0:T(8,128)(2,1)S(1)} %terms_0.3), channel_id=1, source_target_pairs={{0,16},{4,20},{8,24},{12,28},{16,0},{20,4},{24,8},{28,12},{1,17},{... | collective-permute-start | bytes 393224 | tf_op jit(solution)/shard_map/ppermute | solution.py:400
  58.6 8.5 %collective-permute-start.17 = (bf16[256,256]{1,0:T(8,128)(2,1)S(1)}, bf16[256,256]{1,0:T(8,128)(2,1)S(1)}, u32[]{:S(2)}, u32[]{:S(2)}) collective-permute-start(bf16[256,256]{1,0:T(8,128)(2,1)S(1)} %add_convert_fusion.1.refs_0_), channel_id=1, source_target_pairs={{0,8},{4,12},{8,0},{12,4},{16,24},{20,28},{24,16},{28,20},{1,9},{5... | collective-permute-start | bytes 393224 | tf_op jit(solution)/shard_map/ppermute | solution.py:397
  67.2 1.4 %collective-permute-start.21 = (bf16[256,256]{1,0:T(8,128)(2,1)S(1)}, bf16[256,256]{1,0:T(8,128)(2,1)S(1)}, u32[]{:S(2)}, u32[]{:S(2)}) collective-permute-start(bf16[256,256]{1,0:T(8,128)(2,1)S(1)} %add_convert_fusion.refs_0_), channel_id=1, source_target_pairs={{0,4},{4,0},{8,12},{12,8},{16,20},{20,16},{24,28},{28,24},{1,5},{5... | collective-permute-start | bytes 393224 | tf_op jit(solution)/shard_map/ppermute | solution.py:386
  67.2 7.0 %collective-permute-start.23 = (bf16[256,256]{1,0:T(8,128)(2,1)S(1)}, bf16[256,256]{1,0:T(8,128)(2,1)S(1)}, u32[]{:S(2)}, u32[]{:S(2)}) collective-permute-start(bf16[256,256]{1,0:T(8,128)(2,1)S(1)} %add_convert_fusion.refs_0_), channel_id=1, source_target_pairs={{0,8},{4,12},{8,0},{12,4},{16,24},{20,28},{24,16},{28,20},{1,9},{5... | collective-permute-start | bytes 393224 | tf_op jit(solution)/shard_map/ppermute | solution.py:397
  74.2 1.4 %collective-permute-start.22 = (bf16[256,256]{1,0:T(8,128)(2,1)S(1)}, bf16[256,256]{1,0:T(8,128)(2,1)S(1)}, u32[]{:S(2)}, u32[]{:S(2)}) collective-permute-start(bf16[256,256]{1,0:T(8,128)(2,1)S(1)} %collective-permute-done.17.refs_0_), channel_id=1, source_target_pairs={{0,4},{4,0},{8,12},{12,8},{16,20},{20,16},{24,28},{28,24},{1,5},{5... | collective-permute-start | bytes 393224 | tf_op jit(solution)/shard_map/ppermute | solution.py:386
  (5 other events, 51.9 us)

commit v4 on v3

--- a/solution.py
+++ b/solution.py
@@ -240,45 +240,21 @@
 
     def body(w, *refs):
         grad_refs, refs = refs[: len(flat)], refs[len(flat) :]
-        projs, ins = refs[:2], refs[2:4]
-        first_out, second_out, update = refs[-11:-8]
-        moment, proj, direction, out = refs[-8:-4]
-        moment_in, moment_out, proj_in, update_out = refs[-4:]
+        own, other, ins = refs[0], refs[1], refs[2:4]
+        outs, update = refs[-9:-7], refs[-7]
+        moment, direction, out = refs[-6:-3]
+        moment_in, moment_out, update_out = refs[-3:]
         base = lax.rem(w[2] + pieces - k, pieces) * (features // pieces) + low
         features_at = pl.ds(pl.multiple_of(base, chunk), span)
-
-        def columns(h):
-            core = w[1] if h == 0 else 1 - w[1]
-            return pl.ds(pl.multiple_of(core * half, half), half)
-
-        def here(h):
-            return pl.ds(h * half, half)
-
-        def each(make):
-            return [[make(h, n) for n in range(2)] for h in range(2)]
-
-        loads = each(
-            lambda h, n: pltpu.make_async_copy(
-                ins[n].at[features_at, columns(h)], moment.at[n, :, here(h)], moment_in.at[h, n]
-            )
-        )
-        stores = each(
-            lambda h, n: pltpu.make_async_copy(
-                moment.at[n, :, here(h)],
-                (first_out, second_out)[n].at[features_at, columns(h)],
-                moment_out.at[h, n],
-            )
-        )
-        proj_loads = [
-            [
-                pltpu.make_async_copy(
-                    projs[h].at[pl.ds(r * rows, rows), :],
-                    proj.at[pl.ds(r * rows, rows), here(h)],
-                    proj_in.at[h, r],
-                )
-                for h in range(2)
-            ]
-            for r in range(steps)
+        own_rows = pl.ds(pl.multiple_of(w[1] * half, half), half)
+        other_rows = pl.ds(pl.multiple_of((1 - w[1]) * half, half), half)
+        loads = [
+            pltpu.make_async_copy(ins[n].at[features_at, :], moment.at[n], moment_in.at[n])
+            for n in range(2)
+        ]
+        stores = [
+            pltpu.make_async_copy(moment.at[n], outs[n].at[features_at, :], moment_out.at[n])
+            for n in range(2)
         ]
         update_stores = [
             [
@@ -291,39 +267,41 @@
             ]
             for r in range(steps)
         ]
-        for copy in sum(loads, []) + sum(proj_loads, []):
+        for copy in loads:
             copy.start()
+        for copy in loads:
+            copy.wait()
         first_scale = 1.0 / (1.0 - 0.9**STEP)
         second_scale = 1.0 / (1.0 - 0.999**STEP)
-        for h in range(2):
-            for copy in loads[h]:
-                copy.wait()
-            for m in range(len(grads)):
-                at = pl.ds(m * chunk, chunk)
-                grad_low = grad_refs[2 * m + h][...].T.astype(F32)
-                first_new = 0.9 * moment[0, at, here(h)] + 0.1 * grad_low
-                second_new = 0.999 * moment[1, at, here(h)] + 0.001 * grad_low * grad_low
-                moment[0, at, here(h)] = first_new
-                moment[1, at, here(h)] = second_new
+        for m in range(len(grads)):
+            at = pl.ds(m * chunk, chunk)
+            mine, others = grad_refs[2 * m][...], grad_refs[2 * m + 1][...]
+            for h in range(2):
+                here = pl.ds(h * half, half)
+                grad_low = jnp.where(w[1] == h, mine, others).T.astype(F32)
+                first_new = 0.9 * moment[0, at, here] + 0.1 * grad_low
+                second_new = 0.999 * moment[1, at, here] + 0.001 * grad_low * grad_low
+                moment[0, at, here] = first_new
+                moment[1, at, here] = second_new
                 ratio = (first_new * first_scale) / (
                     jnp.sqrt(second_new * second_scale) + 1e-08
                 )
-                direction[here(h), at] = ratio.astype(BF16).T
-            for copy in stores[h]:
-                copy.start()
+                direction[here, at] = ratio.astype(BF16).T
+        for copy in stores:
+            copy.start()
         for r in range(steps):
-            for copy in proj_loads[r]:
-                copy.wait()
             at = pl.ds(r * rows, rows)
-            out[at, :] = jnp.dot(proj[at, :], direction[...], preferred_element_type=F32)
+            out[at, :] = jnp.dot(
+                own[at, :], direction[own_rows, :], preferred_element_type=F32
+            ) + jnp.dot(other[at, :], direction[other_rows, :], preferred_element_type=F32)
             for copy in update_stores[r]:
                 copy.start()
-        for copy in sum(stores, []) + sum(update_stores, []):
+        for copy in stores + sum(update_stores, []):
             copy.wait()
 
     inputs = [*flat, own_proj, other_proj, *moments]
     any_space = pl.BlockSpec(memory_space=pl.ANY)
-    in_specs = [whole(x) for x in flat] + [any_space] * 4
+    in_specs = [whole(x) for x in (*flat, own_proj, other_proj)] + [any_space] * 2
     aliases = {}
     if before is not None:
         aliases = {1 + len(inputs) + n: n for n in range(3)}
@@ -340,12 +318,10 @@
             out_specs=[any_space] * 3,
             scratch_shapes=[
                 pltpu.VMEM((2, span, rank), F32),
-                pltpu.VMEM((width, rank), BF16),
                 pltpu.VMEM((rank, span), BF16),
                 pltpu.VMEM((width, span), F32),
-                pltpu.SemaphoreType.DMA((2, 2)),
-                pltpu.SemaphoreType.DMA((2, 2)),
-                pltpu.SemaphoreType.DMA((2, steps)),
+                pltpu.SemaphoreType.DMA((2,)),
+                pltpu.SemaphoreType.DMA((2,)),
                 pltpu.SemaphoreType.DMA((steps, rows // part)),
             ],
         ),
@@ -473,24 +449,17 @@
         entries = [(0, 0, j, landed[0] + near[j], full)]
         (x,) = terms_step(where, [], None, entries, pieces, span, chunk, "terms_0", BF16, 1)
         parts.append([x] + [to_base(x, k) for k in range(1, groups // pieces)])
-    parts[0] = [after(x, parts[-1][0]) for x in parts[0]]
 
     blocks = [(s, low, after(x, total)) for s in range(fsdp) for s, low, x in held[s]]
     own_proj = assemble(where, blocks, rows, fsdp)
     other_proj = to_core(own_proj)
     common = (own_proj, other_proj, (first_moment, second_moment))
-    outputs, others = None, []
-    for j in chunks:
-        if outputs is not None:
-            parts[j] = [after(x, *outputs, *others) for x in parts[j]]
-        mine = add_up(parts[j])
-        if pieces > 1:
-            others.append(to_piece(mine, 1))
-        pair = (mine, to_core(mine))
-        outputs = update_step(where, 0, pieces, j * chunk, [pair], *common, outputs)
+    mine = jnp.concatenate([add_up(x) for x in parts], axis=1)
+    outputs = update_step(where, 0, pieces, 0, [(mine, to_core(mine))], *common, None)
     if pieces > 1:
-        pairs = [(x, to_core(after(x, *outputs))) for x in others]
-        outputs = update_step(where, 1, pieces, 0, pairs, *common, outputs)
+        others = to_piece(mine, 1)
+        pair = (others, to_core(after(others, *outputs)))
+        outputs = update_step(where, 1, pieces, 0, [pair], *common, outputs)
     return tuple(outputs)
 
 

time: 82.7 us -> 77.6 us (0.938)
  Pallas kernels: 28.6 us -> 23.8 us
  starting transfers between devices: 27.4 us -> 24.2 us
  waiting for transfers between devices: 25.5 us -> 28.4 us
    pallas_call x3 -> x2, Pallas kernels: 18 us -> 13.2 us  [update_step(): pl.pallas_call(body, out_shape=[jax.ShapeDtypeStruct(x.shape, F32) for x...]
    ppermute x5 -> x4, starting transfers between devices: 7.86 us -> 5.27 us  [to_piece(): return lax.ppermute(x, 'dp', pairs)]
    ppermute x2, waiting for transfers between devices: 4.09 us -> 5.86 us  [to_base(): lax.ppermute(x, 'dp', [(i, (i + k * pieces * CORES) % dp) for i in range(...]
    ppermute x8 -> x6, starting transfers between devices: 1.81 us -> 1.17 us  [to_core(): return lax.ppermute(x, 'dp', [(i, i ^ 1) for i in range(dp)])]
    ppermute x5 -> x4, waiting for transfers between devices: 2.51 us -> 3.07 us  [to_piece(): return lax.ppermute(x, 'dp', pairs)]
    ppermute x8 -> x6, waiting for transfers between devices: 2.14 us -> 2.66 us  [to_core(): return lax.ppermute(x, 'dp', [(i, i ^ 1) for i in range(dp)])]
  transfers between devices with their start and end apart: 25 -> 22, of which waited for: 12 -> 13; matrix products, arithmetic and copies ran while one was open for 0% -> 0% of each run, Pallas kernels for 27% -> 22%
where the time goes in v4:
time: 77.6 us; the launch traced here: 77.4 us
  waiting for transfers between devices  28.4 us (37%)
  starting transfers between devices  24.2 us (31%)
  Pallas kernels  23.8 us (31%)
  between operations  0.79 us (1%)
    ppermute x10, waiting for transfers between devices, to_fsdp(): return lax.ppermute(x, 'fsdp', [(i, i ^ s) for i in range(fsdp)])  16.8 us
    ppermute x10, starting transfers between devices, to_fsdp(): return lax.ppermute(x, 'fsdp', [(i, i ^ s) for i in range(fsdp)])  13.7 us
    pallas_call x2, Pallas kernels, update_step(): pl.pallas_call(body, out_shape=[jax.ShapeDtypeStruct(x.shape, F32) for x...  13.2 us
    pallas_call x9, Pallas kernels, call(): pl.pallas_call(body, out_shape=out_shape, grid_spec=pltpu.PrefetchScalarG...  8.41 us
    ppermute x2, waiting for transfers between devices, to_base(): lax.ppermute(x, 'dp', [(i, (i + k * pieces * CORES) % dp) for i in range(...  5.86 us
    ppermute x4, starting transfers between devices, to_piece(): return lax.ppermute(x, 'dp', pairs)  5.27 us
    ppermute x2, starting transfers between devices, to_base(): lax.ppermute(x, 'dp', [(i, (i + k * pieces * CORES) % dp) for i in range(...  4.07 us
    ppermute x4, waiting for transfers between devices, to_piece(): return lax.ppermute(x, 'dp', pairs)  3.07 us
  transfers between devices with their start and end apart: 22, of which 13 were waited for; matrix products, arithmetic and copies ran while one was open for 0% of the time, Pallas kernels for 22%

profile of v4, /device:TPU:0, one launch (start us, length us, event | category | flops | bytes accessed | tf_op | source)
XLA Modules:
  0.0 77.4 jit_solution(17803767532562910355)
XLA Ops:
  1.2 1.5 %cut_out.1 = (bf16[1024,256]{1,0:T(8,128)(2,1)S(1)}, bf16[256,1536]{1,0:T(8,128)(2,1)S(1)}) custom-call(s32[1]{0:T(128)} %bitcast.fsdp_ref, s32[1]{0:T(128)} %bitcast.1.core_ref, s32[1]{0:T(128)} %bitcast.2.piece_ref, bf16[1024,512]{1,0:T(8,128)(2,1)} %proj_ref.1, bf16[256,4096]{1,0:T(8,128)(2,1)} %refs_1_.3), custom_call_target="tpu_custom_call" | custom-call | flops 1150000000 | tf_op jit(solution)/shard_map/cut_out/pallas_call | solution.py:71
  2.6 2.6 %collective-permute-start.3 = (bf16[1024,256]{1,0:T(8,128)(2,1)S(1)}, bf16[1024,256]{1,0:T(8,128)(2,1)S(1)}, u32[]{:S(2)}, u32[]{:S(2)}) collective-permute-start(bf16[1024,256]{1,0:T(8,128)(2,1)S(1)} %get-tuple-element.40.refs_2_.refs_0_), channel_id=1, source_target_pairs={{0,1},{1,0},{2,3},{3,2},{4,5},{5,4},{6,7},{7,6},{8,9},{9,8},{10,11... | collective-permute-start | bytes 1572872 | tf_op jit(solution)/shard_map/ppermute | solution.py:365
  5.3 1.5 %collective-permute-start.1 = (bf16[1024,256]{1,0:T(8,128)(2,1)S(1)}, bf16[1024,256]{1,0:T(8,128)(2,1)S(1)}, u32[]{:S(2)}, u32[]{:S(2)}) collective-permute-start(bf16[1024,256]{1,0:T(8,128)(2,1)S(1)} %get-tuple-element.40.refs_2_.refs_0_), channel_id=1, source_target_pairs={{0,2},{1,3},{2,0},{3,1},{4,6},{5,7},{6,4},{7,5},{8,10},{9,11},{10,... | collective-permute-start | bytes 1572872 | tf_op jit(solution)/shard_map/ppermute | solution.py:365
  6.8 1.6 %collective-permute-start.8 = (bf16[256,1536]{1,0:T(8,128)(2,1)S(1)}, bf16[256,1536]{1,0:T(8,128)(2,1)S(1)}, u32[]{:S(2)}, u32[]{:S(2)}) collective-permute-start(bf16[256,1536]{1,0:T(8,128)(2,1)S(1)} %get-tuple-element.29), channel_id=1, source_target_pairs={{0,8},{4,12},{8,0},{12,4},{16,24},{20,28},{24,16},{28,20},{1,9},{5... | collective-permute-start | bytes 2359304 | tf_op jit(solution)/shard_map/ppermute | solution.py:373
  8.4 9.3 %collective-permute-done.3.refs_2_.refs_1_ = bf16[1024,256]{1,0:T(8,128)(2,1)S(1)} collective-permute-done((bf16[1024,256]{1,0:T(8,128)(2,1)S(1)}, bf16[1024,256]{1,0:T(8,128)(2,1)S(1)}, u32[]{:S(2)}, u32[]{:S(2)}) %collective-permute-start.3) | collective-permute-done | bytes 524320 | tf_op jit(solution)/shard_map/ppermute | solution.py:365
  17.8 1.8 %collective-permute-start.4 = (bf16[512,256]{1,0:T(8,128)(2,1)S(1)}, bf16[512,256]{1,0:T(8,128)(2,1)S(1)}, u32[]{:S(2)}, u32[]{:S(2)}) collective-permute-start(bf16[512,256]{1,0:T(8,128)(2,1)S(1)} %slice.9), channel_id=1, source_target_pairs={{0,2},{1,3},{2,0},{3,1},{4,6},{5,7},{6,4},{7,5},{8,10},{9,11},{10,... | collective-permute-start | bytes 786440 | tf_op jit(solution)/shard_map/ppermute | solution.py:365
  19.7 1.6 %collective-permute-start.2 = (bf16[512,256]{1,0:T(8,128)(2,1)S(1)}, bf16[512,256]{1,0:T(8,128)(2,1)S(1)}, u32[]{:S(2)}, u32[]{:S(2)}) collective-permute-start(bf16[512,256]{1,0:T(8,128)(2,1)S(1)} %slice.8), channel_id=1, source_target_pairs={{0,1},{1,0},{2,3},{3,2},{4,5},{5,4},{6,7},{7,6},{8,9},{9,8},{10,11... | collective-permute-start | bytes 786440 | tf_op jit(solution)/shard_map/ppermute | solution.py:365
  22.2 1.3 %coords_1.1.refs_6_ = f32[512,256]{1,0:T(8,128)S(1)} custom-call(s32[3]{0:T(128)S(1)} %pad_add_fusion.w, bf16[256,4096]{1,0:T(8,128)(2,1)S(1)} %copy-done.3, bf16[256,4096]{1,0:T(8,128)(2,1)S(1)} %collective-permute-done.refs_1_.refs_4_, bf16[1024,256]{1,0:T(8,128)(2,1)S(1)} %collective-permute-done.3.refs_2_.refs_1_, bf16[256,4096]{1,0:T(8,128)(2,1)S(1)} %copy-done.3, ...), custom_call_target="tpu_custom_call" | custom-call | flops 9200000000 | tf_op jit(solution)/shard_map/coords_1/pallas_call | solution.py:31
  23.5 2.5 %collective-permute-done.4.refs_5_.refs_4_ = bf16[512,256]{1,0:T(8,128)(2,1)S(1)} collective-permute-done((bf16[512,256]{1,0:T(8,128)(2,1)S(1)}, bf16[512,256]{1,0:T(8,128)(2,1)S(1)}, u32[]{:S(2)}, u32[]{:S(2)}) %collective-permute-start.4) | collective-permute-done | bytes 262176 | tf_op jit(solution)/shard_map/ppermute | solution.py:365
  25.9 1.4 %collective-permute-done.2.refs_2_.refs_3_ = bf16[512,256]{1,0:T(8,128)(2,1)S(1)} collective-permute-done((bf16[512,256]{1,0:T(8,128)(2,1)S(1)}, bf16[512,256]{1,0:T(8,128)(2,1)S(1)}, u32[]{:S(2)}, u32[]{:S(2)}) %collective-permute-start.2) | collective-permute-done | bytes 262176 | tf_op jit(solution)/shard_map/ppermute | solution.py:365
  28.4 1.6 %collective-permute-start.7 = (bf16[256,512]{1,0:T(8,128)(2,1)S(1)}, bf16[256,512]{1,0:T(8,128)(2,1)S(1)}, u32[]{:S(2)}, u32[]{:S(2)}) collective-permute-start(bf16[256,512]{1,0:T(8,128)(2,1)S(1)} %coords_2.1.refs_0_), channel_id=1, source_target_pairs={{0,8},{4,12},{8,0},{12,4},{16,24},{20,28},{24,16},{28,20},{1,9},{5... | collective-permute-start | bytes 786440 | tf_op jit(solution)/shard_map/ppermute | solution.py:373
  31.4 1.2 %terms_chip.1 = (f32[256,512]{1,0:T(8,128)S(1)}, f32[256,512]{1,0:T(8,128)S(1)}, f32[256,512]{1,0:T(8,128)S(1)}, f32[256,512]{1,0:T(8,128)S(1)}) custom-call(s32[3]{0:T(128)S(1)} %pad_add_fusion.w, bf16[256,512]{1,0:T(8,128)(2,1)S(1)} %coords_2.1.refs_0_, bf16[256,4096]{1,0:T(8,128)(2,1)S(1)} %copy-done.2, ...), custom_call_target="tpu_custom_call" | custom-call | flops 13799999488 | tf_op jit(solution)/shard_map/terms_chip/pallas_call | solution.py:31
  32.6 2.5 %collective-permute-done.7.refs_0_ = bf16[256,512]{1,0:T(8,128)(2,1)S(1)} collective-permute-done((bf16[256,512]{1,0:T(8,128)(2,1)S(1)}, bf16[256,512]{1,0:T(8,128)(2,1)S(1)}, u32[]{:S(2)}, u32[]{:S(2)}) %collective-permute-start.7) | collective-permute-done | bytes 262176 | tf_op jit(solution)/shard_map/ppermute | solution.py:373
  38.9 1.6 %collective-permute-start.6 = (bf16[256,512]{1,0:T(8,128)(2,1)S(1)}, bf16[256,512]{1,0:T(8,128)(2,1)S(1)}, u32[]{:S(2)}, u32[]{:S(2)}) collective-permute-start(bf16[256,512]{1,0:T(8,128)(2,1)S(1)} %terms_pair.1), channel_id=1, source_target_pairs={{0,8},{4,12},{8,0},{12,4},{16,24},{20,28},{24,16},{28,20},{1,9},{5... | collective-permute-start | bytes 786440 | tf_op jit(solution)/shard_map/ppermute | solution.py:373
  41.0 1.2 %collective-permute-done.11.refs_8_.refs_16_ = bf16[128,512]{1,0:T(8,128)(2,1)S(1)} collective-permute-done((bf16[128,512]{1,0:T(8,128)(2,1)S(1)}, bf16[128,512]{1,0:T(8,128)(2,1)S(1)}, u32[]{:S(2)}, u32[]{:S(2)}) %collective-permute-start.11) | collective-permute-done | bytes 131104 | tf_op jit(solution)/shard_map/ppermute | solution.py:365
  44.3 1.5 %collective-permute-start.13 = (bf16[256,256]{1,0:T(8,128)(2,1)S(1)}, bf16[256,256]{1,0:T(8,128)(2,1)S(1)}, u32[]{:S(2)}, u32[]{:S(2)}) collective-permute-start(bf16[256,256]{1,0:T(8,128)(2,1)S(1)} %get-tuple-element.37), channel_id=1, source_target_pairs={{0,2},{1,3},{2,0},{3,1},{4,6},{5,7},{6,4},{7,5},{8,10},{9,11},{10,... | collective-permute-start | bytes 393224 | tf_op jit(solution)/shard_map/ppermute | solution.py:365
  49.9 2.6 %collective-permute-start.14 = (bf16[256,256]{1,0:T(8,128)(2,1)S(1)}, bf16[256,256]{1,0:T(8,128)(2,1)S(1)}, u32[]{:S(2)}, u32[]{:S(2)}) collective-permute-start(bf16[256,256]{1,0:T(8,128)(2,1)S(1)} %terms_0.2), channel_id=1, source_target_pairs={{0,16},{4,20},{8,24},{12,28},{16,0},{20,4},{24,8},{28,12},{1,17},{... | collective-permute-start | bytes 393224 | tf_op jit(solution)/shard_map/ppermute | solution.py:376
  53.1 1.4 %collective-permute-start.17 = (bf16[256,256]{1,0:T(8,128)(2,1)S(1)}, bf16[256,256]{1,0:T(8,128)(2,1)S(1)}, u32[]{:S(2)}, u32[]{:S(2)}) collective-permute-start(bf16[256,256]{1,0:T(8,128)(2,1)S(1)} %terms_0.3), channel_id=1, source_target_pairs={{0,16},{4,20},{8,24},{12,28},{16,0},{20,4},{24,8},{28,12},{1,17},{... | collective-permute-start | bytes 393224 | tf_op jit(solution)/shard_map/ppermute | solution.py:376
  54.5 2.7 %collective-permute-done.14 = bf16[256,256]{1,0:T(8,128)(2,1)S(1)} collective-permute-done((bf16[256,256]{1,0:T(8,128)(2,1)S(1)}, bf16[256,256]{1,0:T(8,128)(2,1)S(1)}, u32[]{:S(2)}, u32[]{:S(2)}) %collective-permute-start.14) | collective-permute-done | bytes 131104 | tf_op jit(solution)/shard_map/ppermute | solution.py:376
  57.2 3.2 %collective-permute-done.17 = bf16[256,256]{1,0:T(8,128)(2,1)S(1)} collective-permute-done((bf16[256,256]{1,0:T(8,128)(2,1)S(1)}, bf16[256,256]{1,0:T(8,128)(2,1)S(1)}, u32[]{:S(2)}, u32[]{:S(2)}) %collective-permute-start.17) | collective-permute-done | bytes 131104 | tf_op jit(solution)/shard_map/ppermute | solution.py:376
  61.0 1.1 %collective-permute-done.19.refs_1_ = bf16[256,512]{1,0:T(8,128)(2,1)S(1)} collective-permute-done((bf16[256,512]{1,0:T(8,128)(2,1)S(1)}, bf16[256,512]{1,0:T(8,128)(2,1)S(1)}, u32[]{:S(2)}, u32[]{:S(2)}) %collective-permute-start.19) | collective-permute-done | bytes 262176 | tf_op jit(solution)/shard_map/ppermute | solution.py:362
  62.1 6.6 %update_step.2 = (f32[1024,512]{1,0:T(8,128)}, f32[1024,512]{1,0:T(8,128)}, f32[4096,1024]{1,0:T(8,128)}) custom-call(s32[3]{0:T(128)S(1)} %pad_add_fusion.w, bf16[256,512]{1,0:T(8,128)(2,1)S(1)} %pad_maximum_fusion.refs_0_, bf16[256,512]{1,0:T(8,128)(2,1)S(1)} %collective-permute-done.19.refs_1_, bf16[4096,256]{1,0:T(8,128)(2,1)S(1)} %assemble.1.refs_2_, ...), custom_call_target="tpu_custom_call" | custom-call | flops 6899999744 | tf_op jit(solution)/shard_map/update_step/pallas_call | solution.py:310
  69.3 1.5 %collective-permute-done.21.refs_1_ = bf16[256,512]{1,0:T(8,128)(2,1)S(1)} collective-permute-done((bf16[256,512]{1,0:T(8,128)(2,1)S(1)}, bf16[256,512]{1,0:T(8,128)(2,1)S(1)}, u32[]{:S(2)}, u32[]{:S(2)}) %collective-permute-start.21) | collective-permute-done | bytes 262176 | tf_op jit(solution)/shard_map/ppermute | solution.py:362
  70.8 6.6 %update_step.3 = (f32[1024,512]{1,0:T(8,128)}, f32[1024,512]{1,0:T(8,128)}, f32[4096,1024]{1,0:T(8,128)}) custom-call(s32[3]{0:T(128)S(1)} %pad_add_fusion.w, bf16[256,512]{1,0:T(8,128)(2,1)S(1)} %collective-permute-done.18.refs_0_, bf16[256,512]{1,0:T(8,128)(2,1)S(1)} %collective-permute-done.21.refs_1_, ...), custom_call_target="tpu_custom_call", output_to_operand_aliasing={{0}: (7, {}), {1}: (8, {}), {2}: (9, {})} | custom-call | flops 6899999744 | tf_op jit(solution)/shard_map/update_step/pallas_call | solution.py:310
  (47 shorter events, 16.1 us)
Async XLA Ops:
  0.6 20.6 %collective-permute-start = (bf16[256,4096]{1,0:T(8,128)(2,1)}, bf16[256,4096]{1,0:T(8,128)(2,1)S(1)}, u32[]{:S(2)}, u32[]{:S(2)}) collective-permute-start(bf16[256,4096]{1,0:T(8,128)(2,1)} %refs_3_.4), channel_id=1, source_target_pairs={{0,4},{4,0},{8,12},{12,8},{16,20},{20,16},{24,28},{28,24},{1,5},{5... | collective-permute-start | bytes 6291464 | tf_op jit(solution)/shard_map/ppermute | solution.py:362
  1.2 20.1 %copy-start.3 = (bf16[256,4096]{1,0:T(8,128)(2,1)S(1)}, bf16[256,4096]{1,0:T(8,128)(2,1)}, u32[]{:S(2)}) copy-start(bf16[256,4096]{1,0:T(8,128)(2,1)} %refs_3_.4) | copy-start | bytes 6291460
  2.6 15.2 %collective-permute-start.3 = (bf16[1024,256]{1,0:T(8,128)(2,1)S(1)}, bf16[1024,256]{1,0:T(8,128)(2,1)S(1)}, u32[]{:S(2)}, u32[]{:S(2)}) collective-permute-start(bf16[1024,256]{1,0:T(8,128)(2,1)S(1)} %get-tuple-element.40.refs_2_.refs_0_), channel_id=1, source_target_pairs={{0,1},{1,0},{2,3},{3,2},{4,5},{5,4},{6,7},{7,6},{8,9},{9,8},{10,11... | collective-permute-start | bytes 1572872 | tf_op jit(solution)/shard_map/ppermute | solution.py:365
  5.3 14.4 %collective-permute-start.1 = (bf16[1024,256]{1,0:T(8,128)(2,1)S(1)}, bf16[1024,256]{1,0:T(8,128)(2,1)S(1)}, u32[]{:S(2)}, u32[]{:S(2)}) collective-permute-start(bf16[1024,256]{1,0:T(8,128)(2,1)S(1)} %get-tuple-element.40.refs_2_.refs_0_), channel_id=1, source_target_pairs={{0,2},{1,3},{2,0},{3,1},{4,6},{5,7},{6,4},{7,5},{8,10},{9,11},{10,... | collective-permute-start | bytes 1572872 | tf_op jit(solution)/shard_map/ppermute | solution.py:365
  6.8 23.3 %collective-permute-start.8 = (bf16[256,1536]{1,0:T(8,128)(2,1)S(1)}, bf16[256,1536]{1,0:T(8,128)(2,1)S(1)}, u32[]{:S(2)}, u32[]{:S(2)}) collective-permute-start(bf16[256,1536]{1,0:T(8,128)(2,1)S(1)} %get-tuple-element.29), channel_id=1, source_target_pairs={{0,8},{4,12},{8,0},{12,4},{16,24},{20,28},{24,16},{28,20},{1,9},{5... | collective-permute-start | bytes 2359304 | tf_op jit(solution)/shard_map/ppermute | solution.py:373
  8.4 23.0 %collective-permute-start.5 = (bf16[256,4096]{1,0:T(8,128)(2,1)S(1)}, bf16[256,4096]{1,0:T(8,128)(2,1)S(1)}, u32[]{:S(2)}, u32[]{:S(2)}) collective-permute-start(bf16[256,4096]{1,0:T(8,128)(2,1)S(1)} %copy-done.2), channel_id=1, source_target_pairs={{0,4},{4,0},{8,12},{12,8},{16,20},{20,16},{24,28},{28,24},{1,5},{5... | collective-permute-start | bytes 6291464 | tf_op jit(solution)/shard_map/ppermute | solution.py:362
  17.8 8.1 %collective-permute-start.4 = (bf16[512,256]{1,0:T(8,128)(2,1)S(1)}, bf16[512,256]{1,0:T(8,128)(2,1)S(1)}, u32[]{:S(2)}, u32[]{:S(2)}) collective-permute-start(bf16[512,256]{1,0:T(8,128)(2,1)S(1)} %slice.9), channel_id=1, source_target_pairs={{0,2},{1,3},{2,0},{3,1},{4,6},{5,7},{6,4},{7,5},{8,10},{9,11},{10,... | collective-permute-start | bytes 786440 | tf_op jit(solution)/shard_map/ppermute | solution.py:365
  19.7 7.6 %collective-permute-start.2 = (bf16[512,256]{1,0:T(8,128)(2,1)S(1)}, bf16[512,256]{1,0:T(8,128)(2,1)S(1)}, u32[]{:S(2)}, u32[]{:S(2)}) collective-permute-start(bf16[512,256]{1,0:T(8,128)(2,1)S(1)} %slice.8), channel_id=1, source_target_pairs={{0,1},{1,0},{2,3},{3,2},{4,5},{5,4},{6,7},{7,6},{8,9},{9,8},{10,11... | collective-permute-start | bytes 786440 | tf_op jit(solution)/shard_map/ppermute | solution.py:365
  28.4 6.7 %collective-permute-start.7 = (bf16[256,512]{1,0:T(8,128)(2,1)S(1)}, bf16[256,512]{1,0:T(8,128)(2,1)S(1)}, u32[]{:S(2)}, u32[]{:S(2)}) collective-permute-start(bf16[256,512]{1,0:T(8,128)(2,1)S(1)} %coords_2.1.refs_0_), channel_id=1, source_target_pairs={{0,8},{4,12},{8,0},{12,4},{16,24},{20,28},{24,16},{28,20},{1,9},{5... | collective-permute-start | bytes 786440 | tf_op jit(solution)/shard_map/ppermute | solution.py:373
  30.0 5.1 %collective-permute-start.9 = (bf16[256,1536]{1,0:T(8,128)(2,1)S(1)}, bf16[256,1536]{1,0:T(8,128)(2,1)S(1)}, u32[]{:S(2)}, u32[]{:S(2)}) collective-permute-start(bf16[256,1536]{1,0:T(8,128)(2,1)S(1)} %collective-permute-done.8.refs_1_.refs_5_.refs_9_.refs_13_), channel_id=1, source_target_pairs={{0,4},{4,0},{8,12},{12,8},{16,20},{20,16},{24,28},{28,24},{1,5},{5... | collective-permute-start | bytes 2359304 | tf_op jit(solution)/shard_map/ppermute | solution.py:362
  30.8 31.3 %collective-permute-start.20 = (bf16[4096,256]{1,0:T(8,128)(2,1)S(1)}, bf16[4096,256]{1,0:T(8,128)(2,1)S(1)}, u32[]{:S(2)}, u32[]{:S(2)}) collective-permute-start(bf16[4096,256]{1,0:T(8,128)(2,1)S(1)} %assemble.1.refs_2_), channel_id=1, source_target_pairs={{0,4},{4,0},{8,12},{12,8},{16,20},{20,16},{24,28},{28,24},{1,5},{5... | collective-permute-start | bytes 6291464 | tf_op jit(solution)/shard_map/ppermute | solution.py:362
  36.0 5.0 %collective-permute-start.10 = (bf16[128,512]{1,0:T(8,128)(2,1)S(1)}, bf16[128,512]{1,0:T(8,128)(2,1)S(1)}, u32[]{:S(2)}, u32[]{:S(2)}) collective-permute-start(bf16[128,512]{1,0:T(8,128)(2,1)S(1)} %get-tuple-element.33), channel_id=1, source_target_pairs={{0,2},{1,3},{2,0},{3,1},{4,6},{5,7},{6,4},{7,5},{8,10},{9,11},{10,... | collective-permute-start | bytes 393224 | tf_op jit(solution)/shard_map/ppermute | solution.py:365
  37.1 5.1 %collective-permute-start.11 = (bf16[128,512]{1,0:T(8,128)(2,1)S(1)}, bf16[128,512]{1,0:T(8,128)(2,1)S(1)}, u32[]{:S(2)}, u32[]{:S(2)}) collective-permute-start(bf16[128,512]{1,0:T(8,128)(2,1)S(1)} %get-tuple-element.35), channel_id=1, source_target_pairs={{0,1},{1,0},{2,3},{3,2},{4,5},{5,4},{6,7},{7,6},{8,9},{9,8},{10,11... | collective-permute-start | bytes 393224 | tf_op jit(solution)/shard_map/ppermute | solution.py:365
  38.9 7.4 %collective-permute-start.6 = (bf16[256,512]{1,0:T(8,128)(2,1)S(1)}, bf16[256,512]{1,0:T(8,128)(2,1)S(1)}, u32[]{:S(2)}, u32[]{:S(2)}) collective-permute-start(bf16[256,512]{1,0:T(8,128)(2,1)S(1)} %terms_pair.1), channel_id=1, source_target_pairs={{0,8},{4,12},{8,0},{12,4},{16,24},{20,28},{24,16},{28,20},{1,9},{5... | collective-permute-start | bytes 786440 | tf_op jit(solution)/shard_map/ppermute | solution.py:373
  43.2 5.0 %collective-permute-start.12 = (bf16[256,256]{1,0:T(8,128)(2,1)S(1)}, bf16[256,256]{1,0:T(8,128)(2,1)S(1)}, u32[]{:S(2)}, u32[]{:S(2)}) collective-permute-start(bf16[256,256]{1,0:T(8,128)(2,1)S(1)} %get-tuple-element.36), channel_id=1, source_target_pairs={{0,1},{1,0},{2,3},{3,2},{4,5},{5,4},{6,7},{7,6},{8,9},{9,8},{10,11... | collective-permute-start | bytes 393224 | tf_op jit(solution)/shard_map/ppermute | solution.py:365
  44.3 5.0 %collective-permute-start.13 = (bf16[256,256]{1,0:T(8,128)(2,1)S(1)}, bf16[256,256]{1,0:T(8,128)(2,1)S(1)}, u32[]{:S(2)}, u32[]{:S(2)}) collective-permute-start(bf16[256,256]{1,0:T(8,128)(2,1)S(1)} %get-tuple-element.37), channel_id=1, source_target_pairs={{0,2},{1,3},{2,0},{3,1},{4,6},{5,7},{6,4},{7,5},{8,10},{9,11},{10,... | collective-permute-start | bytes 393224 | tf_op jit(solution)/shard_map/ppermute | solution.py:365
  45.8 6.7 %collective-permute-start.15 = (bf16[256,256]{1,0:T(8,128)(2,1)S(1)}, bf16[256,256]{1,0:T(8,128)(2,1)S(1)}, u32[]{:S(2)}, u32[]{:S(2)}) collective-permute-start(bf16[256,256]{1,0:T(8,128)(2,1)S(1)} %get-tuple-element.38), channel_id=1, source_target_pairs={{0,1},{1,0},{2,3},{3,2},{4,5},{5,4},{6,7},{7,6},{8,9},{9,8},{10,11... | collective-permute-start | bytes 393224 | tf_op jit(solution)/shard_map/ppermute | solution.py:365
  46.3 6.2 %collective-permute-start.16 = (bf16[256,256]{1,0:T(8,128)(2,1)S(1)}, bf16[256,256]{1,0:T(8,128)(2,1)S(1)}, u32[]{:S(2)}, u32[]{:S(2)}) collective-permute-start(bf16[256,256]{1,0:T(8,128)(2,1)S(1)} %get-tuple-element.39), channel_id=1, source_target_pairs={{0,2},{1,3},{2,0},{3,1},{4,6},{5,7},{6,4},{7,5},{8,10},{9,11},{10,... | collective-permute-start | bytes 393224 | tf_op jit(solution)/shard_map/ppermute | solution.py:365
  49.8 12.3 %copy-start = (f32[1024,512]{1,0:T(8,128)S(1)}, f32[1024,512]{1,0:T(8,128)}, u32[]{:S(2)}) copy-start(f32[1024,512]{1,0:T(8,128)} %refs_4_.3) | copy-start | bytes 6291460
  49.9 7.3 %collective-permute-start.14 = (bf16[256,256]{1,0:T(8,128)(2,1)S(1)}, bf16[256,256]{1,0:T(8,128)(2,1)S(1)}, u32[]{:S(2)}, u32[]{:S(2)}) collective-permute-start(bf16[256,256]{1,0:T(8,128)(2,1)S(1)} %terms_0.2), channel_id=1, source_target_pairs={{0,16},{4,20},{8,24},{12,28},{16,0},{20,4},{24,8},{28,12},{1,17},{... | collective-permute-start | bytes 393224 | tf_op jit(solution)/shard_map/ppermute | solution.py:376
  53.1 7.3 %collective-permute-start.17 = (bf16[256,256]{1,0:T(8,128)(2,1)S(1)}, bf16[256,256]{1,0:T(8,128)(2,1)S(1)}, u32[]{:S(2)}, u32[]{:S(2)}) collective-permute-start(bf16[256,256]{1,0:T(8,128)(2,1)S(1)} %terms_0.3), channel_id=1, source_target_pairs={{0,16},{4,20},{8,24},{12,28},{16,0},{20,4},{24,8},{28,12},{1,17},{... | collective-permute-start | bytes 393224 | tf_op jit(solution)/shard_map/ppermute | solution.py:376
  60.5 1.6 %collective-permute-start.19 = (bf16[256,512]{1,0:T(8,128)(2,1)S(1)}, bf16[256,512]{1,0:T(8,128)(2,1)S(1)}, u32[]{:S(2)}, u32[]{:S(2)}) collective-permute-start(bf16[256,512]{1,0:T(8,128)(2,1)S(1)} %pad_maximum_fusion.refs_0_), channel_id=1, source_target_pairs={{0,4},{4,0},{8,12},{12,8},{16,20},{20,16},{24,28},{28,24},{1,5},{5... | collective-permute-start | bytes 786440 | tf_op jit(solution)/shard_map/ppermute | solution.py:362
  60.6 8.7 %collective-permute-start.18 = (bf16[256,512]{1,0:T(8,128)(2,1)S(1)}, bf16[256,512]{1,0:T(8,128)(2,1)S(1)}, u32[]{:S(2)}, u32[]{:S(2)}) collective-permute-start(bf16[256,512]{1,0:T(8,128)(2,1)S(1)} %pad_maximum_fusion.refs_0_), channel_id=1, source_target_pairs={{0,8},{4,12},{8,0},{12,4},{16,24},{20,28},{24,16},{28,20},{1,9},{5... | collective-permute-start | bytes 786440 | tf_op jit(solution)/shard_map/ppermute | solution.py:373
  69.3 1.5 %collective-permute-start.21 = (bf16[256,512]{1,0:T(8,128)(2,1)S(1)}, bf16[256,512]{1,0:T(8,128)(2,1)S(1)}, u32[]{:S(2)}, u32[]{:S(2)}) collective-permute-start(bf16[256,512]{1,0:T(8,128)(2,1)S(1)} %collective-permute-done.18.refs_0_), channel_id=1, source_target_pairs={{0,4},{4,0},{8,12},{12,8},{16,20},{20,16},{24,28},{28,24},{1,5},{5... | collective-permute-start | bytes 786440 | tf_op jit(solution)/shard_map/ppermute | solution.py:362
  (2 other events, 19.5 us)

commit v5 on v4

--- a/solution.py
+++ b/solution.py
@@ -227,81 +227,93 @@
     )(where, *inputs)
 
 
-def update_step(where, k, pieces, low, grads, own_proj, other_proj, moments, before):
-    half, chunk = grads[0][0].shape
-    span = chunk * len(grads)
+def join(where, own, other):
+    width, half = own.shape
+
+    def body(w, own_ref, other_ref, out):
+        @pl.when(w[1] == 0)
+        def _():
+            out[:, :half] = own_ref[...]
+            out[:, half:] = other_ref[...]
+
+        @pl.when(w[1] != 0)
+        def _():
+            out[:, :half] = other_ref[...]
+            out[:, half:] = own_ref[...]
+
+    return call(
+        body,
+        where,
+        [own, other],
+        [whole(own), whole(other)],
+        [jax.ShapeDtypeStruct((width, 2 * half), BF16)],
+        20 * MIB,
+        name="join",
+        estimate=busy(1),
+    )[0]
+
+
+def update_step(where, k, pieces, grads, proj, moments, before):
+    half, span = grads[0].shape
     rank = CORES * half
     features = moments[0].shape[0]
-    width = own_proj.shape[0]
+    width = proj.shape[0]
     rows = min(1024, width)
     steps = width // rows
-    part = min(256, rows)
-    flat = [x for pair in grads for x in pair]
-
-    def body(w, *refs):
-        grad_refs, refs = refs[: len(flat)], refs[len(flat) :]
-        own, other, ins = refs[0], refs[1], refs[2:4]
-        outs, update = refs[-9:-7], refs[-7]
-        moment, direction, out = refs[-6:-3]
-        moment_in, moment_out, update_out = refs[-3:]
-        base = lax.rem(w[2] + pieces - k, pieces) * (features // pieces) + low
-        features_at = pl.ds(pl.multiple_of(base, chunk), span)
-        own_rows = pl.ds(pl.multiple_of(w[1] * half, half), half)
-        other_rows = pl.ds(pl.multiple_of((1 - w[1]) * half, half), half)
-        loads = [
-            pltpu.make_async_copy(ins[n].at[features_at, :], moment.at[n], moment_in.at[n])
-            for n in range(2)
-        ]
+    some = 16
+
+    def piece(w):
+        return lax.rem(w[2] + pieces - k, pieces)
+
+    def body(w, own, other, proj_ref, first_ref, second_ref, *refs):
+        outs, update = refs[-10:-8], refs[-8]
+        moment, grad, ratio, direction, out = refs[-7:-2]
+        moment_out, update_out = refs[-2:]
+        features_at = pl.ds(pl.multiple_of(piece(w) * span, span), span)
         stores = [
             pltpu.make_async_copy(moment.at[n], outs[n].at[features_at, :], moment_out.at[n])
             for n in range(2)
         ]
         update_stores = [
-            [
-                pltpu.make_async_copy(
-                    out.at[pl.ds(r * rows + m * part, part), :],
-                    update.at[pl.ds(r * rows + m * part, part), features_at],
-                    update_out.at[r, m],
-                )
-                for m in range(rows // part)
-            ]
+            pltpu.make_async_copy(
+                out.at[pl.ds(r * rows, rows), :],
+                update.at[pl.ds(r * rows, rows), features_at],
+                update_out.at[r],
+            )
             for r in range(steps)
         ]
-        for copy in loads:
-            copy.start()
-        for copy in loads:
-            copy.wait()
+        for h in range(2):
+            grad[:, pl.ds(h * half, half)] = jnp.where(w[1] == h, own[...], other[...]).T
         first_scale = 1.0 / (1.0 - 0.9**STEP)
         second_scale = 1.0 / (1.0 - 0.999**STEP)
-        for m in range(len(grads)):
-            at = pl.ds(m * chunk, chunk)
-            mine, others = grad_refs[2 * m][...], grad_refs[2 * m + 1][...]
-            for h in range(2):
-                here = pl.ds(h * half, half)
-                grad_low = jnp.where(w[1] == h, mine, others).T.astype(F32)
-                first_new = 0.9 * moment[0, at, here] + 0.1 * grad_low
-                second_new = 0.999 * moment[1, at, here] + 0.001 * grad_low * grad_low
-                moment[0, at, here] = first_new
-                moment[1, at, here] = second_new
-                ratio = (first_new * first_scale) / (
-                    jnp.sqrt(second_new * second_scale) + 1e-08
-                )
-                direction[here, at] = ratio.astype(BF16).T
+
+        def adam(n, _):
+            at = pl.ds(pl.multiple_of(n * some, some), some)
+            grad_low = grad[at, :].astype(F32)
+            first_new = 0.9 * first_ref[at, :] + 0.1 * grad_low
+            second_new = 0.999 * second_ref[at, :] + 0.001 * grad_low * grad_low
+            moment[0, at, :] = first_new
+            moment[1, at, :] = second_new
+            ratio[at, :] = (
+                (first_new * first_scale) / (jnp.sqrt(second_new * second_scale) + 1e-08)
+            ).astype(BF16)
+            return 0
+
+        lax.fori_loop(0, span // some, adam, 0, unroll=2)
         for copy in stores:
             copy.start()
+        direction[...] = ratio[...].T
         for r in range(steps):
             at = pl.ds(r * rows, rows)
-            out[at, :] = jnp.dot(
-                own[at, :], direction[own_rows, :], preferred_element_type=F32
-            ) + jnp.dot(other[at, :], direction[other_rows, :], preferred_element_type=F32)
-            for copy in update_stores[r]:
-                copy.start()
-        for copy in stores + sum(update_stores, []):
+            out[at, :] = jnp.dot(proj_ref[at, :], direction[...], preferred_element_type=F32)
+            update_stores[r].start()
+        for copy in stores + update_stores:
             copy.wait()
 
-    inputs = [*flat, own_proj, other_proj, *moments]
+    inputs = [*grads, proj, *moments]
     any_space = pl.BlockSpec(memory_space=pl.ANY)
-    in_specs = [whole(x) for x in (*flat, own_proj, other_proj)] + [any_space] * 2
+    in_specs = [whole(x) for x in (*grads, proj)]
+    in_specs += [pl.BlockSpec((span, rank), lambda i, w: (piece(w), 0))] * 2
     aliases = {}
     if before is not None:
         aliases = {1 + len(inputs) + n: n for n in range(3)}
@@ -318,11 +330,12 @@
             out_specs=[any_space] * 3,
             scratch_shapes=[
                 pltpu.VMEM((2, span, rank), F32),
+                pltpu.VMEM((span, rank), BF16),
+                pltpu.VMEM((span, rank), BF16),
                 pltpu.VMEM((rank, span), BF16),
                 pltpu.VMEM((width, span), F32),
                 pltpu.SemaphoreType.DMA((2,)),
-                pltpu.SemaphoreType.DMA((2,)),
-                pltpu.SemaphoreType.DMA((steps, rows // part)),
+                pltpu.SemaphoreType.DMA((steps,)),
             ],
         ),
         input_output_aliases=aliases,
@@ -424,42 +437,34 @@
         )
         landed[0].append((0, to_piece(pair_sum, 1)))
 
-    middle = half // 2
-    halves = [(0, middle), (middle, half)]
-    for n in range(len(levels) - 1, 1, -1):
-        entries = [(s, 0, 0, landed[s], halves) for s in levels[n]]
-        outs = iter(
-            terms_step(
-                where, cots_far, far_coords, entries, pieces, span, span, f"terms_{n}"
-            )
-        )
-        for s in levels[n]:
-            for m, link in enumerate(links(s)):
-                landed[s ^ link].append((m * middle, to_fsdp(next(outs), link)))
-    near = {j: [] for j in chunks}
+    got = {j: list(landed[0]) for j in chunks}
     if fsdp > 1:
-        entries = [(s, 0, j, landed[s], full) for j in chunks for s in levels[1]]
+        entries = [
+            (s, 0, j, landed[s], full) for j in chunks for s in range(fsdp - 1, 0, -1)
+        ]
         outs = terms_step(
-            where, cots_far, far_coords, entries, pieces, span, chunk, "terms_1"
+            where, cots_far, after(far_coords, pair_sum), entries, pieces, span, chunk, "terms_peers", BF16, 8
         )
         for (s, _, j, _, _), x in zip(entries, outs):
-            near[j].append((0, to_fsdp(x, s)))
+            got[j].append((0, to_fsdp(x, s)))
     parts = []
     for j in chunks:
-        entries = [(0, 0, j, landed[0] + near[j], full)]
-        (x,) = terms_step(where, [], None, entries, pieces, span, chunk, "terms_0", BF16, 1)
+        entries = [(0, 0, j, got[j], full)]
+        (x,) = terms_step(where, [], None, entries, pieces, span, chunk, "terms_own")
         parts.append([x] + [to_base(x, k) for k in range(1, groups // pieces)])
 
     blocks = [(s, low, after(x, total)) for s in range(fsdp) for s, low, x in held[s]]
     own_proj = assemble(where, blocks, rows, fsdp)
     other_proj = to_core(own_proj)
-    common = (own_proj, other_proj, (first_moment, second_moment))
+    proj = join(where, own_proj, after(other_proj, total))
+    moments = (first_moment, second_moment)
+    parts[0] = [after(x, proj) for x in parts[0]]
     mine = jnp.concatenate([add_up(x) for x in parts], axis=1)
-    outputs = update_step(where, 0, pieces, 0, [(mine, to_core(mine))], *common, None)
+    outputs = update_step(where, 0, pieces, (mine, to_core(mine)), proj, moments, None)
     if pieces > 1:
         others = to_piece(mine, 1)
         pair = (others, to_core(after(others, *outputs)))
-        outputs = update_step(where, 1, pieces, 0, [pair], *common, outputs)
+        outputs = update_step(where, 1, pieces, pair, proj, moments, outputs)
     return tuple(outputs)
 
 

time: 77.6 us -> 77.3 us (level)
  waiting for transfers between devices: 28.4 us -> 26 us
  starting transfers between devices: 24.2 us -> 26.3 us
    ppermute x2, waiting for transfers between devices: 5.86 us -> 3.72 us  [to_base(): lax.ppermute(x, 'dp', [(i, (i + k * pieces * CORES) % dp) for i in range(...]
    ppermute x10, starting transfers between devices: 13.7 us -> 15.4 us  [to_fsdp(): return lax.ppermute(x, 'fsdp', [(i, i ^ s) for i in range(fsdp)])]
    ppermute x4, waiting for transfers between devices: 3.07 us -> 4.41 us  [to_piece(): return lax.ppermute(x, 'dp', pairs)]
    ppermute x10, waiting for transfers between devices: 16.8 us -> 15.5 us  [to_fsdp(): return lax.ppermute(x, 'fsdp', [(i, i ^ s) for i in range(fsdp)])]
    ppermute x2, starting transfers between devices: 4.07 us -> 5.29 us  [to_base(): lax.ppermute(x, 'dp', [(i, (i + k * pieces * CORES) % dp) for i in range(...]
    ppermute x4, starting transfers between devices: 5.27 us -> 4.47 us  [to_piece(): return lax.ppermute(x, 'dp', pairs)]
  transfers between devices with their start and end apart: 22 -> 22, of which waited for: 13 -> 12; matrix products, arithmetic and copies ran while one was open for 0% -> 0% of each run, Pallas kernels for 22% -> 22%
where the time goes in v5:
time: 77.3 us; the launch traced here: 77.2 us
  starting transfers between devices  26.3 us (34%)
  waiting for transfers between devices  26 us (34%)
  Pallas kernels  23.8 us (31%)
  between operations  0.8 us (1%)
    ppermute x10, waiting for transfers between devices, to_fsdp(): return lax.ppermute(x, 'fsdp', [(i, i ^ s) for i in range(fsdp)])  15.5 us
    ppermute x10, starting transfers between devices, to_fsdp(): return lax.ppermute(x, 'fsdp', [(i, i ^ s) for i in range(fsdp)])  15.4 us
    pallas_call x2, Pallas kernels, update_step(): pl.pallas_call(body, out_shape=[jax.ShapeDtypeStruct(x.shape, F32) for x...  13 us
    pallas_call x9, Pallas kernels, call(): pl.pallas_call(body, out_shape=out_shape, grid_spec=pltpu.PrefetchScalarG...  8.62 us
    ppermute x2, starting transfers between devices, to_base(): lax.ppermute(x, 'dp', [(i, (i + k * pieces * CORES) % dp) for i in range(...  5.29 us
    ppermute x4, starting transfers between devices, to_piece(): return lax.ppermute(x, 'dp', pairs)  4.47 us
    ppermute x4, waiting for transfers between devices, to_piece(): return lax.ppermute(x, 'dp', pairs)  4.41 us
    ppermute x2, waiting for transfers between devices, to_base(): lax.ppermute(x, 'dp', [(i, (i + k * pieces * CORES) % dp) for i in range(...  3.72 us
  transfers between devices with their start and end apart: 22, of which 12 were waited for; matrix products, arithmetic and copies ran while one was open for 0% of the time, Pallas kernels for 22%

profile of v5, /device:TPU:0, one launch (start us, length us, event | category | flops | bytes accessed | tf_op | source)
XLA Modules:
  0.0 77.2 jit_solution(7958765899973993744)
XLA Ops:
  1.2 1.5 %cut_out.1 = (bf16[1024,256]{1,0:T(8,128)(2,1)S(1)}, bf16[256,1536]{1,0:T(8,128)(2,1)S(1)}) custom-call(s32[1]{0:T(128)} %bitcast.fsdp_ref, s32[1]{0:T(128)} %bitcast.1.core_ref, s32[1]{0:T(128)} %bitcast.2.piece_ref, bf16[1024,512]{1,0:T(8,128)(2,1)} %proj_ref.1, bf16[256,4096]{1,0:T(8,128)(2,1)} %refs_1_.3), custom_call_target="tpu_custom_call" | custom-call | flops 1150000000 | tf_op jit(solution)/shard_map/cut_out/pallas_call | solution.py:71
  2.6 2.6 %collective-permute-start.3 = (bf16[1024,256]{1,0:T(8,128)(2,1)S(1)}, bf16[1024,256]{1,0:T(8,128)(2,1)S(1)}, u32[]{:S(2)}, u32[]{:S(2)}) collective-permute-start(bf16[1024,256]{1,0:T(8,128)(2,1)S(1)} %get-tuple-element.42.refs_2_.refs_0_), channel_id=1, source_target_pairs={{0,1},{1,0},{2,3},{3,2},{4,5},{5,4},{6,7},{7,6},{8,9},{9,8},{10,11... | collective-permute-start | bytes 1572872 | tf_op jit(solution)/shard_map/ppermute | solution.py:378
  5.3 1.5 %collective-permute-start.1 = (bf16[1024,256]{1,0:T(8,128)(2,1)S(1)}, bf16[1024,256]{1,0:T(8,128)(2,1)S(1)}, u32[]{:S(2)}, u32[]{:S(2)}) collective-permute-start(bf16[1024,256]{1,0:T(8,128)(2,1)S(1)} %get-tuple-element.42.refs_2_.refs_0_), channel_id=1, source_target_pairs={{0,2},{1,3},{2,0},{3,1},{4,6},{5,7},{6,4},{7,5},{8,10},{9,11},{10,... | collective-permute-start | bytes 1572872 | tf_op jit(solution)/shard_map/ppermute | solution.py:378
  6.8 1.6 %collective-permute-start.8 = (bf16[256,1536]{1,0:T(8,128)(2,1)S(1)}, bf16[256,1536]{1,0:T(8,128)(2,1)S(1)}, u32[]{:S(2)}, u32[]{:S(2)}) collective-permute-start(bf16[256,1536]{1,0:T(8,128)(2,1)S(1)} %get-tuple-element.34), channel_id=1, source_target_pairs={{0,8},{4,12},{8,0},{12,4},{16,24},{20,28},{24,16},{28,20},{1,9},{5... | collective-permute-start | bytes 2359304 | tf_op jit(solution)/shard_map/ppermute | solution.py:386
  8.4 9.3 %collective-permute-done.3.refs_2_.refs_1_ = bf16[1024,256]{1,0:T(8,128)(2,1)S(1)} collective-permute-done((bf16[1024,256]{1,0:T(8,128)(2,1)S(1)}, bf16[1024,256]{1,0:T(8,128)(2,1)S(1)}, u32[]{:S(2)}, u32[]{:S(2)}) %collective-permute-start.3) | collective-permute-done | bytes 524320 | tf_op jit(solution)/shard_map/ppermute | solution.py:378
  17.8 1.8 %collective-permute-start.4 = (bf16[512,256]{1,0:T(8,128)(2,1)S(1)}, bf16[512,256]{1,0:T(8,128)(2,1)S(1)}, u32[]{:S(2)}, u32[]{:S(2)}) collective-permute-start(bf16[512,256]{1,0:T(8,128)(2,1)S(1)} %slice.9), channel_id=1, source_target_pairs={{0,2},{1,3},{2,0},{3,1},{4,6},{5,7},{6,4},{7,5},{8,10},{9,11},{10,... | collective-permute-start | bytes 786440 | tf_op jit(solution)/shard_map/ppermute | solution.py:378
  19.7 1.6 %collective-permute-start.2 = (bf16[512,256]{1,0:T(8,128)(2,1)S(1)}, bf16[512,256]{1,0:T(8,128)(2,1)S(1)}, u32[]{:S(2)}, u32[]{:S(2)}) collective-permute-start(bf16[512,256]{1,0:T(8,128)(2,1)S(1)} %slice.8), channel_id=1, source_target_pairs={{0,1},{1,0},{2,3},{3,2},{4,5},{5,4},{6,7},{7,6},{8,9},{9,8},{10,11... | collective-permute-start | bytes 786440 | tf_op jit(solution)/shard_map/ppermute | solution.py:378
  22.2 1.3 %coords_1.1.refs_6_ = f32[512,256]{1,0:T(8,128)S(1)} custom-call(s32[3]{0:T(128)S(1)} %pad_add_fusion.w, bf16[256,4096]{1,0:T(8,128)(2,1)S(1)} %copy-done.3, bf16[256,4096]{1,0:T(8,128)(2,1)S(1)} %collective-permute-done.refs_1_.refs_4_, bf16[1024,256]{1,0:T(8,128)(2,1)S(1)} %collective-permute-done.3.refs_2_.refs_1_, bf16[256,4096]{1,0:T(8,128)(2,1)S(1)} %copy-done.3, ...), custom_call_target="tpu_custom_call" | custom-call | flops 9200000000 | tf_op jit(solution)/shard_map/coords_1/pallas_call | solution.py:31
  23.5 2.5 %collective-permute-done.4.refs_5_.refs_4_ = bf16[512,256]{1,0:T(8,128)(2,1)S(1)} collective-permute-done((bf16[512,256]{1,0:T(8,128)(2,1)S(1)}, bf16[512,256]{1,0:T(8,128)(2,1)S(1)}, u32[]{:S(2)}, u32[]{:S(2)}) %collective-permute-start.4) | collective-permute-done | bytes 262176 | tf_op jit(solution)/shard_map/ppermute | solution.py:378
  25.9 1.4 %collective-permute-done.2.refs_2_.refs_3_ = bf16[512,256]{1,0:T(8,128)(2,1)S(1)} collective-permute-done((bf16[512,256]{1,0:T(8,128)(2,1)S(1)}, bf16[512,256]{1,0:T(8,128)(2,1)S(1)}, u32[]{:S(2)}, u32[]{:S(2)}) %collective-permute-start.2) | collective-permute-done | bytes 262176 | tf_op jit(solution)/shard_map/ppermute | solution.py:378
  28.4 1.6 %collective-permute-start.7 = (bf16[256,512]{1,0:T(8,128)(2,1)S(1)}, bf16[256,512]{1,0:T(8,128)(2,1)S(1)}, u32[]{:S(2)}, u32[]{:S(2)}) collective-permute-start(bf16[256,512]{1,0:T(8,128)(2,1)S(1)} %coords_2.1.refs_0_), channel_id=1, source_target_pairs={{0,8},{4,12},{8,0},{12,4},{16,24},{20,28},{24,16},{28,20},{1,9},{5... | collective-permute-start | bytes 786440 | tf_op jit(solution)/shard_map/ppermute | solution.py:386
  34.0 3.7 %collective-permute-done.7.refs_0_ = bf16[256,512]{1,0:T(8,128)(2,1)S(1)} collective-permute-done((bf16[256,512]{1,0:T(8,128)(2,1)S(1)}, bf16[256,512]{1,0:T(8,128)(2,1)S(1)}, u32[]{:S(2)}, u32[]{:S(2)}) %collective-permute-start.7) | collective-permute-done | bytes 262176 | tf_op jit(solution)/shard_map/ppermute | solution.py:386
  38.8 1.5 %collective-permute-start.15 = (bf16[256,256]{1,0:T(8,128)(2,1)S(1)}, bf16[256,256]{1,0:T(8,128)(2,1)S(1)}, u32[]{:S(2)}, u32[]{:S(2)}) collective-permute-start(bf16[256,256]{1,0:T(8,128)(2,1)S(1)} %get-tuple-element.50), channel_id=1, source_target_pairs={{0,3},{1,2},{2,1},{3,0},{4,7},{5,6},{6,5},{7,4},{8,11},{9,10},{10,... | collective-permute-start | bytes 393224 | tf_op jit(solution)/shard_map/ppermute | solution.py:378
  40.3 1.5 %collective-permute-start.16 = (bf16[256,256]{1,0:T(8,128)(2,1)S(1)}, bf16[256,256]{1,0:T(8,128)(2,1)S(1)}, u32[]{:S(2)}, u32[]{:S(2)}) collective-permute-start(bf16[256,256]{1,0:T(8,128)(2,1)S(1)} %get-tuple-element.51), channel_id=1, source_target_pairs={{0,2},{1,3},{2,0},{3,1},{4,6},{5,7},{6,4},{7,5},{8,10},{9,11},{10,... | collective-permute-start | bytes 393224 | tf_op jit(solution)/shard_map/ppermute | solution.py:378
  42.4 1.4 %collective-permute-start.10 = (bf16[256,256]{1,0:T(8,128)(2,1)S(1)}, bf16[256,256]{1,0:T(8,128)(2,1)S(1)}, u32[]{:S(2)}, u32[]{:S(2)}) collective-permute-start(bf16[256,256]{1,0:T(8,128)(2,1)S(1)} %get-tuple-element.39), channel_id=1, source_target_pairs={{0,3},{1,2},{2,1},{3,0},{4,7},{5,6},{6,5},{7,4},{8,11},{9,10},{10,... | collective-permute-start | bytes 393224 | tf_op jit(solution)/shard_map/ppermute | solution.py:378
  45.1 1.4 %collective-permute-start.11 = (bf16[256,256]{1,0:T(8,128)(2,1)S(1)}, bf16[256,256]{1,0:T(8,128)(2,1)S(1)}, u32[]{:S(2)}, u32[]{:S(2)}) collective-permute-start(bf16[256,256]{1,0:T(8,128)(2,1)S(1)} %get-tuple-element.40), channel_id=1, source_target_pairs={{0,2},{1,3},{2,0},{3,1},{4,6},{5,7},{6,4},{7,5},{8,10},{9,11},{10,... | collective-permute-start | bytes 393224 | tf_op jit(solution)/shard_map/ppermute | solution.py:378
  47.4 1.5 %collective-permute-start.12 = (bf16[256,256]{1,0:T(8,128)(2,1)S(1)}, bf16[256,256]{1,0:T(8,128)(2,1)S(1)}, u32[]{:S(2)}, u32[]{:S(2)}) collective-permute-start(bf16[256,256]{1,0:T(8,128)(2,1)S(1)} %get-tuple-element.41), channel_id=1, source_target_pairs={{0,1},{1,0},{2,3},{3,2},{4,5},{5,4},{6,7},{7,6},{8,9},{9,8},{10,11... | collective-permute-start | bytes 393224 | tf_op jit(solution)/shard_map/ppermute | solution.py:378
  49.5 2.6 %collective-permute-start.18 = (bf16[256,256]{1,0:T(8,128)(2,1)S(1)}, bf16[256,256]{1,0:T(8,128)(2,1)S(1)}, u32[]{:S(2)}, u32[]{:S(2)}) collective-permute-start(bf16[256,256]{1,0:T(8,128)(2,1)S(1)} %terms_own.3), channel_id=1, source_target_pairs={{0,16},{4,20},{8,24},{12,28},{16,0},{20,4},{24,8},{28,12},{1,17},{... | collective-permute-start | bytes 393224 | tf_op jit(solution)/shard_map/ppermute | solution.py:389
  53.0 2.7 %collective-permute-start.14 = (bf16[256,256]{1,0:T(8,128)(2,1)S(1)}, bf16[256,256]{1,0:T(8,128)(2,1)S(1)}, u32[]{:S(2)}, u32[]{:S(2)}) collective-permute-start(bf16[256,256]{1,0:T(8,128)(2,1)S(1)} %terms_own.2), channel_id=1, source_target_pairs={{0,16},{4,20},{8,24},{12,28},{16,0},{20,4},{24,8},{28,12},{1,17},{... | collective-permute-start | bytes 393224 | tf_op jit(solution)/shard_map/ppermute | solution.py:389
  55.6 1.4 %collective-permute-done.18 = bf16[256,256]{1,0:T(8,128)(2,1)S(1)} collective-permute-done((bf16[256,256]{1,0:T(8,128)(2,1)S(1)}, bf16[256,256]{1,0:T(8,128)(2,1)S(1)}, u32[]{:S(2)}, u32[]{:S(2)}) %collective-permute-start.18) | collective-permute-done | bytes 131104 | tf_op jit(solution)/shard_map/ppermute | solution.py:389
  58.0 2.3 %collective-permute-done.14 = bf16[256,256]{1,0:T(8,128)(2,1)S(1)} collective-permute-done((bf16[256,256]{1,0:T(8,128)(2,1)S(1)}, bf16[256,256]{1,0:T(8,128)(2,1)S(1)}, u32[]{:S(2)}, u32[]{:S(2)}) %collective-permute-start.14) | collective-permute-done | bytes 131104 | tf_op jit(solution)/shard_map/ppermute | solution.py:389
  62.0 6.5 %update_step.2 = (f32[1024,512]{1,0:T(8,128)}, f32[1024,512]{1,0:T(8,128)}, f32[4096,1024]{1,0:T(8,128)}) custom-call(s32[3]{0:T(128)S(1)} %pad_add_fusion.w, bf16[256,512]{1,0:T(8,128)(2,1)S(1)} %pad_maximum_fusion.own, bf16[256,512]{1,0:T(8,128)(2,1)S(1)} %collective-permute-done.20.other, bf16[4096,512]{1,0:T(8,128)(2,1)S(1)} %join.1.proj_ref, ...), custom_call_target="tpu_custom_call" | custom-call | flops 6899999744 | tf_op jit(solution)/shard_map/update_step/pallas_call | solution.py:322
  69.2 1.5 %collective-permute-done.21.other = bf16[256,512]{1,0:T(8,128)(2,1)S(1)} collective-permute-done((bf16[256,512]{1,0:T(8,128)(2,1)S(1)}, bf16[256,512]{1,0:T(8,128)(2,1)S(1)}, u32[]{:S(2)}, u32[]{:S(2)}) %collective-permute-start.21) | collective-permute-done | bytes 262176 | tf_op jit(solution)/shard_map/ppermute | solution.py:375
  70.7 6.5 %update_step.3 = (f32[1024,512]{1,0:T(8,128)}, f32[1024,512]{1,0:T(8,128)}, f32[4096,1024]{1,0:T(8,128)}) custom-call(s32[3]{0:T(128)S(1)} %pad_add_fusion.w, bf16[256,512]{1,0:T(8,128)(2,1)S(1)} %collective-permute-done.19.own, bf16[256,512]{1,0:T(8,128)(2,1)S(1)} %collective-permute-done.21.other, ...), custom_call_target="tpu_custom_call", output_to_operand_aliasing={{0}: (6, {}), {1}: (7, {}), {2}: (8, {})} | custom-call | flops 6899999744 | tf_op jit(solution)/shard_map/update_step/pallas_call | solution.py:322
  (47 shorter events, 15.1 us)
Async XLA Ops:
  0.6 20.6 %collective-permute-start = (bf16[256,4096]{1,0:T(8,128)(2,1)}, bf16[256,4096]{1,0:T(8,128)(2,1)S(1)}, u32[]{:S(2)}, u32[]{:S(2)}) collective-permute-start(bf16[256,4096]{1,0:T(8,128)(2,1)} %refs_3_.4), channel_id=1, source_target_pairs={{0,4},{4,0},{8,12},{12,8},{16,20},{20,16},{24,28},{28,24},{1,5},{5... | collective-permute-start | bytes 6291464 | tf_op jit(solution)/shard_map/ppermute | solution.py:375
  1.1 7.2 %copy-start.2 = (bf16[256,4096]{1,0:T(8,128)(2,1)S(1)}, bf16[256,4096]{1,0:T(8,128)(2,1)}, u32[]{:S(2)}) copy-start(bf16[256,4096]{1,0:T(8,128)(2,1)} %refs_1_.3) | copy-start | bytes 6291460
  1.2 20.1 %copy-start.3 = (bf16[256,4096]{1,0:T(8,128)(2,1)S(1)}, bf16[256,4096]{1,0:T(8,128)(2,1)}, u32[]{:S(2)}) copy-start(bf16[256,4096]{1,0:T(8,128)(2,1)} %refs_3_.4) | copy-start | bytes 6291460
  2.6 15.2 %collective-permute-start.3 = (bf16[1024,256]{1,0:T(8,128)(2,1)S(1)}, bf16[1024,256]{1,0:T(8,128)(2,1)S(1)}, u32[]{:S(2)}, u32[]{:S(2)}) collective-permute-start(bf16[1024,256]{1,0:T(8,128)(2,1)S(1)} %get-tuple-element.42.refs_2_.refs_0_), channel_id=1, source_target_pairs={{0,1},{1,0},{2,3},{3,2},{4,5},{5,4},{6,7},{7,6},{8,9},{9,8},{10,11... | collective-permute-start | bytes 1572872 | tf_op jit(solution)/shard_map/ppermute | solution.py:378
  5.3 14.4 %collective-permute-start.1 = (bf16[1024,256]{1,0:T(8,128)(2,1)S(1)}, bf16[1024,256]{1,0:T(8,128)(2,1)S(1)}, u32[]{:S(2)}, u32[]{:S(2)}) collective-permute-start(bf16[1024,256]{1,0:T(8,128)(2,1)S(1)} %get-tuple-element.42.refs_2_.refs_0_), channel_id=1, source_target_pairs={{0,2},{1,3},{2,0},{3,1},{4,6},{5,7},{6,4},{7,5},{8,10},{9,11},{10,... | collective-permute-start | bytes 1572872 | tf_op jit(solution)/shard_map/ppermute | solution.py:378
  6.8 23.3 %collective-permute-start.8 = (bf16[256,1536]{1,0:T(8,128)(2,1)S(1)}, bf16[256,1536]{1,0:T(8,128)(2,1)S(1)}, u32[]{:S(2)}, u32[]{:S(2)}) collective-permute-start(bf16[256,1536]{1,0:T(8,128)(2,1)S(1)} %get-tuple-element.34), channel_id=1, source_target_pairs={{0,8},{4,12},{8,0},{12,4},{16,24},{20,28},{24,16},{28,20},{1,9},{5... | collective-permute-start | bytes 2359304 | tf_op jit(solution)/shard_map/ppermute | solution.py:386
  8.4 21.7 %collective-permute-start.5 = (bf16[256,4096]{1,0:T(8,128)(2,1)S(1)}, bf16[256,4096]{1,0:T(8,128)(2,1)S(1)}, u32[]{:S(2)}, u32[]{:S(2)}) collective-permute-start(bf16[256,4096]{1,0:T(8,128)(2,1)S(1)} %copy-done.2), channel_id=1, source_target_pairs={{0,4},{4,0},{8,12},{12,8},{16,20},{20,16},{24,28},{28,24},{1,5},{5... | collective-permute-start | bytes 6291464 | tf_op jit(solution)/shard_map/ppermute | solution.py:375
  17.8 8.1 %collective-permute-start.4 = (bf16[512,256]{1,0:T(8,128)(2,1)S(1)}, bf16[512,256]{1,0:T(8,128)(2,1)S(1)}, u32[]{:S(2)}, u32[]{:S(2)}) collective-permute-start(bf16[512,256]{1,0:T(8,128)(2,1)S(1)} %slice.9), channel_id=1, source_target_pairs={{0,2},{1,3},{2,0},{3,1},{4,6},{5,7},{6,4},{7,5},{8,10},{9,11},{10,... | collective-permute-start | bytes 786440 | tf_op jit(solution)/shard_map/ppermute | solution.py:378
  19.7 7.6 %collective-permute-start.2 = (bf16[512,256]{1,0:T(8,128)(2,1)S(1)}, bf16[512,256]{1,0:T(8,128)(2,1)S(1)}, u32[]{:S(2)}, u32[]{:S(2)}) collective-permute-start(bf16[512,256]{1,0:T(8,128)(2,1)S(1)} %slice.8), channel_id=1, source_target_pairs={{0,1},{1,0},{2,3},{3,2},{4,5},{5,4},{6,7},{7,6},{8,9},{9,8},{10,11... | collective-permute-start | bytes 786440 | tf_op jit(solution)/shard_map/ppermute | solution.py:378
  28.4 9.3 %collective-permute-start.7 = (bf16[256,512]{1,0:T(8,128)(2,1)S(1)}, bf16[256,512]{1,0:T(8,128)(2,1)S(1)}, u32[]{:S(2)}, u32[]{:S(2)}) collective-permute-start(bf16[256,512]{1,0:T(8,128)(2,1)S(1)} %coords_2.1.refs_0_), channel_id=1, source_target_pairs={{0,8},{4,12},{8,0},{12,4},{16,24},{20,28},{24,16},{28,20},{1,9},{5... | collective-permute-start | bytes 786440 | tf_op jit(solution)/shard_map/ppermute | solution.py:386
  30.9 11.5 %collective-permute-start.6 = (bf16[256,512]{1,0:T(8,128)(2,1)S(1)}, bf16[256,512]{1,0:T(8,128)(2,1)S(1)}, u32[]{:S(2)}, u32[]{:S(2)}) collective-permute-start(bf16[256,512]{1,0:T(8,128)(2,1)S(1)} %terms_pair.1), channel_id=1, source_target_pairs={{0,8},{4,12},{8,0},{12,4},{16,24},{20,28},{24,16},{28,20},{1,9},{5... | collective-permute-start | bytes 786440 | tf_op jit(solution)/shard_map/ppermute | solution.py:386
  31.4 6.3 %collective-permute-start.9 = (bf16[256,1536]{1,0:T(8,128)(2,1)S(1)}, bf16[256,1536]{1,0:T(8,128)(2,1)S(1)}, u32[]{:S(2)}, u32[]{:S(2)}) collective-permute-start(bf16[256,1536]{1,0:T(8,128)(2,1)S(1)} %collective-permute-done.8.refs_1_.refs_4_.refs_7_.refs_10_.refs_13_.refs_16_), channel_id=1, source_target_pairs={{0,4},{4,0},{8,12},{12,8},{16,20},{20,16},{24,28},{28,24},{1,5},{5... | collective-permute-start | bytes 2359304 | tf_op jit(solution)/shard_map/ppermute | solution.py:375
  32.2 24.9 %collective-permute-start.13 = (bf16[4096,256]{1,0:T(8,128)(2,1)S(1)}, bf16[4096,256]{1,0:T(8,128)(2,1)S(1)}, u32[]{:S(2)}, u32[]{:S(2)}) collective-permute-start(bf16[4096,256]{1,0:T(8,128)(2,1)S(1)} %assemble.1.own_ref), channel_id=1, source_target_pairs={{0,4},{4,0},{8,12},{12,8},{16,20},{20,16},{24,28},{28,24},{1,5},{5... | collective-permute-start | bytes 6291464 | tf_op jit(solution)/shard_map/ppermute | solution.py:375
  38.8 6.2 %collective-permute-start.15 = (bf16[256,256]{1,0:T(8,128)(2,1)S(1)}, bf16[256,256]{1,0:T(8,128)(2,1)S(1)}, u32[]{:S(2)}, u32[]{:S(2)}) collective-permute-start(bf16[256,256]{1,0:T(8,128)(2,1)S(1)} %get-tuple-element.50), channel_id=1, source_target_pairs={{0,3},{1,2},{2,1},{3,0},{4,7},{5,6},{6,5},{7,4},{8,11},{9,10},{10,... | collective-permute-start | bytes 393224 | tf_op jit(solution)/shard_map/ppermute | solution.py:378
  40.3 7.0 %collective-permute-start.16 = (bf16[256,256]{1,0:T(8,128)(2,1)S(1)}, bf16[256,256]{1,0:T(8,128)(2,1)S(1)}, u32[]{:S(2)}, u32[]{:S(2)}) collective-permute-start(bf16[256,256]{1,0:T(8,128)(2,1)S(1)} %get-tuple-element.51), channel_id=1, source_target_pairs={{0,2},{1,3},{2,0},{3,1},{4,6},{5,7},{6,4},{7,5},{8,10},{9,11},{10,... | collective-permute-start | bytes 393224 | tf_op jit(solution)/shard_map/ppermute | solution.py:378
  41.9 7.0 %collective-permute-start.17 = (bf16[256,256]{1,0:T(8,128)(2,1)S(1)}, bf16[256,256]{1,0:T(8,128)(2,1)S(1)}, u32[]{:S(2)}, u32[]{:S(2)}) collective-permute-start(bf16[256,256]{1,0:T(8,128)(2,1)S(1)} %get-tuple-element.52), channel_id=1, source_target_pairs={{0,1},{1,0},{2,3},{3,2},{4,5},{5,4},{6,7},{7,6},{8,9},{9,8},{10,11... | collective-permute-start | bytes 393224 | tf_op jit(solution)/shard_map/ppermute | solution.py:378
  42.4 9.7 %collective-permute-start.10 = (bf16[256,256]{1,0:T(8,128)(2,1)S(1)}, bf16[256,256]{1,0:T(8,128)(2,1)S(1)}, u32[]{:S(2)}, u32[]{:S(2)}) collective-permute-start(bf16[256,256]{1,0:T(8,128)(2,1)S(1)} %get-tuple-element.39), channel_id=1, source_target_pairs={{0,3},{1,2},{2,1},{3,0},{4,7},{5,6},{6,5},{7,4},{8,11},{9,10},{10,... | collective-permute-start | bytes 393224 | tf_op jit(solution)/shard_map/ppermute | solution.py:378
  45.1 7.1 %collective-permute-start.11 = (bf16[256,256]{1,0:T(8,128)(2,1)S(1)}, bf16[256,256]{1,0:T(8,128)(2,1)S(1)}, u32[]{:S(2)}, u32[]{:S(2)}) collective-permute-start(bf16[256,256]{1,0:T(8,128)(2,1)S(1)} %get-tuple-element.40), channel_id=1, source_target_pairs={{0,2},{1,3},{2,0},{3,1},{4,6},{5,7},{6,4},{7,5},{8,10},{9,11},{10,... | collective-permute-start | bytes 393224 | tf_op jit(solution)/shard_map/ppermute | solution.py:378
  47.4 5.0 %collective-permute-start.12 = (bf16[256,256]{1,0:T(8,128)(2,1)S(1)}, bf16[256,256]{1,0:T(8,128)(2,1)S(1)}, u32[]{:S(2)}, u32[]{:S(2)}) collective-permute-start(bf16[256,256]{1,0:T(8,128)(2,1)S(1)} %get-tuple-element.41), channel_id=1, source_target_pairs={{0,1},{1,0},{2,3},{3,2},{4,5},{5,4},{6,7},{7,6},{8,9},{9,8},{10,11... | collective-permute-start | bytes 393224 | tf_op jit(solution)/shard_map/ppermute | solution.py:378
  49.5 7.5 %collective-permute-start.18 = (bf16[256,256]{1,0:T(8,128)(2,1)S(1)}, bf16[256,256]{1,0:T(8,128)(2,1)S(1)}, u32[]{:S(2)}, u32[]{:S(2)}) collective-permute-start(bf16[256,256]{1,0:T(8,128)(2,1)S(1)} %terms_own.3), channel_id=1, source_target_pairs={{0,16},{4,20},{8,24},{12,28},{16,0},{20,4},{24,8},{28,12},{1,17},{... | collective-permute-start | bytes 393224 | tf_op jit(solution)/shard_map/ppermute | solution.py:389
  53.0 7.3 %collective-permute-start.14 = (bf16[256,256]{1,0:T(8,128)(2,1)S(1)}, bf16[256,256]{1,0:T(8,128)(2,1)S(1)}, u32[]{:S(2)}, u32[]{:S(2)}) collective-permute-start(bf16[256,256]{1,0:T(8,128)(2,1)S(1)} %terms_own.2), channel_id=1, source_target_pairs={{0,16},{4,20},{8,24},{12,28},{16,0},{20,4},{24,8},{28,12},{1,17},{... | collective-permute-start | bytes 393224 | tf_op jit(solution)/shard_map/ppermute | solution.py:389
  60.4 1.6 %collective-permute-start.20 = (bf16[256,512]{1,0:T(8,128)(2,1)S(1)}, bf16[256,512]{1,0:T(8,128)(2,1)S(1)}, u32[]{:S(2)}, u32[]{:S(2)}) collective-permute-start(bf16[256,512]{1,0:T(8,128)(2,1)S(1)} %pad_maximum_fusion.own), channel_id=1, source_target_pairs={{0,4},{4,0},{8,12},{12,8},{16,20},{20,16},{24,28},{28,24},{1,5},{5... | collective-permute-start | bytes 786440 | tf_op jit(solution)/shard_map/ppermute | solution.py:375
  60.4 8.7 %collective-permute-start.19 = (bf16[256,512]{1,0:T(8,128)(2,1)S(1)}, bf16[256,512]{1,0:T(8,128)(2,1)S(1)}, u32[]{:S(2)}, u32[]{:S(2)}) collective-permute-start(bf16[256,512]{1,0:T(8,128)(2,1)S(1)} %pad_maximum_fusion.own), channel_id=1, source_target_pairs={{0,8},{4,12},{8,0},{12,4},{16,24},{20,28},{24,16},{28,20},{1,9},{5... | collective-permute-start | bytes 786440 | tf_op jit(solution)/shard_map/ppermute | solution.py:386
  69.2 1.5 %collective-permute-start.21 = (bf16[256,512]{1,0:T(8,128)(2,1)S(1)}, bf16[256,512]{1,0:T(8,128)(2,1)S(1)}, u32[]{:S(2)}, u32[]{:S(2)}) collective-permute-start(bf16[256,512]{1,0:T(8,128)(2,1)S(1)} %collective-permute-done.19.own), channel_id=1, source_target_pairs={{0,4},{4,0},{8,12},{12,8},{16,20},{20,16},{24,28},{28,24},{1,5},{5... | collective-permute-start | bytes 786440 | tf_op jit(solution)/shard_map/ppermute | solution.py:375
  (2 other events, 9.8 us)

commit v6 on v5

--- a/solution.py
+++ b/solution.py
@@ -258,14 +258,15 @@
     rank = CORES * half
     features = moments[0].shape[0]
     width = proj.shape[0]
-    rows = min(1024, width)
+    rows = min(512, width)
     steps = width // rows
     some = 16
 
     def piece(w):
         return lax.rem(w[2] + pieces - k, pieces)
 
-    def body(w, own, other, proj_ref, first_ref, second_ref, *refs):
+    def body(w, own, *refs):
+        others, (proj_ref, first_ref, second_ref) = refs[: len(grads) - 1], refs[len(grads) - 1 :][:3]
         outs, update = refs[-10:-8], refs[-8]
         moment, grad, ratio, direction, out = refs[-7:-2]
         moment_out, update_out = refs[-2:]
@@ -282,8 +283,12 @@
             )
             for r in range(steps)
         ]
-        for h in range(2):
-            grad[:, pl.ds(h * half, half)] = jnp.where(w[1] == h, own[...], other[...]).T
+        for n, other in enumerate(others):
+            size = other.shape[1]
+            at = pl.ds(n * size, size)
+            for h in range(2):
+                part = jnp.where(w[1] == h, own[:, at], other[...])
+                grad[at, pl.ds(h * half, half)] = part.T
         first_scale = 1.0 / (1.0 - 0.9**STEP)
         second_scale = 1.0 / (1.0 - 0.999**STEP)
 
@@ -340,7 +345,7 @@
         ),
         input_output_aliases=aliases,
         compiler_params=pltpu.CompilerParams(vmem_limit_bytes=28 * MIB),
-        cost_estimate=busy(6),
+        cost_estimate=busy(0.5),
         name="update_step",
     )(where, *inputs)
 
@@ -437,20 +442,30 @@
         )
         landed[0].append((0, to_piece(pair_sum, 1)))
 
-    got = {j: list(landed[0]) for j in chunks}
+    middle = half // 2
+    halves = [(0, middle), (middle, half)]
+    for n in range(len(levels) - 1, 1, -1):
+        entries = [(s, 0, 0, landed[s], halves) for s in levels[n]]
+        outs = iter(
+            terms_step(
+                where, cots_far, far_coords, entries, pieces, span, span, f"terms_{n}"
+            )
+        )
+        for s in levels[n]:
+            for m, link in enumerate(links(s)):
+                landed[s ^ link].append((m * middle, to_fsdp(next(outs), link)))
+    near = {j: [] for j in chunks}
     if fsdp > 1:
-        entries = [
-            (s, 0, j, landed[s], full) for j in chunks for s in range(fsdp - 1, 0, -1)
-        ]
+        entries = [(s, 0, j, landed[s], full) for j in chunks for s in levels[1]]
         outs = terms_step(
-            where, cots_far, after(far_coords, pair_sum), entries, pieces, span, chunk, "terms_peers", BF16, 8
+            where, cots_far, far_coords, entries, pieces, span, chunk, "terms_1"
         )
         for (s, _, j, _, _), x in zip(entries, outs):
-            got[j].append((0, to_fsdp(x, s)))
+            near[j].append((0, to_fsdp(x, s)))
     parts = []
     for j in chunks:
-        entries = [(0, 0, j, got[j], full)]
-        (x,) = terms_step(where, [], None, entries, pieces, span, chunk, "terms_own")
+        entries = [(0, 0, j, landed[0] + near[j], full)]
+        (x,) = terms_step(where, [], None, entries, pieces, span, chunk, "terms_0", BF16, 1)
         parts.append([x] + [to_base(x, k) for k in range(1, groups // pieces)])
 
     blocks = [(s, low, after(x, total)) for s in range(fsdp) for s, low, x in held[s]]
@@ -459,8 +474,12 @@
     proj = join(where, own_proj, after(other_proj, total))
     moments = (first_moment, second_moment)
     parts[0] = [after(x, proj) for x in parts[0]]
-    mine = jnp.concatenate([add_up(x) for x in parts], axis=1)
-    outputs = update_step(where, 0, pieces, (mine, to_core(mine)), proj, moments, None)
+    sums, others = [], []
+    for x in parts:
+        sums.append(add_up([after(y, *others) for y in x]))
+        others.append(to_core(sums[-1]))
+    mine = jnp.concatenate(sums, axis=1)
+    outputs = update_step(where, 0, pieces, (mine, *others), proj, moments, None)
     if pieces > 1:
         others = to_piece(mine, 1)
         pair = (others, to_core(after(others, *outputs)))

time: 77.3 us -> 81.2 us (1.050)
  waiting for transfers between devices: 26 us -> 31.8 us
  starting transfers between devices: 26.3 us -> 24.3 us
    ppermute x2, waiting for transfers between devices: 3.72 us -> 6.48 us  [to_base(): lax.ppermute(x, 'dp', [(i, (i + k * pieces * CORES) % dp) for i in range(...]
    ppermute x2, starting transfers between devices: 5.29 us -> 3.45 us  [to_base(): lax.ppermute(x, 'dp', [(i, (i + k * pieces * CORES) % dp) for i in range(...]
    ppermute x4, waiting for transfers between devices: 4.41 us -> 5.78 us  [to_piece(): return lax.ppermute(x, 'dp', pairs)]
    ppermute x10, waiting for transfers between devices: 15.5 us -> 16.8 us  [to_fsdp(): return lax.ppermute(x, 'fsdp', [(i, i ^ s) for i in range(fsdp)])]
    ppermute x10, starting transfers between devices: 15.4 us -> 14.2 us  [to_fsdp(): return lax.ppermute(x, 'fsdp', [(i, i ^ s) for i in range(fsdp)])]
    ppermute x4, starting transfers between devices: 4.47 us -> 5.64 us  [to_piece(): return lax.ppermute(x, 'dp', pairs)]
    pallas_call x9 -> x10, Pallas kernels: 8.62 us -> 9.29 us  [call(): pl.pallas_call(body, out_shape=out_shape, grid_spec=pltpu.PrefetchScalarG...]
    ppermute x6 -> x7, waiting for transfers between devices: 2.33 us -> 2.75 us  [to_core(): return lax.ppermute(x, 'dp', [(i, i ^ 1) for i in range(dp)])]
  transfers between devices with their start and end apart: 22 -> 23, of which waited for: 12 -> 13; matrix products, arithmetic and copies ran while one was open for 0% -> 0% of each run, Pallas kernels for 22% -> 22%
where the time goes in v6:
time: 81.2 us; the launch traced here: 81.1 us
  waiting for transfers between devices  31.8 us (39%)
  starting transfers between devices  24.3 us (30%)
  Pallas kernels  24 us (30%)
    ppermute x10, waiting for transfers between devices, to_fsdp(): return lax.ppermute(x, 'fsdp', [(i, i ^ s) for i in range(fsdp)])  16.8 us
    ppermute x10, starting transfers between devices, to_fsdp(): return lax.ppermute(x, 'fsdp', [(i, i ^ s) for i in range(fsdp)])  14.2 us
    pallas_call x2, Pallas kernels, update_step(): pl.pallas_call(body, out_shape=[jax.ShapeDtypeStruct(x.shape, F32) for x...  12.4 us
    pallas_call x10, Pallas kernels, call(): pl.pallas_call(body, out_shape=out_shape, grid_spec=pltpu.PrefetchScalarG...  9.29 us
    ppermute x2, waiting for transfers between devices, to_base(): lax.ppermute(x, 'dp', [(i, (i + k * pieces * CORES) % dp) for i in range(...  6.48 us
    ppermute x4, waiting for transfers between devices, to_piece(): return lax.ppermute(x, 'dp', pairs)  5.78 us
    ppermute x4, starting transfers between devices, to_piece(): return lax.ppermute(x, 'dp', pairs)  5.64 us
    ppermute x2, starting transfers between devices, to_base(): lax.ppermute(x, 'dp', [(i, (i + k * pieces * CORES) % dp) for i in range(...  3.45 us
  transfers between devices with their start and end apart: 23, of which 13 were waited for; matrix products, arithmetic and copies ran while one was open for 0% of the time, Pallas kernels for 22%

profile of v6, /device:TPU:0, one launch (start us, length us, event | category | flops | bytes accessed | tf_op | source)
XLA Modules:
  0.0 81.1 jit_solution(1192275721627454172)
XLA Ops:
  1.2 1.5 %cut_out.1 = (bf16[1024,256]{1,0:T(8,128)(2,1)S(1)}, bf16[256,1536]{1,0:T(8,128)(2,1)S(1)}) custom-call(s32[1]{0:T(128)} %bitcast.fsdp_ref, s32[1]{0:T(128)} %bitcast.1.core_ref, s32[1]{0:T(128)} %bitcast.2.piece_ref, bf16[1024,512]{1,0:T(8,128)(2,1)} %proj_ref.1, bf16[256,4096]{1,0:T(8,128)(2,1)} %refs_1_.3), custom_call_target="tpu_custom_call" | custom-call | flops 1150000000 | tf_op jit(solution)/shard_map/cut_out/pallas_call | solution.py:71
  2.6 2.6 %collective-permute-start.3 = (bf16[1024,256]{1,0:T(8,128)(2,1)S(1)}, bf16[1024,256]{1,0:T(8,128)(2,1)S(1)}, u32[]{:S(2)}, u32[]{:S(2)}) collective-permute-start(bf16[1024,256]{1,0:T(8,128)(2,1)S(1)} %get-tuple-element.43.refs_2_.refs_0_), channel_id=1, source_target_pairs={{0,1},{1,0},{2,3},{3,2},{4,5},{5,4},{6,7},{7,6},{8,9},{9,8},{10,11... | collective-permute-start | bytes 1572872 | tf_op jit(solution)/shard_map/ppermute | solution.py:383
  5.3 1.5 %collective-permute-start.1 = (bf16[1024,256]{1,0:T(8,128)(2,1)S(1)}, bf16[1024,256]{1,0:T(8,128)(2,1)S(1)}, u32[]{:S(2)}, u32[]{:S(2)}) collective-permute-start(bf16[1024,256]{1,0:T(8,128)(2,1)S(1)} %get-tuple-element.43.refs_2_.refs_0_), channel_id=1, source_target_pairs={{0,2},{1,3},{2,0},{3,1},{4,6},{5,7},{6,4},{7,5},{8,10},{9,11},{10,... | collective-permute-start | bytes 1572872 | tf_op jit(solution)/shard_map/ppermute | solution.py:383
  6.8 1.6 %collective-permute-start.8 = (bf16[256,1536]{1,0:T(8,128)(2,1)S(1)}, bf16[256,1536]{1,0:T(8,128)(2,1)S(1)}, u32[]{:S(2)}, u32[]{:S(2)}) collective-permute-start(bf16[256,1536]{1,0:T(8,128)(2,1)S(1)} %get-tuple-element.34), channel_id=1, source_target_pairs={{0,8},{4,12},{8,0},{12,4},{16,24},{20,28},{24,16},{28,20},{1,9},{5... | collective-permute-start | bytes 2359304 | tf_op jit(solution)/shard_map/ppermute | solution.py:391
  8.4 9.3 %collective-permute-done.3.refs_2_.refs_1_ = bf16[1024,256]{1,0:T(8,128)(2,1)S(1)} collective-permute-done((bf16[1024,256]{1,0:T(8,128)(2,1)S(1)}, bf16[1024,256]{1,0:T(8,128)(2,1)S(1)}, u32[]{:S(2)}, u32[]{:S(2)}) %collective-permute-start.3) | collective-permute-done | bytes 524320 | tf_op jit(solution)/shard_map/ppermute | solution.py:383
  17.8 1.8 %collective-permute-start.4 = (bf16[512,256]{1,0:T(8,128)(2,1)S(1)}, bf16[512,256]{1,0:T(8,128)(2,1)S(1)}, u32[]{:S(2)}, u32[]{:S(2)}) collective-permute-start(bf16[512,256]{1,0:T(8,128)(2,1)S(1)} %slice.9), channel_id=1, source_target_pairs={{0,2},{1,3},{2,0},{3,1},{4,6},{5,7},{6,4},{7,5},{8,10},{9,11},{10,... | collective-permute-start | bytes 786440 | tf_op jit(solution)/shard_map/ppermute | solution.py:383
  19.7 1.6 %collective-permute-start.2 = (bf16[512,256]{1,0:T(8,128)(2,1)S(1)}, bf16[512,256]{1,0:T(8,128)(2,1)S(1)}, u32[]{:S(2)}, u32[]{:S(2)}) collective-permute-start(bf16[512,256]{1,0:T(8,128)(2,1)S(1)} %slice.8), channel_id=1, source_target_pairs={{0,1},{1,0},{2,3},{3,2},{4,5},{5,4},{6,7},{7,6},{8,9},{9,8},{10,11... | collective-permute-start | bytes 786440 | tf_op jit(solution)/shard_map/ppermute | solution.py:383
  22.2 1.3 %coords_1.1.refs_6_ = f32[512,256]{1,0:T(8,128)S(1)} custom-call(s32[3]{0:T(128)S(1)} %pad_add_fusion.w, bf16[256,4096]{1,0:T(8,128)(2,1)S(1)} %copy-done.3, bf16[256,4096]{1,0:T(8,128)(2,1)S(1)} %collective-permute-done.refs_1_.refs_4_, bf16[1024,256]{1,0:T(8,128)(2,1)S(1)} %collective-permute-done.3.refs_2_.refs_1_, bf16[256,4096]{1,0:T(8,128)(2,1)S(1)} %copy-done.3, ...), custom_call_target="tpu_custom_call" | custom-call | flops 9200000000 | tf_op jit(solution)/shard_map/coords_1/pallas_call | solution.py:31
  23.5 2.5 %collective-permute-done.4.refs_5_.refs_4_ = bf16[512,256]{1,0:T(8,128)(2,1)S(1)} collective-permute-done((bf16[512,256]{1,0:T(8,128)(2,1)S(1)}, bf16[512,256]{1,0:T(8,128)(2,1)S(1)}, u32[]{:S(2)}, u32[]{:S(2)}) %collective-permute-start.4) | collective-permute-done | bytes 262176 | tf_op jit(solution)/shard_map/ppermute | solution.py:383
  25.9 1.4 %collective-permute-done.2.refs_2_.refs_3_ = bf16[512,256]{1,0:T(8,128)(2,1)S(1)} collective-permute-done((bf16[512,256]{1,0:T(8,128)(2,1)S(1)}, bf16[512,256]{1,0:T(8,128)(2,1)S(1)}, u32[]{:S(2)}, u32[]{:S(2)}) %collective-permute-start.2) | collective-permute-done | bytes 262176 | tf_op jit(solution)/shard_map/ppermute | solution.py:383
  29.2 1.6 %collective-permute-start.7 = (bf16[256,512]{1,0:T(8,128)(2,1)S(1)}, bf16[256,512]{1,0:T(8,128)(2,1)S(1)}, u32[]{:S(2)}, u32[]{:S(2)}) collective-permute-start(bf16[256,512]{1,0:T(8,128)(2,1)S(1)} %coords_2.1.refs_0_), channel_id=1, source_target_pairs={{0,8},{4,12},{8,0},{12,4},{16,24},{20,28},{24,16},{28,20},{1,9},{5... | collective-permute-start | bytes 786440 | tf_op jit(solution)/shard_map/ppermute | solution.py:391
  31.1 1.3 %terms_chip.1 = (f32[256,512]{1,0:T(8,128)S(1)}, f32[256,512]{1,0:T(8,128)S(1)}, f32[256,512]{1,0:T(8,128)S(1)}, f32[256,512]{1,0:T(8,128)S(1)}) custom-call(s32[3]{0:T(128)S(1)} %pad_add_fusion.w, bf16[256,512]{1,0:T(8,128)(2,1)S(1)} %coords_2.1.refs_0_, bf16[256,4096]{1,0:T(8,128)(2,1)S(1)} %copy-done.2, ...), custom_call_target="tpu_custom_call" | custom-call | flops 13799999488 | tf_op jit(solution)/shard_map/terms_chip/pallas_call | solution.py:31
  32.3 5.6 %collective-permute-done.7.refs_0_ = bf16[256,512]{1,0:T(8,128)(2,1)S(1)} collective-permute-done((bf16[256,512]{1,0:T(8,128)(2,1)S(1)}, bf16[256,512]{1,0:T(8,128)(2,1)S(1)}, u32[]{:S(2)}, u32[]{:S(2)}) %collective-permute-start.7) | collective-permute-done | bytes 262176 | tf_op jit(solution)/shard_map/ppermute | solution.py:391
  41.7 1.6 %collective-permute-start.6 = (bf16[256,512]{1,0:T(8,128)(2,1)S(1)}, bf16[256,512]{1,0:T(8,128)(2,1)S(1)}, u32[]{:S(2)}, u32[]{:S(2)}) collective-permute-start(bf16[256,512]{1,0:T(8,128)(2,1)S(1)} %terms_pair.1), channel_id=1, source_target_pairs={{0,8},{4,12},{8,0},{12,4},{16,24},{20,28},{24,16},{28,20},{1,9},{5... | collective-permute-start | bytes 786440 | tf_op jit(solution)/shard_map/ppermute | solution.py:391
  46.9 1.5 %collective-permute-start.13 = (bf16[256,256]{1,0:T(8,128)(2,1)S(1)}, bf16[256,256]{1,0:T(8,128)(2,1)S(1)}, u32[]{:S(2)}, u32[]{:S(2)}) collective-permute-start(bf16[256,256]{1,0:T(8,128)(2,1)S(1)} %get-tuple-element.42), channel_id=1, source_target_pairs={{0,2},{1,3},{2,0},{3,1},{4,6},{5,7},{6,4},{7,5},{8,10},{9,11},{10,... | collective-permute-start | bytes 393224 | tf_op jit(solution)/shard_map/ppermute | solution.py:383
  49.1 1.5 %collective-permute-start.17 = (bf16[256,256]{1,0:T(8,128)(2,1)S(1)}, bf16[256,256]{1,0:T(8,128)(2,1)S(1)}, u32[]{:S(2)}, u32[]{:S(2)}) collective-permute-start(bf16[256,256]{1,0:T(8,128)(2,1)S(1)} %get-tuple-element.52), channel_id=1, source_target_pairs={{0,2},{1,3},{2,0},{3,1},{4,6},{5,7},{6,4},{7,5},{8,10},{9,11},{10,... | collective-permute-start | bytes 393224 | tf_op jit(solution)/shard_map/ppermute | solution.py:383
  50.6 1.2 %collective-permute-done.12.refs_2_ = bf16[256,256]{1,0:T(8,128)(2,1)S(1)} collective-permute-done((bf16[256,256]{1,0:T(8,128)(2,1)S(1)}, bf16[256,256]{1,0:T(8,128)(2,1)S(1)}, u32[]{:S(2)}, u32[]{:S(2)}) %collective-permute-start.12) | collective-permute-done | bytes 131104 | tf_op jit(solution)/shard_map/ppermute | solution.py:383
  53.3 2.7 %collective-permute-start.15 = (bf16[256,256]{1,0:T(8,128)(2,1)S(1)}, bf16[256,256]{1,0:T(8,128)(2,1)S(1)}, u32[]{:S(2)}, u32[]{:S(2)}) collective-permute-start(bf16[256,256]{1,0:T(8,128)(2,1)S(1)} %terms_0.2), channel_id=1, source_target_pairs={{0,16},{4,20},{8,24},{12,28},{16,0},{20,4},{24,8},{28,12},{1,17},{... | collective-permute-start | bytes 393224 | tf_op jit(solution)/shard_map/ppermute | solution.py:394
  58.2 3.8 %collective-permute-done.15 = bf16[256,256]{1,0:T(8,128)(2,1)S(1)} collective-permute-done((bf16[256,256]{1,0:T(8,128)(2,1)S(1)}, bf16[256,256]{1,0:T(8,128)(2,1)S(1)}, u32[]{:S(2)}, u32[]{:S(2)}) %collective-permute-start.15) | collective-permute-done | bytes 131104 | tf_op jit(solution)/shard_map/ppermute | solution.py:394
  62.1 2.7 %collective-permute-done.19 = bf16[256,256]{1,0:T(8,128)(2,1)S(1)} collective-permute-done((bf16[256,256]{1,0:T(8,128)(2,1)S(1)}, bf16[256,256]{1,0:T(8,128)(2,1)S(1)}, u32[]{:S(2)}, u32[]{:S(2)}) %collective-permute-start.19) | collective-permute-done | bytes 131104 | tf_op jit(solution)/shard_map/ppermute | solution.py:394
  65.7 1.3 %collective-permute-done.21.refs_1_ = bf16[256,256]{1,0:T(8,128)(2,1)S(1)} collective-permute-done((bf16[256,256]{1,0:T(8,128)(2,1)S(1)}, bf16[256,256]{1,0:T(8,128)(2,1)S(1)}, u32[]{:S(2)}, u32[]{:S(2)}) %collective-permute-start.21) | collective-permute-done | bytes 131104 | tf_op jit(solution)/shard_map/ppermute | solution.py:380
  67.0 6.2 %update_step.2 = (f32[1024,512]{1,0:T(8,128)}, f32[1024,512]{1,0:T(8,128)}, f32[4096,1024]{1,0:T(8,128)}) custom-call(s32[3]{0:T(128)S(1)} %pad_add_fusion.w, bf16[256,512]{1,0:T(8,128)(2,1)S(1)} %pad_maximum_fusion.own, bf16[256,256]{1,0:T(8,128)(2,1)S(1)} %collective-permute-done.18.refs_0_, bf16[256,256]{1,0:T(8,128)(2,1)S(1)} %collective-permute-done.21.refs_1_, ...), custom_call_target="tpu_custom_call" | custom-call | flops 575000000 | tf_op jit(solution)/shard_map/update_step/pallas_call | solution.py:327
  73.5 1.4 %collective-permute-done.22.refs_0_ = bf16[256,512]{1,0:T(8,128)(2,1)S(1)} collective-permute-done((bf16[256,512]{1,0:T(8,128)(2,1)S(1)}, bf16[256,512]{1,0:T(8,128)(2,1)S(1)}, u32[]{:S(2)}, u32[]{:S(2)}) %collective-permute-start.22) | collective-permute-done | bytes 262176 | tf_op jit(solution)/shard_map/ppermute | solution.py:380
  74.9 6.2 %update_step.3 = (f32[1024,512]{1,0:T(8,128)}, f32[1024,512]{1,0:T(8,128)}, f32[4096,1024]{1,0:T(8,128)}) custom-call(s32[3]{0:T(128)S(1)} %pad_add_fusion.w, bf16[256,512]{1,0:T(8,128)(2,1)S(1)} %collective-permute-done.20.own, bf16[256,512]{1,0:T(8,128)(2,1)S(1)} %collective-permute-done.22.refs_0_, ...), custom_call_target="tpu_custom_call", output_to_operand_aliasing={{0}: (6, {}), {1}: (7, {}), {2}: (8, {})} | custom-call | flops 575000000 | tf_op jit(solution)/shard_map/update_step/pallas_call | solution.py:327
  (50 shorter events, 16.5 us)
Async XLA Ops:
  0.6 20.6 %collective-permute-start = (bf16[256,4096]{1,0:T(8,128)(2,1)}, bf16[256,4096]{1,0:T(8,128)(2,1)S(1)}, u32[]{:S(2)}, u32[]{:S(2)}) collective-permute-start(bf16[256,4096]{1,0:T(8,128)(2,1)} %refs_3_.6), channel_id=1, source_target_pairs={{0,4},{4,0},{8,12},{12,8},{16,20},{20,16},{24,28},{28,24},{1,5},{5... | collective-permute-start | bytes 6291464 | tf_op jit(solution)/shard_map/ppermute | solution.py:380
  1.2 20.1 %copy-start.3 = (bf16[256,4096]{1,0:T(8,128)(2,1)S(1)}, bf16[256,4096]{1,0:T(8,128)(2,1)}, u32[]{:S(2)}) copy-start(bf16[256,4096]{1,0:T(8,128)(2,1)} %refs_3_.6) | copy-start | bytes 6291460
  2.6 15.2 %collective-permute-start.3 = (bf16[1024,256]{1,0:T(8,128)(2,1)S(1)}, bf16[1024,256]{1,0:T(8,128)(2,1)S(1)}, u32[]{:S(2)}, u32[]{:S(2)}) collective-permute-start(bf16[1024,256]{1,0:T(8,128)(2,1)S(1)} %get-tuple-element.43.refs_2_.refs_0_), channel_id=1, source_target_pairs={{0,1},{1,0},{2,3},{3,2},{4,5},{5,4},{6,7},{7,6},{8,9},{9,8},{10,11... | collective-permute-start | bytes 1572872 | tf_op jit(solution)/shard_map/ppermute | solution.py:383
  5.3 14.4 %collective-permute-start.1 = (bf16[1024,256]{1,0:T(8,128)(2,1)S(1)}, bf16[1024,256]{1,0:T(8,128)(2,1)S(1)}, u32[]{:S(2)}, u32[]{:S(2)}) collective-permute-start(bf16[1024,256]{1,0:T(8,128)(2,1)S(1)} %get-tuple-element.43.refs_2_.refs_0_), channel_id=1, source_target_pairs={{0,2},{1,3},{2,0},{3,1},{4,6},{5,7},{6,4},{7,5},{8,10},{9,11},{10,... | collective-permute-start | bytes 1572872 | tf_op jit(solution)/shard_map/ppermute | solution.py:383
  6.8 24.1 %collective-permute-start.8 = (bf16[256,1536]{1,0:T(8,128)(2,1)S(1)}, bf16[256,1536]{1,0:T(8,128)(2,1)S(1)}, u32[]{:S(2)}, u32[]{:S(2)}) collective-permute-start(bf16[256,1536]{1,0:T(8,128)(2,1)S(1)} %get-tuple-element.34), channel_id=1, source_target_pairs={{0,8},{4,12},{8,0},{12,4},{16,24},{20,28},{24,16},{28,20},{1,9},{5... | collective-permute-start | bytes 2359304 | tf_op jit(solution)/shard_map/ppermute | solution.py:391
  8.4 22.7 %collective-permute-start.5 = (bf16[256,4096]{1,0:T(8,128)(2,1)S(1)}, bf16[256,4096]{1,0:T(8,128)(2,1)S(1)}, u32[]{:S(2)}, u32[]{:S(2)}) collective-permute-start(bf16[256,4096]{1,0:T(8,128)(2,1)S(1)} %copy-done.2), channel_id=1, source_target_pairs={{0,4},{4,0},{8,12},{12,8},{16,20},{20,16},{24,28},{28,24},{1,5},{5... | collective-permute-start | bytes 6291464 | tf_op jit(solution)/shard_map/ppermute | solution.py:380
  17.8 8.1 %collective-permute-start.4 = (bf16[512,256]{1,0:T(8,128)(2,1)S(1)}, bf16[512,256]{1,0:T(8,128)(2,1)S(1)}, u32[]{:S(2)}, u32[]{:S(2)}) collective-permute-start(bf16[512,256]{1,0:T(8,128)(2,1)S(1)} %slice.9), channel_id=1, source_target_pairs={{0,2},{1,3},{2,0},{3,1},{4,6},{5,7},{6,4},{7,5},{8,10},{9,11},{10,... | collective-permute-start | bytes 786440 | tf_op jit(solution)/shard_map/ppermute | solution.py:383
  19.7 7.6 %collective-permute-start.2 = (bf16[512,256]{1,0:T(8,128)(2,1)S(1)}, bf16[512,256]{1,0:T(8,128)(2,1)S(1)}, u32[]{:S(2)}, u32[]{:S(2)}) collective-permute-start(bf16[512,256]{1,0:T(8,128)(2,1)S(1)} %slice.8), channel_id=1, source_target_pairs={{0,1},{1,0},{2,3},{3,2},{4,5},{5,4},{6,7},{7,6},{8,9},{9,8},{10,11... | collective-permute-start | bytes 786440 | tf_op jit(solution)/shard_map/ppermute | solution.py:383
  29.2 28.2 %collective-permute-start.14 = (bf16[4096,256]{1,0:T(8,128)(2,1)S(1)}, bf16[4096,256]{1,0:T(8,128)(2,1)S(1)}, u32[]{:S(2)}, u32[]{:S(2)}) collective-permute-start(bf16[4096,256]{1,0:T(8,128)(2,1)S(1)} %assemble.1.own_ref), channel_id=1, source_target_pairs={{0,4},{4,0},{8,12},{12,8},{16,20},{20,16},{24,28},{28,24},{1,5},{5... | collective-permute-start | bytes 6291464 | tf_op jit(solution)/shard_map/ppermute | solution.py:380
  29.2 8.7 %collective-permute-start.7 = (bf16[256,512]{1,0:T(8,128)(2,1)S(1)}, bf16[256,512]{1,0:T(8,128)(2,1)S(1)}, u32[]{:S(2)}, u32[]{:S(2)}) collective-permute-start(bf16[256,512]{1,0:T(8,128)(2,1)S(1)} %coords_2.1.refs_0_), channel_id=1, source_target_pairs={{0,8},{4,12},{8,0},{12,4},{16,24},{20,28},{24,16},{28,20},{1,9},{5... | collective-permute-start | bytes 786440 | tf_op jit(solution)/shard_map/ppermute | solution.py:391
  30.9 7.1 %collective-permute-start.9 = (bf16[256,1536]{1,0:T(8,128)(2,1)S(1)}, bf16[256,1536]{1,0:T(8,128)(2,1)S(1)}, u32[]{:S(2)}, u32[]{:S(2)}) collective-permute-start(bf16[256,1536]{1,0:T(8,128)(2,1)S(1)} %collective-permute-done.8.refs_1_.refs_5_.refs_9_.refs_13_), channel_id=1, source_target_pairs={{0,4},{4,0},{8,12},{12,8},{16,20},{20,16},{24,28},{28,24},{1,5},{5... | collective-permute-start | bytes 2359304 | tf_op jit(solution)/shard_map/ppermute | solution.py:380
  38.8 5.1 %collective-permute-start.10 = (bf16[128,512]{1,0:T(8,128)(2,1)S(1)}, bf16[128,512]{1,0:T(8,128)(2,1)S(1)}, u32[]{:S(2)}, u32[]{:S(2)}) collective-permute-start(bf16[128,512]{1,0:T(8,128)(2,1)S(1)} %get-tuple-element.38), channel_id=1, source_target_pairs={{0,2},{1,3},{2,0},{3,1},{4,6},{5,7},{6,4},{7,5},{8,10},{9,11},{10,... | collective-permute-start | bytes 393224 | tf_op jit(solution)/shard_map/ppermute | solution.py:383
  40.0 5.0 %collective-permute-start.11 = (bf16[128,512]{1,0:T(8,128)(2,1)S(1)}, bf16[128,512]{1,0:T(8,128)(2,1)S(1)}, u32[]{:S(2)}, u32[]{:S(2)}) collective-permute-start(bf16[128,512]{1,0:T(8,128)(2,1)S(1)} %get-tuple-element.40), channel_id=1, source_target_pairs={{0,1},{1,0},{2,3},{3,2},{4,5},{5,4},{6,7},{7,6},{8,9},{9,8},{10,11... | collective-permute-start | bytes 393224 | tf_op jit(solution)/shard_map/ppermute | solution.py:383
  41.7 7.4 %collective-permute-start.6 = (bf16[256,512]{1,0:T(8,128)(2,1)S(1)}, bf16[256,512]{1,0:T(8,128)(2,1)S(1)}, u32[]{:S(2)}, u32[]{:S(2)}) collective-permute-start(bf16[256,512]{1,0:T(8,128)(2,1)S(1)} %terms_pair.1), channel_id=1, source_target_pairs={{0,8},{4,12},{8,0},{12,4},{16,24},{20,28},{24,16},{28,20},{1,9},{5... | collective-permute-start | bytes 786440 | tf_op jit(solution)/shard_map/ppermute | solution.py:391
  45.9 5.9 %collective-permute-start.12 = (bf16[256,256]{1,0:T(8,128)(2,1)S(1)}, bf16[256,256]{1,0:T(8,128)(2,1)S(1)}, u32[]{:S(2)}, u32[]{:S(2)}) collective-permute-start(bf16[256,256]{1,0:T(8,128)(2,1)S(1)} %get-tuple-element.41), channel_id=1, source_target_pairs={{0,1},{1,0},{2,3},{3,2},{4,5},{5,4},{6,7},{7,6},{8,9},{9,8},{10,11... | collective-permute-start | bytes 393224 | tf_op jit(solution)/shard_map/ppermute | solution.py:383
  46.9 5.8 %collective-permute-start.13 = (bf16[256,256]{1,0:T(8,128)(2,1)S(1)}, bf16[256,256]{1,0:T(8,128)(2,1)S(1)}, u32[]{:S(2)}, u32[]{:S(2)}) collective-permute-start(bf16[256,256]{1,0:T(8,128)(2,1)S(1)} %get-tuple-element.42), channel_id=1, source_target_pairs={{0,2},{1,3},{2,0},{3,1},{4,6},{5,7},{6,4},{7,5},{8,10},{9,11},{10,... | collective-permute-start | bytes 393224 | tf_op jit(solution)/shard_map/ppermute | solution.py:383
  48.4 7.5 %collective-permute-start.16 = (bf16[256,256]{1,0:T(8,128)(2,1)S(1)}, bf16[256,256]{1,0:T(8,128)(2,1)S(1)}, u32[]{:S(2)}, u32[]{:S(2)}) collective-permute-start(bf16[256,256]{1,0:T(8,128)(2,1)S(1)} %get-tuple-element.51), channel_id=1, source_target_pairs={{0,1},{1,0},{2,3},{3,2},{4,5},{5,4},{6,7},{7,6},{8,9},{9,8},{10,11... | collective-permute-start | bytes 393224 | tf_op jit(solution)/shard_map/ppermute | solution.py:383
  49.1 6.8 %collective-permute-start.17 = (bf16[256,256]{1,0:T(8,128)(2,1)S(1)}, bf16[256,256]{1,0:T(8,128)(2,1)S(1)}, u32[]{:S(2)}, u32[]{:S(2)}) collective-permute-start(bf16[256,256]{1,0:T(8,128)(2,1)S(1)} %get-tuple-element.52), channel_id=1, source_target_pairs={{0,2},{1,3},{2,0},{3,1},{4,6},{5,7},{6,4},{7,5},{8,10},{9,11},{10,... | collective-permute-start | bytes 393224 | tf_op jit(solution)/shard_map/ppermute | solution.py:383
  53.3 8.7 %collective-permute-start.15 = (bf16[256,256]{1,0:T(8,128)(2,1)S(1)}, bf16[256,256]{1,0:T(8,128)(2,1)S(1)}, u32[]{:S(2)}, u32[]{:S(2)}) collective-permute-start(bf16[256,256]{1,0:T(8,128)(2,1)S(1)} %terms_0.2), channel_id=1, source_target_pairs={{0,16},{4,20},{8,24},{12,28},{16,0},{20,4},{24,8},{28,12},{1,17},{... | collective-permute-start | bytes 393224 | tf_op jit(solution)/shard_map/ppermute | solution.py:394
  56.6 8.3 %collective-permute-start.19 = (bf16[256,256]{1,0:T(8,128)(2,1)S(1)}, bf16[256,256]{1,0:T(8,128)(2,1)S(1)}, u32[]{:S(2)}, u32[]{:S(2)}) collective-permute-start(bf16[256,256]{1,0:T(8,128)(2,1)S(1)} %terms_0.3), channel_id=1, source_target_pairs={{0,16},{4,20},{8,24},{12,28},{16,0},{20,4},{24,8},{28,12},{1,17},{... | collective-permute-start | bytes 393224 | tf_op jit(solution)/shard_map/ppermute | solution.py:394
  62.1 2.8 %collective-permute-start.18 = (bf16[256,256]{1,0:T(8,128)(2,1)S(1)}, bf16[256,256]{1,0:T(8,128)(2,1)S(1)}, u32[]{:S(2)}, u32[]{:S(2)}) collective-permute-start(bf16[256,256]{1,0:T(8,128)(2,1)S(1)} %add_convert_fusion.1), channel_id=1, source_target_pairs={{0,4},{4,0},{8,12},{12,8},{16,20},{20,16},{24,28},{28,24},{1,5},{5... | collective-permute-start | bytes 393224 | tf_op jit(solution)/shard_map/ppermute | solution.py:380
  64.9 8.4 %collective-permute-start.20 = (bf16[256,512]{1,0:T(8,128)(2,1)S(1)}, bf16[256,512]{1,0:T(8,128)(2,1)S(1)}, u32[]{:S(2)}, u32[]{:S(2)}) collective-permute-start(bf16[256,512]{1,0:T(8,128)(2,1)S(1)} %pad_maximum_fusion.own), channel_id=1, source_target_pairs={{0,8},{4,12},{8,0},{12,4},{16,24},{20,28},{24,16},{28,20},{1,9},{5... | collective-permute-start | bytes 786440 | tf_op jit(solution)/shard_map/ppermute | solution.py:391
  65.7 1.3 %collective-permute-start.21 = (bf16[256,256]{1,0:T(8,128)(2,1)S(1)}, bf16[256,256]{1,0:T(8,128)(2,1)S(1)}, u32[]{:S(2)}, u32[]{:S(2)}) collective-permute-start(bf16[256,256]{1,0:T(8,128)(2,1)S(1)} %add_convert_fusion), channel_id=1, source_target_pairs={{0,4},{4,0},{8,12},{12,8},{16,20},{20,16},{24,28},{28,24},{1,5},{5... | collective-permute-start | bytes 393224 | tf_op jit(solution)/shard_map/ppermute | solution.py:380
  73.3 1.6 %collective-permute-start.22 = (bf16[256,512]{1,0:T(8,128)(2,1)S(1)}, bf16[256,512]{1,0:T(8,128)(2,1)S(1)}, u32[]{:S(2)}, u32[]{:S(2)}) collective-permute-start(bf16[256,512]{1,0:T(8,128)(2,1)S(1)} %collective-permute-done.20.own), channel_id=1, source_target_pairs={{0,4},{4,0},{8,12},{12,8},{16,20},{20,16},{24,28},{28,24},{1,5},{5... | collective-permute-start | bytes 786440 | tf_op jit(solution)/shard_map/ppermute | solution.py:380
  (3 other events, 26.6 us)

commit v7 on v6

--- a/solution.py
+++ b/solution.py
@@ -265,8 +265,7 @@
     def piece(w):
         return lax.rem(w[2] + pieces - k, pieces)
 
-    def body(w, own, *refs):
-        others, (proj_ref, first_ref, second_ref) = refs[: len(grads) - 1], refs[len(grads) - 1 :][:3]
+    def body(w, own, other, proj_ref, first_ref, second_ref, *refs):
         outs, update = refs[-10:-8], refs[-8]
         moment, grad, ratio, direction, out = refs[-7:-2]
         moment_out, update_out = refs[-2:]
@@ -283,12 +282,8 @@
             )
             for r in range(steps)
         ]
-        for n, other in enumerate(others):
-            size = other.shape[1]
-            at = pl.ds(n * size, size)
-            for h in range(2):
-                part = jnp.where(w[1] == h, own[:, at], other[...])
-                grad[at, pl.ds(h * half, half)] = part.T
+        for h in range(2):
+            grad[:, pl.ds(h * half, half)] = jnp.where(w[1] == h, own[...], other[...]).T
         first_scale = 1.0 / (1.0 - 0.9**STEP)
         second_scale = 1.0 / (1.0 - 0.999**STEP)
 
@@ -299,12 +294,12 @@
             second_new = 0.999 * second_ref[at, :] + 0.001 * grad_low * grad_low
             moment[0, at, :] = first_new
             moment[1, at, :] = second_new
-            ratio[at, :] = (
-                (first_new * first_scale) / (jnp.sqrt(second_new * second_scale) + 1e-08)
-            ).astype(BF16)
+            scaled = second_new * second_scale
+            root = scaled * lax.rsqrt(scaled)
+            ratio[at, :] = ((first_new * first_scale) / (root + 1e-08)).astype(BF16)
             return 0
 
-        lax.fori_loop(0, span // some, adam, 0, unroll=2)
+        lax.fori_loop(0, span // some, adam, 0, unroll=8)
         for copy in stores:
             copy.start()
         direction[...] = ratio[...].T
@@ -345,7 +340,7 @@
         ),
         input_output_aliases=aliases,
         compiler_params=pltpu.CompilerParams(vmem_limit_bytes=28 * MIB),
-        cost_estimate=busy(0.5),
+        cost_estimate=busy(6),
         name="update_step",
     )(where, *inputs)
 
@@ -474,12 +469,8 @@
     proj = join(where, own_proj, after(other_proj, total))
     moments = (first_moment, second_moment)
     parts[0] = [after(x, proj) for x in parts[0]]
-    sums, others = [], []
-    for x in parts:
-        sums.append(add_up([after(y, *others) for y in x]))
-        others.append(to_core(sums[-1]))
-    mine = jnp.concatenate(sums, axis=1)
-    outputs = update_step(where, 0, pieces, (mine, *others), proj, moments, None)
+    mine = jnp.concatenate([add_up(x) for x in parts], axis=1)
+    outputs = update_step(where, 0, pieces, (mine, to_core(mine)), proj, moments, None)
     if pieces > 1:
         others = to_piece(mine, 1)
         pair = (others, to_core(after(others, *outputs)))

time: 81.2 us -> 77 us (0.948)
  waiting for transfers between devices: 31.8 us -> 28 us
    ppermute x4, waiting for transfers between devices: 5.78 us -> 3.69 us  [to_piece(): return lax.ppermute(x, 'dp', pairs)]
    ppermute x2, waiting for transfers between devices: 6.48 us -> 4.92 us  [to_base(): lax.ppermute(x, 'dp', [(i, (i + k * pieces * CORES) % dp) for i in range(...]
    ppermute x7 -> x6, waiting for transfers between devices: 2.75 us -> 2.66 us  [to_core(): return lax.ppermute(x, 'dp', [(i, i ^ 1) for i in range(dp)])]
  transfers between devices with their start and end apart: 23 -> 22, of which waited for: 13 -> 13; matrix products, arithmetic and copies ran while one was open for 0% -> 0% of each run, Pallas kernels for 22% -> 23%
where the time goes in v7:
time: 77 us; the launch traced here: 76.8 us
  waiting for transfers between devices  28 us (36%)
  starting transfers between devices  24.2 us (31%)
  Pallas kernels  23.5 us (31%)
  between operations  0.81 us (1%)
    ppermute x10, waiting for transfers between devices, to_fsdp(): return lax.ppermute(x, 'fsdp', [(i, i ^ s) for i in range(fsdp)])  16.8 us
    ppermute x10, starting transfers between devices, to_fsdp(): return lax.ppermute(x, 'fsdp', [(i, i ^ s) for i in range(fsdp)])  13.7 us
    pallas_call x2, Pallas kernels, update_step(): pl.pallas_call(body, out_shape=[jax.ShapeDtypeStruct(x.shape, F32) for x...  12 us
    pallas_call x10, Pallas kernels, call(): pl.pallas_call(body, out_shape=out_shape, grid_spec=pltpu.PrefetchScalarG...  9.29 us
    ppermute x4, starting transfers between devices, to_piece(): return lax.ppermute(x, 'dp', pairs)  5.27 us
    ppermute x2, waiting for transfers between devices, to_base(): lax.ppermute(x, 'dp', [(i, (i + k * pieces * CORES) % dp) for i in range(...  4.92 us
    ppermute x2, starting transfers between devices, to_base(): lax.ppermute(x, 'dp', [(i, (i + k * pieces * CORES) % dp) for i in range(...  4.09 us
    ppermute x4, waiting for transfers between devices, to_piece(): return lax.ppermute(x, 'dp', pairs)  3.69 us
  transfers between devices with their start and end apart: 22, of which 13 were waited for; matrix products, arithmetic and copies ran while one was open for 0% of the time, Pallas kernels for 23%

profile of v7, /device:TPU:0, one launch (start us, length us, event | category | flops | bytes accessed | tf_op | source)
XLA Modules:
  0.0 76.8 jit_solution(12877049435156434915)
XLA Ops:
  1.2 1.5 %cut_out.1 = (bf16[1024,256]{1,0:T(8,128)(2,1)S(1)}, bf16[256,1536]{1,0:T(8,128)(2,1)S(1)}) custom-call(s32[1]{0:T(128)} %bitcast.fsdp_ref, s32[1]{0:T(128)} %bitcast.1.core_ref, s32[1]{0:T(128)} %bitcast.2.piece_ref, bf16[1024,512]{1,0:T(8,128)(2,1)} %proj_ref.1, bf16[256,4096]{1,0:T(8,128)(2,1)} %refs_1_.3), custom_call_target="tpu_custom_call" | custom-call | flops 1150000000 | tf_op jit(solution)/shard_map/cut_out/pallas_call | solution.py:71
  2.6 2.6 %collective-permute-start.3 = (bf16[1024,256]{1,0:T(8,128)(2,1)S(1)}, bf16[1024,256]{1,0:T(8,128)(2,1)S(1)}, u32[]{:S(2)}, u32[]{:S(2)}) collective-permute-start(bf16[1024,256]{1,0:T(8,128)(2,1)S(1)} %get-tuple-element.41.refs_2_.refs_0_), channel_id=1, source_target_pairs={{0,1},{1,0},{2,3},{3,2},{4,5},{5,4},{6,7},{7,6},{8,9},{9,8},{10,11... | collective-permute-start | bytes 1572872 | tf_op jit(solution)/shard_map/ppermute | solution.py:378
  5.3 1.5 %collective-permute-start.1 = (bf16[1024,256]{1,0:T(8,128)(2,1)S(1)}, bf16[1024,256]{1,0:T(8,128)(2,1)S(1)}, u32[]{:S(2)}, u32[]{:S(2)}) collective-permute-start(bf16[1024,256]{1,0:T(8,128)(2,1)S(1)} %get-tuple-element.41.refs_2_.refs_0_), channel_id=1, source_target_pairs={{0,2},{1,3},{2,0},{3,1},{4,6},{5,7},{6,4},{7,5},{8,10},{9,11},{10,... | collective-permute-start | bytes 1572872 | tf_op jit(solution)/shard_map/ppermute | solution.py:378
  6.8 1.6 %collective-permute-start.8 = (bf16[256,1536]{1,0:T(8,128)(2,1)S(1)}, bf16[256,1536]{1,0:T(8,128)(2,1)S(1)}, u32[]{:S(2)}, u32[]{:S(2)}) collective-permute-start(bf16[256,1536]{1,0:T(8,128)(2,1)S(1)} %get-tuple-element.32), channel_id=1, source_target_pairs={{0,8},{4,12},{8,0},{12,4},{16,24},{20,28},{24,16},{28,20},{1,9},{5... | collective-permute-start | bytes 2359304 | tf_op jit(solution)/shard_map/ppermute | solution.py:386
  8.4 9.3 %collective-permute-done.3.refs_2_.refs_1_ = bf16[1024,256]{1,0:T(8,128)(2,1)S(1)} collective-permute-done((bf16[1024,256]{1,0:T(8,128)(2,1)S(1)}, bf16[1024,256]{1,0:T(8,128)(2,1)S(1)}, u32[]{:S(2)}, u32[]{:S(2)}) %collective-permute-start.3) | collective-permute-done | bytes 524320 | tf_op jit(solution)/shard_map/ppermute | solution.py:378
  17.8 1.8 %collective-permute-start.4 = (bf16[512,256]{1,0:T(8,128)(2,1)S(1)}, bf16[512,256]{1,0:T(8,128)(2,1)S(1)}, u32[]{:S(2)}, u32[]{:S(2)}) collective-permute-start(bf16[512,256]{1,0:T(8,128)(2,1)S(1)} %slice.9), channel_id=1, source_target_pairs={{0,2},{1,3},{2,0},{3,1},{4,6},{5,7},{6,4},{7,5},{8,10},{9,11},{10,... | collective-permute-start | bytes 786440 | tf_op jit(solution)/shard_map/ppermute | solution.py:378
  19.7 1.6 %collective-permute-start.2 = (bf16[512,256]{1,0:T(8,128)(2,1)S(1)}, bf16[512,256]{1,0:T(8,128)(2,1)S(1)}, u32[]{:S(2)}, u32[]{:S(2)}) collective-permute-start(bf16[512,256]{1,0:T(8,128)(2,1)S(1)} %slice.8), channel_id=1, source_target_pairs={{0,1},{1,0},{2,3},{3,2},{4,5},{5,4},{6,7},{7,6},{8,9},{9,8},{10,11... | collective-permute-start | bytes 786440 | tf_op jit(solution)/shard_map/ppermute | solution.py:378
  22.2 1.3 %coords_1.1.refs_6_ = f32[512,256]{1,0:T(8,128)S(1)} custom-call(s32[3]{0:T(128)S(1)} %pad_add_fusion.w, bf16[256,4096]{1,0:T(8,128)(2,1)S(1)} %copy-done.3, bf16[256,4096]{1,0:T(8,128)(2,1)S(1)} %collective-permute-done.refs_1_.refs_4_, bf16[1024,256]{1,0:T(8,128)(2,1)S(1)} %collective-permute-done.3.refs_2_.refs_1_, bf16[256,4096]{1,0:T(8,128)(2,1)S(1)} %copy-done.3, ...), custom_call_target="tpu_custom_call" | custom-call | flops 9200000000 | tf_op jit(solution)/shard_map/coords_1/pallas_call | solution.py:31
  23.5 2.5 %collective-permute-done.4.refs_5_.refs_4_ = bf16[512,256]{1,0:T(8,128)(2,1)S(1)} collective-permute-done((bf16[512,256]{1,0:T(8,128)(2,1)S(1)}, bf16[512,256]{1,0:T(8,128)(2,1)S(1)}, u32[]{:S(2)}, u32[]{:S(2)}) %collective-permute-start.4) | collective-permute-done | bytes 262176 | tf_op jit(solution)/shard_map/ppermute | solution.py:378
  25.9 1.4 %collective-permute-done.2.refs_2_.refs_3_ = bf16[512,256]{1,0:T(8,128)(2,1)S(1)} collective-permute-done((bf16[512,256]{1,0:T(8,128)(2,1)S(1)}, bf16[512,256]{1,0:T(8,128)(2,1)S(1)}, u32[]{:S(2)}, u32[]{:S(2)}) %collective-permute-start.2) | collective-permute-done | bytes 262176 | tf_op jit(solution)/shard_map/ppermute | solution.py:378
  28.4 1.6 %collective-permute-start.7 = (bf16[256,512]{1,0:T(8,128)(2,1)S(1)}, bf16[256,512]{1,0:T(8,128)(2,1)S(1)}, u32[]{:S(2)}, u32[]{:S(2)}) collective-permute-start(bf16[256,512]{1,0:T(8,128)(2,1)S(1)} %coords_2.1.refs_0_), channel_id=1, source_target_pairs={{0,8},{4,12},{8,0},{12,4},{16,24},{20,28},{24,16},{28,20},{1,9},{5... | collective-permute-start | bytes 786440 | tf_op jit(solution)/shard_map/ppermute | solution.py:386
  31.4 1.2 %terms_chip.1 = (f32[256,512]{1,0:T(8,128)S(1)}, f32[256,512]{1,0:T(8,128)S(1)}, f32[256,512]{1,0:T(8,128)S(1)}, f32[256,512]{1,0:T(8,128)S(1)}) custom-call(s32[3]{0:T(128)S(1)} %pad_add_fusion.w, bf16[256,512]{1,0:T(8,128)(2,1)S(1)} %coords_2.1.refs_0_, bf16[256,4096]{1,0:T(8,128)(2,1)S(1)} %copy-done.2, ...), custom_call_target="tpu_custom_call" | custom-call | flops 13799999488 | tf_op jit(solution)/shard_map/terms_chip/pallas_call | solution.py:31
  32.6 2.5 %collective-permute-done.7.refs_0_ = bf16[256,512]{1,0:T(8,128)(2,1)S(1)} collective-permute-done((bf16[256,512]{1,0:T(8,128)(2,1)S(1)}, bf16[256,512]{1,0:T(8,128)(2,1)S(1)}, u32[]{:S(2)}, u32[]{:S(2)}) %collective-permute-start.7) | collective-permute-done | bytes 262176 | tf_op jit(solution)/shard_map/ppermute | solution.py:386
  38.9 1.6 %collective-permute-start.6 = (bf16[256,512]{1,0:T(8,128)(2,1)S(1)}, bf16[256,512]{1,0:T(8,128)(2,1)S(1)}, u32[]{:S(2)}, u32[]{:S(2)}) collective-permute-start(bf16[256,512]{1,0:T(8,128)(2,1)S(1)} %terms_pair.1), channel_id=1, source_target_pairs={{0,8},{4,12},{8,0},{12,4},{16,24},{20,28},{24,16},{28,20},{1,9},{5... | collective-permute-start | bytes 786440 | tf_op jit(solution)/shard_map/ppermute | solution.py:386
  41.0 1.2 %collective-permute-done.11.refs_8_.refs_16_ = bf16[128,512]{1,0:T(8,128)(2,1)S(1)} collective-permute-done((bf16[128,512]{1,0:T(8,128)(2,1)S(1)}, bf16[128,512]{1,0:T(8,128)(2,1)S(1)}, u32[]{:S(2)}, u32[]{:S(2)}) %collective-permute-start.11) | collective-permute-done | bytes 131104 | tf_op jit(solution)/shard_map/ppermute | solution.py:378
  44.3 1.5 %collective-permute-start.17 = (bf16[256,256]{1,0:T(8,128)(2,1)S(1)}, bf16[256,256]{1,0:T(8,128)(2,1)S(1)}, u32[]{:S(2)}, u32[]{:S(2)}) collective-permute-start(bf16[256,256]{1,0:T(8,128)(2,1)S(1)} %get-tuple-element.50), channel_id=1, source_target_pairs={{0,2},{1,3},{2,0},{3,1},{4,6},{5,7},{6,4},{7,5},{8,10},{9,11},{10,... | collective-permute-start | bytes 393224 | tf_op jit(solution)/shard_map/ppermute | solution.py:378
  49.8 2.6 %collective-permute-start.18 = (bf16[256,256]{1,0:T(8,128)(2,1)S(1)}, bf16[256,256]{1,0:T(8,128)(2,1)S(1)}, u32[]{:S(2)}, u32[]{:S(2)}) collective-permute-start(bf16[256,256]{1,0:T(8,128)(2,1)S(1)} %terms_0.3), channel_id=1, source_target_pairs={{0,16},{4,20},{8,24},{12,28},{16,0},{20,4},{24,8},{28,12},{1,17},{... | collective-permute-start | bytes 393224 | tf_op jit(solution)/shard_map/ppermute | solution.py:389
  53.1 1.5 %collective-permute-start.15 = (bf16[256,256]{1,0:T(8,128)(2,1)S(1)}, bf16[256,256]{1,0:T(8,128)(2,1)S(1)}, u32[]{:S(2)}, u32[]{:S(2)}) collective-permute-start(bf16[256,256]{1,0:T(8,128)(2,1)S(1)} %terms_0.2), channel_id=1, source_target_pairs={{0,16},{4,20},{8,24},{12,28},{16,0},{20,4},{24,8},{28,12},{1,17},{... | collective-permute-start | bytes 393224 | tf_op jit(solution)/shard_map/ppermute | solution.py:389
  54.5 2.6 %collective-permute-done.18 = bf16[256,256]{1,0:T(8,128)(2,1)S(1)} collective-permute-done((bf16[256,256]{1,0:T(8,128)(2,1)S(1)}, bf16[256,256]{1,0:T(8,128)(2,1)S(1)}, u32[]{:S(2)}, u32[]{:S(2)}) %collective-permute-start.18) | collective-permute-done | bytes 131104 | tf_op jit(solution)/shard_map/ppermute | solution.py:389
  58.1 2.3 %collective-permute-done.15 = bf16[256,256]{1,0:T(8,128)(2,1)S(1)} collective-permute-done((bf16[256,256]{1,0:T(8,128)(2,1)S(1)}, bf16[256,256]{1,0:T(8,128)(2,1)S(1)}, u32[]{:S(2)}, u32[]{:S(2)}) %collective-permute-start.15) | collective-permute-done | bytes 131104 | tf_op jit(solution)/shard_map/ppermute | solution.py:389
  62.1 6.0 %update_step.2 = (f32[1024,512]{1,0:T(8,128)}, f32[1024,512]{1,0:T(8,128)}, f32[4096,1024]{1,0:T(8,128)}) custom-call(s32[3]{0:T(128)S(1)} %pad_add_fusion.w, bf16[256,512]{1,0:T(8,128)(2,1)S(1)} %pad_maximum_fusion.own, bf16[256,512]{1,0:T(8,128)(2,1)S(1)} %collective-permute-done.20.other, bf16[4096,512]{1,0:T(8,128)(2,1)S(1)} %join.1.proj_ref, ...), custom_call_target="tpu_custom_call" | custom-call | flops 6899999744 | tf_op jit(solution)/shard_map/update_step/pallas_call | solution.py:322
  68.1 1.2 %collective-permute-done.19.own = bf16[256,512]{1,0:T(8,128)(2,1)S(1)} collective-permute-done((bf16[256,512]{1,0:T(8,128)(2,1)S(1)}, bf16[256,512]{1,0:T(8,128)(2,1)S(1)}, u32[]{:S(2)}, u32[]{:S(2)}) %collective-permute-start.19) | collective-permute-done | bytes 262176 | tf_op jit(solution)/shard_map/ppermute | solution.py:386
  69.3 1.5 %collective-permute-done.21.other = bf16[256,512]{1,0:T(8,128)(2,1)S(1)} collective-permute-done((bf16[256,512]{1,0:T(8,128)(2,1)S(1)}, bf16[256,512]{1,0:T(8,128)(2,1)S(1)}, u32[]{:S(2)}, u32[]{:S(2)}) %collective-permute-start.21) | collective-permute-done | bytes 262176 | tf_op jit(solution)/shard_map/ppermute | solution.py:375
  70.8 6.0 %update_step.3 = (f32[1024,512]{1,0:T(8,128)}, f32[1024,512]{1,0:T(8,128)}, f32[4096,1024]{1,0:T(8,128)}) custom-call(s32[3]{0:T(128)S(1)} %pad_add_fusion.w, bf16[256,512]{1,0:T(8,128)(2,1)S(1)} %collective-permute-done.19.own, bf16[256,512]{1,0:T(8,128)(2,1)S(1)} %collective-permute-done.21.other, ...), custom_call_target="tpu_custom_call", output_to_operand_aliasing={{0}: (6, {}), {1}: (7, {}), {2}: (8, {})} | custom-call | flops 6899999744 | tf_op jit(solution)/shard_map/update_step/pallas_call | solution.py:322
  (48 shorter events, 17.5 us)
Async XLA Ops:
  0.6 20.6 %collective-permute-start = (bf16[256,4096]{1,0:T(8,128)(2,1)}, bf16[256,4096]{1,0:T(8,128)(2,1)S(1)}, u32[]{:S(2)}, u32[]{:S(2)}) collective-permute-start(bf16[256,4096]{1,0:T(8,128)(2,1)} %refs_3_.4), channel_id=1, source_target_pairs={{0,4},{4,0},{8,12},{12,8},{16,20},{20,16},{24,28},{28,24},{1,5},{5... | collective-permute-start | bytes 6291464 | tf_op jit(solution)/shard_map/ppermute | solution.py:375
  1.1 7.2 %copy-start.2 = (bf16[256,4096]{1,0:T(8,128)(2,1)S(1)}, bf16[256,4096]{1,0:T(8,128)(2,1)}, u32[]{:S(2)}) copy-start(bf16[256,4096]{1,0:T(8,128)(2,1)} %refs_1_.3) | copy-start | bytes 6291460
  1.2 20.1 %copy-start.3 = (bf16[256,4096]{1,0:T(8,128)(2,1)S(1)}, bf16[256,4096]{1,0:T(8,128)(2,1)}, u32[]{:S(2)}) copy-start(bf16[256,4096]{1,0:T(8,128)(2,1)} %refs_3_.4) | copy-start | bytes 6291460
  2.6 15.2 %collective-permute-start.3 = (bf16[1024,256]{1,0:T(8,128)(2,1)S(1)}, bf16[1024,256]{1,0:T(8,128)(2,1)S(1)}, u32[]{:S(2)}, u32[]{:S(2)}) collective-permute-start(bf16[1024,256]{1,0:T(8,128)(2,1)S(1)} %get-tuple-element.41.refs_2_.refs_0_), channel_id=1, source_target_pairs={{0,1},{1,0},{2,3},{3,2},{4,5},{5,4},{6,7},{7,6},{8,9},{9,8},{10,11... | collective-permute-start | bytes 1572872 | tf_op jit(solution)/shard_map/ppermute | solution.py:378
  5.3 14.4 %collective-permute-start.1 = (bf16[1024,256]{1,0:T(8,128)(2,1)S(1)}, bf16[1024,256]{1,0:T(8,128)(2,1)S(1)}, u32[]{:S(2)}, u32[]{:S(2)}) collective-permute-start(bf16[1024,256]{1,0:T(8,128)(2,1)S(1)} %get-tuple-element.41.refs_2_.refs_0_), channel_id=1, source_target_pairs={{0,2},{1,3},{2,0},{3,1},{4,6},{5,7},{6,4},{7,5},{8,10},{9,11},{10,... | collective-permute-start | bytes 1572872 | tf_op jit(solution)/shard_map/ppermute | solution.py:378
  6.8 23.3 %collective-permute-start.8 = (bf16[256,1536]{1,0:T(8,128)(2,1)S(1)}, bf16[256,1536]{1,0:T(8,128)(2,1)S(1)}, u32[]{:S(2)}, u32[]{:S(2)}) collective-permute-start(bf16[256,1536]{1,0:T(8,128)(2,1)S(1)} %get-tuple-element.32), channel_id=1, source_target_pairs={{0,8},{4,12},{8,0},{12,4},{16,24},{20,28},{24,16},{28,20},{1,9},{5... | collective-permute-start | bytes 2359304 | tf_op jit(solution)/shard_map/ppermute | solution.py:386
  8.4 23.0 %collective-permute-start.5 = (bf16[256,4096]{1,0:T(8,128)(2,1)S(1)}, bf16[256,4096]{1,0:T(8,128)(2,1)S(1)}, u32[]{:S(2)}, u32[]{:S(2)}) collective-permute-start(bf16[256,4096]{1,0:T(8,128)(2,1)S(1)} %copy-done.2), channel_id=1, source_target_pairs={{0,4},{4,0},{8,12},{12,8},{16,20},{20,16},{24,28},{28,24},{1,5},{5... | collective-permute-start | bytes 6291464 | tf_op jit(solution)/shard_map/ppermute | solution.py:375
  17.8 8.1 %collective-permute-start.4 = (bf16[512,256]{1,0:T(8,128)(2,1)S(1)}, bf16[512,256]{1,0:T(8,128)(2,1)S(1)}, u32[]{:S(2)}, u32[]{:S(2)}) collective-permute-start(bf16[512,256]{1,0:T(8,128)(2,1)S(1)} %slice.9), channel_id=1, source_target_pairs={{0,2},{1,3},{2,0},{3,1},{4,6},{5,7},{6,4},{7,5},{8,10},{9,11},{10,... | collective-permute-start | bytes 786440 | tf_op jit(solution)/shard_map/ppermute | solution.py:378
  19.7 7.6 %collective-permute-start.2 = (bf16[512,256]{1,0:T(8,128)(2,1)S(1)}, bf16[512,256]{1,0:T(8,128)(2,1)S(1)}, u32[]{:S(2)}, u32[]{:S(2)}) collective-permute-start(bf16[512,256]{1,0:T(8,128)(2,1)S(1)} %slice.8), channel_id=1, source_target_pairs={{0,1},{1,0},{2,3},{3,2},{4,5},{5,4},{6,7},{7,6},{8,9},{9,8},{10,11... | collective-permute-start | bytes 786440 | tf_op jit(solution)/shard_map/ppermute | solution.py:378
  28.4 6.7 %collective-permute-start.7 = (bf16[256,512]{1,0:T(8,128)(2,1)S(1)}, bf16[256,512]{1,0:T(8,128)(2,1)S(1)}, u32[]{:S(2)}, u32[]{:S(2)}) collective-permute-start(bf16[256,512]{1,0:T(8,128)(2,1)S(1)} %coords_2.1.refs_0_), channel_id=1, source_target_pairs={{0,8},{4,12},{8,0},{12,4},{16,24},{20,28},{24,16},{28,20},{1,9},{5... | collective-permute-start | bytes 786440 | tf_op jit(solution)/shard_map/ppermute | solution.py:386
  30.0 5.1 %collective-permute-start.9 = (bf16[256,1536]{1,0:T(8,128)(2,1)S(1)}, bf16[256,1536]{1,0:T(8,128)(2,1)S(1)}, u32[]{:S(2)}, u32[]{:S(2)}) collective-permute-start(bf16[256,1536]{1,0:T(8,128)(2,1)S(1)} %collective-permute-done.8.refs_1_.refs_5_.refs_9_.refs_13_), channel_id=1, source_target_pairs={{0,4},{4,0},{8,12},{12,8},{16,20},{20,16},{24,28},{28,24},{1,5},{5... | collective-permute-start | bytes 2359304 | tf_op jit(solution)/shard_map/ppermute | solution.py:375
  30.8 26.4 %collective-permute-start.14 = (bf16[4096,256]{1,0:T(8,128)(2,1)S(1)}, bf16[4096,256]{1,0:T(8,128)(2,1)S(1)}, u32[]{:S(2)}, u32[]{:S(2)}) collective-permute-start(bf16[4096,256]{1,0:T(8,128)(2,1)S(1)} %assemble.1.own_ref), channel_id=1, source_target_pairs={{0,4},{4,0},{8,12},{12,8},{16,20},{20,16},{24,28},{28,24},{1,5},{5... | collective-permute-start | bytes 6291464 | tf_op jit(solution)/shard_map/ppermute | solution.py:375
  36.0 5.0 %collective-permute-start.10 = (bf16[128,512]{1,0:T(8,128)(2,1)S(1)}, bf16[128,512]{1,0:T(8,128)(2,1)S(1)}, u32[]{:S(2)}, u32[]{:S(2)}) collective-permute-start(bf16[128,512]{1,0:T(8,128)(2,1)S(1)} %get-tuple-element.36), channel_id=1, source_target_pairs={{0,2},{1,3},{2,0},{3,1},{4,6},{5,7},{6,4},{7,5},{8,10},{9,11},{10,... | collective-permute-start | bytes 393224 | tf_op jit(solution)/shard_map/ppermute | solution.py:378
  37.1 5.1 %collective-permute-start.11 = (bf16[128,512]{1,0:T(8,128)(2,1)S(1)}, bf16[128,512]{1,0:T(8,128)(2,1)S(1)}, u32[]{:S(2)}, u32[]{:S(2)}) collective-permute-start(bf16[128,512]{1,0:T(8,128)(2,1)S(1)} %get-tuple-element.38), channel_id=1, source_target_pairs={{0,1},{1,0},{2,3},{3,2},{4,5},{5,4},{6,7},{7,6},{8,9},{9,8},{10,11... | collective-permute-start | bytes 393224 | tf_op jit(solution)/shard_map/ppermute | solution.py:378
  38.9 7.4 %collective-permute-start.6 = (bf16[256,512]{1,0:T(8,128)(2,1)S(1)}, bf16[256,512]{1,0:T(8,128)(2,1)S(1)}, u32[]{:S(2)}, u32[]{:S(2)}) collective-permute-start(bf16[256,512]{1,0:T(8,128)(2,1)S(1)} %terms_pair.1), channel_id=1, source_target_pairs={{0,8},{4,12},{8,0},{12,4},{16,24},{20,28},{24,16},{28,20},{1,9},{5... | collective-permute-start | bytes 786440 | tf_op jit(solution)/shard_map/ppermute | solution.py:386
  43.2 5.0 %collective-permute-start.16 = (bf16[256,256]{1,0:T(8,128)(2,1)S(1)}, bf16[256,256]{1,0:T(8,128)(2,1)S(1)}, u32[]{:S(2)}, u32[]{:S(2)}) collective-permute-start(bf16[256,256]{1,0:T(8,128)(2,1)S(1)} %get-tuple-element.49), channel_id=1, source_target_pairs={{0,1},{1,0},{2,3},{3,2},{4,5},{5,4},{6,7},{7,6},{8,9},{9,8},{10,11... | collective-permute-start | bytes 393224 | tf_op jit(solution)/shard_map/ppermute | solution.py:378
  44.3 5.0 %collective-permute-start.17 = (bf16[256,256]{1,0:T(8,128)(2,1)S(1)}, bf16[256,256]{1,0:T(8,128)(2,1)S(1)}, u32[]{:S(2)}, u32[]{:S(2)}) collective-permute-start(bf16[256,256]{1,0:T(8,128)(2,1)S(1)} %get-tuple-element.50), channel_id=1, source_target_pairs={{0,2},{1,3},{2,0},{3,1},{4,6},{5,7},{6,4},{7,5},{8,10},{9,11},{10,... | collective-permute-start | bytes 393224 | tf_op jit(solution)/shard_map/ppermute | solution.py:378
  45.8 6.7 %collective-permute-start.12 = (bf16[256,256]{1,0:T(8,128)(2,1)S(1)}, bf16[256,256]{1,0:T(8,128)(2,1)S(1)}, u32[]{:S(2)}, u32[]{:S(2)}) collective-permute-start(bf16[256,256]{1,0:T(8,128)(2,1)S(1)} %get-tuple-element.39), channel_id=1, source_target_pairs={{0,1},{1,0},{2,3},{3,2},{4,5},{5,4},{6,7},{7,6},{8,9},{9,8},{10,11... | collective-permute-start | bytes 393224 | tf_op jit(solution)/shard_map/ppermute | solution.py:378
  46.3 6.2 %collective-permute-start.13 = (bf16[256,256]{1,0:T(8,128)(2,1)S(1)}, bf16[256,256]{1,0:T(8,128)(2,1)S(1)}, u32[]{:S(2)}, u32[]{:S(2)}) collective-permute-start(bf16[256,256]{1,0:T(8,128)(2,1)S(1)} %get-tuple-element.40), channel_id=1, source_target_pairs={{0,2},{1,3},{2,0},{3,1},{4,6},{5,7},{6,4},{7,5},{8,10},{9,11},{10,... | collective-permute-start | bytes 393224 | tf_op jit(solution)/shard_map/ppermute | solution.py:378
  49.8 7.3 %collective-permute-start.18 = (bf16[256,256]{1,0:T(8,128)(2,1)S(1)}, bf16[256,256]{1,0:T(8,128)(2,1)S(1)}, u32[]{:S(2)}, u32[]{:S(2)}) collective-permute-start(bf16[256,256]{1,0:T(8,128)(2,1)S(1)} %terms_0.3), channel_id=1, source_target_pairs={{0,16},{4,20},{8,24},{12,28},{16,0},{20,4},{24,8},{28,12},{1,17},{... | collective-permute-start | bytes 393224 | tf_op jit(solution)/shard_map/ppermute | solution.py:389
  53.1 7.3 %collective-permute-start.15 = (bf16[256,256]{1,0:T(8,128)(2,1)S(1)}, bf16[256,256]{1,0:T(8,128)(2,1)S(1)}, u32[]{:S(2)}, u32[]{:S(2)}) collective-permute-start(bf16[256,256]{1,0:T(8,128)(2,1)S(1)} %terms_0.2), channel_id=1, source_target_pairs={{0,16},{4,20},{8,24},{12,28},{16,0},{20,4},{24,8},{28,12},{1,17},{... | collective-permute-start | bytes 393224 | tf_op jit(solution)/shard_map/ppermute | solution.py:389
  60.5 1.6 %collective-permute-start.20 = (bf16[256,512]{1,0:T(8,128)(2,1)S(1)}, bf16[256,512]{1,0:T(8,128)(2,1)S(1)}, u32[]{:S(2)}, u32[]{:S(2)}) collective-permute-start(bf16[256,512]{1,0:T(8,128)(2,1)S(1)} %pad_maximum_fusion.own), channel_id=1, source_target_pairs={{0,4},{4,0},{8,12},{12,8},{16,20},{20,16},{24,28},{28,24},{1,5},{5... | collective-permute-start | bytes 786440 | tf_op jit(solution)/shard_map/ppermute | solution.py:375
  60.6 8.7 %collective-permute-start.19 = (bf16[256,512]{1,0:T(8,128)(2,1)S(1)}, bf16[256,512]{1,0:T(8,128)(2,1)S(1)}, u32[]{:S(2)}, u32[]{:S(2)}) collective-permute-start(bf16[256,512]{1,0:T(8,128)(2,1)S(1)} %pad_maximum_fusion.own), channel_id=1, source_target_pairs={{0,8},{4,12},{8,0},{12,4},{16,24},{20,28},{24,16},{28,20},{1,9},{5... | collective-permute-start | bytes 786440 | tf_op jit(solution)/shard_map/ppermute | solution.py:386
  69.3 1.5 %collective-permute-start.21 = (bf16[256,512]{1,0:T(8,128)(2,1)S(1)}, bf16[256,512]{1,0:T(8,128)(2,1)S(1)}, u32[]{:S(2)}, u32[]{:S(2)}) collective-permute-start(bf16[256,512]{1,0:T(8,128)(2,1)S(1)} %collective-permute-done.19.own), channel_id=1, source_target_pairs={{0,4},{4,0},{8,12},{12,8},{16,20},{20,16},{24,28},{28,24},{1,5},{5... | collective-permute-start | bytes 786440 | tf_op jit(solution)/shard_map/ppermute | solution.py:375
  (2 other events, 9.7 us)

commit v8 on v6

--- a/solution.py
+++ b/solution.py
@@ -258,7 +258,7 @@
     rank = CORES * half
     features = moments[0].shape[0]
     width = proj.shape[0]
-    rows = min(512, width)
+    rows = min(256, width)
     steps = width // rows
     some = 16
 
@@ -299,12 +299,12 @@
             second_new = 0.999 * second_ref[at, :] + 0.001 * grad_low * grad_low
             moment[0, at, :] = first_new
             moment[1, at, :] = second_new
-            ratio[at, :] = (
-                (first_new * first_scale) / (jnp.sqrt(second_new * second_scale) + 1e-08)
-            ).astype(BF16)
+            scaled = second_new * second_scale
+            root = scaled * lax.rsqrt(scaled)
+            ratio[at, :] = ((first_new * first_scale) / (root + 1e-08)).astype(BF16)
             return 0
 
-        lax.fori_loop(0, span // some, adam, 0, unroll=2)
+        lax.fori_loop(0, span // some, adam, 0, unroll=8)
         for copy in stores:
             copy.start()
         direction[...] = ratio[...].T
@@ -474,11 +474,9 @@
     proj = join(where, own_proj, after(other_proj, total))
     moments = (first_moment, second_moment)
     parts[0] = [after(x, proj) for x in parts[0]]
-    sums, others = [], []
-    for x in parts:
-        sums.append(add_up([after(y, *others) for y in x]))
-        others.append(to_core(sums[-1]))
-    mine = jnp.concatenate(sums, axis=1)
+    sums_of = [add_up(x) for x in parts]
+    mine = jnp.concatenate(sums_of, axis=1)
+    others = [to_core(x) for x in sums_of]
     outputs = update_step(where, 0, pieces, (mine, *others), proj, moments, None)
     if pieces > 1:
         others = to_piece(mine, 1)

time: 81.2 us -> 77.2 us (0.951)
  waiting for transfers between devices: 31.8 us -> 25.4 us
  starting transfers between devices: 24.3 us -> 27.3 us
    ppermute x4, waiting for transfers between devices: 5.78 us -> 2.49 us  [to_piece(): return lax.ppermute(x, 'dp', pairs)]
    ppermute x2, waiting for transfers between devices: 6.48 us -> 3.89 us  [to_base(): lax.ppermute(x, 'dp', [(i, (i + k * pieces * CORES) % dp) for i in range(...]
    ppermute x4, starting transfers between devices: 5.64 us -> 7.53 us  [to_piece(): return lax.ppermute(x, 'dp', pairs)]
    ppermute x7, starting transfers between devices: 1.04 us -> 1.99 us  [to_core(): return lax.ppermute(x, 'dp', [(i, i ^ 1) for i in range(dp)])]
  transfers between devices with their start and end apart: 23 -> 23, of which waited for: 13 -> 13; matrix products, arithmetic and copies ran while one was open for 0% -> 0% of each run, Pallas kernels for 22% -> 23%
where the time goes in v8:
time: 77.2 us; the launch traced here: 77.1 us
  starting transfers between devices  27.3 us (35%)
  waiting for transfers between devices  25.4 us (33%)
  Pallas kernels  23.3 us (30%)
  between operations  0.81 us (1%)
    ppermute x10, waiting for transfers between devices, to_fsdp(): return lax.ppermute(x, 'fsdp', [(i, i ^ s) for i in range(fsdp)])  16.8 us
    ppermute x10, starting transfers between devices, to_fsdp(): return lax.ppermute(x, 'fsdp', [(i, i ^ s) for i in range(fsdp)])  13.7 us
    pallas_call x2, Pallas kernels, update_step(): pl.pallas_call(body, out_shape=[jax.ShapeDtypeStruct(x.shape, F32) for x...  11.8 us
    pallas_call x10, Pallas kernels, call(): pl.pallas_call(body, out_shape=out_shape, grid_spec=pltpu.PrefetchScalarG...  9.29 us
    ppermute x4, starting transfers between devices, to_piece(): return lax.ppermute(x, 'dp', pairs)  7.53 us
    ppermute x2, starting transfers between devices, to_base(): lax.ppermute(x, 'dp', [(i, (i + k * pieces * CORES) % dp) for i in range(...  4.09 us
    ppermute x2, waiting for transfers between devices, to_base(): lax.ppermute(x, 'dp', [(i, (i + k * pieces * CORES) % dp) for i in range(...  3.89 us
    ppermute x4, waiting for transfers between devices, to_piece(): return lax.ppermute(x, 'dp', pairs)  2.49 us
  transfers between devices with their start and end apart: 23, of which 13 were waited for; matrix products, arithmetic and copies ran while one was open for 0% of the time, Pallas kernels for 23%

profile of v8, /device:TPU:0, one launch (start us, length us, event | category | flops | bytes accessed | tf_op | source)
XLA Modules:
  0.0 77.1 jit_solution(12767019904390651791)
XLA Ops:
  1.2 1.5 %cut_out.1 = (bf16[1024,256]{1,0:T(8,128)(2,1)S(1)}, bf16[256,1536]{1,0:T(8,128)(2,1)S(1)}) custom-call(s32[1]{0:T(128)} %bitcast.fsdp_ref, s32[1]{0:T(128)} %bitcast.1.core_ref, s32[1]{0:T(128)} %bitcast.2.piece_ref, bf16[1024,512]{1,0:T(8,128)(2,1)} %proj_ref.1, bf16[256,4096]{1,0:T(8,128)(2,1)} %refs_1_.3), custom_call_target="tpu_custom_call" | custom-call | flops 1150000000 | tf_op jit(solution)/shard_map/cut_out/pallas_call | solution.py:71
  2.6 2.6 %collective-permute-start.3 = (bf16[1024,256]{1,0:T(8,128)(2,1)S(1)}, bf16[1024,256]{1,0:T(8,128)(2,1)S(1)}, u32[]{:S(2)}, u32[]{:S(2)}) collective-permute-start(bf16[1024,256]{1,0:T(8,128)(2,1)S(1)} %get-tuple-element.41.refs_2_.refs_0_), channel_id=1, source_target_pairs={{0,1},{1,0},{2,3},{3,2},{4,5},{5,4},{6,7},{7,6},{8,9},{9,8},{10,11... | collective-permute-start | bytes 1572872 | tf_op jit(solution)/shard_map/ppermute | solution.py:383
  5.3 1.5 %collective-permute-start.1 = (bf16[1024,256]{1,0:T(8,128)(2,1)S(1)}, bf16[1024,256]{1,0:T(8,128)(2,1)S(1)}, u32[]{:S(2)}, u32[]{:S(2)}) collective-permute-start(bf16[1024,256]{1,0:T(8,128)(2,1)S(1)} %get-tuple-element.41.refs_2_.refs_0_), channel_id=1, source_target_pairs={{0,2},{1,3},{2,0},{3,1},{4,6},{5,7},{6,4},{7,5},{8,10},{9,11},{10,... | collective-permute-start | bytes 1572872 | tf_op jit(solution)/shard_map/ppermute | solution.py:383
  6.8 1.6 %collective-permute-start.8 = (bf16[256,1536]{1,0:T(8,128)(2,1)S(1)}, bf16[256,1536]{1,0:T(8,128)(2,1)S(1)}, u32[]{:S(2)}, u32[]{:S(2)}) collective-permute-start(bf16[256,1536]{1,0:T(8,128)(2,1)S(1)} %get-tuple-element.32), channel_id=1, source_target_pairs={{0,8},{4,12},{8,0},{12,4},{16,24},{20,28},{24,16},{28,20},{1,9},{5... | collective-permute-start | bytes 2359304 | tf_op jit(solution)/shard_map/ppermute | solution.py:391
  8.4 9.3 %collective-permute-done.3.refs_2_.refs_1_ = bf16[1024,256]{1,0:T(8,128)(2,1)S(1)} collective-permute-done((bf16[1024,256]{1,0:T(8,128)(2,1)S(1)}, bf16[1024,256]{1,0:T(8,128)(2,1)S(1)}, u32[]{:S(2)}, u32[]{:S(2)}) %collective-permute-start.3) | collective-permute-done | bytes 524320 | tf_op jit(solution)/shard_map/ppermute | solution.py:383
  17.8 1.8 %collective-permute-start.4 = (bf16[512,256]{1,0:T(8,128)(2,1)S(1)}, bf16[512,256]{1,0:T(8,128)(2,1)S(1)}, u32[]{:S(2)}, u32[]{:S(2)}) collective-permute-start(bf16[512,256]{1,0:T(8,128)(2,1)S(1)} %slice.9), channel_id=1, source_target_pairs={{0,2},{1,3},{2,0},{3,1},{4,6},{5,7},{6,4},{7,5},{8,10},{9,11},{10,... | collective-permute-start | bytes 786440 | tf_op jit(solution)/shard_map/ppermute | solution.py:383
  19.7 1.6 %collective-permute-start.2 = (bf16[512,256]{1,0:T(8,128)(2,1)S(1)}, bf16[512,256]{1,0:T(8,128)(2,1)S(1)}, u32[]{:S(2)}, u32[]{:S(2)}) collective-permute-start(bf16[512,256]{1,0:T(8,128)(2,1)S(1)} %slice.8), channel_id=1, source_target_pairs={{0,1},{1,0},{2,3},{3,2},{4,5},{5,4},{6,7},{7,6},{8,9},{9,8},{10,11... | collective-permute-start | bytes 786440 | tf_op jit(solution)/shard_map/ppermute | solution.py:383
  22.2 1.3 %coords_1.1.refs_6_ = f32[512,256]{1,0:T(8,128)S(1)} custom-call(s32[3]{0:T(128)S(1)} %pad_add_fusion.w, bf16[256,4096]{1,0:T(8,128)(2,1)S(1)} %copy-done.3, bf16[256,4096]{1,0:T(8,128)(2,1)S(1)} %collective-permute-done.refs_1_.refs_4_, bf16[1024,256]{1,0:T(8,128)(2,1)S(1)} %collective-permute-done.3.refs_2_.refs_1_, bf16[256,4096]{1,0:T(8,128)(2,1)S(1)} %copy-done.3, ...), custom_call_target="tpu_custom_call" | custom-call | flops 9200000000 | tf_op jit(solution)/shard_map/coords_1/pallas_call | solution.py:31
  23.5 2.5 %collective-permute-done.4.refs_5_.refs_4_ = bf16[512,256]{1,0:T(8,128)(2,1)S(1)} collective-permute-done((bf16[512,256]{1,0:T(8,128)(2,1)S(1)}, bf16[512,256]{1,0:T(8,128)(2,1)S(1)}, u32[]{:S(2)}, u32[]{:S(2)}) %collective-permute-start.4) | collective-permute-done | bytes 262176 | tf_op jit(solution)/shard_map/ppermute | solution.py:383
  25.9 1.4 %collective-permute-done.2.refs_2_.refs_3_ = bf16[512,256]{1,0:T(8,128)(2,1)S(1)} collective-permute-done((bf16[512,256]{1,0:T(8,128)(2,1)S(1)}, bf16[512,256]{1,0:T(8,128)(2,1)S(1)}, u32[]{:S(2)}, u32[]{:S(2)}) %collective-permute-start.2) | collective-permute-done | bytes 262176 | tf_op jit(solution)/shard_map/ppermute | solution.py:383
  28.4 1.6 %collective-permute-start.7 = (bf16[256,512]{1,0:T(8,128)(2,1)S(1)}, bf16[256,512]{1,0:T(8,128)(2,1)S(1)}, u32[]{:S(2)}, u32[]{:S(2)}) collective-permute-start(bf16[256,512]{1,0:T(8,128)(2,1)S(1)} %coords_2.1.refs_0_), channel_id=1, source_target_pairs={{0,8},{4,12},{8,0},{12,4},{16,24},{20,28},{24,16},{28,20},{1,9},{5... | collective-permute-start | bytes 786440 | tf_op jit(solution)/shard_map/ppermute | solution.py:391
  31.4 1.2 %terms_chip.1 = (f32[256,512]{1,0:T(8,128)S(1)}, f32[256,512]{1,0:T(8,128)S(1)}, f32[256,512]{1,0:T(8,128)S(1)}, f32[256,512]{1,0:T(8,128)S(1)}) custom-call(s32[3]{0:T(128)S(1)} %pad_add_fusion.w, bf16[256,512]{1,0:T(8,128)(2,1)S(1)} %coords_2.1.refs_0_, bf16[256,4096]{1,0:T(8,128)(2,1)S(1)} %copy-done.2, ...), custom_call_target="tpu_custom_call" | custom-call | flops 13799999488 | tf_op jit(solution)/shard_map/terms_chip/pallas_call | solution.py:31
  32.6 2.5 %collective-permute-done.7.refs_0_ = bf16[256,512]{1,0:T(8,128)(2,1)S(1)} collective-permute-done((bf16[256,512]{1,0:T(8,128)(2,1)S(1)}, bf16[256,512]{1,0:T(8,128)(2,1)S(1)}, u32[]{:S(2)}, u32[]{:S(2)}) %collective-permute-start.7) | collective-permute-done | bytes 262176 | tf_op jit(solution)/shard_map/ppermute | solution.py:391
  38.9 1.6 %collective-permute-start.6 = (bf16[256,512]{1,0:T(8,128)(2,1)S(1)}, bf16[256,512]{1,0:T(8,128)(2,1)S(1)}, u32[]{:S(2)}, u32[]{:S(2)}) collective-permute-start(bf16[256,512]{1,0:T(8,128)(2,1)S(1)} %terms_pair.1), channel_id=1, source_target_pairs={{0,8},{4,12},{8,0},{12,4},{16,24},{20,28},{24,16},{28,20},{1,9},{5... | collective-permute-start | bytes 786440 | tf_op jit(solution)/shard_map/ppermute | solution.py:391
  41.0 1.2 %collective-permute-done.11.refs_8_.refs_16_ = bf16[128,512]{1,0:T(8,128)(2,1)S(1)} collective-permute-done((bf16[128,512]{1,0:T(8,128)(2,1)S(1)}, bf16[128,512]{1,0:T(8,128)(2,1)S(1)}, u32[]{:S(2)}, u32[]{:S(2)}) %collective-permute-start.11) | collective-permute-done | bytes 131104 | tf_op jit(solution)/shard_map/ppermute | solution.py:383
  44.3 1.5 %collective-permute-start.17 = (bf16[256,256]{1,0:T(8,128)(2,1)S(1)}, bf16[256,256]{1,0:T(8,128)(2,1)S(1)}, u32[]{:S(2)}, u32[]{:S(2)}) collective-permute-start(bf16[256,256]{1,0:T(8,128)(2,1)S(1)} %get-tuple-element.50), channel_id=1, source_target_pairs={{0,2},{1,3},{2,0},{3,1},{4,6},{5,7},{6,4},{7,5},{8,10},{9,11},{10,... | collective-permute-start | bytes 393224 | tf_op jit(solution)/shard_map/ppermute | solution.py:383
  49.8 2.6 %collective-permute-start.18 = (bf16[256,256]{1,0:T(8,128)(2,1)S(1)}, bf16[256,256]{1,0:T(8,128)(2,1)S(1)}, u32[]{:S(2)}, u32[]{:S(2)}) collective-permute-start(bf16[256,256]{1,0:T(8,128)(2,1)S(1)} %terms_0.3), channel_id=1, source_target_pairs={{0,16},{4,20},{8,24},{12,28},{16,0},{20,4},{24,8},{28,12},{1,17},{... | collective-permute-start | bytes 393224 | tf_op jit(solution)/shard_map/ppermute | solution.py:394
  53.1 1.5 %collective-permute-start.15 = (bf16[256,256]{1,0:T(8,128)(2,1)S(1)}, bf16[256,256]{1,0:T(8,128)(2,1)S(1)}, u32[]{:S(2)}, u32[]{:S(2)}) collective-permute-start(bf16[256,256]{1,0:T(8,128)(2,1)S(1)} %terms_0.2), channel_id=1, source_target_pairs={{0,16},{4,20},{8,24},{12,28},{16,0},{20,4},{24,8},{28,12},{1,17},{... | collective-permute-start | bytes 393224 | tf_op jit(solution)/shard_map/ppermute | solution.py:394
  54.5 2.7 %collective-permute-done.18 = bf16[256,256]{1,0:T(8,128)(2,1)S(1)} collective-permute-done((bf16[256,256]{1,0:T(8,128)(2,1)S(1)}, bf16[256,256]{1,0:T(8,128)(2,1)S(1)}, u32[]{:S(2)}, u32[]{:S(2)}) %collective-permute-start.18) | collective-permute-done | bytes 131104 | tf_op jit(solution)/shard_map/ppermute | solution.py:394
  58.2 1.2 %collective-permute-done.15 = bf16[256,256]{1,0:T(8,128)(2,1)S(1)} collective-permute-done((bf16[256,256]{1,0:T(8,128)(2,1)S(1)}, bf16[256,256]{1,0:T(8,128)(2,1)S(1)}, u32[]{:S(2)}, u32[]{:S(2)}) %collective-permute-start.15) | collective-permute-done | bytes 131104 | tf_op jit(solution)/shard_map/ppermute | solution.py:394
  59.5 2.7 %collective-permute-start.19 = (bf16[256,512]{1,0:T(8,128)(2,1)S(1)}, bf16[256,512]{1,0:T(8,128)(2,1)S(1)}, u32[]{:S(2)}, u32[]{:S(2)}) collective-permute-start(bf16[256,512]{1,0:T(8,128)(2,1)S(1)} %pad_maximum_fusion.own), channel_id=1, source_target_pairs={{0,8},{4,12},{8,0},{12,4},{16,24},{20,28},{24,16},{28,20},{1,9},{5... | collective-permute-start | bytes 786440 | tf_op jit(solution)/shard_map/ppermute | solution.py:391
  63.7 5.9 %update_step.2 = (f32[1024,512]{1,0:T(8,128)}, f32[1024,512]{1,0:T(8,128)}, f32[4096,1024]{1,0:T(8,128)}) custom-call(s32[3]{0:T(128)S(1)} %pad_add_fusion.w, bf16[256,512]{1,0:T(8,128)(2,1)S(1)} %pad_maximum_fusion.own, bf16[256,256]{1,0:T(8,128)(2,1)S(1)} %collective-permute-done.20.refs_0_, bf16[256,256]{1,0:T(8,128)(2,1)S(1)} %collective-permute-done.21.refs_1_, ...), custom_call_target="tpu_custom_call" | custom-call | flops 575000000 | tf_op jit(solution)/shard_map/update_step/pallas_call | solution.py:327
  70.0 1.2 %collective-permute-done.22.refs_0_ = bf16[256,512]{1,0:T(8,128)(2,1)S(1)} collective-permute-done((bf16[256,512]{1,0:T(8,128)(2,1)S(1)}, bf16[256,512]{1,0:T(8,128)(2,1)S(1)}, u32[]{:S(2)}, u32[]{:S(2)}) %collective-permute-start.22) | collective-permute-done | bytes 262176 | tf_op jit(solution)/shard_map/ppermute | solution.py:380
  71.2 5.9 %update_step.3 = (f32[1024,512]{1,0:T(8,128)}, f32[1024,512]{1,0:T(8,128)}, f32[4096,1024]{1,0:T(8,128)}) custom-call(s32[3]{0:T(128)S(1)} %pad_add_fusion.w, bf16[256,512]{1,0:T(8,128)(2,1)S(1)} %collective-permute-done.19.own, bf16[256,512]{1,0:T(8,128)(2,1)S(1)} %collective-permute-done.22.refs_0_, ...), custom_call_target="tpu_custom_call", output_to_operand_aliasing={{0}: (6, {}), {1}: (7, {}), {2}: (8, {})} | custom-call | flops 575000000 | tf_op jit(solution)/shard_map/update_step/pallas_call | solution.py:327
  (50 shorter events, 17.8 us)
Async XLA Ops:
  0.6 20.6 %collective-permute-start = (bf16[256,4096]{1,0:T(8,128)(2,1)}, bf16[256,4096]{1,0:T(8,128)(2,1)S(1)}, u32[]{:S(2)}, u32[]{:S(2)}) collective-permute-start(bf16[256,4096]{1,0:T(8,128)(2,1)} %refs_3_.6), channel_id=1, source_target_pairs={{0,4},{4,0},{8,12},{12,8},{16,20},{20,16},{24,28},{28,24},{1,5},{5... | collective-permute-start | bytes 6291464 | tf_op jit(solution)/shard_map/ppermute | solution.py:380
  1.2 20.1 %copy-start.3 = (bf16[256,4096]{1,0:T(8,128)(2,1)S(1)}, bf16[256,4096]{1,0:T(8,128)(2,1)}, u32[]{:S(2)}) copy-start(bf16[256,4096]{1,0:T(8,128)(2,1)} %refs_3_.6) | copy-start | bytes 6291460
  2.6 15.2 %collective-permute-start.3 = (bf16[1024,256]{1,0:T(8,128)(2,1)S(1)}, bf16[1024,256]{1,0:T(8,128)(2,1)S(1)}, u32[]{:S(2)}, u32[]{:S(2)}) collective-permute-start(bf16[1024,256]{1,0:T(8,128)(2,1)S(1)} %get-tuple-element.41.refs_2_.refs_0_), channel_id=1, source_target_pairs={{0,1},{1,0},{2,3},{3,2},{4,5},{5,4},{6,7},{7,6},{8,9},{9,8},{10,11... | collective-permute-start | bytes 1572872 | tf_op jit(solution)/shard_map/ppermute | solution.py:383
  5.3 14.4 %collective-permute-start.1 = (bf16[1024,256]{1,0:T(8,128)(2,1)S(1)}, bf16[1024,256]{1,0:T(8,128)(2,1)S(1)}, u32[]{:S(2)}, u32[]{:S(2)}) collective-permute-start(bf16[1024,256]{1,0:T(8,128)(2,1)S(1)} %get-tuple-element.41.refs_2_.refs_0_), channel_id=1, source_target_pairs={{0,2},{1,3},{2,0},{3,1},{4,6},{5,7},{6,4},{7,5},{8,10},{9,11},{10,... | collective-permute-start | bytes 1572872 | tf_op jit(solution)/shard_map/ppermute | solution.py:383
  6.8 23.3 %collective-permute-start.8 = (bf16[256,1536]{1,0:T(8,128)(2,1)S(1)}, bf16[256,1536]{1,0:T(8,128)(2,1)S(1)}, u32[]{:S(2)}, u32[]{:S(2)}) collective-permute-start(bf16[256,1536]{1,0:T(8,128)(2,1)S(1)} %get-tuple-element.32), channel_id=1, source_target_pairs={{0,8},{4,12},{8,0},{12,4},{16,24},{20,28},{24,16},{28,20},{1,9},{5... | collective-permute-start | bytes 2359304 | tf_op jit(solution)/shard_map/ppermute | solution.py:391
  8.4 23.0 %collective-permute-start.5 = (bf16[256,4096]{1,0:T(8,128)(2,1)S(1)}, bf16[256,4096]{1,0:T(8,128)(2,1)S(1)}, u32[]{:S(2)}, u32[]{:S(2)}) collective-permute-start(bf16[256,4096]{1,0:T(8,128)(2,1)S(1)} %copy-done.2), channel_id=1, source_target_pairs={{0,4},{4,0},{8,12},{12,8},{16,20},{20,16},{24,28},{28,24},{1,5},{5... | collective-permute-start | bytes 6291464 | tf_op jit(solution)/shard_map/ppermute | solution.py:380
  17.8 8.1 %collective-permute-start.4 = (bf16[512,256]{1,0:T(8,128)(2,1)S(1)}, bf16[512,256]{1,0:T(8,128)(2,1)S(1)}, u32[]{:S(2)}, u32[]{:S(2)}) collective-permute-start(bf16[512,256]{1,0:T(8,128)(2,1)S(1)} %slice.9), channel_id=1, source_target_pairs={{0,2},{1,3},{2,0},{3,1},{4,6},{5,7},{6,4},{7,5},{8,10},{9,11},{10,... | collective-permute-start | bytes 786440 | tf_op jit(solution)/shard_map/ppermute | solution.py:383
  19.7 7.6 %collective-permute-start.2 = (bf16[512,256]{1,0:T(8,128)(2,1)S(1)}, bf16[512,256]{1,0:T(8,128)(2,1)S(1)}, u32[]{:S(2)}, u32[]{:S(2)}) collective-permute-start(bf16[512,256]{1,0:T(8,128)(2,1)S(1)} %slice.8), channel_id=1, source_target_pairs={{0,1},{1,0},{2,3},{3,2},{4,5},{5,4},{6,7},{7,6},{8,9},{9,8},{10,11... | collective-permute-start | bytes 786440 | tf_op jit(solution)/shard_map/ppermute | solution.py:383
  28.4 6.7 %collective-permute-start.7 = (bf16[256,512]{1,0:T(8,128)(2,1)S(1)}, bf16[256,512]{1,0:T(8,128)(2,1)S(1)}, u32[]{:S(2)}, u32[]{:S(2)}) collective-permute-start(bf16[256,512]{1,0:T(8,128)(2,1)S(1)} %coords_2.1.refs_0_), channel_id=1, source_target_pairs={{0,8},{4,12},{8,0},{12,4},{16,24},{20,28},{24,16},{28,20},{1,9},{5... | collective-permute-start | bytes 786440 | tf_op jit(solution)/shard_map/ppermute | solution.py:391
  30.0 5.1 %collective-permute-start.9 = (bf16[256,1536]{1,0:T(8,128)(2,1)S(1)}, bf16[256,1536]{1,0:T(8,128)(2,1)S(1)}, u32[]{:S(2)}, u32[]{:S(2)}) collective-permute-start(bf16[256,1536]{1,0:T(8,128)(2,1)S(1)} %collective-permute-done.8.refs_1_.refs_5_.refs_9_.refs_13_), channel_id=1, source_target_pairs={{0,4},{4,0},{8,12},{12,8},{16,20},{20,16},{24,28},{28,24},{1,5},{5... | collective-permute-start | bytes 2359304 | tf_op jit(solution)/shard_map/ppermute | solution.py:380
  30.8 26.5 %collective-permute-start.14 = (bf16[4096,256]{1,0:T(8,128)(2,1)S(1)}, bf16[4096,256]{1,0:T(8,128)(2,1)S(1)}, u32[]{:S(2)}, u32[]{:S(2)}) collective-permute-start(bf16[4096,256]{1,0:T(8,128)(2,1)S(1)} %assemble.1.own_ref), channel_id=1, source_target_pairs={{0,4},{4,0},{8,12},{12,8},{16,20},{20,16},{24,28},{28,24},{1,5},{5... | collective-permute-start | bytes 6291464 | tf_op jit(solution)/shard_map/ppermute | solution.py:380
  36.0 5.0 %collective-permute-start.10 = (bf16[128,512]{1,0:T(8,128)(2,1)S(1)}, bf16[128,512]{1,0:T(8,128)(2,1)S(1)}, u32[]{:S(2)}, u32[]{:S(2)}) collective-permute-start(bf16[128,512]{1,0:T(8,128)(2,1)S(1)} %get-tuple-element.36), channel_id=1, source_target_pairs={{0,2},{1,3},{2,0},{3,1},{4,6},{5,7},{6,4},{7,5},{8,10},{9,11},{10,... | collective-permute-start | bytes 393224 | tf_op jit(solution)/shard_map/ppermute | solution.py:383
  37.1 5.1 %collective-permute-start.11 = (bf16[128,512]{1,0:T(8,128)(2,1)S(1)}, bf16[128,512]{1,0:T(8,128)(2,1)S(1)}, u32[]{:S(2)}, u32[]{:S(2)}) collective-permute-start(bf16[128,512]{1,0:T(8,128)(2,1)S(1)} %get-tuple-element.38), channel_id=1, source_target_pairs={{0,1},{1,0},{2,3},{3,2},{4,5},{5,4},{6,7},{7,6},{8,9},{9,8},{10,11... | collective-permute-start | bytes 393224 | tf_op jit(solution)/shard_map/ppermute | solution.py:383
  38.9 7.4 %collective-permute-start.6 = (bf16[256,512]{1,0:T(8,128)(2,1)S(1)}, bf16[256,512]{1,0:T(8,128)(2,1)S(1)}, u32[]{:S(2)}, u32[]{:S(2)}) collective-permute-start(bf16[256,512]{1,0:T(8,128)(2,1)S(1)} %terms_pair.1), channel_id=1, source_target_pairs={{0,8},{4,12},{8,0},{12,4},{16,24},{20,28},{24,16},{28,20},{1,9},{5... | collective-permute-start | bytes 786440 | tf_op jit(solution)/shard_map/ppermute | solution.py:391
  43.2 5.0 %collective-permute-start.16 = (bf16[256,256]{1,0:T(8,128)(2,1)S(1)}, bf16[256,256]{1,0:T(8,128)(2,1)S(1)}, u32[]{:S(2)}, u32[]{:S(2)}) collective-permute-start(bf16[256,256]{1,0:T(8,128)(2,1)S(1)} %get-tuple-element.49), channel_id=1, source_target_pairs={{0,1},{1,0},{2,3},{3,2},{4,5},{5,4},{6,7},{7,6},{8,9},{9,8},{10,11... | collective-permute-start | bytes 393224 | tf_op jit(solution)/shard_map/ppermute | solution.py:383
  44.3 5.0 %collective-permute-start.17 = (bf16[256,256]{1,0:T(8,128)(2,1)S(1)}, bf16[256,256]{1,0:T(8,128)(2,1)S(1)}, u32[]{:S(2)}, u32[]{:S(2)}) collective-permute-start(bf16[256,256]{1,0:T(8,128)(2,1)S(1)} %get-tuple-element.50), channel_id=1, source_target_pairs={{0,2},{1,3},{2,0},{3,1},{4,6},{5,7},{6,4},{7,5},{8,10},{9,11},{10,... | collective-permute-start | bytes 393224 | tf_op jit(solution)/shard_map/ppermute | solution.py:383
  45.8 6.7 %collective-permute-start.12 = (bf16[256,256]{1,0:T(8,128)(2,1)S(1)}, bf16[256,256]{1,0:T(8,128)(2,1)S(1)}, u32[]{:S(2)}, u32[]{:S(2)}) collective-permute-start(bf16[256,256]{1,0:T(8,128)(2,1)S(1)} %get-tuple-element.39), channel_id=1, source_target_pairs={{0,1},{1,0},{2,3},{3,2},{4,5},{5,4},{6,7},{7,6},{8,9},{9,8},{10,11... | collective-permute-start | bytes 393224 | tf_op jit(solution)/shard_map/ppermute | solution.py:383
  46.3 6.2 %collective-permute-start.13 = (bf16[256,256]{1,0:T(8,128)(2,1)S(1)}, bf16[256,256]{1,0:T(8,128)(2,1)S(1)}, u32[]{:S(2)}, u32[]{:S(2)}) collective-permute-start(bf16[256,256]{1,0:T(8,128)(2,1)S(1)} %get-tuple-element.40), channel_id=1, source_target_pairs={{0,2},{1,3},{2,0},{3,1},{4,6},{5,7},{6,4},{7,5},{8,10},{9,11},{10,... | collective-permute-start | bytes 393224 | tf_op jit(solution)/shard_map/ppermute | solution.py:383
  49.8 7.4 %collective-permute-start.18 = (bf16[256,256]{1,0:T(8,128)(2,1)S(1)}, bf16[256,256]{1,0:T(8,128)(2,1)S(1)}, u32[]{:S(2)}, u32[]{:S(2)}) collective-permute-start(bf16[256,256]{1,0:T(8,128)(2,1)S(1)} %terms_0.3), channel_id=1, source_target_pairs={{0,16},{4,20},{8,24},{12,28},{16,0},{20,4},{24,8},{28,12},{1,17},{... | collective-permute-start | bytes 393224 | tf_op jit(solution)/shard_map/ppermute | solution.py:394
  53.1 6.3 %collective-permute-start.15 = (bf16[256,256]{1,0:T(8,128)(2,1)S(1)}, bf16[256,256]{1,0:T(8,128)(2,1)S(1)}, u32[]{:S(2)}, u32[]{:S(2)}) collective-permute-start(bf16[256,256]{1,0:T(8,128)(2,1)S(1)} %terms_0.2), channel_id=1, source_target_pairs={{0,16},{4,20},{8,24},{12,28},{16,0},{20,4},{24,8},{28,12},{1,17},{... | collective-permute-start | bytes 393224 | tf_op jit(solution)/shard_map/ppermute | solution.py:394
  59.5 10.1 %collective-permute-start.19 = (bf16[256,512]{1,0:T(8,128)(2,1)S(1)}, bf16[256,512]{1,0:T(8,128)(2,1)S(1)}, u32[]{:S(2)}, u32[]{:S(2)}) collective-permute-start(bf16[256,512]{1,0:T(8,128)(2,1)S(1)} %pad_maximum_fusion.own), channel_id=1, source_target_pairs={{0,8},{4,12},{8,0},{12,4},{16,24},{20,28},{24,16},{28,20},{1,9},{5... | collective-permute-start | bytes 786440 | tf_op jit(solution)/shard_map/ppermute | solution.py:391
  62.1 1.3 %collective-permute-start.21 = (bf16[256,256]{1,0:T(8,128)(2,1)S(1)}, bf16[256,256]{1,0:T(8,128)(2,1)S(1)}, u32[]{:S(2)}, u32[]{:S(2)}) collective-permute-start(bf16[256,256]{1,0:T(8,128)(2,1)S(1)} %add_convert_fusion), channel_id=1, source_target_pairs={{0,4},{4,0},{8,12},{12,8},{16,20},{20,16},{24,28},{28,24},{1,5},{5... | collective-permute-start | bytes 393224 | tf_op jit(solution)/shard_map/ppermute | solution.py:380
  62.1 1.5 %collective-permute-start.20 = (bf16[256,256]{1,0:T(8,128)(2,1)S(1)}, bf16[256,256]{1,0:T(8,128)(2,1)S(1)}, u32[]{:S(2)}, u32[]{:S(2)}) collective-permute-start(bf16[256,256]{1,0:T(8,128)(2,1)S(1)} %add_convert_fusion.1), channel_id=1, source_target_pairs={{0,4},{4,0},{8,12},{12,8},{16,20},{20,16},{24,28},{28,24},{1,5},{5... | collective-permute-start | bytes 393224 | tf_op jit(solution)/shard_map/ppermute | solution.py:380
  69.6 1.6 %collective-permute-start.22 = (bf16[256,512]{1,0:T(8,128)(2,1)S(1)}, bf16[256,512]{1,0:T(8,128)(2,1)S(1)}, u32[]{:S(2)}, u32[]{:S(2)}) collective-permute-start(bf16[256,512]{1,0:T(8,128)(2,1)S(1)} %collective-permute-done.19.own), channel_id=1, source_target_pairs={{0,4},{4,0},{8,12},{12,8},{16,20},{20,16},{24,28},{28,24},{1,5},{5... | collective-permute-start | bytes 786440 | tf_op jit(solution)/shard_map/ppermute | solution.py:380
  (3 other events, 19.9 us)

commit v9 on v8

--- a/solution.py
+++ b/solution.py
@@ -253,13 +253,13 @@
     )[0]
 
 
-def update_step(where, k, pieces, grads, proj, moments, before):
+def update_step(where, k, pieces, grads, proj, moments, before, written):
     half, span = grads[0].shape
     rank = CORES * half
     features = moments[0].shape[0]
     width = proj.shape[0]
     rows = min(256, width)
-    steps = width // rows
+    steps = written // rows
     some = 16
 
     def piece(w):
@@ -267,8 +267,8 @@
 
     def body(w, own, *refs):
         others, (proj_ref, first_ref, second_ref) = refs[: len(grads) - 1], refs[len(grads) - 1 :][:3]
-        outs, update = refs[-10:-8], refs[-8]
-        moment, grad, ratio, direction, out = refs[-7:-2]
+        outs, update, direction = refs[-10:-8], refs[-8], refs[-7]
+        moment, grad, ratio, out = refs[-6:-2]
         moment_out, update_out = refs[-2:]
         features_at = pl.ds(pl.multiple_of(piece(w) * span, span), span)
         stores = [
@@ -327,18 +327,21 @@
     return pl.pallas_call(
         body,
         out_shape=[jax.ShapeDtypeStruct(x.shape, F32) for x in moments]
-        + [jax.ShapeDtypeStruct((width, features), F32)],
+        + [
+            jax.ShapeDtypeStruct((width, features), F32),
+            jax.ShapeDtypeStruct((rank, span), BF16),
+        ],
         grid_spec=pltpu.PrefetchScalarGridSpec(
             num_scalar_prefetch=1,
             grid=(1,),
             in_specs=in_specs,
-            out_specs=[any_space] * 3,
+            out_specs=[any_space] * 3
+            + [pl.BlockSpec((rank, span), lambda i, w: (0, 0))],
             scratch_shapes=[
                 pltpu.VMEM((2, span, rank), F32),
                 pltpu.VMEM((span, rank), BF16),
                 pltpu.VMEM((span, rank), BF16),
-                pltpu.VMEM((rank, span), BF16),
-                pltpu.VMEM((width, span), F32),
+                pltpu.VMEM((written, span), F32),
                 pltpu.SemaphoreType.DMA((2,)),
                 pltpu.SemaphoreType.DMA((steps,)),
             ],
@@ -348,6 +351,50 @@
         cost_estimate=busy(0.5),
         name="update_step",
     )(where, *inputs)
+
+
+def expand_rest(where, pieces, direction, proj, update, written):
+    rank, span = direction.shape
+    width = proj.shape[0]
+    rows = min(256, width - written)
+    steps = (width - written) // rows
+
+    def body(w, direction_ref, proj_ref, _, update_ref, out, sems):
+        features_at = pl.ds(pl.multiple_of(w[2] * span, span), span)
+        copies = []
+        for r in range(steps):
+            at = pl.ds(r * rows, rows)
+            there = pl.ds(written + r * rows, rows)
+            out[at, :] = jnp.dot(
+                proj_ref[there, :], direction_ref[...], preferred_element_type=F32
+            )
+            copy = pltpu.make_async_copy(
+                out.at[at, :], update_ref.at[there, features_at], sems.at[r]
+            )
+            copy.start()
+            copies.append(copy)
+        for copy in copies:
+            copy.wait()
+
+    any_space = pl.BlockSpec(memory_space=pl.ANY)
+    return pl.pallas_call(
+        body,
+        out_shape=jax.ShapeDtypeStruct(update.shape, F32),
+        grid_spec=pltpu.PrefetchScalarGridSpec(
+            num_scalar_prefetch=1,
+            grid=(1,),
+            in_specs=[whole(direction), whole(proj), any_space],
+            out_specs=any_space,
+            scratch_shapes=[
+                pltpu.VMEM((width - written, span), F32),
+                pltpu.SemaphoreType.DMA((steps,)),
+            ],
+        ),
+        input_output_aliases={3: 0},
+        compiler_params=pltpu.CompilerParams(vmem_limit_bytes=16 * MIB),
+        cost_estimate=busy(2),
+        name="expand_rest",
+    )(where, direction, proj, update)
 
 
 def in_vmem(x):
@@ -477,11 +524,16 @@
     sums_of = [add_up(x) for x in parts]
     mine = jnp.concatenate(sums_of, axis=1)
     others = [to_core(x) for x in sums_of]
-    outputs = update_step(where, 0, pieces, (mine, *others), proj, moments, None)
+    width = proj.shape[0]
+    written = width * 3 // 4 if pieces > 1 else width
+    *outputs, direction = update_step(
+        where, 0, pieces, (mine, *others), proj, moments, None, written
+    )
     if pieces > 1:
         others = to_piece(mine, 1)
-        pair = (others, to_core(after(others, *outputs)))
-        outputs = update_step(where, 1, pieces, pair, proj, moments, outputs)
+        pair = (others, to_core(after(others, direction)))
+        outputs[2] = expand_rest(where, pieces, direction, proj, outputs[2], written)
+        *outputs, _ = update_step(where, 1, pieces, pair, proj, moments, outputs, width)
     return tuple(outputs)
 
 

time: 77.2 us -> 78.4 us (1.016)
  Pallas kernels: 23.3 us -> 25.6 us
  waiting for transfers between devices: 25.4 us -> 24.2 us
    pallas_call x0 -> x1, Pallas kernels: none -> 2.18 us  [expand_rest(): pl.pallas_call(body, out_shape=jax.ShapeDtypeStruct(update.shape, F32), g...]
    ppermute x7, waiting for transfers between devices: 2.25 us -> 1.04 us  [to_core(): return lax.ppermute(x, 'dp', [(i, i ^ 1) for i in range(dp)])]
  transfers between devices with their start and end apart: 23 -> 23, of which waited for: 13 -> 12; matrix products, arithmetic and copies ran while one was open for 0% -> 0% of each run, Pallas kernels for 23% -> 24%
where the time goes in v9:
time: 78.4 us; the launch traced here: 78.2 us
  starting transfers between devices  27.3 us (35%)
  Pallas kernels  25.6 us (33%)
  waiting for transfers between devices  24.2 us (31%)
  between operations  0.82 us (1%)
    ppermute x10, waiting for transfers between devices, to_fsdp(): return lax.ppermute(x, 'fsdp', [(i, i ^ s) for i in range(fsdp)])  16.8 us
    ppermute x10, starting transfers between devices, to_fsdp(): return lax.ppermute(x, 'fsdp', [(i, i ^ s) for i in range(fsdp)])  13.7 us
    pallas_call x2, Pallas kernels, update_step(): pl.pallas_call(body, out_shape=[jax.ShapeDtypeStruct(x.shape, F32) for x...  11.9 us
    pallas_call x10, Pallas kernels, call(): pl.pallas_call(body, out_shape=out_shape, grid_spec=pltpu.PrefetchScalarG...  9.29 us
    ppermute x4, starting transfers between devices, to_piece(): return lax.ppermute(x, 'dp', pairs)  7.53 us
    ppermute x2, starting transfers between devices, to_base(): lax.ppermute(x, 'dp', [(i, (i + k * pieces * CORES) % dp) for i in range(...  4.09 us
    ppermute x2, waiting for transfers between devices, to_base(): lax.ppermute(x, 'dp', [(i, (i + k * pieces * CORES) % dp) for i in range(...  3.89 us
    ppermute x4, waiting for transfers between devices, to_piece(): return lax.ppermute(x, 'dp', pairs)  2.49 us
  transfers between devices with their start and end apart: 23, of which 12 were waited for; matrix products, arithmetic and copies ran while one was open for 0% of the time, Pallas kernels for 24%

profile of v9, /device:TPU:0, one launch (start us, length us, event | category | flops | bytes accessed | tf_op | source)
XLA Modules:
  0.0 78.2 jit_solution(5142223086943808432)
XLA Ops:
  1.2 1.5 %cut_out.1 = (bf16[1024,256]{1,0:T(8,128)(2,1)S(1)}, bf16[256,1536]{1,0:T(8,128)(2,1)S(1)}) custom-call(s32[1]{0:T(128)} %bitcast.fsdp_ref, s32[1]{0:T(128)} %bitcast.1.core_ref, s32[1]{0:T(128)} %bitcast.2.piece_ref, bf16[1024,512]{1,0:T(8,128)(2,1)} %proj_ref.1, bf16[256,4096]{1,0:T(8,128)(2,1)} %refs_1_.3), custom_call_target="tpu_custom_call" | custom-call | flops 1150000000 | tf_op jit(solution)/shard_map/cut_out/pallas_call | solution.py:71
  2.6 2.6 %collective-permute-start.3 = (bf16[1024,256]{1,0:T(8,128)(2,1)S(1)}, bf16[1024,256]{1,0:T(8,128)(2,1)S(1)}, u32[]{:S(2)}, u32[]{:S(2)}) collective-permute-start(bf16[1024,256]{1,0:T(8,128)(2,1)S(1)} %get-tuple-element.45.refs_2_.refs_0_), channel_id=1, source_target_pairs={{0,1},{1,0},{2,3},{3,2},{4,5},{5,4},{6,7},{7,6},{8,9},{9,8},{10,11... | collective-permute-start | bytes 1572872 | tf_op jit(solution)/shard_map/ppermute | solution.py:430
  5.3 1.5 %collective-permute-start.1 = (bf16[1024,256]{1,0:T(8,128)(2,1)S(1)}, bf16[1024,256]{1,0:T(8,128)(2,1)S(1)}, u32[]{:S(2)}, u32[]{:S(2)}) collective-permute-start(bf16[1024,256]{1,0:T(8,128)(2,1)S(1)} %get-tuple-element.45.refs_2_.refs_0_), channel_id=1, source_target_pairs={{0,2},{1,3},{2,0},{3,1},{4,6},{5,7},{6,4},{7,5},{8,10},{9,11},{10,... | collective-permute-start | bytes 1572872 | tf_op jit(solution)/shard_map/ppermute | solution.py:430
  6.8 1.6 %collective-permute-start.8 = (bf16[256,1536]{1,0:T(8,128)(2,1)S(1)}, bf16[256,1536]{1,0:T(8,128)(2,1)S(1)}, u32[]{:S(2)}, u32[]{:S(2)}) collective-permute-start(bf16[256,1536]{1,0:T(8,128)(2,1)S(1)} %get-tuple-element.36), channel_id=1, source_target_pairs={{0,8},{4,12},{8,0},{12,4},{16,24},{20,28},{24,16},{28,20},{1,9},{5... | collective-permute-start | bytes 2359304 | tf_op jit(solution)/shard_map/ppermute | solution.py:438
  8.4 9.3 %collective-permute-done.3.refs_2_.refs_1_ = bf16[1024,256]{1,0:T(8,128)(2,1)S(1)} collective-permute-done((bf16[1024,256]{1,0:T(8,128)(2,1)S(1)}, bf16[1024,256]{1,0:T(8,128)(2,1)S(1)}, u32[]{:S(2)}, u32[]{:S(2)}) %collective-permute-start.3) | collective-permute-done | bytes 524320 | tf_op jit(solution)/shard_map/ppermute | solution.py:430
  17.8 1.8 %collective-permute-start.4 = (bf16[512,256]{1,0:T(8,128)(2,1)S(1)}, bf16[512,256]{1,0:T(8,128)(2,1)S(1)}, u32[]{:S(2)}, u32[]{:S(2)}) collective-permute-start(bf16[512,256]{1,0:T(8,128)(2,1)S(1)} %slice.9), channel_id=1, source_target_pairs={{0,2},{1,3},{2,0},{3,1},{4,6},{5,7},{6,4},{7,5},{8,10},{9,11},{10,... | collective-permute-start | bytes 786440 | tf_op jit(solution)/shard_map/ppermute | solution.py:430
  19.7 1.6 %collective-permute-start.2 = (bf16[512,256]{1,0:T(8,128)(2,1)S(1)}, bf16[512,256]{1,0:T(8,128)(2,1)S(1)}, u32[]{:S(2)}, u32[]{:S(2)}) collective-permute-start(bf16[512,256]{1,0:T(8,128)(2,1)S(1)} %slice.8), channel_id=1, source_target_pairs={{0,1},{1,0},{2,3},{3,2},{4,5},{5,4},{6,7},{7,6},{8,9},{9,8},{10,11... | collective-permute-start | bytes 786440 | tf_op jit(solution)/shard_map/ppermute | solution.py:430
  22.2 1.3 %coords_1.1.refs_6_ = f32[512,256]{1,0:T(8,128)S(1)} custom-call(s32[3]{0:T(128)S(1)} %pad_add_fusion.w, bf16[256,4096]{1,0:T(8,128)(2,1)S(1)} %copy-done.3, bf16[256,4096]{1,0:T(8,128)(2,1)S(1)} %collective-permute-done.refs_1_.refs_4_, bf16[1024,256]{1,0:T(8,128)(2,1)S(1)} %collective-permute-done.3.refs_2_.refs_1_, bf16[256,4096]{1,0:T(8,128)(2,1)S(1)} %copy-done.3, ...), custom_call_target="tpu_custom_call" | custom-call | flops 9200000000 | tf_op jit(solution)/shard_map/coords_1/pallas_call | solution.py:31
  23.5 2.5 %collective-permute-done.4.refs_5_.refs_4_ = bf16[512,256]{1,0:T(8,128)(2,1)S(1)} collective-permute-done((bf16[512,256]{1,0:T(8,128)(2,1)S(1)}, bf16[512,256]{1,0:T(8,128)(2,1)S(1)}, u32[]{:S(2)}, u32[]{:S(2)}) %collective-permute-start.4) | collective-permute-done | bytes 262176 | tf_op jit(solution)/shard_map/ppermute | solution.py:430
  25.9 1.4 %collective-permute-done.2.refs_2_.refs_3_ = bf16[512,256]{1,0:T(8,128)(2,1)S(1)} collective-permute-done((bf16[512,256]{1,0:T(8,128)(2,1)S(1)}, bf16[512,256]{1,0:T(8,128)(2,1)S(1)}, u32[]{:S(2)}, u32[]{:S(2)}) %collective-permute-start.2) | collective-permute-done | bytes 262176 | tf_op jit(solution)/shard_map/ppermute | solution.py:430
  28.4 1.6 %collective-permute-start.7 = (bf16[256,512]{1,0:T(8,128)(2,1)S(1)}, bf16[256,512]{1,0:T(8,128)(2,1)S(1)}, u32[]{:S(2)}, u32[]{:S(2)}) collective-permute-start(bf16[256,512]{1,0:T(8,128)(2,1)S(1)} %coords_2.1.refs_0_), channel_id=1, source_target_pairs={{0,8},{4,12},{8,0},{12,4},{16,24},{20,28},{24,16},{28,20},{1,9},{5... | collective-permute-start | bytes 786440 | tf_op jit(solution)/shard_map/ppermute | solution.py:438
  31.4 1.2 %terms_chip.1 = (f32[256,512]{1,0:T(8,128)S(1)}, f32[256,512]{1,0:T(8,128)S(1)}, f32[256,512]{1,0:T(8,128)S(1)}, f32[256,512]{1,0:T(8,128)S(1)}) custom-call(s32[3]{0:T(128)S(1)} %pad_add_fusion.w, bf16[256,512]{1,0:T(8,128)(2,1)S(1)} %coords_2.1.refs_0_, bf16[256,4096]{1,0:T(8,128)(2,1)S(1)} %copy-done.2, ...), custom_call_target="tpu_custom_call" | custom-call | flops 13799999488 | tf_op jit(solution)/shard_map/terms_chip/pallas_call | solution.py:31
  32.6 2.5 %collective-permute-done.7.refs_0_ = bf16[256,512]{1,0:T(8,128)(2,1)S(1)} collective-permute-done((bf16[256,512]{1,0:T(8,128)(2,1)S(1)}, bf16[256,512]{1,0:T(8,128)(2,1)S(1)}, u32[]{:S(2)}, u32[]{:S(2)}) %collective-permute-start.7) | collective-permute-done | bytes 262176 | tf_op jit(solution)/shard_map/ppermute | solution.py:438
  38.9 1.6 %collective-permute-start.6 = (bf16[256,512]{1,0:T(8,128)(2,1)S(1)}, bf16[256,512]{1,0:T(8,128)(2,1)S(1)}, u32[]{:S(2)}, u32[]{:S(2)}) collective-permute-start(bf16[256,512]{1,0:T(8,128)(2,1)S(1)} %terms_pair.1), channel_id=1, source_target_pairs={{0,8},{4,12},{8,0},{12,4},{16,24},{20,28},{24,16},{28,20},{1,9},{5... | collective-permute-start | bytes 786440 | tf_op jit(solution)/shard_map/ppermute | solution.py:438
  41.0 1.2 %collective-permute-done.11.refs_8_.refs_16_ = bf16[128,512]{1,0:T(8,128)(2,1)S(1)} collective-permute-done((bf16[128,512]{1,0:T(8,128)(2,1)S(1)}, bf16[128,512]{1,0:T(8,128)(2,1)S(1)}, u32[]{:S(2)}, u32[]{:S(2)}) %collective-permute-start.11) | collective-permute-done | bytes 131104 | tf_op jit(solution)/shard_map/ppermute | solution.py:430
  44.3 1.5 %collective-permute-start.17 = (bf16[256,256]{1,0:T(8,128)(2,1)S(1)}, bf16[256,256]{1,0:T(8,128)(2,1)S(1)}, u32[]{:S(2)}, u32[]{:S(2)}) collective-permute-start(bf16[256,256]{1,0:T(8,128)(2,1)S(1)} %get-tuple-element.54), channel_id=1, source_target_pairs={{0,2},{1,3},{2,0},{3,1},{4,6},{5,7},{6,4},{7,5},{8,10},{9,11},{10,... | collective-permute-start | bytes 393224 | tf_op jit(solution)/shard_map/ppermute | solution.py:430
  49.8 2.6 %collective-permute-start.18 = (bf16[256,256]{1,0:T(8,128)(2,1)S(1)}, bf16[256,256]{1,0:T(8,128)(2,1)S(1)}, u32[]{:S(2)}, u32[]{:S(2)}) collective-permute-start(bf16[256,256]{1,0:T(8,128)(2,1)S(1)} %terms_0.3), channel_id=1, source_target_pairs={{0,16},{4,20},{8,24},{12,28},{16,0},{20,4},{24,8},{28,12},{1,17},{... | collective-permute-start | bytes 393224 | tf_op jit(solution)/shard_map/ppermute | solution.py:441
  53.1 1.5 %collective-permute-start.15 = (bf16[256,256]{1,0:T(8,128)(2,1)S(1)}, bf16[256,256]{1,0:T(8,128)(2,1)S(1)}, u32[]{:S(2)}, u32[]{:S(2)}) collective-permute-start(bf16[256,256]{1,0:T(8,128)(2,1)S(1)} %terms_0.2), channel_id=1, source_target_pairs={{0,16},{4,20},{8,24},{12,28},{16,0},{20,4},{24,8},{28,12},{1,17},{... | collective-permute-start | bytes 393224 | tf_op jit(solution)/shard_map/ppermute | solution.py:441
  54.5 2.7 %collective-permute-done.18 = bf16[256,256]{1,0:T(8,128)(2,1)S(1)} collective-permute-done((bf16[256,256]{1,0:T(8,128)(2,1)S(1)}, bf16[256,256]{1,0:T(8,128)(2,1)S(1)}, u32[]{:S(2)}, u32[]{:S(2)}) %collective-permute-start.18) | collective-permute-done | bytes 131104 | tf_op jit(solution)/shard_map/ppermute | solution.py:441
  58.2 1.2 %collective-permute-done.15 = bf16[256,256]{1,0:T(8,128)(2,1)S(1)} collective-permute-done((bf16[256,256]{1,0:T(8,128)(2,1)S(1)}, bf16[256,256]{1,0:T(8,128)(2,1)S(1)}, u32[]{:S(2)}, u32[]{:S(2)}) %collective-permute-start.15) | collective-permute-done | bytes 131104 | tf_op jit(solution)/shard_map/ppermute | solution.py:441
  59.5 2.7 %collective-permute-start.19 = (bf16[256,512]{1,0:T(8,128)(2,1)S(1)}, bf16[256,512]{1,0:T(8,128)(2,1)S(1)}, u32[]{:S(2)}, u32[]{:S(2)}) collective-permute-start(bf16[256,512]{1,0:T(8,128)(2,1)S(1)} %pad_maximum_fusion.own), channel_id=1, source_target_pairs={{0,8},{4,12},{8,0},{12,4},{16,24},{20,28},{24,16},{28,20},{1,9},{5... | collective-permute-start | bytes 786440 | tf_op jit(solution)/shard_map/ppermute | solution.py:438
  63.7 5.2 %update_step.2 = (f32[1024,512]{1,0:T(8,128)}, f32[1024,512]{1,0:T(8,128)}, f32[4096,1024]{1,0:T(8,128)}, bf16[512,512]{1,0:T(8,128)(2,1)S(1)}) custom-call(s32[3]{0:T(128)S(1)} %pad_add_fusion.w, bf16[256,512]{1,0:T(8,128)(2,1)S(1)} %pad_maximum_fusion.own, bf16[256,256]{1,0:T(8,128)(2,1)S(1)} %collective-permute-done.20.refs_0_, ...), custom_call_target="tpu_custom_call" | custom-call | flops 575000000 | tf_op jit(solution)/shard_map/update_step/pallas_call | solution.py:327
  69.3 2.2 %expand_rest.1.refs_6_ = f32[4096,1024]{1,0:T(8,128)} custom-call(s32[3]{0:T(128)S(1)} %pad_add_fusion.w, bf16[512,512]{1,0:T(8,128)(2,1)S(1)} %get-tuple-element.55.direction_ref, bf16[4096,512]{1,0:T(8,128)(2,1)S(1)} %join.1.refs_2_.proj_ref.refs_1_, f32[4096,1024]{1,0:T(8,128)} %get-tuple-element.59._), custom_call_target="tpu_custom_call", output_to_operand_aliasing={{}: (3, {})} | custom-call | flops 2300000000 | tf_op jit(solution)/shard_map/expand_rest/pallas_call | solution.py:380
  71.5 6.7 %update_step.3 = (f32[1024,512]{1,0:T(8,128)}, f32[1024,512]{1,0:T(8,128)}, f32[4096,1024]{1,0:T(8,128)}, bf16[512,512]{1,0:T(8,128)(2,1)}) custom-call(s32[3]{0:T(128)S(1)} %pad_add_fusion.w, bf16[256,512]{1,0:T(8,128)(2,1)S(1)} %collective-permute-done.19.own, ...), custom_call_target="tpu_custom_call", output_to_operand_aliasing={{0}: (6, {}), {1}: (7, {}), {2}: (8, {})} | custom-call | flops 575000000 | tf_op jit(solution)/shard_map/update_step/pallas_call | solution.py:327
  (51 shorter events, 17.8 us)
Async XLA Ops:
  0.6 20.6 %collective-permute-start = (bf16[256,4096]{1,0:T(8,128)(2,1)}, bf16[256,4096]{1,0:T(8,128)(2,1)S(1)}, u32[]{:S(2)}, u32[]{:S(2)}) collective-permute-start(bf16[256,4096]{1,0:T(8,128)(2,1)} %refs_3_.6), channel_id=1, source_target_pairs={{0,4},{4,0},{8,12},{12,8},{16,20},{20,16},{24,28},{28,24},{1,5},{5... | collective-permute-start | bytes 6291464 | tf_op jit(solution)/shard_map/ppermute | solution.py:427
  1.2 20.1 %copy-start.3 = (bf16[256,4096]{1,0:T(8,128)(2,1)S(1)}, bf16[256,4096]{1,0:T(8,128)(2,1)}, u32[]{:S(2)}) copy-start(bf16[256,4096]{1,0:T(8,128)(2,1)} %refs_3_.6) | copy-start | bytes 6291460
  2.6 15.2 %collective-permute-start.3 = (bf16[1024,256]{1,0:T(8,128)(2,1)S(1)}, bf16[1024,256]{1,0:T(8,128)(2,1)S(1)}, u32[]{:S(2)}, u32[]{:S(2)}) collective-permute-start(bf16[1024,256]{1,0:T(8,128)(2,1)S(1)} %get-tuple-element.45.refs_2_.refs_0_), channel_id=1, source_target_pairs={{0,1},{1,0},{2,3},{3,2},{4,5},{5,4},{6,7},{7,6},{8,9},{9,8},{10,11... | collective-permute-start | bytes 1572872 | tf_op jit(solution)/shard_map/ppermute | solution.py:430
  5.3 14.4 %collective-permute-start.1 = (bf16[1024,256]{1,0:T(8,128)(2,1)S(1)}, bf16[1024,256]{1,0:T(8,128)(2,1)S(1)}, u32[]{:S(2)}, u32[]{:S(2)}) collective-permute-start(bf16[1024,256]{1,0:T(8,128)(2,1)S(1)} %get-tuple-element.45.refs_2_.refs_0_), channel_id=1, source_target_pairs={{0,2},{1,3},{2,0},{3,1},{4,6},{5,7},{6,4},{7,5},{8,10},{9,11},{10,... | collective-permute-start | bytes 1572872 | tf_op jit(solution)/shard_map/ppermute | solution.py:430
  6.8 23.3 %collective-permute-start.8 = (bf16[256,1536]{1,0:T(8,128)(2,1)S(1)}, bf16[256,1536]{1,0:T(8,128)(2,1)S(1)}, u32[]{:S(2)}, u32[]{:S(2)}) collective-permute-start(bf16[256,1536]{1,0:T(8,128)(2,1)S(1)} %get-tuple-element.36), channel_id=1, source_target_pairs={{0,8},{4,12},{8,0},{12,4},{16,24},{20,28},{24,16},{28,20},{1,9},{5... | collective-permute-start | bytes 2359304 | tf_op jit(solution)/shard_map/ppermute | solution.py:438
  8.4 23.0 %collective-permute-start.5 = (bf16[256,4096]{1,0:T(8,128)(2,1)S(1)}, bf16[256,4096]{1,0:T(8,128)(2,1)S(1)}, u32[]{:S(2)}, u32[]{:S(2)}) collective-permute-start(bf16[256,4096]{1,0:T(8,128)(2,1)S(1)} %copy-done.2), channel_id=1, source_target_pairs={{0,4},{4,0},{8,12},{12,8},{16,20},{20,16},{24,28},{28,24},{1,5},{5... | collective-permute-start | bytes 6291464 | tf_op jit(solution)/shard_map/ppermute | solution.py:427
  17.8 8.1 %collective-permute-start.4 = (bf16[512,256]{1,0:T(8,128)(2,1)S(1)}, bf16[512,256]{1,0:T(8,128)(2,1)S(1)}, u32[]{:S(2)}, u32[]{:S(2)}) collective-permute-start(bf16[512,256]{1,0:T(8,128)(2,1)S(1)} %slice.9), channel_id=1, source_target_pairs={{0,2},{1,3},{2,0},{3,1},{4,6},{5,7},{6,4},{7,5},{8,10},{9,11},{10,... | collective-permute-start | bytes 786440 | tf_op jit(solution)/shard_map/ppermute | solution.py:430
  19.7 7.6 %collective-permute-start.2 = (bf16[512,256]{1,0:T(8,128)(2,1)S(1)}, bf16[512,256]{1,0:T(8,128)(2,1)S(1)}, u32[]{:S(2)}, u32[]{:S(2)}) collective-permute-start(bf16[512,256]{1,0:T(8,128)(2,1)S(1)} %slice.8), channel_id=1, source_target_pairs={{0,1},{1,0},{2,3},{3,2},{4,5},{5,4},{6,7},{7,6},{8,9},{9,8},{10,11... | collective-permute-start | bytes 786440 | tf_op jit(solution)/shard_map/ppermute | solution.py:430
  28.4 6.7 %collective-permute-start.7 = (bf16[256,512]{1,0:T(8,128)(2,1)S(1)}, bf16[256,512]{1,0:T(8,128)(2,1)S(1)}, u32[]{:S(2)}, u32[]{:S(2)}) collective-permute-start(bf16[256,512]{1,0:T(8,128)(2,1)S(1)} %coords_2.1.refs_0_), channel_id=1, source_target_pairs={{0,8},{4,12},{8,0},{12,4},{16,24},{20,28},{24,16},{28,20},{1,9},{5... | collective-permute-start | bytes 786440 | tf_op jit(solution)/shard_map/ppermute | solution.py:438
  30.0 5.1 %collective-permute-start.9 = (bf16[256,1536]{1,0:T(8,128)(2,1)S(1)}, bf16[256,1536]{1,0:T(8,128)(2,1)S(1)}, u32[]{:S(2)}, u32[]{:S(2)}) collective-permute-start(bf16[256,1536]{1,0:T(8,128)(2,1)S(1)} %collective-permute-done.8.refs_1_.refs_5_.refs_9_.refs_13_), channel_id=1, source_target_pairs={{0,4},{4,0},{8,12},{12,8},{16,20},{20,16},{24,28},{28,24},{1,5},{5... | collective-permute-start | bytes 2359304 | tf_op jit(solution)/shard_map/ppermute | solution.py:427
  30.8 26.5 %collective-permute-start.14 = (bf16[4096,256]{1,0:T(8,128)(2,1)S(1)}, bf16[4096,256]{1,0:T(8,128)(2,1)S(1)}, u32[]{:S(2)}, u32[]{:S(2)}) collective-permute-start(bf16[4096,256]{1,0:T(8,128)(2,1)S(1)} %assemble.1.own_ref), channel_id=1, source_target_pairs={{0,4},{4,0},{8,12},{12,8},{16,20},{20,16},{24,28},{28,24},{1,5},{5... | collective-permute-start | bytes 6291464 | tf_op jit(solution)/shard_map/ppermute | solution.py:427
  36.0 5.0 %collective-permute-start.10 = (bf16[128,512]{1,0:T(8,128)(2,1)S(1)}, bf16[128,512]{1,0:T(8,128)(2,1)S(1)}, u32[]{:S(2)}, u32[]{:S(2)}) collective-permute-start(bf16[128,512]{1,0:T(8,128)(2,1)S(1)} %get-tuple-element.40), channel_id=1, source_target_pairs={{0,2},{1,3},{2,0},{3,1},{4,6},{5,7},{6,4},{7,5},{8,10},{9,11},{10,... | collective-permute-start | bytes 393224 | tf_op jit(solution)/shard_map/ppermute | solution.py:430
  37.1 5.1 %collective-permute-start.11 = (bf16[128,512]{1,0:T(8,128)(2,1)S(1)}, bf16[128,512]{1,0:T(8,128)(2,1)S(1)}, u32[]{:S(2)}, u32[]{:S(2)}) collective-permute-start(bf16[128,512]{1,0:T(8,128)(2,1)S(1)} %get-tuple-element.42), channel_id=1, source_target_pairs={{0,1},{1,0},{2,3},{3,2},{4,5},{5,4},{6,7},{7,6},{8,9},{9,8},{10,11... | collective-permute-start | bytes 393224 | tf_op jit(solution)/shard_map/ppermute | solution.py:430
  38.9 7.4 %collective-permute-start.6 = (bf16[256,512]{1,0:T(8,128)(2,1)S(1)}, bf16[256,512]{1,0:T(8,128)(2,1)S(1)}, u32[]{:S(2)}, u32[]{:S(2)}) collective-permute-start(bf16[256,512]{1,0:T(8,128)(2,1)S(1)} %terms_pair.1), channel_id=1, source_target_pairs={{0,8},{4,12},{8,0},{12,4},{16,24},{20,28},{24,16},{28,20},{1,9},{5... | collective-permute-start | bytes 786440 | tf_op jit(solution)/shard_map/ppermute | solution.py:438
  43.2 5.0 %collective-permute-start.16 = (bf16[256,256]{1,0:T(8,128)(2,1)S(1)}, bf16[256,256]{1,0:T(8,128)(2,1)S(1)}, u32[]{:S(2)}, u32[]{:S(2)}) collective-permute-start(bf16[256,256]{1,0:T(8,128)(2,1)S(1)} %get-tuple-element.53), channel_id=1, source_target_pairs={{0,1},{1,0},{2,3},{3,2},{4,5},{5,4},{6,7},{7,6},{8,9},{9,8},{10,11... | collective-permute-start | bytes 393224 | tf_op jit(solution)/shard_map/ppermute | solution.py:430
  44.3 5.0 %collective-permute-start.17 = (bf16[256,256]{1,0:T(8,128)(2,1)S(1)}, bf16[256,256]{1,0:T(8,128)(2,1)S(1)}, u32[]{:S(2)}, u32[]{:S(2)}) collective-permute-start(bf16[256,256]{1,0:T(8,128)(2,1)S(1)} %get-tuple-element.54), channel_id=1, source_target_pairs={{0,2},{1,3},{2,0},{3,1},{4,6},{5,7},{6,4},{7,5},{8,10},{9,11},{10,... | collective-permute-start | bytes 393224 | tf_op jit(solution)/shard_map/ppermute | solution.py:430
  45.8 6.7 %collective-permute-start.12 = (bf16[256,256]{1,0:T(8,128)(2,1)S(1)}, bf16[256,256]{1,0:T(8,128)(2,1)S(1)}, u32[]{:S(2)}, u32[]{:S(2)}) collective-permute-start(bf16[256,256]{1,0:T(8,128)(2,1)S(1)} %get-tuple-element.43), channel_id=1, source_target_pairs={{0,1},{1,0},{2,3},{3,2},{4,5},{5,4},{6,7},{7,6},{8,9},{9,8},{10,11... | collective-permute-start | bytes 393224 | tf_op jit(solution)/shard_map/ppermute | solution.py:430
  46.3 6.2 %collective-permute-start.13 = (bf16[256,256]{1,0:T(8,128)(2,1)S(1)}, bf16[256,256]{1,0:T(8,128)(2,1)S(1)}, u32[]{:S(2)}, u32[]{:S(2)}) collective-permute-start(bf16[256,256]{1,0:T(8,128)(2,1)S(1)} %get-tuple-element.44), channel_id=1, source_target_pairs={{0,2},{1,3},{2,0},{3,1},{4,6},{5,7},{6,4},{7,5},{8,10},{9,11},{10,... | collective-permute-start | bytes 393224 | tf_op jit(solution)/shard_map/ppermute | solution.py:430
  49.8 7.4 %collective-permute-start.18 = (bf16[256,256]{1,0:T(8,128)(2,1)S(1)}, bf16[256,256]{1,0:T(8,128)(2,1)S(1)}, u32[]{:S(2)}, u32[]{:S(2)}) collective-permute-start(bf16[256,256]{1,0:T(8,128)(2,1)S(1)} %terms_0.3), channel_id=1, source_target_pairs={{0,16},{4,20},{8,24},{12,28},{16,0},{20,4},{24,8},{28,12},{1,17},{... | collective-permute-start | bytes 393224 | tf_op jit(solution)/shard_map/ppermute | solution.py:441
  53.1 6.3 %collective-permute-start.15 = (bf16[256,256]{1,0:T(8,128)(2,1)S(1)}, bf16[256,256]{1,0:T(8,128)(2,1)S(1)}, u32[]{:S(2)}, u32[]{:S(2)}) collective-permute-start(bf16[256,256]{1,0:T(8,128)(2,1)S(1)} %terms_0.2), channel_id=1, source_target_pairs={{0,16},{4,20},{8,24},{12,28},{16,0},{20,4},{24,8},{28,12},{1,17},{... | collective-permute-start | bytes 393224 | tf_op jit(solution)/shard_map/ppermute | solution.py:441
  59.5 9.5 %collective-permute-start.19 = (bf16[256,512]{1,0:T(8,128)(2,1)S(1)}, bf16[256,512]{1,0:T(8,128)(2,1)S(1)}, u32[]{:S(2)}, u32[]{:S(2)}) collective-permute-start(bf16[256,512]{1,0:T(8,128)(2,1)S(1)} %pad_maximum_fusion.own), channel_id=1, source_target_pairs={{0,8},{4,12},{8,0},{12,4},{16,24},{20,28},{24,16},{28,20},{1,9},{5... | collective-permute-start | bytes 786440 | tf_op jit(solution)/shard_map/ppermute | solution.py:438
  62.1 1.3 %collective-permute-start.21 = (bf16[256,256]{1,0:T(8,128)(2,1)S(1)}, bf16[256,256]{1,0:T(8,128)(2,1)S(1)}, u32[]{:S(2)}, u32[]{:S(2)}) collective-permute-start(bf16[256,256]{1,0:T(8,128)(2,1)S(1)} %add_convert_fusion), channel_id=1, source_target_pairs={{0,4},{4,0},{8,12},{12,8},{16,20},{20,16},{24,28},{28,24},{1,5},{5... | collective-permute-start | bytes 393224 | tf_op jit(solution)/shard_map/ppermute | solution.py:427
  62.1 1.5 %collective-permute-start.20 = (bf16[256,256]{1,0:T(8,128)(2,1)S(1)}, bf16[256,256]{1,0:T(8,128)(2,1)S(1)}, u32[]{:S(2)}, u32[]{:S(2)}) collective-permute-start(bf16[256,256]{1,0:T(8,128)(2,1)S(1)} %add_convert_fusion.1), channel_id=1, source_target_pairs={{0,4},{4,0},{8,12},{12,8},{16,20},{20,16},{24,28},{28,24},{1,5},{5... | collective-permute-start | bytes 393224 | tf_op jit(solution)/shard_map/ppermute | solution.py:427
  68.9 2.6 %collective-permute-start.22 = (bf16[256,512]{1,0:T(8,128)(2,1)S(1)}, bf16[256,512]{1,0:T(8,128)(2,1)S(1)}, u32[]{:S(2)}, u32[]{:S(2)}) collective-permute-start(bf16[256,512]{1,0:T(8,128)(2,1)S(1)} %collective-permute-done.19.own), channel_id=1, source_target_pairs={{0,4},{4,0},{8,12},{12,8},{16,20},{20,16},{24,28},{28,24},{1,5},{5... | collective-permute-start | bytes 786440 | tf_op jit(solution)/shard_map/ppermute | solution.py:427
  (3 other events, 19.9 us)

commit v10 on v8

--- a/solution.py
+++ b/solution.py
@@ -345,7 +345,7 @@
         ),
         input_output_aliases=aliases,
         compiler_params=pltpu.CompilerParams(vmem_limit_bytes=28 * MIB),
-        cost_estimate=busy(0.5),
+        cost_estimate=busy(6),
         name="update_step",
     )(where, *inputs)
 

time: 77.2 us -> 76.9 us (level)
  starting transfers between devices: 27.3 us -> 24.3 us
  waiting for transfers between devices: 25.4 us -> 28.1 us
    ppermute x4, starting transfers between devices: 7.53 us -> 5.27 us  [to_piece(): return lax.ppermute(x, 'dp', pairs)]
    ppermute x4, waiting for transfers between devices: 2.49 us -> 4.03 us  [to_piece(): return lax.ppermute(x, 'dp', pairs)]
    ppermute x2, waiting for transfers between devices: 3.89 us -> 4.84 us  [to_base(): lax.ppermute(x, 'dp', [(i, (i + k * pieces * CORES) % dp) for i in range(...]
where the time goes in v10:
time: 76.9 us; the launch traced here: 76.8 us
  waiting for transfers between devices  28.1 us (37%)
  starting transfers between devices  24.3 us (32%)
  Pallas kernels  23.3 us (30%)
  between operations  0.82 us (1%)
    ppermute x10, waiting for transfers between devices, to_fsdp(): return lax.ppermute(x, 'fsdp', [(i, i ^ s) for i in range(fsdp)])  16.8 us
    ppermute x10, starting transfers between devices, to_fsdp(): return lax.ppermute(x, 'fsdp', [(i, i ^ s) for i in range(fsdp)])  13.7 us
    pallas_call x2, Pallas kernels, update_step(): pl.pallas_call(body, out_shape=[jax.ShapeDtypeStruct(x.shape, F32) for x...  11.8 us
    pallas_call x10, Pallas kernels, call(): pl.pallas_call(body, out_shape=out_shape, grid_spec=pltpu.PrefetchScalarG...  9.28 us
    ppermute x4, starting transfers between devices, to_piece(): return lax.ppermute(x, 'dp', pairs)  5.27 us
    ppermute x2, waiting for transfers between devices, to_base(): lax.ppermute(x, 'dp', [(i, (i + k * pieces * CORES) % dp) for i in range(...  4.84 us
    ppermute x2, starting transfers between devices, to_base(): lax.ppermute(x, 'dp', [(i, (i + k * pieces * CORES) % dp) for i in range(...  4.09 us
    ppermute x4, waiting for transfers between devices, to_piece(): return lax.ppermute(x, 'dp', pairs)  4.03 us
  transfers between devices with their start and end apart: 23, of which 13 were waited for; matrix products, arithmetic and copies ran while one was open for 0% of the time, Pallas kernels for 23%

profile of v10, /device:TPU:0, one launch (start us, length us, event | category | flops | bytes accessed | tf_op | source)
XLA Modules:
  0.0 76.8 jit_solution(15661475907210403871)
XLA Ops:
  1.2 1.5 %cut_out.1 = (bf16[1024,256]{1,0:T(8,128)(2,1)S(1)}, bf16[256,1536]{1,0:T(8,128)(2,1)S(1)}) custom-call(s32[1]{0:T(128)} %bitcast.fsdp_ref, s32[1]{0:T(128)} %bitcast.1.core_ref, s32[1]{0:T(128)} %bitcast.2.piece_ref, bf16[1024,512]{1,0:T(8,128)(2,1)} %proj_ref.1, bf16[256,4096]{1,0:T(8,128)(2,1)} %refs_1_.3), custom_call_target="tpu_custom_call" | custom-call | flops 1150000000 | tf_op jit(solution)/shard_map/cut_out/pallas_call | solution.py:71
  2.6 2.6 %collective-permute-start.3 = (bf16[1024,256]{1,0:T(8,128)(2,1)S(1)}, bf16[1024,256]{1,0:T(8,128)(2,1)S(1)}, u32[]{:S(2)}, u32[]{:S(2)}) collective-permute-start(bf16[1024,256]{1,0:T(8,128)(2,1)S(1)} %get-tuple-element.41.refs_2_.refs_0_), channel_id=1, source_target_pairs={{0,1},{1,0},{2,3},{3,2},{4,5},{5,4},{6,7},{7,6},{8,9},{9,8},{10,11... | collective-permute-start | bytes 1572872 | tf_op jit(solution)/shard_map/ppermute | solution.py:383
  5.3 1.5 %collective-permute-start.1 = (bf16[1024,256]{1,0:T(8,128)(2,1)S(1)}, bf16[1024,256]{1,0:T(8,128)(2,1)S(1)}, u32[]{:S(2)}, u32[]{:S(2)}) collective-permute-start(bf16[1024,256]{1,0:T(8,128)(2,1)S(1)} %get-tuple-element.41.refs_2_.refs_0_), channel_id=1, source_target_pairs={{0,2},{1,3},{2,0},{3,1},{4,6},{5,7},{6,4},{7,5},{8,10},{9,11},{10,... | collective-permute-start | bytes 1572872 | tf_op jit(solution)/shard_map/ppermute | solution.py:383
  6.8 1.6 %collective-permute-start.8 = (bf16[256,1536]{1,0:T(8,128)(2,1)S(1)}, bf16[256,1536]{1,0:T(8,128)(2,1)S(1)}, u32[]{:S(2)}, u32[]{:S(2)}) collective-permute-start(bf16[256,1536]{1,0:T(8,128)(2,1)S(1)} %get-tuple-element.32), channel_id=1, source_target_pairs={{0,8},{4,12},{8,0},{12,4},{16,24},{20,28},{24,16},{28,20},{1,9},{5... | collective-permute-start | bytes 2359304 | tf_op jit(solution)/shard_map/ppermute | solution.py:391
  8.4 9.3 %collective-permute-done.3.refs_2_.refs_1_ = bf16[1024,256]{1,0:T(8,128)(2,1)S(1)} collective-permute-done((bf16[1024,256]{1,0:T(8,128)(2,1)S(1)}, bf16[1024,256]{1,0:T(8,128)(2,1)S(1)}, u32[]{:S(2)}, u32[]{:S(2)}) %collective-permute-start.3) | collective-permute-done | bytes 524320 | tf_op jit(solution)/shard_map/ppermute | solution.py:383
  17.8 1.8 %collective-permute-start.4 = (bf16[512,256]{1,0:T(8,128)(2,1)S(1)}, bf16[512,256]{1,0:T(8,128)(2,1)S(1)}, u32[]{:S(2)}, u32[]{:S(2)}) collective-permute-start(bf16[512,256]{1,0:T(8,128)(2,1)S(1)} %slice.9), channel_id=1, source_target_pairs={{0,2},{1,3},{2,0},{3,1},{4,6},{5,7},{6,4},{7,5},{8,10},{9,11},{10,... | collective-permute-start | bytes 786440 | tf_op jit(solution)/shard_map/ppermute | solution.py:383
  19.7 1.6 %collective-permute-start.2 = (bf16[512,256]{1,0:T(8,128)(2,1)S(1)}, bf16[512,256]{1,0:T(8,128)(2,1)S(1)}, u32[]{:S(2)}, u32[]{:S(2)}) collective-permute-start(bf16[512,256]{1,0:T(8,128)(2,1)S(1)} %slice.8), channel_id=1, source_target_pairs={{0,1},{1,0},{2,3},{3,2},{4,5},{5,4},{6,7},{7,6},{8,9},{9,8},{10,11... | collective-permute-start | bytes 786440 | tf_op jit(solution)/shard_map/ppermute | solution.py:383
  22.2 1.3 %coords_1.1.refs_6_ = f32[512,256]{1,0:T(8,128)S(1)} custom-call(s32[3]{0:T(128)S(1)} %pad_add_fusion.w, bf16[256,4096]{1,0:T(8,128)(2,1)S(1)} %copy-done.3, bf16[256,4096]{1,0:T(8,128)(2,1)S(1)} %collective-permute-done.refs_1_.refs_4_, bf16[1024,256]{1,0:T(8,128)(2,1)S(1)} %collective-permute-done.3.refs_2_.refs_1_, bf16[256,4096]{1,0:T(8,128)(2,1)S(1)} %copy-done.3, ...), custom_call_target="tpu_custom_call" | custom-call | flops 9200000000 | tf_op jit(solution)/shard_map/coords_1/pallas_call | solution.py:31
  23.5 2.5 %collective-permute-done.4.refs_5_.refs_4_ = bf16[512,256]{1,0:T(8,128)(2,1)S(1)} collective-permute-done((bf16[512,256]{1,0:T(8,128)(2,1)S(1)}, bf16[512,256]{1,0:T(8,128)(2,1)S(1)}, u32[]{:S(2)}, u32[]{:S(2)}) %collective-permute-start.4) | collective-permute-done | bytes 262176 | tf_op jit(solution)/shard_map/ppermute | solution.py:383
  25.9 1.4 %collective-permute-done.2.refs_2_.refs_3_ = bf16[512,256]{1,0:T(8,128)(2,1)S(1)} collective-permute-done((bf16[512,256]{1,0:T(8,128)(2,1)S(1)}, bf16[512,256]{1,0:T(8,128)(2,1)S(1)}, u32[]{:S(2)}, u32[]{:S(2)}) %collective-permute-start.2) | collective-permute-done | bytes 262176 | tf_op jit(solution)/shard_map/ppermute | solution.py:383
  28.4 1.6 %collective-permute-start.7 = (bf16[256,512]{1,0:T(8,128)(2,1)S(1)}, bf16[256,512]{1,0:T(8,128)(2,1)S(1)}, u32[]{:S(2)}, u32[]{:S(2)}) collective-permute-start(bf16[256,512]{1,0:T(8,128)(2,1)S(1)} %coords_2.1.refs_0_), channel_id=1, source_target_pairs={{0,8},{4,12},{8,0},{12,4},{16,24},{20,28},{24,16},{28,20},{1,9},{5... | collective-permute-start | bytes 786440 | tf_op jit(solution)/shard_map/ppermute | solution.py:391
  31.4 1.2 %terms_chip.1 = (f32[256,512]{1,0:T(8,128)S(1)}, f32[256,512]{1,0:T(8,128)S(1)}, f32[256,512]{1,0:T(8,128)S(1)}, f32[256,512]{1,0:T(8,128)S(1)}) custom-call(s32[3]{0:T(128)S(1)} %pad_add_fusion.w, bf16[256,512]{1,0:T(8,128)(2,1)S(1)} %coords_2.1.refs_0_, bf16[256,4096]{1,0:T(8,128)(2,1)S(1)} %copy-done.2, ...), custom_call_target="tpu_custom_call" | custom-call | flops 13799999488 | tf_op jit(solution)/shard_map/terms_chip/pallas_call | solution.py:31
  32.6 2.5 %collective-permute-done.7.refs_0_ = bf16[256,512]{1,0:T(8,128)(2,1)S(1)} collective-permute-done((bf16[256,512]{1,0:T(8,128)(2,1)S(1)}, bf16[256,512]{1,0:T(8,128)(2,1)S(1)}, u32[]{:S(2)}, u32[]{:S(2)}) %collective-permute-start.7) | collective-permute-done | bytes 262176 | tf_op jit(solution)/shard_map/ppermute | solution.py:391
  38.9 1.6 %collective-permute-start.6 = (bf16[256,512]{1,0:T(8,128)(2,1)S(1)}, bf16[256,512]{1,0:T(8,128)(2,1)S(1)}, u32[]{:S(2)}, u32[]{:S(2)}) collective-permute-start(bf16[256,512]{1,0:T(8,128)(2,1)S(1)} %terms_pair.1), channel_id=1, source_target_pairs={{0,8},{4,12},{8,0},{12,4},{16,24},{20,28},{24,16},{28,20},{1,9},{5... | collective-permute-start | bytes 786440 | tf_op jit(solution)/shard_map/ppermute | solution.py:391
  41.0 1.2 %collective-permute-done.11.refs_8_.refs_16_ = bf16[128,512]{1,0:T(8,128)(2,1)S(1)} collective-permute-done((bf16[128,512]{1,0:T(8,128)(2,1)S(1)}, bf16[128,512]{1,0:T(8,128)(2,1)S(1)}, u32[]{:S(2)}, u32[]{:S(2)}) %collective-permute-start.11) | collective-permute-done | bytes 131104 | tf_op jit(solution)/shard_map/ppermute | solution.py:383
  44.3 1.5 %collective-permute-start.17 = (bf16[256,256]{1,0:T(8,128)(2,1)S(1)}, bf16[256,256]{1,0:T(8,128)(2,1)S(1)}, u32[]{:S(2)}, u32[]{:S(2)}) collective-permute-start(bf16[256,256]{1,0:T(8,128)(2,1)S(1)} %get-tuple-element.50), channel_id=1, source_target_pairs={{0,2},{1,3},{2,0},{3,1},{4,6},{5,7},{6,4},{7,5},{8,10},{9,11},{10,... | collective-permute-start | bytes 393224 | tf_op jit(solution)/shard_map/ppermute | solution.py:383
  49.8 2.6 %collective-permute-start.18 = (bf16[256,256]{1,0:T(8,128)(2,1)S(1)}, bf16[256,256]{1,0:T(8,128)(2,1)S(1)}, u32[]{:S(2)}, u32[]{:S(2)}) collective-permute-start(bf16[256,256]{1,0:T(8,128)(2,1)S(1)} %terms_0.3), channel_id=1, source_target_pairs={{0,16},{4,20},{8,24},{12,28},{16,0},{20,4},{24,8},{28,12},{1,17},{... | collective-permute-start | bytes 393224 | tf_op jit(solution)/shard_map/ppermute | solution.py:394
  53.1 1.5 %collective-permute-start.15 = (bf16[256,256]{1,0:T(8,128)(2,1)S(1)}, bf16[256,256]{1,0:T(8,128)(2,1)S(1)}, u32[]{:S(2)}, u32[]{:S(2)}) collective-permute-start(bf16[256,256]{1,0:T(8,128)(2,1)S(1)} %terms_0.2), channel_id=1, source_target_pairs={{0,16},{4,20},{8,24},{12,28},{16,0},{20,4},{24,8},{28,12},{1,17},{... | collective-permute-start | bytes 393224 | tf_op jit(solution)/shard_map/ppermute | solution.py:394
  54.5 2.6 %collective-permute-done.18 = bf16[256,256]{1,0:T(8,128)(2,1)S(1)} collective-permute-done((bf16[256,256]{1,0:T(8,128)(2,1)S(1)}, bf16[256,256]{1,0:T(8,128)(2,1)S(1)}, u32[]{:S(2)}, u32[]{:S(2)}) %collective-permute-start.18) | collective-permute-done | bytes 131104 | tf_op jit(solution)/shard_map/ppermute | solution.py:394
  58.2 2.2 %collective-permute-done.15 = bf16[256,256]{1,0:T(8,128)(2,1)S(1)} collective-permute-done((bf16[256,256]{1,0:T(8,128)(2,1)S(1)}, bf16[256,256]{1,0:T(8,128)(2,1)S(1)}, u32[]{:S(2)}, u32[]{:S(2)}) %collective-permute-start.15) | collective-permute-done | bytes 131104 | tf_op jit(solution)/shard_map/ppermute | solution.py:394
  61.9 5.9 %update_step.2 = (f32[1024,512]{1,0:T(8,128)}, f32[1024,512]{1,0:T(8,128)}, f32[4096,1024]{1,0:T(8,128)}) custom-call(s32[3]{0:T(128)S(1)} %pad_add_fusion.w, bf16[256,512]{1,0:T(8,128)(2,1)S(1)} %pad_maximum_fusion.own, bf16[256,256]{1,0:T(8,128)(2,1)S(1)} %collective-permute-done.20.refs_0_, bf16[256,256]{1,0:T(8,128)(2,1)S(1)} %collective-permute-done.21.refs_1_, ...), custom_call_target="tpu_custom_call" | custom-call | flops 6899999744 | tf_op jit(solution)/shard_map/update_step/pallas_call | solution.py:327
  67.8 1.5 %collective-permute-done.19.own = bf16[256,512]{1,0:T(8,128)(2,1)S(1)} collective-permute-done((bf16[256,512]{1,0:T(8,128)(2,1)S(1)}, bf16[256,512]{1,0:T(8,128)(2,1)S(1)}, u32[]{:S(2)}, u32[]{:S(2)}) %collective-permute-start.19) | collective-permute-done | bytes 262176 | tf_op jit(solution)/shard_map/ppermute | solution.py:391
  69.3 1.5 %collective-permute-done.22.refs_0_ = bf16[256,512]{1,0:T(8,128)(2,1)S(1)} collective-permute-done((bf16[256,512]{1,0:T(8,128)(2,1)S(1)}, bf16[256,512]{1,0:T(8,128)(2,1)S(1)}, u32[]{:S(2)}, u32[]{:S(2)}) %collective-permute-start.22) | collective-permute-done | bytes 262176 | tf_op jit(solution)/shard_map/ppermute | solution.py:380
  70.9 5.9 %update_step.3 = (f32[1024,512]{1,0:T(8,128)}, f32[1024,512]{1,0:T(8,128)}, f32[4096,1024]{1,0:T(8,128)}) custom-call(s32[3]{0:T(128)S(1)} %pad_add_fusion.w, bf16[256,512]{1,0:T(8,128)(2,1)S(1)} %collective-permute-done.19.own, bf16[256,512]{1,0:T(8,128)(2,1)S(1)} %collective-permute-done.22.refs_0_, ...), custom_call_target="tpu_custom_call", output_to_operand_aliasing={{0}: (6, {}), {1}: (7, {}), {2}: (8, {})} | custom-call | flops 6899999744 | tf_op jit(solution)/shard_map/update_step/pallas_call | solution.py:327
  (50 shorter events, 17.4 us)
Async XLA Ops:
  0.6 20.6 %collective-permute-start = (bf16[256,4096]{1,0:T(8,128)(2,1)}, bf16[256,4096]{1,0:T(8,128)(2,1)S(1)}, u32[]{:S(2)}, u32[]{:S(2)}) collective-permute-start(bf16[256,4096]{1,0:T(8,128)(2,1)} %refs_3_.6), channel_id=1, source_target_pairs={{0,4},{4,0},{8,12},{12,8},{16,20},{20,16},{24,28},{28,24},{1,5},{5... | collective-permute-start | bytes 6291464 | tf_op jit(solution)/shard_map/ppermute | solution.py:380
  1.2 20.1 %copy-start.3 = (bf16[256,4096]{1,0:T(8,128)(2,1)S(1)}, bf16[256,4096]{1,0:T(8,128)(2,1)}, u32[]{:S(2)}) copy-start(bf16[256,4096]{1,0:T(8,128)(2,1)} %refs_3_.6) | copy-start | bytes 6291460
  2.6 15.2 %collective-permute-start.3 = (bf16[1024,256]{1,0:T(8,128)(2,1)S(1)}, bf16[1024,256]{1,0:T(8,128)(2,1)S(1)}, u32[]{:S(2)}, u32[]{:S(2)}) collective-permute-start(bf16[1024,256]{1,0:T(8,128)(2,1)S(1)} %get-tuple-element.41.refs_2_.refs_0_), channel_id=1, source_target_pairs={{0,1},{1,0},{2,3},{3,2},{4,5},{5,4},{6,7},{7,6},{8,9},{9,8},{10,11... | collective-permute-start | bytes 1572872 | tf_op jit(solution)/shard_map/ppermute | solution.py:383
  5.3 14.4 %collective-permute-start.1 = (bf16[1024,256]{1,0:T(8,128)(2,1)S(1)}, bf16[1024,256]{1,0:T(8,128)(2,1)S(1)}, u32[]{:S(2)}, u32[]{:S(2)}) collective-permute-start(bf16[1024,256]{1,0:T(8,128)(2,1)S(1)} %get-tuple-element.41.refs_2_.refs_0_), channel_id=1, source_target_pairs={{0,2},{1,3},{2,0},{3,1},{4,6},{5,7},{6,4},{7,5},{8,10},{9,11},{10,... | collective-permute-start | bytes 1572872 | tf_op jit(solution)/shard_map/ppermute | solution.py:383
  6.8 23.3 %collective-permute-start.8 = (bf16[256,1536]{1,0:T(8,128)(2,1)S(1)}, bf16[256,1536]{1,0:T(8,128)(2,1)S(1)}, u32[]{:S(2)}, u32[]{:S(2)}) collective-permute-start(bf16[256,1536]{1,0:T(8,128)(2,1)S(1)} %get-tuple-element.32), channel_id=1, source_target_pairs={{0,8},{4,12},{8,0},{12,4},{16,24},{20,28},{24,16},{28,20},{1,9},{5... | collective-permute-start | bytes 2359304 | tf_op jit(solution)/shard_map/ppermute | solution.py:391
  8.4 23.0 %collective-permute-start.5 = (bf16[256,4096]{1,0:T(8,128)(2,1)S(1)}, bf16[256,4096]{1,0:T(8,128)(2,1)S(1)}, u32[]{:S(2)}, u32[]{:S(2)}) collective-permute-start(bf16[256,4096]{1,0:T(8,128)(2,1)S(1)} %copy-done.2), channel_id=1, source_target_pairs={{0,4},{4,0},{8,12},{12,8},{16,20},{20,16},{24,28},{28,24},{1,5},{5... | collective-permute-start | bytes 6291464 | tf_op jit(solution)/shard_map/ppermute | solution.py:380
  17.8 8.1 %collective-permute-start.4 = (bf16[512,256]{1,0:T(8,128)(2,1)S(1)}, bf16[512,256]{1,0:T(8,128)(2,1)S(1)}, u32[]{:S(2)}, u32[]{:S(2)}) collective-permute-start(bf16[512,256]{1,0:T(8,128)(2,1)S(1)} %slice.9), channel_id=1, source_target_pairs={{0,2},{1,3},{2,0},{3,1},{4,6},{5,7},{6,4},{7,5},{8,10},{9,11},{10,... | collective-permute-start | bytes 786440 | tf_op jit(solution)/shard_map/ppermute | solution.py:383
  19.7 7.6 %collective-permute-start.2 = (bf16[512,256]{1,0:T(8,128)(2,1)S(1)}, bf16[512,256]{1,0:T(8,128)(2,1)S(1)}, u32[]{:S(2)}, u32[]{:S(2)}) collective-permute-start(bf16[512,256]{1,0:T(8,128)(2,1)S(1)} %slice.8), channel_id=1, source_target_pairs={{0,1},{1,0},{2,3},{3,2},{4,5},{5,4},{6,7},{7,6},{8,9},{9,8},{10,11... | collective-permute-start | bytes 786440 | tf_op jit(solution)/shard_map/ppermute | solution.py:383
  28.4 6.7 %collective-permute-start.7 = (bf16[256,512]{1,0:T(8,128)(2,1)S(1)}, bf16[256,512]{1,0:T(8,128)(2,1)S(1)}, u32[]{:S(2)}, u32[]{:S(2)}) collective-permute-start(bf16[256,512]{1,0:T(8,128)(2,1)S(1)} %coords_2.1.refs_0_), channel_id=1, source_target_pairs={{0,8},{4,12},{8,0},{12,4},{16,24},{20,28},{24,16},{28,20},{1,9},{5... | collective-permute-start | bytes 786440 | tf_op jit(solution)/shard_map/ppermute | solution.py:391
  30.0 5.1 %collective-permute-start.9 = (bf16[256,1536]{1,0:T(8,128)(2,1)S(1)}, bf16[256,1536]{1,0:T(8,128)(2,1)S(1)}, u32[]{:S(2)}, u32[]{:S(2)}) collective-permute-start(bf16[256,1536]{1,0:T(8,128)(2,1)S(1)} %collective-permute-done.8.refs_1_.refs_5_.refs_9_.refs_13_), channel_id=1, source_target_pairs={{0,4},{4,0},{8,12},{12,8},{16,20},{20,16},{24,28},{28,24},{1,5},{5... | collective-permute-start | bytes 2359304 | tf_op jit(solution)/shard_map/ppermute | solution.py:380
  30.8 26.5 %collective-permute-start.14 = (bf16[4096,256]{1,0:T(8,128)(2,1)S(1)}, bf16[4096,256]{1,0:T(8,128)(2,1)S(1)}, u32[]{:S(2)}, u32[]{:S(2)}) collective-permute-start(bf16[4096,256]{1,0:T(8,128)(2,1)S(1)} %assemble.1.own_ref), channel_id=1, source_target_pairs={{0,4},{4,0},{8,12},{12,8},{16,20},{20,16},{24,28},{28,24},{1,5},{5... | collective-permute-start | bytes 6291464 | tf_op jit(solution)/shard_map/ppermute | solution.py:380
  36.0 5.0 %collective-permute-start.10 = (bf16[128,512]{1,0:T(8,128)(2,1)S(1)}, bf16[128,512]{1,0:T(8,128)(2,1)S(1)}, u32[]{:S(2)}, u32[]{:S(2)}) collective-permute-start(bf16[128,512]{1,0:T(8,128)(2,1)S(1)} %get-tuple-element.36), channel_id=1, source_target_pairs={{0,2},{1,3},{2,0},{3,1},{4,6},{5,7},{6,4},{7,5},{8,10},{9,11},{10,... | collective-permute-start | bytes 393224 | tf_op jit(solution)/shard_map/ppermute | solution.py:383
  37.1 5.1 %collective-permute-start.11 = (bf16[128,512]{1,0:T(8,128)(2,1)S(1)}, bf16[128,512]{1,0:T(8,128)(2,1)S(1)}, u32[]{:S(2)}, u32[]{:S(2)}) collective-permute-start(bf16[128,512]{1,0:T(8,128)(2,1)S(1)} %get-tuple-element.38), channel_id=1, source_target_pairs={{0,1},{1,0},{2,3},{3,2},{4,5},{5,4},{6,7},{7,6},{8,9},{9,8},{10,11... | collective-permute-start | bytes 393224 | tf_op jit(solution)/shard_map/ppermute | solution.py:383
  38.9 7.4 %collective-permute-start.6 = (bf16[256,512]{1,0:T(8,128)(2,1)S(1)}, bf16[256,512]{1,0:T(8,128)(2,1)S(1)}, u32[]{:S(2)}, u32[]{:S(2)}) collective-permute-start(bf16[256,512]{1,0:T(8,128)(2,1)S(1)} %terms_pair.1), channel_id=1, source_target_pairs={{0,8},{4,12},{8,0},{12,4},{16,24},{20,28},{24,16},{28,20},{1,9},{5... | collective-permute-start | bytes 786440 | tf_op jit(solution)/shard_map/ppermute | solution.py:391
  43.2 5.0 %collective-permute-start.16 = (bf16[256,256]{1,0:T(8,128)(2,1)S(1)}, bf16[256,256]{1,0:T(8,128)(2,1)S(1)}, u32[]{:S(2)}, u32[]{:S(2)}) collective-permute-start(bf16[256,256]{1,0:T(8,128)(2,1)S(1)} %get-tuple-element.49), channel_id=1, source_target_pairs={{0,1},{1,0},{2,3},{3,2},{4,5},{5,4},{6,7},{7,6},{8,9},{9,8},{10,11... | collective-permute-start | bytes 393224 | tf_op jit(solution)/shard_map/ppermute | solution.py:383
  44.3 5.0 %collective-permute-start.17 = (bf16[256,256]{1,0:T(8,128)(2,1)S(1)}, bf16[256,256]{1,0:T(8,128)(2,1)S(1)}, u32[]{:S(2)}, u32[]{:S(2)}) collective-permute-start(bf16[256,256]{1,0:T(8,128)(2,1)S(1)} %get-tuple-element.50), channel_id=1, source_target_pairs={{0,2},{1,3},{2,0},{3,1},{4,6},{5,7},{6,4},{7,5},{8,10},{9,11},{10,... | collective-permute-start | bytes 393224 | tf_op jit(solution)/shard_map/ppermute | solution.py:383
  45.8 6.7 %collective-permute-start.12 = (bf16[256,256]{1,0:T(8,128)(2,1)S(1)}, bf16[256,256]{1,0:T(8,128)(2,1)S(1)}, u32[]{:S(2)}, u32[]{:S(2)}) collective-permute-start(bf16[256,256]{1,0:T(8,128)(2,1)S(1)} %get-tuple-element.39), channel_id=1, source_target_pairs={{0,1},{1,0},{2,3},{3,2},{4,5},{5,4},{6,7},{7,6},{8,9},{9,8},{10,11... | collective-permute-start | bytes 393224 | tf_op jit(solution)/shard_map/ppermute | solution.py:383
  46.3 6.2 %collective-permute-start.13 = (bf16[256,256]{1,0:T(8,128)(2,1)S(1)}, bf16[256,256]{1,0:T(8,128)(2,1)S(1)}, u32[]{:S(2)}, u32[]{:S(2)}) collective-permute-start(bf16[256,256]{1,0:T(8,128)(2,1)S(1)} %get-tuple-element.40), channel_id=1, source_target_pairs={{0,2},{1,3},{2,0},{3,1},{4,6},{5,7},{6,4},{7,5},{8,10},{9,11},{10,... | collective-permute-start | bytes 393224 | tf_op jit(solution)/shard_map/ppermute | solution.py:383
  49.8 7.3 %collective-permute-start.18 = (bf16[256,256]{1,0:T(8,128)(2,1)S(1)}, bf16[256,256]{1,0:T(8,128)(2,1)S(1)}, u32[]{:S(2)}, u32[]{:S(2)}) collective-permute-start(bf16[256,256]{1,0:T(8,128)(2,1)S(1)} %terms_0.3), channel_id=1, source_target_pairs={{0,16},{4,20},{8,24},{12,28},{16,0},{20,4},{24,8},{28,12},{1,17},{... | collective-permute-start | bytes 393224 | tf_op jit(solution)/shard_map/ppermute | solution.py:394
  53.1 7.3 %collective-permute-start.15 = (bf16[256,256]{1,0:T(8,128)(2,1)S(1)}, bf16[256,256]{1,0:T(8,128)(2,1)S(1)}, u32[]{:S(2)}, u32[]{:S(2)}) collective-permute-start(bf16[256,256]{1,0:T(8,128)(2,1)S(1)} %terms_0.2), channel_id=1, source_target_pairs={{0,16},{4,20},{8,24},{12,28},{16,0},{20,4},{24,8},{28,12},{1,17},{... | collective-permute-start | bytes 393224 | tf_op jit(solution)/shard_map/ppermute | solution.py:394
  57.2 3.7 %collective-permute-start.21 = (bf16[256,256]{1,0:T(8,128)(2,1)S(1)}, bf16[256,256]{1,0:T(8,128)(2,1)S(1)}, u32[]{:S(2)}, u32[]{:S(2)}) collective-permute-start(bf16[256,256]{1,0:T(8,128)(2,1)S(1)} %add_convert_fusion), channel_id=1, source_target_pairs={{0,4},{4,0},{8,12},{12,8},{16,20},{20,16},{24,28},{28,24},{1,5},{5... | collective-permute-start | bytes 393224 | tf_op jit(solution)/shard_map/ppermute | solution.py:380
  60.5 1.4 %collective-permute-start.20 = (bf16[256,256]{1,0:T(8,128)(2,1)S(1)}, bf16[256,256]{1,0:T(8,128)(2,1)S(1)}, u32[]{:S(2)}, u32[]{:S(2)}) collective-permute-start(bf16[256,256]{1,0:T(8,128)(2,1)S(1)} %add_convert_fusion.1), channel_id=1, source_target_pairs={{0,4},{4,0},{8,12},{12,8},{16,20},{20,16},{24,28},{28,24},{1,5},{5... | collective-permute-start | bytes 393224 | tf_op jit(solution)/shard_map/ppermute | solution.py:380
  60.6 8.8 %collective-permute-start.19 = (bf16[256,512]{1,0:T(8,128)(2,1)S(1)}, bf16[256,512]{1,0:T(8,128)(2,1)S(1)}, u32[]{:S(2)}, u32[]{:S(2)}) collective-permute-start(bf16[256,512]{1,0:T(8,128)(2,1)S(1)} %pad_maximum_fusion.own), channel_id=1, source_target_pairs={{0,8},{4,12},{8,0},{12,4},{16,24},{20,28},{24,16},{28,20},{1,9},{5... | collective-permute-start | bytes 786440 | tf_op jit(solution)/shard_map/ppermute | solution.py:391
  69.3 1.5 %collective-permute-start.22 = (bf16[256,512]{1,0:T(8,128)(2,1)S(1)}, bf16[256,512]{1,0:T(8,128)(2,1)S(1)}, u32[]{:S(2)}, u32[]{:S(2)}) collective-permute-start(bf16[256,512]{1,0:T(8,128)(2,1)S(1)} %collective-permute-done.19.own), channel_id=1, source_target_pairs={{0,4},{4,0},{8,12},{12,8},{16,20},{20,16},{24,28},{28,24},{1,5},{5... | collective-permute-start | bytes 786440 | tf_op jit(solution)/shard_map/ppermute | solution.py:380
  (3 other events, 16.5 us)
